TPU v7x, 32 devices: a whole 2x2x4 slice. The times are simulated.
32 devices in a mesh: parts: 2 (over y), dp: 4 (over z), tensor: 2 (over x), sub: 2 (over core).
Axes of the slice: x: 2, y: 2, z: 4, core: 2. Of those that a mesh axis runs over, the one named last changes fastest.
Arguments:
- tokens: bfloat16 [6144, 8192], P(('parts', 'dp'), ('tensor', 'sub')), parts along dimension 0, may hold values from -6 to 6
- key_value_weight: bfloat16 [8192, 1024], P(('tensor', 'sub')), may hold values from -0.09375 to 0.09375
- adapter_down_weight: bfloat16 [96, 128, 8192], P('dp', None, ('tensor', 'sub')), may hold values from -0.0625 to 0.0625
- adapter_up_weight: bfloat16 [96, 64, 1024], P('dp', None, ('tensor', 'sub')), may hold values from -0.75 to 0.75
- adapter_scale: float32 [96], P('dp'), may hold values from 0.5 to 2
- token_adapter_index: int32 [6144, 1], P(('parts', 'dp')), parts along dimension 0, may hold values from 0 to 95; in each aligned block of 768 rows (0 to 767, 768 to 1535, ...) at most 12 rows name the same one
Outputs:
- kv_out: bfloat16 [6144, 1024], P(('parts', 'dp'), ('tensor', 'sub')), parts along dimension 0
There are 2 independent parts, one for each index of `parts`. A program takes and returns all parts, laid end to end along the dimension named above; an argument that names none is the same for every part. Nothing has to cross between parts.
Inputs may be any that keep to these rules, and one draw needn't show every extreme that they name: `token_adapter_index`: within the 768 rows of one index of dp no adapter is named by more than 12 rows, and one adapter is named by exactly 12 rows of some index; every adapter is named by some row.
All inputs are finite; a program needn't handle non-finite values.
Results may differ from a plain program's by a relative error of at most 0.001.
Values may be sent and summed in bfloat16 or wider, within the bound.
No kernel may reach another device: no remote copies, remote signals or barrier semaphores. Data moves between devices by JAX's collectives and lax.ppermute only.
A program may use at most 128 MiB of HBM per device.

v0:
```python
import jax
import jax.numpy as jnp
from jax import lax
from jax.sharding import PartitionSpec as P

ADAPTER_RANK = 64
ADAPTER_COUNT = 96
TOKEN_LIMIT = 12


def local(
    tokens,
    key_value_weight,
    adapter_down_weight,
    adapter_up_weight,
    adapter_scale,
    token_adapter_index,
):
    row_count, local_width = tokens.shape
    owner_indices = lax.axis_size("dp")
    owned_count = adapter_down_weight.shape[0]
    slot_total = ADAPTER_COUNT * TOKEN_LIMIT
    width_halved = key_value_weight.shape[1] // 2
    adapter_ids = token_adapter_index[:, 0]
    onehot = (adapter_ids[:, None] == jnp.arange(ADAPTER_COUNT, dtype=jnp.int32)[None, :]).astype(
        jnp.int32
    )
    before = jnp.cumsum(onehot, axis=0) - onehot
    slot_rank = jnp.sum(before * onehot, axis=1)
    target = adapter_ids * TOKEN_LIMIT + slot_rank
    slot_row = (
        jnp.zeros((slot_total,), jnp.int32).at[target].set(jnp.arange(row_count, dtype=jnp.int32))
    )
    filled = jnp.zeros((slot_total,), jnp.bool_).at[target].set(True)
    outgoing = jnp.where(filled[:, None], tokens[slot_row], jnp.zeros((), tokens.dtype))
    received_rows = lax.all_to_all(
        outgoing.reshape(owner_indices, owned_count * TOKEN_LIMIT, local_width),
        "dp",
        split_axis=0,
        concat_axis=0,
        tiled=True,
    )
    received_rows = received_rows.reshape(owner_indices, owned_count, TOKEN_LIMIT, local_width)
    shrink_part = jnp.einsum(
        "fhyz,hbz->fhyb", received_rows, adapter_down_weight, preferred_element_type=jnp.float32
    )
    base_part = jnp.dot(tokens, key_value_weight, preferred_element_type=jnp.float32)
    scale_broadcast = adapter_scale[None, :, None, None]
    up_matrix_whole = lax.all_gather(
        adapter_up_weight, ("tensor", "sub"), axis=2, tiled=True
    ).astype(jnp.float32)
    key_portion = jnp.einsum(
        "samr,arc->samc",
        shrink_part[..., :ADAPTER_RANK],
        up_matrix_whole[:, :, :width_halved],
        precision=lax.Precision.HIGHEST,
    )
    value_portion = jnp.einsum(
        "samr,arc->samc",
        shrink_part[..., ADAPTER_RANK:],
        up_matrix_whole[:, :, width_halved:],
        precision=lax.Precision.HIGHEST,
    )
    adapter_update = jnp.concatenate([key_portion, value_portion], axis=3) * scale_broadcast
    returned = lax.all_to_all(
        adapter_update.reshape(owner_indices, owned_count * TOKEN_LIMIT, 2 * width_halved),
        "dp",
        split_axis=0,
        concat_axis=0,
        tiled=True,
    )
    returned = returned.reshape(slot_total, 2 * width_halved)
    combined = base_part + returned[target]
    result = lax.psum_scatter(combined, ("tensor", "sub"), scatter_dimension=1, tiled=True)
    return result.astype(jnp.bfloat16)


def solution(mesh):
    return jax.shard_map(
        local,
        mesh=mesh,
        in_specs=(
            P(("parts", "dp"), ("tensor", "sub")),
            P(("tensor", "sub"), None),
            P("dp", None, ("tensor", "sub")),
            P("dp", None, ("tensor", "sub")),
            P("dp"),
            P(("parts", "dp"), None),
        ),
        out_specs=P(("parts", "dp"), ("tensor", "sub")),
        check_vma=False,
    )
```

profile of v0, /device:TPU:0, one launch (start us, length us, event | category | flops | bytes accessed | tf_op | source)
XLA Modules:
  0.0 344.5 jit_solution(17744193605786957264)
XLA Ops:
  6.5 0.0 copy-start
  6.5 0.8 reduce
  7.4 0.7 fusion.13
  8.1 3.6 %reduce-window.6 = s32[96,6,128]{2,0,1:T(8,128)S(1)} reduce-window(s32[96,6,128]{2,0,1:T(8,128)} %fusion.13, s32[]{:T(128)} %constant.9.clone.1), window={size=1x1x128 pad=0_0x0_0x127_0}, to_apply=%region_0.0 | reduce-window | flops 9363456 | bytes 589828 | tf_op jit(solution)/shard_map/reduce-window
  11.8 0.3 slice_reduce_fusion
  12.1 0.2 fusion.12
  12.2 0.7 fusion.18
  12.9 3.4 scatter_custom_fusion.1
  16.4 3.4 scatter_custom_fusion
  19.8 0.1 broadcast_in_dim.31
  19.9 0.0 copy-done
  19.9 5.9 %gather_fusion = bf16[1152,2048]{1,0:T(8,128)(2,1)} fusion(bf16[768,2048]{1,0:T(8,128)(2,1)S(1)} %copy-done, s32[2048]{0:T(1024)S(1)} %pad_clamp_fusion), kind=kCustom, calls=%fused_computation | custom fusion | bytes 9441792 | tf_op jit(solution)/shard_map/gather | solution.py:35
  25.8 4.9 %broadcast_select_fusion = bf16[4,288,2048]{2,1,0:T(8,128)(2,1)} fusion(bf16[4,288,2048]{2,1,0:T(8,128)(2,1)} %bitcast.52, pred[4,288]{1,0:T(4,128)(4,1)S(1)} %broadcast_in_dim.31), kind=kLoop, calls=%fused_computation.8 | loop fusion | flops 2359296 | bytes 9438336 | tf_op jit(solution)/shard_map/jit(_where)/select_n | solution.py:35
  30.7 0.0 copy-start.3
  30.7 6.4 %all-to-all-start = ((bf16[4,288,2048]{2,1,0:T(8,128)(2,1)}), bf16[4,288,2048]{2,1,0:T(8,128)(2,1)}, u32[]{:S(2)}, u32[]{:S(2)}) async-start(bf16[4,288,2048]{2,1,0:T(8,128)(2,1)} %broadcast_select_fusion), calls=%async_computation | async-start | bytes 9437184 | tf_op jit(solution)/shard_map/all_to_all | solution.py:36
  37.2 0.0 all-gather.2.cloned.1.call-start
  37.2 0.7 all-gather.2.cloned.1.call-update
  37.9 0.0 copy-done.3
  37.9 0.1 mul.26
  38.0 0.1 mul.27
  38.1 103.8 %all-to-all-done = bf16[4,288,2048]{2,1,0:T(8,128)(2,1)} async-done(((bf16[4,288,2048]{2,1,0:T(8,128)(2,1)}), bf16[4,288,2048]{2,1,0:T(8,128)(2,1)}, u32[]{:S(2)}, u32[]{:S(2)}) %all-to-all-start) | async-done | bytes 4718624 | tf_op jit(solution)/shard_map/all_to_all | solution.py:36
  141.9 8.1 %copy.27 = bf16[4,288,2048]{2,0,1:T(4,128)(2,1)} copy(bf16[4,288,2048]{2,1,0:T(8,128)(2,1)} %all-to-all-done) | data formatting | bytes 9437184 | tf_op jit(solution)/shard_map/all_to_all | solution.py:36
  150.0 11.1 %fusion.3 = f32[4,24,12,128]{3,2,0,1:T(8,128)} fusion(bf16[24,128,2048]{2,1,0:T(8,128)(2,1)} %param.8, bf16[4,24,12,2048]{3,0,2,1:T(4,128)(2,1)} %bitcast.51), kind=kOutput, calls=%fused_computation.14 | convolution fusion | flops 603979776 | bytes 17891328 | tf_op jit(solution)/shard_map/fhyz,hbz->fhyb/dot_general | solution.py:44
  161.1 0.0 all-gather.2.cloned.1.call-done
  161.1 3.1 convolution_bitcast_fusion.1
  164.3 1.9 copy.29
  166.2 0.0 copy-start.1
  166.2 0.0 copy-start.2
  166.2 1.0 copy.31
  167.2 0.1 copy-done.1
  167.3 1.0 copy-done.2
  168.3 1.5 convolution_bitcast_fusion
  169.8 1.9 copy.30
  171.7 0.8 copy.32
  172.5 2.7 maximum_multiply_fusion
  175.2 4.9 %all-to-all-start.1 = ((f32[4,288,1024]{2,1,0:T(8,128)}), f32[4,288,1024]{2,1,0:T(8,128)}, u32[]{:S(2)}, u32[]{:S(2)}) async-start(f32[4,288,1024]{2,1,0:T(8,128)} %maximum_multiply_fusion), calls=%async_computation.1 | async-start | bytes 9437184 | tf_op jit(solution)/shard_map/all_to_all | solution.py:65
  180.1 0.0 reduce-scatter.2.cloned.1.call-start
  180.2 103.8 %all-to-all-done.1 = f32[4,288,1024]{2,1,0:T(8,128)} async-done(((f32[4,288,1024]{2,1,0:T(8,128)}), f32[4,288,1024]{2,1,0:T(8,128)}, u32[]{:S(2)}, u32[]{:S(2)}) %all-to-all-start.1) | async-done | bytes 4718624 | tf_op jit(solution)/shard_map/all_to_all | solution.py:65
  284.0 7.0 %gather_fusion.1 = f32[768,1024]{1,0:T(8,128)} fusion(f32[1152,1024]{1,0:T(8,128)} %bitcast.14, s32[1024]{0:T(1024)S(1)} %pad_clamp_fusion.1), kind=kCustom, calls=%fused_computation.1 | custom fusion | bytes 6294528 | tf_op jit(solution)/shard_map/gather | solution.py:73
  291.0 7.4 %convolution_add_fusion = f32[768,1024]{1,0:T(8,128)} fusion(f32[768,1024]{1,0:T(8,128)} %gather_fusion.1, bf16[768,2048]{1,0:T(8,128)(2,1)S(1)} %copy-done, bf16[2048,1024]{1,0:T(8,128)(2,1)} %param.7), kind=kOutput, calls=%fused_computation.11 | convolution fusion | flops 3222011904 | bytes 13631488 | tf_op jit(solution)/shard_map/dot_general | solution.py:47
  298.4 0.0 reduce-scatter.2.cloned.1.call-update
  298.4 37.3 %reduce-scatter.2.cloned.1.call-done = f32[768,256]{1,0:T(8,128)} async-done(((f32[768,1024]{1,0:T(8,128)}), f32[768,256]{1,0:T(8,128)}) %reduce-scatter.2.cloned.1.call-update) | async-done | bytes 786448 | tf_op jit(solution)/shard_map/reduce_scatter | solution.py:74
  335.7 1.9 convert_element_type.13
  (6 shorter events, 0.0 us)
Async XLA Ops:
  6.5 13.3 %copy-start = (bf16[768,2048]{1,0:T(8,128)(2,1)S(1)}, bf16[768,2048]{1,0:T(8,128)(2,1)}, u32[]{:S(2)}) copy-start(bf16[768,2048]{1,0:T(8,128)(2,1)} %param.6) | copy-start | bytes 9437188
  30.7 7.2 %copy-start.3 = (f32[24]{0:T(128)S(1)}, f32[24]{0:T(128)}, u32[]{:S(2)}) copy-start(f32[24]{0:T(128)} %param.10) | copy-start | bytes 292
  30.7 111.2 %all-to-all-start = ((bf16[4,288,2048]{2,1,0:T(8,128)(2,1)}), bf16[4,288,2048]{2,1,0:T(8,128)(2,1)}, u32[]{:S(2)}, u32[]{:S(2)}) async-start(bf16[4,288,2048]{2,1,0:T(8,128)(2,1)} %broadcast_select_fusion), calls=%async_computation | async-start | bytes 9437184 | tf_op jit(solution)/shard_map/all_to_all | solution.py:36
  37.2 124.0 %all-gather.2.cloned.1.call-start = ((), (), s32[]{:S(2)}) async-start(), calls=%async_computation.3 | async-start | bytes 3932160 | tf_op jit(solution)/shard_map/all_gather | solution.py:49
  166.2 1.1 copy-start.1
  166.2 2.1 copy-start.2
  175.2 108.8 %all-to-all-start.1 = ((f32[4,288,1024]{2,1,0:T(8,128)}), f32[4,288,1024]{2,1,0:T(8,128)}, u32[]{:S(2)}, u32[]{:S(2)}) async-start(f32[4,288,1024]{2,1,0:T(8,128)} %maximum_multiply_fusion), calls=%async_computation.1 | async-start | bytes 9437184 | tf_op jit(solution)/shard_map/all_to_all | solution.py:65
  180.1 155.6 %reduce-scatter.2.cloned.1.call-start = ((), (), s32[]{:S(2)}) async-start(), calls=%async_computation.4 | async-start | bytes 3932160 | tf_op jit(solution)/shard_map/reduce_scatter | solution.py:74
Sparse Core Ops, SparseCore 0:
  39.5 30.4 all-gather.1
  298.5 37.1 reduce-scatter.1
where the time goes:
time: 345 us; the launch traced here: 344 us
  waiting for transfers between devices  246 us (71%)
  local copies, waits for them, and re-layouts  35 us (10%)
  matrix products  23.1 us (7%)
  other arithmetic  15.6 us (5%)
  between operations  13.6 us (4%)
  starting transfers between devices  11.4 us (3%)
    all_to_all x1, waiting for transfers between devices, local(): lax.all_to_all(outgoing.reshape(owner_indices, owned_count * TOKEN_LIMIT,...  104 us
    all_to_all x1, waiting for transfers between devices, local(): lax.all_to_all(adapter_update.reshape(owner_indices, owned_count * TOKEN_...  104 us
    reduce_scatter x1, waiting for transfers between devices, local(): lax.psum_scatter(combined, ('tensor', 'sub'), scatter_dimension=1, tiled=...  37.3 us
    dot_general x1, matrix products, local(): jnp.einsum('fhyz,hbz->fhyb', received_rows, adapter_down_weight, preferre...  11.1 us
    all_to_all x1, local copies, waits for them, and re-layouts, local(): lax.all_to_all(outgoing.reshape(owner_indices, owned_count * TOKEN_LIMIT,...  8.15 us
    dot_general x1, matrix products, local(): jnp.dot(tokens, key_value_weight, preferred_element_type=jnp.float32)  7.41 us
    gather x1, local copies, waits for them, and re-layouts, local(): combined = base_part + returned[target]  6.98 us
  transfers between devices with their start and end apart: 4, of which 3 were waited for; matrix products, arithmetic and copies ran while one was open for 6% of the time, Pallas kernels for 0%

commit v1 on v0

v1 whole, which is shorter than its diff:
```python
import functools

import jax
import jax.numpy as jnp
from jax import lax
from jax.experimental import pallas as pl
from jax.experimental.pallas import tpu as pltpu
from jax.sharding import PartitionSpec as P

ADAPTER_RANK = 64
TOKEN_LIMIT = 12
VMEM_LIMIT = 60 * 1024 * 1024
F32 = jnp.float32
BF16 = jnp.bfloat16
I32 = jnp.int32


def owner_of(ids, owners, owned):
    total = jnp.zeros_like(ids)
    for o in range(1, owners):
        total = total + jnp.where(ids >= o * owned, 1, 0)
    return total


def pack_kernel(owners, owned, cap, pieces, me_ref, row_ref, col_ref, tok_ref, *refs):
    outs, target_ref, place = refs[: len(pieces)], refs[-2], refs[-1]
    rows = col_ref.shape[0]

    @pl.when(pl.program_id(0) == 0)
    def _():
        me = me_ref[0]
        id_row, id_col = row_ref[...], col_ref[...]
        key_row = id_row * rows + lax.broadcasted_iota(I32, (1, rows), 1)
        key_col = id_col * rows + lax.broadcasted_iota(I32, (rows, 1), 0)
        own_row, own_col = owner_of(id_row, owners, owned), owner_of(id_col, owners, owned)
        low_row, low_col = own_row * owned * rows, own_col * owned * rows
        before = (key_col < key_row) & (key_col >= low_row)
        rank_row = jnp.sum(jnp.where(before, 1, 0), axis=0, keepdims=True)
        before = (key_row < key_col) & (key_row >= low_col)
        rank_col = jnp.sum(jnp.where(before, 1, 0), axis=1, keepdims=True)
        target_ref[...] = (own_col ^ me) * cap + rank_col
        slot = (own_row ^ me) * cap + rank_row
        at = lax.broadcasted_iota(I32, (owners * cap, rows), 0)
        place[...] = jnp.where(at == slot, 1.0, 0.0).astype(BF16)

    for (block, first, count), out in zip(pieces, outs):
        begin = block * cap + first
        out[...] = jnp.dot(
            place[begin : begin + count, :], tok_ref[...], preferred_element_type=F32
        ).astype(BF16)


def pack(tokens, ids_row, ids_col, me, owners, owned, cap, pieces):
    rows, width = tokens.shape
    step = min(512, width)
    res = pl.pallas_call(
        functools.partial(pack_kernel, owners, owned, cap, pieces),
        grid=(width // step,),
        in_specs=[
            pl.BlockSpec(memory_space=pltpu.SMEM),
            pl.BlockSpec((1, rows), lambda i: (0, 0)),
            pl.BlockSpec((rows, 1), lambda i: (0, 0)),
            pl.BlockSpec((rows, step), lambda i: (0, i)),
        ],
        out_specs=[pl.BlockSpec((count, step), lambda i: (0, i)) for _, _, count in pieces]
        + [pl.BlockSpec((rows, 1), lambda i: (0, 0))],
        out_shape=[jax.ShapeDtypeStruct((count, width), BF16) for _, _, count in pieces]
        + [jax.ShapeDtypeStruct((rows, 1), I32)],
        scratch_shapes=[pltpu.VMEM((owners * cap, rows), BF16)],
        compiler_params=pltpu.CompilerParams(vmem_limit_bytes=VMEM_LIMIT),
        name="pack",
    )(me, ids_row, ids_col, tokens)
    return res[:-1], res[-1]


def shrink_kernel(sizes, group, half_ref, which_ref, down_ref, *refs):
    blocks, (mine_ref, other_ref, acc) = refs[: len(sizes)], refs[len(sizes) :]
    step = pl.program_id(0)
    factors = down_ref[...].reshape(group * 2 * ADAPTER_RANK, down_ref.shape[2])
    begin = 0
    for size, block in zip(sizes, blocks):
        product = lax.dot_general(
            block[...], factors, (((1,), (1,)), ((), ())), preferred_element_type=F32
        )
        which = which_ref[begin : begin + size, :]
        found = jnp.zeros((size, 2 * ADAPTER_RANK), F32)
        for q in range(group):
            part = product[:, q * 2 * ADAPTER_RANK : (q + 1) * 2 * ADAPTER_RANK]
            found = found + jnp.where(which == step * group + q, part, 0.0)
        here = slice(begin, begin + size)
        acc[here, :] = jnp.where(step == 0, found, acc[here, :] + found)
        begin += size

    @pl.when(step == pl.num_programs(0) - 1)
    def _():
        total = sum(sizes)
        upper, lower = acc[: total // 2, :], acc[total // 2 :, :]
        keys = jnp.concatenate([upper[:, :ADAPTER_RANK], lower[:, :ADAPTER_RANK]], axis=1)
        values = jnp.concatenate([upper[:, ADAPTER_RANK:], lower[:, ADAPTER_RANK:]], axis=1)
        second = half_ref[0] == 1
        mine_ref[...] = jnp.where(second, values, keys)
        other_ref[...] = jnp.where(second, keys, values)


def shrink(blocks, which, down, half):
    sizes = tuple(b.shape[0] for b in blocks)
    total = sum(sizes)
    owned, rank2, width = down.shape
    group = next(g for g in (4, 3, 2, 1) if owned % g == 0)
    line = jax.ShapeDtypeStruct((total // 2, 2 * ADAPTER_RANK), F32)
    return pl.pallas_call(
        functools.partial(shrink_kernel, sizes, group),
        grid=(owned // group,),
        in_specs=[
            pl.BlockSpec(memory_space=pltpu.SMEM),
            pl.BlockSpec((total, 1), lambda i: (0, 0)),
            pl.BlockSpec((group, rank2, width), lambda i: (i, 0, 0)),
        ]
        + [pl.BlockSpec((s, width), lambda i: (0, 0)) for s in sizes],
        out_specs=[pl.BlockSpec((total // 2, rank2), lambda i: (0, 0))] * 2,
        out_shape=[line, line],
        scratch_shapes=[pltpu.VMEM((total, rank2), F32)],
        compiler_params=pltpu.CompilerParams(vmem_limit_bytes=VMEM_LIMIT),
        name="shrink",
    )(half, which, down, *blocks)


def three_way(x):
    high = x.astype(BF16).astype(F32)
    middle = (x - high).astype(BF16).astype(F32)
    return high, middle, x - high - middle


def expand_kernel(sizes, heard, which_ref, scale_ref, up_ref, *refs):
    lines, outs = refs[:heard], refs[heard:]
    total = lines[0][...]
    for line in lines[1:]:
        total = total + line[...]
    upper, lower = total[:, :ADAPTER_RANK], total[:, ADAPTER_RANK:]
    twice = jnp.concatenate(
        [jnp.concatenate([upper, upper], axis=1), jnp.concatenate([lower, lower], axis=1)], axis=0
    )
    which = which_ref[...]
    parity = jnp.where(lax.broadcasted_iota(I32, (1, 2 * ADAPTER_RANK), 1) >= ADAPTER_RANK, 1, 0)
    pairs = up_ref.shape[0] // (2 * ADAPTER_RANK)
    wanted = [which == 2 * p + parity for p in range(pairs)]
    delta = None
    for term in three_way(twice):
        spread = jnp.concatenate(
            [jnp.where(w, term, 0.0).astype(BF16) for w in wanted], axis=1
        )
        product = jnp.dot(spread, up_ref[...], preferred_element_type=F32)
        delta = product if delta is None else delta + product
    adapters = lax.broadcasted_iota(I32, scale_ref.shape, 1)
    gain = jnp.sum(jnp.where(which == adapters, scale_ref[...], 0.0), axis=1, keepdims=True)
    delta = delta * gain
    begin = 0
    for size, out in zip(sizes, outs):
        out[...] = delta[begin : begin + size, :]
        begin += size


def expand(lines, which, scale, up, sizes):
    columns = up.shape[1]
    return pl.pallas_call(
        functools.partial(expand_kernel, sizes, len(lines)),
        out_shape=[jax.ShapeDtypeStruct((s, columns), F32) for s in sizes],
        compiler_params=pltpu.CompilerParams(vmem_limit_bytes=VMEM_LIMIT),
        name="expand",
    )(which, scale, up, *lines)


def merge_kernel(begins, base_ref, target_ref, *refs):
    blocks, out_ref = refs[:-1], refs[-1]
    returned = jnp.concatenate([b[...] for b in blocks], axis=0)
    target = target_ref[...]
    place = jnp.concatenate(
        [
            jnp.where(
                target == begin + lax.broadcasted_iota(I32, (1, block.shape[0]), 1), 1.0, 0.0
            ).astype(BF16)
            for begin, block in zip(begins, blocks)
        ],
        axis=1,
    )
    total = None
    for term in three_way(returned):
        moved = jnp.dot(place, term.astype(BF16), preferred_element_type=F32)
        total = moved if total is None else total + moved
    out_ref[...] = (base_ref[...] + total).astype(BF16)


def merge(base, target, begins, blocks):
    return pl.pallas_call(
        functools.partial(merge_kernel, begins),
        out_shape=jax.ShapeDtypeStruct(base.shape, BF16),
        compiler_params=pltpu.CompilerParams(vmem_limit_bytes=VMEM_LIMIT),
        name="merge",
    )(base, target, *blocks)


def swap(x, axes, size, distance):
    return lax.ppermute(x, axes, [(i, i ^ distance) for i in range(size)])


def local(
    tokens,
    key_value_weight,
    adapter_down_weight,
    adapter_up_weight,
    adapter_scale,
    token_adapter_index,
):
    feature_axes = ("tensor", "sub")
    rows = tokens.shape[0]
    owned, _, width = adapter_down_weight.shape
    owners = lax.axis_size("dp")
    sharers = lax.axis_size(feature_axes)
    me = lax.axis_index("dp")
    half = (lax.axis_index(feature_axes) >= sharers // 2).astype(I32).reshape(1)
    cap = -(-owned * TOKEN_LIMIT // 16) * 16

    first = cap if owners > 4 else 144
    parts = [(0, first)] + ([(first, cap - first)] if first < cap else [])
    pieces = [(0, 0, cap)] + [(j, f, c) for f, c in parts for j in range(1, owners)]

    ids_row = token_adapter_index.reshape(1, rows)
    ids_heard = [ids_row] + [swap(ids_row, "dp", owners, j) for j in range(1, owners)]
    packed, target = pack(
        tokens, ids_row, token_adapter_index, me.reshape(1), owners, owned, cap, pieces
    )
    received = [packed[0]] + [
        swap(rows_out, "dp", owners, j) for (j, _, _), rows_out in zip(pieces[1:], packed[1:])
    ]

    base_part = jnp.dot(tokens, key_value_weight, preferred_element_type=F32)
    base = lax.psum_scatter(base_part, feature_axes, scatter_dimension=1, tiled=True)

    heard = jnp.concatenate(ids_heard, axis=0) - me * owned
    adapters = jnp.arange(owned, dtype=I32)
    upto = jnp.sum(
        (heard[:, None, :] >= 0) & (heard[:, None, :] <= adapters[None, :, None]), axis=2, dtype=I32
    )
    at = jnp.arange(cap, dtype=I32)
    which = jnp.sum(upto[:, None, :] <= at[None, :, None], axis=2, dtype=I32)

    if owned % 2:
        adapter_up_weight = jnp.pad(adapter_up_weight, ((0, 1), (0, 0), (0, 0)))
    up = adapter_up_weight.reshape(-1, adapter_up_weight.shape[2])
    scale = adapter_scale.reshape(1, owned)

    sets = [[0]]
    for p in range(len(parts)):
        sets.append([1 + p * (owners - 1) + j for j in range(owners - 1)])
    returned = [None] * len(pieces)
    for members in sets:
        blocks = [received[m] for m in members]
        sizes = tuple(pieces[m][2] for m in members)
        names = jnp.concatenate(
            [which[b, f : f + c] for b, f, c in (pieces[m] for m in members)]
        ).reshape(-1, 1)
        mine, other = shrink(blocks, names, adapter_down_weight, half)
        lines = [mine] + [
            swap(mine if d < sharers // 2 else other, feature_axes, sharers, d)
            for d in range(1, sharers)
        ]
        deltas = expand(lines, names, scale, up, sizes)
        for m, delta in zip(members, deltas):
            block = pieces[m][0]
            returned[m] = swap(delta, "dp", owners, block) if block else delta
    begins = tuple(b * cap + f for b, f, _ in pieces)
    return merge(base, target, begins, returned)


def solution(mesh):
    return jax.shard_map(
        local,
        mesh=mesh,
        in_specs=(
            P(("parts", "dp"), ("tensor", "sub")),
            P(("tensor", "sub"), None),
            P("dp", None, ("tensor", "sub")),
            P("dp", None, ("tensor", "sub")),
            P("dp"),
            P(("parts", "dp"), None),
        ),
        out_specs=P(("parts", "dp"), ("tensor", "sub")),
        check_vma=False,
    )
```

time: 345 us -> 212 us (0.61)
  waiting for transfers between devices: 246 us -> 74.3 us
  Pallas kernels: 0 us -> 65 us
  starting transfers between devices: 11.4 us -> 40.1 us
  local copies, waits for them, and re-layouts: 35 us -> 8.79 us
  other arithmetic: 15.6 us -> 0.45 us
  matrix products: 23.1 us -> 8.18 us
    all_to_all x2 -> x0, waiting for transfers between devices: 208 us -> none  [the longest x1 104 us: local(): lax.all_to_all(outgoing.reshape(owner_indices, owned_count * TOKEN_LIMIT,...]
    ppermute x0 -> x24, waiting for transfers between devices: none -> 74.2 us  [swap(): return lax.ppermute(x, axes, [(i, i ^ distance) for i in range(size)])]
    pallas_call x0 -> x8, Pallas kernels: none -> 65 us  [the longest x3 42 us: shrink(): pl.pallas_call(functools.partial(shrink_kernel, sizes, group), grid=(owne...]
    ppermute x0 -> x24, starting transfers between devices: none -> 40.1 us  [swap(): return lax.ppermute(x, axes, [(i, i ^ distance) for i in range(size)])]
    reduce_scatter x1, waiting for transfers between devices: 37.3 us -> 0.02 us  [local(): lax.psum_scatter(base_part, feature_axes, scatter_dimension=1, tiled=True)]
    dot_general x4 -> x1, matrix products: 23.1 us -> 8.18 us  [local(): base_part = jnp.dot(tokens, key_value_weight, preferred_element_type=F32)]
    gather x2 -> x0, local copies, waits for them, and re-layouts: 12.9 us -> none  [the longest x1 6.98 us: local(): combined = base_part + returned[target]]
    all_to_all x2 -> x0, starting transfers between devices: 11.4 us -> none  [the longest x1 6.45 us: local(): lax.all_to_all(outgoing.reshape(owner_indices, owned_count * TOKEN_LIMIT,...]
  transfers between devices with their start and end apart: 4 -> 25, of which waited for: 3 -> 5; matrix products, arithmetic and copies ran while one was open for 6% -> 2% of each run, Pallas kernels for 0% -> 29%
where the time goes in v1:
time: 212 us; the launch traced here: 210 us
  waiting for transfers between devices  74.3 us (35%)
  Pallas kernels  65 us (31%)
  starting transfers between devices  40.1 us (19%)
  between operations  13.6 us (6%)
  local copies, waits for them, and re-layouts  8.79 us (4%)
  matrix products  8.18 us (4%)
    ppermute x24, waiting for transfers between devices, swap(): return lax.ppermute(x, axes, [(i, i ^ distance) for i in range(size)])  74.2 us
    pallas_call x3, Pallas kernels, shrink(): pl.pallas_call(functools.partial(shrink_kernel, sizes, group), grid=(owne...  42 us
    ppermute x24, starting transfers between devices, swap(): return lax.ppermute(x, axes, [(i, i ^ distance) for i in range(size)])  40.1 us
    pallas_call x3, Pallas kernels, expand(): pl.pallas_call(functools.partial(expand_kernel, sizes, len(lines)), out_s...  9.63 us
    pallas_call x1, Pallas kernels, pack(): pl.pallas_call(functools.partial(pack_kernel, owners, owned, cap, pieces)...  8.91 us
    dot_general x1, matrix products, local(): base_part = jnp.dot(tokens, key_value_weight, preferred_element_type=F32)  8.18 us
    unnamed x55, local copies, waits for them, and re-layouts  5.7 us
    pallas_call x1, Pallas kernels, merge(): pl.pallas_call(functools.partial(merge_kernel, begins), out_shape=jax.Sha...  4.39 us
  transfers between devices with their start and end apart: 25, of which 5 were waited for; matrix products, arithmetic and copies ran while one was open for 2% of the time, Pallas kernels for 29%

profile of v1, /device:TPU:0, one launch (start us, length us, event | category | flops | bytes accessed | tf_op | source)
XLA Modules:
  0.0 210.4 jit_solution(4666952603066940164)
XLA Ops:
  6.5 8.2 %fusion.2 = f32[768,1024]{1,0:T(8,128)} fusion(bf16[768,2048]{1,0:T(8,128)(2,1)} %tok_ref.1, bf16[2048,1024]{1,0:T(8,128)(2,1)} %param.7), kind=kOutput, calls=%fused_computation.11 | convolution fusion | flops 3221225472 | bytes 10485760 | tf_op jit(solution)/shard_map/dot_general | solution.py:236
  14.7 0.0 reduce-scatter.2.cloned.1.call-update
  14.8 0.7 copy-done.21
  15.4 0.9 copy.15.col_ref
  16.3 8.9 %pack.1 = (bf16[288,2048]{1,0:T(8,128)(2,1)}, bf16[144,2048]{1,0:T(8,128)(2,1)}, bf16[144,2048]{1,0:T(8,128)(2,1)}, bf16[144,2048]{1,0:T(8,128)(2,1)}, bf16[144,...) custom-call(s32[1]{0:T(128)} %bitcast.me_ref, s32[1,768]{1,0:T(1,128)} %bitcast.20, ...), custom_call_target="tpu_custom_call" | custom-call | tf_op jit(solution)/shard_map/pack/pallas_call | solution.py:56
  25.3 3.1 %collective-permute-start.15 = (bf16[144,2048]{1,0:T(8,128)(2,1)}, bf16[144,2048]{1,0:T(8,128)(2,1)S(1)}, u32[]{:S(2)}, u32[]{:S(2)}) collective-permute-start(bf16[144,2048]{1,0:T(8,128)(2,1)} %get-tuple-element.37), channel_id=1, source_target_pairs={{0,4},{4,0},{8,12},{12,8},{1,5},{5,1},{9,13},{13,9},{2,6},{6,2},{1... | collective-permute-start | bytes 1769480 | tf_op jit(solution)/shard_map/ppermute | solution.py:203
  28.4 0.1 collective-permute-start
  28.4 3.0 %collective-permute-start.1 = (s32[1,768]{1,0:T(1,128)S(1)}, s32[1,768]{1,0:T(1,128)S(1)}, u32[]{:S(2)}, u32[]{:S(2)}) collective-permute-start(s32[1,768]{1,0:T(1,128)S(1)} %bitcast.22), channel_id=1, source_target_pairs={{0,8},{4,12},{8,0},{12,4},{1,9},{5,13},{9,1},{13,5},{2,10},{6,14},... | collective-permute-start | bytes 9224 | tf_op jit(solution)/shard_map/ppermute | solution.py:203
  31.5 1.3 collective-permute-start.2
  32.8 1.8 collective-permute-start.16
  34.5 16.5 %collective-permute-done = s32[1,768]{1,0:T(1,128)S(1)} collective-permute-done((s32[1,768]{1,0:T(1,128)S(1)}, s32[1,768]{1,0:T(1,128)S(1)}, u32[]{:S(2)}, u32[]{:S(2)}) %collective-permute-start) | collective-permute-done | bytes 3104 | tf_op jit(solution)/shard_map/ppermute | solution.py:203
  51.0 2.7 %collective-permute-start.17 = (bf16[144,2048]{1,0:T(8,128)(2,1)}, bf16[144,2048]{1,0:T(8,128)(2,1)S(1)}, u32[]{:S(2)}, u32[]{:S(2)}) collective-permute-start(bf16[144,2048]{1,0:T(8,128)(2,1)} %get-tuple-element.39), channel_id=1, source_target_pairs={{0,12},{4,8},{8,4},{12,0},{1,13},{5,9},{9,5},{13,1},{2,14},{6,10},... | collective-permute-start | bytes 1769480 | tf_op jit(solution)/shard_map/ppermute | solution.py:203
  53.8 0.0 collective-permute-done.2
  53.8 1.6 collective-permute-start.7
  55.4 0.0 collective-permute-done.15.refs_0_
  55.5 2.8 %collective-permute-start.8 = (bf16[144,2048]{1,0:T(8,128)(2,1)}, bf16[144,2048]{1,0:T(8,128)(2,1)S(1)}, u32[]{:S(2)}, u32[]{:S(2)}) collective-permute-start(bf16[144,2048]{1,0:T(8,128)(2,1)} %get-tuple-element.31), channel_id=1, source_target_pairs={{0,12},{4,8},{8,4},{12,0},{1,13},{5,9},{9,5},{13,1},{2,14},{6,10},... | collective-permute-start | bytes 1769480 | tf_op jit(solution)/shard_map/ppermute | solution.py:203
  58.3 0.2 convert_reduce_fusion
  58.4 0.1 convert_reduce_fusion.1
  58.5 0.6 fusion.1
  59.1 0.1 pad_add_fusion.1
  59.2 0.8 copy.21.which_ref
  60.0 15.5 %collective-permute-done.16.refs_1_ = bf16[144,2048]{1,0:T(8,128)(2,1)S(1)} collective-permute-done((bf16[144,2048]{1,0:T(8,128)(2,1)}, bf16[144,2048]{1,0:T(8,128)(2,1)S(1)}, u32[]{:S(2)}, u32[]{:S(2)}) %collective-permute-start.16) | collective-permute-done | bytes 589856 | tf_op jit(solution)/shard_map/ppermute | solution.py:203
  75.6 0.0 collective-permute-done.17.refs_2_
  75.6 0.9 copy-done.1
  76.5 0.2 copy-done.5
  76.7 16.2 %shrink.5 = (f32[216,128]{1,0:T(8,128)}, f32[216,128]{1,0:T(8,128)}) custom-call(s32[1]{0:T(128)} %bitcast.5.half_ref, s32[432,1]{1,0:T(8,128)} %copy.21.which_ref, bf16[24,128,2048]{2,1,0:T(8,128)(2,1)} %down_ref.5, bf16[144,2048]{1,0:T(8,128)(2,1)} %copy-done, bf16[144,2048]{1,0:T(8,128)(2,1)} %copy-done.1, bf16[144,2048]{1,0:T(8,128)(2,1)} %copy-done.5), custom_call_target="tpu_custom_call" | custom-call | tf_op jit(solution)/shard_map/shrink/pallas_call | solution.py:111
  92.9 1.5 collective-permute-start.19
  94.5 0.0 collective-permute-start.20
  94.5 0.0 collective-permute-done.6.refs_0_
  94.5 0.6 collective-permute-start.18
  95.1 0.1 pad_add_fusion
  95.2 0.8 copy.19.which_ref
  96.0 30.1 %collective-permute-done.7.refs_1_ = bf16[144,2048]{1,0:T(8,128)(2,1)S(1)} collective-permute-done((bf16[144,2048]{1,0:T(8,128)(2,1)}, bf16[144,2048]{1,0:T(8,128)(2,1)S(1)}, u32[]{:S(2)}, u32[]{:S(2)}) %collective-permute-start.7) | collective-permute-done | bytes 589856 | tf_op jit(solution)/shard_map/ppermute | solution.py:203
  126.1 0.0 collective-permute-done.8.refs_2_
  126.2 0.8 copy-done.3
  127.0 0.8 copy-done.4
  127.8 16.2 %shrink.4 = (f32[216,128]{1,0:T(8,128)}, f32[216,128]{1,0:T(8,128)}) custom-call(s32[1]{0:T(128)} %bitcast.5.half_ref, s32[432,1]{1,0:T(8,128)} %copy.19.which_ref, bf16[24,128,2048]{2,1,0:T(8,128)(2,1)} %down_ref.5, bf16[144,2048]{1,0:T(8,128)(2,1)} %copy-done.2, bf16[144,2048]{1,0:T(8,128)(2,1)} %copy-done.3, bf16[144,2048]{1,0:T(8,128)(2,1)} %copy-done.4), custom_call_target="tpu_custom_call" | custom-call | tf_op jit(solution)/shard_map/shrink/pallas_call | solution.py:111
  144.0 1.5 collective-permute-start.10
  145.5 0.0 collective-permute-start.11
  145.5 0.0 collective-permute-done.18.refs_1_
  145.5 0.6 collective-permute-start.9
  146.2 0.0 collective-permute-done.19.refs_2_
  146.2 0.0 copy-done.17
  146.2 0.6 copy-done.15
  146.8 0.0 copy-done.16
  146.9 3.4 %expand.5 = (f32[144,256]{1,0:T(8,128)}, f32[144,256]{1,0:T(8,128)}, f32[144,256]{1,0:T(8,128)}) custom-call(s32[432,1]{1,0:T(8,128)} %copy.21.which_ref, f32[1,24]{1,0:T(1,128)} %bitcast.27, bf16[1536,256]{1,0:T(8,128)(2,1)} %bitcast.17, f32[216,128]{1,0:T(8,128)} %get-tuple-element.40.refs_0_, f32[216,128]{1,0:T(8,128)} %copy-done.17, ...), custom_call_target="tpu_custom_call" | custom-call | tf_op jit(solution)/shard_map/expand/pallas_call | solution.py:165
  150.2 10.1 %collective-permute-start.21 = (f32[144,256]{1,0:T(8,128)}, f32[144,256]{1,0:T(8,128)S(1)}, u32[]{:S(2)}, u32[]{:S(2)}) collective-permute-start(f32[144,256]{1,0:T(8,128)} %get-tuple-element.42), channel_id=1, source_target_pairs={{0,4},{4,0},{8,12},{12,8},{1,5},{5,1},{9,13},{13,9},{2,6},{6,2},{1... | collective-permute-start | bytes 442376 | tf_op jit(solution)/shard_map/ppermute | solution.py:203
  160.3 0.8 copy.17.which_ref
  161.1 9.5 %shrink.3 = (f32[144,128]{1,0:T(8,128)}, f32[144,128]{1,0:T(8,128)}) custom-call(s32[1]{0:T(128)} %bitcast.5.half_ref, s32[288,1]{1,0:T(8,128)} %copy.17.which_ref, bf16[24,128,2048]{2,1,0:T(8,128)(2,1)} %down_ref.5, bf16[288,2048]{1,0:T(8,128)(2,1)} %get-tuple-element.26.refs_0_), custom_call_target="tpu_custom_call" | custom-call | tf_op jit(solution)/shard_map/shrink/pallas_call | solution.py:111
  170.7 1.5 collective-permute-start.4
  172.2 0.3 collective-permute-start.5
  172.6 1.0 collective-permute-start.22
  173.5 3.4 %expand.4 = (f32[144,256]{1,0:T(8,128)}, f32[144,256]{1,0:T(8,128)}, f32[144,256]{1,0:T(8,128)}) custom-call(s32[432,1]{1,0:T(8,128)} %copy.19.which_ref, f32[1,24]{1,0:T(1,128)} %bitcast.28, bf16[1536,256]{1,0:T(8,128)(2,1)} %bitcast.18, f32[216,128]{1,0:T(8,128)} %get-tuple-element.32.refs_0_, f32[216,128]{1,0:T(8,128)} %copy-done.14, ...), custom_call_target="tpu_custom_call" | custom-call | tf_op jit(solution)/shard_map/expand/pallas_call | solution.py:165
  176.9 2.1 collective-permute-start.23
  179.0 0.5 collective-permute-start.12
  179.6 1.8 collective-permute-start.13
  181.4 2.0 collective-permute-start.14
  183.4 2.9 %expand.3.refs_0_ = f32[288,256]{1,0:T(8,128)} custom-call(s32[288,1]{1,0:T(8,128)} %copy.17.which_ref, f32[1,24]{1,0:T(1,128)} %bitcast.29, bf16[1536,256]{1,0:T(8,128)(2,1)} %bitcast.19, f32[144,128]{1,0:T(8,128)} %get-tuple-element.27.refs_0_, f32[144,128]{1,0:T(8,128)} %copy-done.18, f32[144,128]{1,0:T(8,128)} %copy-done.19, f32[144,128]{1,0:T(8,128)} %copy-done.20), custom_call_target="tpu_custom_call" | custom-call | tf_op jit(solution)/shard_map/expand/pallas_call | solution.py:165
  186.4 2.5 %collective-permute-done.12.refs_1_ = f32[144,256]{1,0:T(8,128)S(1)} collective-permute-done((f32[144,256]{1,0:T(8,128)}, f32[144,256]{1,0:T(8,128)S(1)}, u32[]{:S(2)}, u32[]{:S(2)}) %collective-permute-start.12) | collective-permute-done | bytes 147488 | tf_op jit(solution)/shard_map/ppermute | solution.py:203
  188.8 9.6 %collective-permute-done.13.refs_2_ = f32[144,256]{1,0:T(8,128)S(1)} collective-permute-done((f32[144,256]{1,0:T(8,128)}, f32[144,256]{1,0:T(8,128)S(1)}, u32[]{:S(2)}, u32[]{:S(2)}) %collective-permute-start.13) | collective-permute-done | bytes 147488 | tf_op jit(solution)/shard_map/ppermute | solution.py:203
  198.4 0.0 reduce-scatter.2.cloned.1.call-done.base_ref
  198.5 0.6 copy-done.10
  199.1 0.0 copy-done.11
  199.1 4.4 %merge.1 = bf16[768,256]{1,0:T(8,128)(2,1)} custom-call(f32[768,256]{1,0:T(8,128)} %reduce-scatter.2.cloned.1.call-done.base_ref, s32[768,1]{1,0:T(8,128)} %get-tuple-element.25.target_ref, f32[288,256]{1,0:T(8,128)} %expand.3.refs_0_, f32[144,256]{1,0:T(8,128)} %copy-done.9, f32[144,256]{1,0:T(8,128)} %copy-done.10, f32[144,256]{1,0:T(8,128)} %copy-done.11, ...), custom_call_target="tpu_custom_call" | custom-call | tf_op jit(solution)/shard_map/merge/pallas_call | solution.py:194
  (61 shorter events, 0.1 us)
Async XLA Ops:
  6.5 191.9 %reduce-scatter.2.cloned.1.call-start = ((), (), s32[]{:S(2)}) async-start(), calls=%async_computation.1 | async-start | bytes 3932160 | tf_op jit(solution)/shard_map/reduce_scatter | solution.py:237
  14.7 0.7 copy-start.21
  14.7 13.6 %copy-start.22 = (s32[768,1]{0,1:T(1,128)S(1)}, s32[768,1]{0,1:T(1,128)}, u32[]{:S(2)}) copy-start(s32[768,1]{0,1:T(1,128)} %param.11) | copy-start | bytes 9220
  25.3 30.2 %collective-permute-start.15 = (bf16[144,2048]{1,0:T(8,128)(2,1)}, bf16[144,2048]{1,0:T(8,128)(2,1)S(1)}, u32[]{:S(2)}, u32[]{:S(2)}) collective-permute-start(bf16[144,2048]{1,0:T(8,128)(2,1)} %get-tuple-element.37), channel_id=1, source_target_pairs={{0,4},{4,0},{8,12},{12,8},{1,5},{5,1},{9,13},{13,9},{2,6},{6,2},{1... | collective-permute-start | bytes 1769480 | tf_op jit(solution)/shard_map/ppermute | solution.py:203
  28.4 22.6 %collective-permute-start = (s32[1,768]{1,0:T(1,128)S(1)}, s32[1,768]{1,0:T(1,128)S(1)}, u32[]{:S(2)}, u32[]{:S(2)}) collective-permute-start(s32[1,768]{1,0:T(1,128)S(1)} %bitcast.21), channel_id=1, source_target_pairs={{0,4},{4,0},{8,12},{12,8},{1,5},{5,1},{9,13},{13,9},{2,6},{6,2},{1... | collective-permute-start | bytes 9224 | tf_op jit(solution)/shard_map/ppermute | solution.py:203
  28.4 25.3 %collective-permute-start.1 = (s32[1,768]{1,0:T(1,128)S(1)}, s32[1,768]{1,0:T(1,128)S(1)}, u32[]{:S(2)}, u32[]{:S(2)}) collective-permute-start(s32[1,768]{1,0:T(1,128)S(1)} %bitcast.22), channel_id=1, source_target_pairs={{0,8},{4,12},{8,0},{12,4},{1,9},{5,13},{9,1},{13,5},{2,10},{6,14},... | collective-permute-start | bytes 9224 | tf_op jit(solution)/shard_map/ppermute | solution.py:203
  31.5 22.3 %collective-permute-start.2 = (s32[1,768]{1,0:T(1,128)S(1)}, s32[1,768]{1,0:T(1,128)S(1)}, u32[]{:S(2)}, u32[]{:S(2)}) collective-permute-start(s32[1,768]{1,0:T(1,128)S(1)} %bitcast.23), channel_id=1, source_target_pairs={{0,12},{4,8},{8,4},{12,0},{1,13},{5,9},{9,5},{13,1},{2,14},{6,10},... | collective-permute-start | bytes 9224 | tf_op jit(solution)/shard_map/ppermute | solution.py:203
  32.8 42.8 %collective-permute-start.16 = (bf16[144,2048]{1,0:T(8,128)(2,1)}, bf16[144,2048]{1,0:T(8,128)(2,1)S(1)}, u32[]{:S(2)}, u32[]{:S(2)}) collective-permute-start(bf16[144,2048]{1,0:T(8,128)(2,1)} %get-tuple-element.38), channel_id=1, source_target_pairs={{0,8},{4,12},{8,0},{12,4},{1,9},{5,13},{9,1},{13,5},{2,10},{6,14},... | collective-permute-start | bytes 1769480 | tf_op jit(solution)/shard_map/ppermute | solution.py:203
  51.0 24.6 %collective-permute-start.17 = (bf16[144,2048]{1,0:T(8,128)(2,1)}, bf16[144,2048]{1,0:T(8,128)(2,1)S(1)}, u32[]{:S(2)}, u32[]{:S(2)}) collective-permute-start(bf16[144,2048]{1,0:T(8,128)(2,1)} %get-tuple-element.39), channel_id=1, source_target_pairs={{0,12},{4,8},{8,4},{12,0},{1,13},{5,9},{9,5},{13,1},{2,14},{6,10},... | collective-permute-start | bytes 1769480 | tf_op jit(solution)/shard_map/ppermute | solution.py:203
  53.8 40.7 %collective-permute-start.6 = (bf16[144,2048]{1,0:T(8,128)(2,1)}, bf16[144,2048]{1,0:T(8,128)(2,1)S(1)}, u32[]{:S(2)}, u32[]{:S(2)}) collective-permute-start(bf16[144,2048]{1,0:T(8,128)(2,1)} %get-tuple-element.29), channel_id=1, source_target_pairs={{0,4},{4,0},{8,12},{12,8},{1,5},{5,1},{9,13},{13,9},{2,6},{6,2},{1... | collective-permute-start | bytes 1769480 | tf_op jit(solution)/shard_map/ppermute | solution.py:203
  53.8 72.4 %collective-permute-start.7 = (bf16[144,2048]{1,0:T(8,128)(2,1)}, bf16[144,2048]{1,0:T(8,128)(2,1)S(1)}, u32[]{:S(2)}, u32[]{:S(2)}) collective-permute-start(bf16[144,2048]{1,0:T(8,128)(2,1)} %get-tuple-element.30), channel_id=1, source_target_pairs={{0,8},{4,12},{8,0},{12,4},{1,9},{5,13},{9,1},{13,5},{2,10},{6,14},... | collective-permute-start | bytes 1769480 | tf_op jit(solution)/shard_map/ppermute | solution.py:203
  55.4 20.2 %copy-start = (bf16[144,2048]{1,0:T(8,128)(2,1)}, bf16[144,2048]{1,0:T(8,128)(2,1)S(1)}, u32[]{:S(2)}) copy-start(bf16[144,2048]{1,0:T(8,128)(2,1)S(1)} %collective-permute-done.15.refs_0_) | copy-start | bytes 1769476
  55.5 70.7 %collective-permute-start.8 = (bf16[144,2048]{1,0:T(8,128)(2,1)}, bf16[144,2048]{1,0:T(8,128)(2,1)S(1)}, u32[]{:S(2)}, u32[]{:S(2)}) collective-permute-start(bf16[144,2048]{1,0:T(8,128)(2,1)} %get-tuple-element.31), channel_id=1, source_target_pairs={{0,12},{4,8},{8,4},{12,0},{1,13},{5,9},{9,5},{13,1},{2,14},{6,10},... | collective-permute-start | bytes 1769480 | tf_op jit(solution)/shard_map/ppermute | solution.py:203
  75.6 0.9 copy-start.1
  75.6 1.1 copy-start.5
  76.7 18.4 %copy-start.23 = (s32[1,144]{1,0:T(1,128)S(1)}, s32[1,144]{1,0:T(1,128)}, u32[]{:S(2)}) copy-start(s32[1,144]{1,0:T(1,128)} %get-tuple-element.51) | copy-start | bytes 1732
  76.7 18.4 %copy-start.24 = (s32[1,144]{1,0:T(1,128)S(1)}, s32[1,144]{1,0:T(1,128)}, u32[]{:S(2)}) copy-start(s32[1,144]{1,0:T(1,128)} %get-tuple-element.52) | copy-start | bytes 1732
  92.9 53.2 %collective-permute-start.19 = (f32[216,128]{1,0:T(8,128)}, f32[216,128]{1,0:T(8,128)S(1)}, u32[]{:S(2)}, u32[]{:S(2)}) collective-permute-start(f32[216,128]{1,0:T(8,128)} %get-tuple-element.41), channel_id=1, source_target_pairs={{0,2},{1,3},{2,0},{3,1},{4,6},{5,7},{6,4},{7,5},{8,10},{9,11},{10,... | collective-permute-start | bytes 331784 | tf_op jit(solution)/shard_map/ppermute | solution.py:203
  94.5 51.7 %collective-permute-start.20 = (f32[216,128]{1,0:T(8,128)}, f32[216,128]{1,0:T(8,128)S(1)}, u32[]{:S(2)}, u32[]{:S(2)}) collective-permute-start(f32[216,128]{1,0:T(8,128)} %get-tuple-element.41), channel_id=1, source_target_pairs={{0,3},{1,2},{2,1},{3,0},{4,7},{5,6},{6,5},{7,4},{8,11},{9,10},{10,... | collective-permute-start | bytes 331784 | tf_op jit(solution)/shard_map/ppermute | solution.py:203
  94.5 31.7 %copy-start.2 = (bf16[144,2048]{1,0:T(8,128)(2,1)}, bf16[144,2048]{1,0:T(8,128)(2,1)S(1)}, u32[]{:S(2)}) copy-start(bf16[144,2048]{1,0:T(8,128)(2,1)S(1)} %collective-permute-done.6.refs_0_) | copy-start | bytes 1769476
  94.5 51.1 %collective-permute-start.18 = (f32[216,128]{1,0:T(8,128)}, f32[216,128]{1,0:T(8,128)S(1)}, u32[]{:S(2)}, u32[]{:S(2)}) collective-permute-start(f32[216,128]{1,0:T(8,128)} %get-tuple-element.40.refs_0_), channel_id=1, source_target_pairs={{0,1},{1,0},{2,3},{3,2},{4,5},{5,4},{6,7},{7,6},{8,9},{9,8},{10,11... | collective-permute-start | bytes 331784 | tf_op jit(solution)/shard_map/ppermute | solution.py:203
  126.1 0.8 copy-start.3
  127.0 0.8 copy-start.4
  144.0 26.6 %collective-permute-start.10 = (f32[216,128]{1,0:T(8,128)}, f32[216,128]{1,0:T(8,128)S(1)}, u32[]{:S(2)}, u32[]{:S(2)}) collective-permute-start(f32[216,128]{1,0:T(8,128)} %get-tuple-element.33), channel_id=1, source_target_pairs={{0,2},{1,3},{2,0},{3,1},{4,6},{5,7},{6,4},{7,5},{8,10},{9,11},{10,... | collective-permute-start | bytes 331784 | tf_op jit(solution)/shard_map/ppermute | solution.py:203
  145.5 26.7 %collective-permute-start.11 = (f32[216,128]{1,0:T(8,128)}, f32[216,128]{1,0:T(8,128)S(1)}, u32[]{:S(2)}, u32[]{:S(2)}) collective-permute-start(f32[216,128]{1,0:T(8,128)} %get-tuple-element.33), channel_id=1, source_target_pairs={{0,3},{1,2},{2,1},{3,0},{4,7},{5,6},{6,5},{7,4},{8,11},{9,10},{10,... | collective-permute-start | bytes 331784 | tf_op jit(solution)/shard_map/ppermute | solution.py:203
  145.5 0.7 copy-start.17
  145.5 27.0 %collective-permute-start.9 = (f32[216,128]{1,0:T(8,128)}, f32[216,128]{1,0:T(8,128)S(1)}, u32[]{:S(2)}, u32[]{:S(2)}) collective-permute-start(f32[216,128]{1,0:T(8,128)} %get-tuple-element.32.refs_0_), channel_id=1, source_target_pairs={{0,1},{1,0},{2,3},{3,2},{4,5},{5,4},{6,7},{7,6},{8,9},{9,8},{10,11... | collective-permute-start | bytes 331784 | tf_op jit(solution)/shard_map/ppermute | solution.py:203
  146.2 0.6 copy-start.15
  146.2 0.7 copy-start.16
  150.2 31.2 %collective-permute-start.21 = (f32[144,256]{1,0:T(8,128)}, f32[144,256]{1,0:T(8,128)S(1)}, u32[]{:S(2)}, u32[]{:S(2)}) collective-permute-start(f32[144,256]{1,0:T(8,128)} %get-tuple-element.42), channel_id=1, source_target_pairs={{0,4},{4,0},{8,12},{12,8},{1,5},{5,1},{9,13},{13,9},{2,6},{6,2},{1... | collective-permute-start | bytes 442376 | tf_op jit(solution)/shard_map/ppermute | solution.py:203
  161.1 11.4 %copy-start.26 = (f32[144,256]{1,0:T(8,128)S(1)}, f32[144,256]{1,0:T(8,128)}, u32[]{:S(2)}) copy-start(f32[144,256]{1,0:T(8,128)} %get-tuple-element.43) | copy-start | bytes 442372
  161.1 15.8 %copy-start.25 = (f32[144,256]{1,0:T(8,128)S(1)}, f32[144,256]{1,0:T(8,128)}, u32[]{:S(2)}) copy-start(f32[144,256]{1,0:T(8,128)} %get-tuple-element.44) | copy-start | bytes 442372
  170.7 6.2 %collective-permute-start.3 = (f32[144,128]{1,0:T(8,128)}, f32[144,128]{1,0:T(8,128)S(1)}, u32[]{:S(2)}, u32[]{:S(2)}) collective-permute-start(f32[144,128]{1,0:T(8,128)} %get-tuple-element.27.refs_0_), channel_id=1, source_target_pairs={{0,1},{1,0},{2,3},{3,2},{4,5},{5,4},{6,7},{7,6},{8,9},{9,8},{10,11... | collective-permute-start | bytes 221192 | tf_op jit(solution)/shard_map/ppermute | solution.py:203
  170.7 2.9 %copy-start.12 = (f32[216,128]{1,0:T(8,128)}, f32[216,128]{1,0:T(8,128)S(1)}, u32[]{:S(2)}) copy-start(f32[216,128]{1,0:T(8,128)S(1)} %collective-permute-done.10.refs_2_) | copy-start | bytes 331780
  170.7 8.3 %collective-permute-start.4 = (f32[144,128]{1,0:T(8,128)}, f32[144,128]{1,0:T(8,128)S(1)}, u32[]{:S(2)}, u32[]{:S(2)}) collective-permute-start(f32[144,128]{1,0:T(8,128)} %get-tuple-element.28), channel_id=1, source_target_pairs={{0,2},{1,3},{2,0},{3,1},{4,6},{5,7},{6,4},{7,5},{8,10},{9,11},{10,... | collective-permute-start | bytes 221192 | tf_op jit(solution)/shard_map/ppermute | solution.py:203
  172.2 1.3 copy-start.13
  172.2 7.3 %collective-permute-start.5 = (f32[144,128]{1,0:T(8,128)}, f32[144,128]{1,0:T(8,128)S(1)}, u32[]{:S(2)}, u32[]{:S(2)}) collective-permute-start(f32[144,128]{1,0:T(8,128)} %get-tuple-element.28), channel_id=1, source_target_pairs={{0,3},{1,2},{2,1},{3,0},{4,7},{5,6},{6,5},{7,4},{8,11},{9,10},{10,... | collective-permute-start | bytes 221192 | tf_op jit(solution)/shard_map/ppermute | solution.py:203
  172.6 1.0 copy-start.14
  172.6 13.8 %collective-permute-start.22 = (f32[144,256]{1,0:T(8,128)S(1)}, f32[144,256]{1,0:T(8,128)S(1)}, u32[]{:S(2)}, u32[]{:S(2)}) collective-permute-start(f32[144,256]{1,0:T(8,128)S(1)} %copy-done.26), channel_id=1, source_target_pairs={{0,8},{4,12},{8,0},{12,4},{1,9},{5,13},{9,1},{13,5},{2,10},{6,14},... | collective-permute-start | bytes 442376 | tf_op jit(solution)/shard_map/ppermute | solution.py:203
  176.9 6.5 %copy-start.18 = (f32[144,128]{1,0:T(8,128)}, f32[144,128]{1,0:T(8,128)S(1)}, u32[]{:S(2)}) copy-start(f32[144,128]{1,0:T(8,128)S(1)} %collective-permute-done.3.refs_1_) | copy-start | bytes 221188
  176.9 9.4 %collective-permute-start.23 = (f32[144,256]{1,0:T(8,128)S(1)}, f32[144,256]{1,0:T(8,128)S(1)}, u32[]{:S(2)}, u32[]{:S(2)}) collective-permute-start(f32[144,256]{1,0:T(8,128)S(1)} %copy-done.25), channel_id=1, source_target_pairs={{0,12},{4,8},{8,4},{12,0},{1,13},{5,9},{9,5},{13,1},{2,14},{6,10},... | collective-permute-start | bytes 442376 | tf_op jit(solution)/shard_map/ppermute | solution.py:203
  179.0 4.4 %copy-start.19 = (f32[144,128]{1,0:T(8,128)}, f32[144,128]{1,0:T(8,128)S(1)}, u32[]{:S(2)}) copy-start(f32[144,128]{1,0:T(8,128)S(1)} %collective-permute-done.4.refs_2_) | copy-start | bytes 221188
  179.0 9.8 %collective-permute-start.12 = (f32[144,256]{1,0:T(8,128)}, f32[144,256]{1,0:T(8,128)S(1)}, u32[]{:S(2)}, u32[]{:S(2)}) collective-permute-start(f32[144,256]{1,0:T(8,128)} %get-tuple-element.34), channel_id=1, source_target_pairs={{0,4},{4,0},{8,12},{12,8},{1,5},{5,1},{9,13},{13,9},{2,6},{6,2},{1... | collective-permute-start | bytes 442376 | tf_op jit(solution)/shard_map/ppermute | solution.py:203
  179.6 3.9 %copy-start.20 = (f32[144,128]{1,0:T(8,128)}, f32[144,128]{1,0:T(8,128)S(1)}, u32[]{:S(2)}) copy-start(f32[144,128]{1,0:T(8,128)S(1)} %collective-permute-done.5.refs_3_) | copy-start | bytes 221188
  179.6 18.8 %collective-permute-start.13 = (f32[144,256]{1,0:T(8,128)}, f32[144,256]{1,0:T(8,128)S(1)}, u32[]{:S(2)}, u32[]{:S(2)}) collective-permute-start(f32[144,256]{1,0:T(8,128)} %get-tuple-element.35), channel_id=1, source_target_pairs={{0,8},{4,12},{8,0},{12,4},{1,9},{5,13},{9,1},{13,5},{2,10},{6,14},... | collective-permute-start | bytes 442376 | tf_op jit(solution)/shard_map/ppermute | solution.py:203
  181.4 17.1 %copy-start.6 = (f32[144,256]{1,0:T(8,128)}, f32[144,256]{1,0:T(8,128)S(1)}, u32[]{:S(2)}) copy-start(f32[144,256]{1,0:T(8,128)S(1)} %collective-permute-done.21.refs_4_) | copy-start | bytes 442372
  181.4 17.0 %collective-permute-start.14 = (f32[144,256]{1,0:T(8,128)}, f32[144,256]{1,0:T(8,128)S(1)}, u32[]{:S(2)}, u32[]{:S(2)}) collective-permute-start(f32[144,256]{1,0:T(8,128)} %get-tuple-element.36), channel_id=1, source_target_pairs={{0,12},{4,8},{8,4},{12,0},{1,13},{5,9},{9,5},{13,1},{2,14},{6,10},... | collective-permute-start | bytes 442376 | tf_op jit(solution)/shard_map/ppermute | solution.py:203
  186.4 12.1 %copy-start.7 = (f32[144,256]{1,0:T(8,128)}, f32[144,256]{1,0:T(8,128)S(1)}, u32[]{:S(2)}) copy-start(f32[144,256]{1,0:T(8,128)S(1)} %collective-permute-done.22.refs_5_) | copy-start | bytes 442372
  186.4 12.1 %copy-start.8 = (f32[144,256]{1,0:T(8,128)}, f32[144,256]{1,0:T(8,128)S(1)}, u32[]{:S(2)}) copy-start(f32[144,256]{1,0:T(8,128)S(1)} %collective-permute-done.23.refs_6_) | copy-start | bytes 442372
  188.8 9.6 %copy-start.9 = (f32[144,256]{1,0:T(8,128)}, f32[144,256]{1,0:T(8,128)S(1)}, u32[]{:S(2)}) copy-start(f32[144,256]{1,0:T(8,128)S(1)} %collective-permute-done.12.refs_1_) | copy-start | bytes 442372
  198.4 0.7 copy-start.10
  198.4 0.7 copy-start.11
Sparse Core Ops, SparseCore 0:
  14.9 40.6 reduce-scatter.1

commit v2 on v1

v2 whole, which is shorter than its diff:
```python
import functools

import jax
import jax.numpy as jnp
from jax import lax
from jax.experimental import pallas as pl
from jax.experimental.pallas import tpu as pltpu
from jax.sharding import PartitionSpec as P

ADAPTER_RANK = 64
TOKEN_LIMIT = 12
VMEM_LIMIT = 48 * 1024 * 1024
F32 = jnp.float32
BF16 = jnp.bfloat16
I32 = jnp.int32
ANYWHERE = pl.BlockSpec(memory_space=pl.ANY)
PARAMS = pltpu.CompilerParams(vmem_limit_bytes=VMEM_LIMIT)


def cost(rows, depth, columns, terms=1):
    return pl.CostEstimate(
        flops=2 * rows * depth * columns * terms,
        transcendentals=0,
        bytes_accessed=2 * terms * (rows + columns) * depth + 4 * rows * columns,
    )


def owner_of(ids, owners, owned):
    total = jnp.zeros_like(ids)
    for o in range(1, owners):
        total = total + jnp.where(ids >= o * owned, 1, 0)
    return total


def move_rows(pieces, cap, slot, tok_ref, outs):
    for (block, first, count), out in zip(pieces, outs):
        at = block * cap + first + lax.broadcasted_iota(I32, (count, slot.shape[1]), 0)
        place = jnp.where(at == slot, 1.0, 0.0).astype(BF16)
        out[...] = jnp.dot(place, tok_ref[...], preferred_element_type=F32).astype(BF16)


def head_kernel(owners, owned, cap, pieces, me_ref, row_ref, tok_ref, *refs):
    outs, slot_ref, slot = refs[: len(pieces)], refs[-2], refs[-1]
    rows = row_ref.shape[1]

    @pl.when(pl.program_id(0) == 0)
    def _():
        id_row = row_ref[...]
        key_row = id_row * rows + lax.broadcasted_iota(I32, (1, rows), 1)
        down = lax.broadcasted_iota(I32, (rows, rows), 0)
        across = lax.broadcasted_iota(I32, (rows, rows), 1)
        key_col = jnp.sum(jnp.where(down == across, key_row, 0), axis=1, keepdims=True)
        own_row = owner_of(id_row, owners, owned)
        before = (key_col < key_row) & (key_col >= own_row * (owned * rows))
        rank = jnp.sum(jnp.where(before, 1, 0), axis=0, keepdims=True)
        found = (own_row ^ me_ref[0]) * cap + rank
        slot[...] = found
        slot_ref[...] = found

    move_rows(pieces, cap, slot[...], tok_ref, outs)


def rest_kernel(cap, pieces, slot_ref, tok_ref, *refs):
    outs, target_ref = refs[: len(pieces)], refs[-1]
    rows = slot_ref.shape[1]

    @pl.when(pl.program_id(0) == 0)
    def _():
        down = lax.broadcasted_iota(I32, (rows, rows), 0)
        across = lax.broadcasted_iota(I32, (rows, rows), 1)
        target_ref[...] = jnp.sum(
            jnp.where(down == across, slot_ref[...], 0), axis=1, keepdims=True
        )

    move_rows(pieces, cap, slot_ref[...], tok_ref, outs)


def sort_rows(tokens, ids_row, me, owners, owned, cap, first, rest):
    rows, width = tokens.shape
    step = min(512, width)
    line = pl.BlockSpec((1, rows), lambda i: (0, 0))
    strip = pl.BlockSpec((rows, step), lambda i: (0, i))

    def outs(pieces):
        specs = [pl.BlockSpec((count, step), lambda i: (0, i)) for _, _, count in pieces]
        return specs, [jax.ShapeDtypeStruct((count, width), BF16) for _, _, count in pieces]

    specs, shapes = outs(first)
    *sent, slot = pl.pallas_call(
        functools.partial(head_kernel, owners, owned, cap, first),
        grid=(width // step,),
        in_specs=[pl.BlockSpec(memory_space=pltpu.SMEM), line, strip],
        out_specs=specs + [line],
        out_shape=shapes + [jax.ShapeDtypeStruct((1, rows), I32)],
        scratch_shapes=[pltpu.VMEM((1, rows), I32)],
        compiler_params=PARAMS,
        cost_estimate=cost(sum(c for _, _, c in first), rows, width),
        name="sort_first",
    )(me, ids_row, tokens)
    specs, shapes = outs(rest)
    *others, target = pl.pallas_call(
        functools.partial(rest_kernel, cap, rest),
        grid=(width // step,),
        in_specs=[line, strip],
        out_specs=specs + [pl.BlockSpec((rows, 1), lambda i: (0, 0))],
        out_shape=shapes + [jax.ShapeDtypeStruct((rows, 1), I32)],
        compiler_params=PARAMS,
        cost_estimate=cost(sum(c for _, _, c in rest), rows, width),
        name="sort_rest",
    )(slot, tokens)
    return sent, others, target


def base_kernel(tok_ref, weight_ref, _, out_ref):
    out_ref[...] = jnp.dot(tok_ref[...], weight_ref[...], preferred_element_type=F32)


def base_product(tokens, weight, later_than):
    (rows, width), columns = tokens.shape, weight.shape[1]
    step = min(256, columns)
    return pl.pallas_call(
        base_kernel,
        grid=(columns // step,),
        in_specs=[
            pl.BlockSpec((rows, width), lambda i: (0, 0)),
            pl.BlockSpec((width, step), lambda i: (0, i)),
            ANYWHERE,
        ],
        out_specs=pl.BlockSpec((rows, step), lambda i: (0, i)),
        out_shape=jax.ShapeDtypeStruct((rows, columns), F32),
        compiler_params=PARAMS,
        cost_estimate=cost(rows, width, columns),
        name="base",
    )(tokens, weight, later_than)


def shrink_kernel(sizes, group, fine, waits, plan_ref, which_ref, down_ref, *refs):
    blocks, (mine_ref, other_ref, rows, acc) = refs[: len(sizes)], refs[len(sizes) + waits :]
    step, rank2 = pl.program_id(0), 2 * ADAPTER_RANK
    low, high, second = plan_ref[0], plan_ref[1], plan_ref[2] == 1
    begin = (low // group + step) * group

    @pl.when(step == 0)
    def _():
        at = 0
        for size, block in zip(sizes, blocks):
            rows[at : at + size, :] = block[...]
            at += size
        acc[...] = jnp.zeros_like(acc)

    for f in range(0, group, fine):

        @pl.when((begin + f <= high) & (begin + f + fine > low))
        def _(f=f):
            factors = down_ref[f : f + fine].reshape(fine * rank2, down_ref.shape[2])
            product = lax.dot_general(
                rows[...], factors, (((1,), (1,)), ((), ())), preferred_element_type=F32
            )
            which = which_ref[...] - (begin + f)
            found = acc[...]
            for q in range(fine):
                part = product[:, q * rank2 : (q + 1) * rank2]
                found = found + jnp.where(which == q, part, 0.0)
            acc[...] = found

    @pl.when(step == pl.num_programs(0) - 1)
    def _():
        total = sum(sizes)
        upper, lower = acc[: total // 2, :], acc[total // 2 :, :]
        keys = jnp.concatenate([upper[:, :ADAPTER_RANK], lower[:, :ADAPTER_RANK]], axis=1)
        values = jnp.concatenate([upper[:, ADAPTER_RANK:], lower[:, ADAPTER_RANK:]], axis=1)
        mine_ref[...] = jnp.where(second, values, keys)
        other_ref[...] = jnp.where(second, keys, values)


def shrink(blocks, names, down, half, later_than=()):
    sizes = tuple(b.shape[0] for b in blocks)
    total = sum(sizes)
    owned, rank2, width = down.shape
    group = next(g for g in (4, 3, 2, 1) if owned % g == 0)
    fine = next(g for g in (2, 3, 1) if group % g == 0)
    low = jnp.minimum(jnp.min(names), owned - 1)
    high = jnp.maximum(jnp.max(jnp.where(names < owned, names, 0)), low)
    line = jax.ShapeDtypeStruct((total // 2, 2 * ADAPTER_RANK), F32)
    return pl.pallas_call(
        functools.partial(shrink_kernel, sizes, group, fine, len(later_than)),
        grid_spec=pltpu.PrefetchScalarGridSpec(
            num_scalar_prefetch=1,
            grid=(owned // group,),
            in_specs=[
                pl.BlockSpec((total, 1), lambda i, p: (0, 0)),
                pl.BlockSpec(
                    (group, rank2, width),
                    lambda i, p: (jnp.minimum(p[0] // group + i, p[1] // group), 0, 0),
                ),
            ]
            + [pl.BlockSpec((s, width), lambda i, p: (0, 0)) for s in sizes]
            + [ANYWHERE] * len(later_than),
            out_specs=[pl.BlockSpec((total // 2, rank2), lambda i, p: (0, 0))] * 2,
            scratch_shapes=[pltpu.VMEM((total, width), BF16), pltpu.VMEM((total, rank2), F32)],
        ),
        out_shape=[line, line],
        compiler_params=PARAMS,
        cost_estimate=cost(total, width, owned * rank2),
        name="shrink",
    )(jnp.stack([low, high, half]).astype(I32), names.reshape(-1, 1), down, *blocks, *later_than)


def split(x, terms):
    parts = []
    for _ in range(terms - 1):
        parts.append(x.astype(BF16).astype(F32))
        x = x - parts[-1]
    return parts + [x]


def expand_kernel(sizes, heard, which_ref, scale_ref, up_ref, *refs):
    lines, outs = refs[:heard], refs[heard:]
    total = lines[0][...]
    for line in lines[1:]:
        total = total + line[...]
    upper, lower = total[:, :ADAPTER_RANK], total[:, ADAPTER_RANK:]
    twice = jnp.concatenate(
        [jnp.concatenate([upper, upper], axis=1), jnp.concatenate([lower, lower], axis=1)], axis=0
    )
    which = which_ref[...]
    parity = jnp.where(lax.broadcasted_iota(I32, (1, 2 * ADAPTER_RANK), 1) >= ADAPTER_RANK, 1, 0)
    pairs = up_ref.shape[0] // (2 * ADAPTER_RANK)
    wanted = [which == 2 * p + parity for p in range(pairs)]
    delta = None
    for term in split(twice, 3):
        spread = jnp.concatenate([jnp.where(w, term, 0.0).astype(BF16) for w in wanted], axis=1)
        product = jnp.dot(spread, up_ref[...], preferred_element_type=F32)
        delta = product if delta is None else delta + product
    adapters = lax.broadcasted_iota(I32, scale_ref.shape, 1)
    gain = jnp.sum(jnp.where(which == adapters, scale_ref[...], 0.0), axis=1, keepdims=True)
    delta = delta * gain
    begin = 0
    for size, out in zip(sizes, outs):
        out[...] = delta[begin : begin + size, :]
        begin += size


def expand(lines, names, scale, up, sizes):
    columns = up.shape[1]
    return pl.pallas_call(
        functools.partial(expand_kernel, sizes, len(lines)),
        out_shape=[jax.ShapeDtypeStruct((s, columns), F32) for s in sizes],
        compiler_params=PARAMS,
        cost_estimate=cost(sum(sizes), up.shape[0], columns, 3),
        name="expand",
    )(names.reshape(-1, 1), scale, up, *lines)


def merge_kernel(begins, parts, target_ref, *refs):
    blocks, out_ref = refs[parts:-1], refs[-1]
    returned = jnp.concatenate([b[...] for b in blocks], axis=0)
    target = target_ref[...]
    place = jnp.concatenate(
        [
            jnp.where(
                target == begin + lax.broadcasted_iota(I32, (1, block.shape[0]), 1), 1.0, 0.0
            ).astype(BF16)
            for begin, block in zip(begins, blocks)
        ],
        axis=1,
    )
    total = refs[0][...]
    for part in refs[1:parts]:
        total = total + part[...]
    for term in split(returned, 3):
        total = total + jnp.dot(place, term.astype(BF16), preferred_element_type=F32)
    out_ref[...] = total.astype(out_ref.dtype)


def merge(parts, target, begins, blocks, kind):
    return pl.pallas_call(
        functools.partial(merge_kernel, tuple(begins), len(parts)),
        out_shape=jax.ShapeDtypeStruct(parts[0].shape, kind),
        compiler_params=PARAMS,
        cost_estimate=cost(parts[0].shape[0], sum(b.shape[0] for b in blocks), parts[0].shape[1], 3),
        name="merge",
    )(target, *parts, *blocks)


def swap(x, axes, size, distance):
    return lax.ppermute(x, axes, [(i, i ^ distance) for i in range(size)])


def up_to_16(count):
    return -(-count // 16) * 16


def local(
    tokens,
    key_value_weight,
    adapter_down_weight,
    adapter_up_weight,
    adapter_scale,
    token_adapter_index,
):
    feature_axes = ("tensor", "sub")
    rows = tokens.shape[0]
    owned = adapter_down_weight.shape[0]
    owners = lax.axis_size("dp")
    sharers = lax.axis_size(feature_axes)
    me = lax.axis_index("dp")
    half = (lax.axis_index(feature_axes) >= sharers // 2).astype(I32)
    cap = up_to_16(owned * TOKEN_LIMIT)

    if owners == 4:
        usual = up_to_16(cap * 5 // 6)
        most = up_to_16(usual * 4 // 5)
        near = [(1, 0, cap)]
        far = [[(3, 0, most), (2, 0, most)], [(3, most, usual - most), (2, most, usual - most)]]
        extra = [(3, usual, cap - usual), (2, usual, cap - usual)]
    else:
        usual, near, extra = cap, [(1, 0, cap)], []
        far = [[(j, 0, cap) for j in range(2, owners)]]
    head = far[0]
    own = (0, 0, cap)

    ids_row = token_adapter_index.reshape(1, rows)
    ids_all = lax.all_gather(ids_row, ("parts", "dp"), axis=0, tiled=True)
    rest = near + [p for s in far[1:] for p in s] + extra + [own]
    sent_first, sent_rest, target = sort_rows(
        tokens, ids_row, me.reshape(1), owners, owned, cap, head, rest
    )
    packed = dict(zip(head + rest, sent_first + sent_rest))
    received = {p: swap(packed[p], "dp", owners, p[0]) for s in [near, *far] for p in s}

    group_of = lax.axis_index("parts") * owners
    sources = group_of + (me ^ jnp.arange(owners, dtype=I32))
    everyone = jnp.arange(ids_all.shape[0], dtype=I32)
    chosen = sources[:, None, None] == everyone[None, :, None]
    heard = jnp.sum(jnp.where(chosen, ids_all[None], 0), axis=1, dtype=I32) - me * owned
    adapters = jnp.arange(owned, dtype=I32)
    upto = jnp.sum(
        (heard[:, None, :] >= 0) & (heard[:, None, :] <= adapters[None, :, None]), axis=2, dtype=I32
    )
    at = jnp.arange(cap, dtype=I32)
    which = jnp.sum(upto[:, None, :] <= at[None, :, None], axis=2, dtype=I32)

    if owned % 2:
        adapter_up_weight = jnp.pad(adapter_up_weight, ((0, 1), (0, 0), (0, 0)))
    up = adapter_up_weight.reshape(-1, adapter_up_weight.shape[2])
    scale = adapter_scale.reshape(1, owned)

    def shares(pieces, blocks, later_than):
        names = jnp.concatenate([which[b, f : f + c] for b, f, c in pieces])
        mine, other = shrink(blocks, names, adapter_down_weight, half, later_than)
        lines = [mine] + [
            swap(mine if d < sharers // 2 else other, feature_axes, sharers, d)
            for d in range(1, sharers)
        ]
        return expand(lines, names, scale, up, tuple(c for _, _, c in pieces))

    def begins(pieces):
        return [b * cap + f for b, f, _ in pieces]

    arrived = received[near[0]]
    base_part = base_product(tokens, key_value_weight, arrived)
    base = lax.psum_scatter(base_part, feature_axes, scatter_dimension=1, tiled=True)
    at_hand = [own] + near
    deltas = shares(at_hand, [packed[own]] + [received[p] for p in near], (base_part,))
    total = jnp.zeros((rows, up.shape[1]), F32)
    total = merge([total], target, begins([own]), deltas[:1], F32)

    if extra:
        counts = jnp.sum(
            (ids_all[:, None, :] >= owned * jnp.arange(owners, dtype=I32)[None, :, None])
            & (ids_all[:, None, :] < owned * (1 + jnp.arange(owners, dtype=I32))[None, :, None]),
            axis=2,
            dtype=I32,
        )
        away = (everyone[:, None] % owners) ^ jnp.arange(owners, dtype=I32)[None, :]
        more = jnp.max(jnp.where(away >= 2, counts, 0)) > usual

        def with_extra(so_far):
            blocks = [swap(packed[p], "dp", owners, p[0]) for p in extra]
            found = shares(extra, blocks, ())
            back = [swap(d, "dp", owners, p[0]) for p, d in zip(extra, found)]
            return merge([so_far], target, begins(extra), back, F32)

        total = lax.cond(more, with_extra, lambda so_far: so_far, total)

    last = total
    returned = [swap(d, "dp", owners, p[0]) for p, d in zip(near, deltas[1:])]
    for pieces in far:
        deltas = shares(pieces, [received[p] for p in pieces], (last,))
        returned += [swap(d, "dp", owners, p[0]) for p, d in zip(pieces, deltas)]
        last = deltas[0]
    pieces = near + [p for s in far for p in s]
    return merge([base, total], target, begins(pieces), returned, BF16)


def solution(mesh):
    return jax.shard_map(
        local,
        mesh=mesh,
        in_specs=(
            P(("parts", "dp"), ("tensor", "sub")),
            P(("tensor", "sub"), None),
            P("dp", None, ("tensor", "sub")),
            P("dp", None, ("tensor", "sub")),
            P("dp"),
            P(("parts", "dp"), None),
        ),
        out_specs=P(("parts", "dp"), ("tensor", "sub")),
        check_vma=False,
    )
```

time: 212 us -> 249 us (1.17)
  blocking collectives: 0 us -> 89.2 us
  waiting for transfers between devices: 74.3 us -> 47.8 us
  starting transfers between devices: 40.1 us -> 23.4 us
  Pallas kernels: 65 us -> 54.4 us
  matrix products: 8.18 us -> 0 us
  between operations: 13.6 us -> 19.9 us
  other arithmetic: 0.45 us -> 6.57 us
    all_gather x0 -> x1, blocking collectives: none -> 89.2 us  [local(): ids_all = lax.all_gather(ids_row, ('parts', 'dp'), axis=0, tiled=True)]
    ppermute x24 -> x19, waiting for transfers between devices: 74.2 us -> 47.8 us  [swap(): return lax.ppermute(x, axes, [(i, i ^ distance) for i in range(size)])]
    ppermute x24 -> x19, starting transfers between devices: 40.1 us -> 23.4 us  [swap(): return lax.ppermute(x, axes, [(i, i ^ distance) for i in range(size)])]
    dot_general x1 -> x0, matrix products: 8.18 us -> none  [local(): base_part = jnp.dot(tokens, key_value_weight, preferred_element_type=F32)]
    pallas_call x5 -> x8, Pallas kernels: 55.3 us -> 49.9 us  [the longest x3 27.3 us: shrink(): pl.pallas_call(functools.partial(shrink_kernel, sizes, group, fine, len(l...]
    pallas_call x3, Pallas kernels: 9.63 us -> 4.48 us  [expand(): pl.pallas_call(functools.partial(expand_kernel, sizes, len(lines)), out_s...]
    reduce_max x0 -> x4, other arithmetic: none -> 2.8 us  [the longest x3 2.16 us: shrink(): high = jnp.maximum(jnp.max(jnp.where(names < owned, names, 0)), low)]
    unnamed x55 -> x20, local copies, waits for them, and re-layouts: 5.7 us -> 6.02 us
  transfers between devices with their start and end apart: 25 -> 20, of which waited for: 5 -> 8; matrix products, arithmetic and copies ran while one was open for 2% -> 3% of each run, Pallas kernels for 29% -> 14%
where the time goes in v2:
time: 249 us; the launch traced here: 248 us
  blocking collectives  89.2 us (36%)
  Pallas kernels  54.4 us (22%)
  waiting for transfers between devices  47.8 us (19%)
  starting transfers between devices  23.4 us (9%)
  between operations  19.9 us (8%)
  local copies, waits for them, and re-layouts  6.93 us (3%)
  other arithmetic  6.57 us (3%)
    all_gather x1, blocking collectives, local(): ids_all = lax.all_gather(ids_row, ('parts', 'dp'), axis=0, tiled=True)  89.2 us
    ppermute x19, waiting for transfers between devices, swap(): return lax.ppermute(x, axes, [(i, i ^ distance) for i in range(size)])  47.8 us
    pallas_call x3, Pallas kernels, shrink(): pl.pallas_call(functools.partial(shrink_kernel, sizes, group, fine, len(l...  27.3 us
    ppermute x19, starting transfers between devices, swap(): return lax.ppermute(x, axes, [(i, i ^ distance) for i in range(size)])  23.4 us
    pallas_call x1, Pallas kernels, base_product(): pl.pallas_call(base_kernel, grid=(columns // step,), in_specs=[pl.BlockSp...  7.73 us
    pallas_call x1, Pallas kernels, sort_rows(): pl.pallas_call(functools.partial(rest_kernel, cap, rest), grid=(width //...  6.27 us
    unnamed x20, local copies, waits for them, and re-layouts  6.02 us
    pallas_call x2, Pallas kernels, merge(): pl.pallas_call(functools.partial(merge_kernel, tuple(begins), len(parts))...  5.71 us
  transfers between devices with their start and end apart: 20, of which 8 were waited for; matrix products, arithmetic and copies ran while one was open for 3% of the time, Pallas kernels for 14%

profile of v2, /device:TPU:0, one launch (start us, length us, event | category | flops | bytes accessed | tf_op | source)
XLA Modules:
  0.0 248.2 jit_solution(17894058248148582400)
XLA Ops:
  6.5 0.7 copy-done
  7.2 1.9 copy-done.2
  9.1 2.9 %sort_first.1 = (bf16[192,2048]{1,0:T(8,128)(2,1)S(1)}, bf16[192,2048]{1,0:T(8,128)(2,1)S(1)}, s32[1,768]{1,0:T(1,128)S(1)}) custom-call(s32[1]{0:T(128)} %bitcast.6.me_ref, s32[1,768]{1,0:T(1,128)S(1)} %bitcast.29, bf16[768,2048]{1,0:T(8,128)(2,1)S(1)} %copy-done.2), custom_call_target="tpu_custom_call" | custom-call | flops 1207959552 | bytes 6881280 | tf_op jit(solution)/shard_map/sort_first/pallas_call | solution.py:89
  12.0 6.3 %sort_rest.1 = (bf16[288,2048]{1,0:T(8,128)(2,1)S(1)}, bf16[48,2048]{1,0:T(8,128)(2,1)S(1)}, bf16[48,2048]{1,0:T(8,128)(2,1)S(1)}, bf16[48,2048]{1,0:T(8,128)(2,...) custom-call(s32[1,768]{1,0:T(1,128)S(1)} %get-tuple-element.62.slot_ref, ...), custom_call_target="tpu_custom_call" | custom-call | flops 2415919104 | bytes 10616832 | tf_op jit(solution)/shard_map/sort_rest/pallas_call | solution.py:101
  18.3 1.0 copy-done.5
  19.3 3.0 %collective-permute-start.7 = (bf16[288,2048]{1,0:T(8,128)(2,1)S(1)}, bf16[288,2048]{1,0:T(8,128)(2,1)S(1)}, u32[]{:S(2)}, u32[]{:S(2)}) collective-permute-start(bf16[288,2048]{1,0:T(8,128)(2,1)S(1)} %get-tuple-element.64), channel_id=1, source_target_pairs={{0,4},{4,0},{8,12},{12,8},{1,5},{5,1},{9,13},{13,9},{2,6},{6,2},{1... | collective-permute-start | bytes 3538952 | tf_op jit(solution)/shard_map/ppermute | solution.py:287
  22.3 26.0 %collective-permute-done.7._.refs_1_ = bf16[288,2048]{1,0:T(8,128)(2,1)S(1)} collective-permute-done((bf16[288,2048]{1,0:T(8,128)(2,1)S(1)}, bf16[288,2048]{1,0:T(8,128)(2,1)S(1)}, u32[]{:S(2)}, u32[]{:S(2)}) %collective-permute-start.7) | collective-permute-done | bytes 1179680 | tf_op jit(solution)/shard_map/ppermute | solution.py:287
  48.3 7.7 %base.1.refs_2_ = f32[768,1024]{1,0:T(8,128)} custom-call(bf16[768,2048]{1,0:T(8,128)(2,1)} %tok_ref.5, bf16[2048,1024]{1,0:T(8,128)(2,1)} %weight_ref.1, bf16[288,2048]{1,0:T(8,128)(2,1)S(1)} %collective-permute-done.7._.refs_1_), custom_call_target="tpu_custom_call" | custom-call | flops 3221225472 | bytes 10485760 | tf_op jit(solution)/shard_map/base/pallas_call | solution.py:121
  56.0 0.0 reduce-scatter.2.cloned.1.call-update
  56.1 3.8 %collective-permute-start.12 = (bf16[192,2048]{1,0:T(8,128)(2,1)S(1)}, bf16[192,2048]{1,0:T(8,128)(2,1)}, u32[]{:S(2)}, u32[]{:S(2)}) collective-permute-start(bf16[192,2048]{1,0:T(8,128)(2,1)S(1)} %get-tuple-element.72), channel_id=1, source_target_pairs={{0,12},{4,8},{8,4},{12,0},{1,13},{5,9},{9,5},{13,1},{2,14},{6,10},... | collective-permute-start | bytes 2359304 | tf_op jit(solution)/shard_map/ppermute | solution.py:287
  59.9 89.2 %all-gather = s32[6144,1]{0,1:T(1,128)S(1)} all-gather(s32[768,1]{0,1:T(1,128)S(1)} %copy-done.1), channel_id=2, replica_groups=mesh['parts'=2,'dp'=4,'tensor'=2,'sub'=2] {'parts','dp'}, dimensions={0}, use_global_device_ids=true | all-gather | bytes 27648 | tf_op jit(solution)/shard_map/all_gather | solution.py:324
  149.0 0.5 broadcast.104
  149.6 0.7 reduce.23
  150.3 0.1 iota_compare_fusion.2
  150.4 0.1 select_reduce_fusion
  150.5 0.2 convert_reduce_fusion
  150.7 0.1 convert_reduce_fusion.1
  150.8 0.7 slice_reduce_fusion.2
  151.5 0.7 fusion.3
  152.2 0.1 reshape.101.which_ref
  154.1 0.1 add_add_fusion.plan_ref
  154.2 0.2 convert_reduce_fusion.2
  154.4 1.3 copy-done.6
  155.7 13.2 %shrink.5 = (f32[288,128]{1,0:T(8,128)}, f32[288,128]{1,0:T(8,128)}) custom-call(s32[3]{0:T(128)S(1)} %add_add_fusion.plan_ref, s32[576,1]{1,0:T(8,128)S(1)} %reshape.101.which_ref, bf16[24,128,2048]{2,1,0:T(8,128)(2,1)} %down_ref.5, bf16[288,2048]{1,0:T(8,128)(2,1)S(1)} %copy-done.6, bf16[288,2048]{1,0:T(8,128)(2,1)S(1)} %collective-permute-done.7._.refs_1_, ...), custom_call_target="tpu_custom_call" | custom-call | flops 7247757312 | bytes 22020096 | tf_op jit(solution)/shard_map/shrink/pallas_call | solution.py:185
  168.9 1.5 collective-permute-start.9
  170.4 0.3 collective-permute-start.8
  170.8 0.6 select_reduce_fusion.1
  172.0 3.2 %collective-permute-done.10.refs_3_ = f32[288,128]{1,0:T(8,128)S(1)} collective-permute-done((f32[288,128]{1,0:T(8,128)}, f32[288,128]{1,0:T(8,128)S(1)}, u32[]{:S(2)}, u32[]{:S(2)}) %collective-permute-start.10) | collective-permute-done | bytes 147488 | tf_op jit(solution)/shard_map/ppermute | solution.py:287
  175.2 3.2 %collective-permute-done.9.refs_2_ = f32[288,128]{1,0:T(8,128)S(1)} collective-permute-done((f32[288,128]{1,0:T(8,128)}, f32[288,128]{1,0:T(8,128)S(1)}, u32[]{:S(2)}, u32[]{:S(2)}) %collective-permute-start.9) | collective-permute-done | bytes 147488 | tf_op jit(solution)/shard_map/ppermute | solution.py:287
  178.4 2.8 %expand.5 = (f32[288,256]{1,0:T(8,128)S(1)}, f32[288,256]{1,0:T(8,128)S(1)}) custom-call(s32[576,1]{1,0:T(8,128)S(1)} %reshape.101.which_ref, f32[1,24]{1,0:T(1,128)S(1)} %bitcast.36, bf16[1536,256]{1,0:T(8,128)(2,1)} %bitcast.30, f32[288,128]{1,0:T(8,128)} %get-tuple-element.66.refs_0_, f32[288,128]{1,0:T(8,128)S(1)} %collective-permute-done.8.refs_1_, ...), custom_call_target="tpu_custom_call" | custom-call | flops 1358954496 | bytes 8257536 | tf_op jit(solution)/shard_map/expand/pallas_call | solution.py:246
  181.2 0.1 broadcast_in_dim.57.refs_0_
  181.3 2.7 %merge.4 = f32[768,256]{1,0:T(8,128)} custom-call(s32[768,1]{1,0:T(8,128)} %get-tuple-element.63.target_ref, f32[768,256]{1,0:T(8,128)S(1)} %broadcast_in_dim.57.refs_0_, f32[288,256]{1,0:T(8,128)S(1)} %get-tuple-element.68.refs_1_), custom_call_target="tpu_custom_call" | custom-call | flops 339738624 | bytes 2555904 | tf_op jit(solution)/shard_map/merge/pallas_call | solution.py:277
  184.0 1.3 collective-permute-start.19
  185.3 0.6 slice_reduce_fusion.8
  187.1 0.7 fusion.4
  187.8 0.1 reshape.102.which_ref
  187.9 0.8 slice_reduce_fusion.6
  190.1 0.8 fusion.5
  190.9 0.1 copy.26.which_ref
  192.4 0.1 add_add_fusion.1.plan_ref
  192.4 11.1 %shrink.6 = (f32[192,128]{1,0:T(8,128)S(1)}, f32[192,128]{1,0:T(8,128)S(1)}) custom-call(s32[3]{0:T(128)S(1)} %add_add_fusion.1.plan_ref, s32[384,1]{1,0:T(8,128)S(1)} %reshape.102.which_ref, bf16[24,128,2048]{2,1,0:T(8,128)(2,1)} %down_ref.5, bf16[192,2048]{1,0:T(8,128)(2,1)} %collective-permute-done.12.refs_0_, ...), custom_call_target="tpu_custom_call" | custom-call | flops 4831838208 | bytes 18874368 | tf_op jit(solution)/shard_map/shrink/pallas_call | solution.py:185
  203.6 0.1 collective-permute-start.15
  203.6 1.1 collective-permute-start.16
  204.8 1.0 collective-permute-start.14
  205.8 0.1 add_add_fusion.2.plan_ref
  205.8 0.9 collective-permute-done.14.refs_1_
  206.7 3.1 %collective-permute-start.11 = (f32[288,256]{1,0:T(8,128)S(1)}, f32[288,256]{1,0:T(8,128)S(1)}, u32[]{:S(2)}, u32[]{:S(2)}) collective-permute-start(f32[288,256]{1,0:T(8,128)S(1)} %get-tuple-element.71), channel_id=1, source_target_pairs={{0,4},{4,0},{8,12},{12,8},{1,5},{5,1},{9,13},{13,9},{2,6},{6,2},{1... | collective-permute-start | bytes 884744 | tf_op jit(solution)/shard_map/ppermute | solution.py:287
  209.8 1.2 expand.6
  211.0 1.9 collective-permute-start.17
  212.9 1.7 collective-permute-start.18
  214.7 3.0 %shrink.7 = (f32[48,128]{1,0:T(8,128)S(1)}, f32[48,128]{1,0:T(8,128)S(1)}) custom-call(s32[3]{0:T(128)S(1)} %add_add_fusion.2.plan_ref, s32[96,1]{1,0:T(8,128)S(1)} %copy.26.which_ref, bf16[24,128,2048]{2,1,0:T(8,128)(2,1)} %down_ref.5, bf16[48,2048]{1,0:T(8,128)(2,1)S(1)} %collective-permute-done.19.refs_0_, ...), custom_call_target="tpu_custom_call" | custom-call | flops 1207959552 | bytes 14155776 | tf_op jit(solution)/shard_map/shrink/pallas_call | solution.py:185
  217.7 0.4 collective-permute-start.21
  218.1 1.2 collective-permute-start.22
  219.3 0.9 collective-permute-start.23
  220.2 1.7 collective-permute-done.22.refs_2_
  221.9 0.7 collective-permute-done.23.refs_3_
  222.5 0.6 expand.7
  223.1 1.4 collective-permute-start.24
  224.5 0.6 collective-permute-start.25
  225.1 4.5 %collective-permute-done.24.refs_5_ = f32[48,256]{1,0:T(8,128)S(1)} collective-permute-done((f32[48,256]{1,0:T(8,128)S(1)}, f32[48,256]{1,0:T(8,128)S(1)}, u32[]{:S(2)}, u32[]{:S(2)}) %collective-permute-start.24) | collective-permute-done | bytes 49184 | tf_op jit(solution)/shard_map/ppermute | solution.py:287
  229.6 7.6 %collective-permute-done.25.refs_6_ = f32[48,256]{1,0:T(8,128)S(1)} collective-permute-done((f32[48,256]{1,0:T(8,128)S(1)}, f32[48,256]{1,0:T(8,128)S(1)}, u32[]{:S(2)}, u32[]{:S(2)}) %collective-permute-start.25) | collective-permute-done | bytes 49184 | tf_op jit(solution)/shard_map/ppermute | solution.py:287
  237.2 0.0 reduce-scatter.2.cloned.1.call-done.refs_0_
  237.2 1.1 copy-done.4
  238.4 3.0 %merge.5 = bf16[768,256]{1,0:T(8,128)(2,1)} custom-call(s32[768,1]{1,0:T(8,128)} %get-tuple-element.63.target_ref, f32[768,256]{1,0:T(8,128)S(1)} %copy-done.4, f32[768,256]{1,0:T(8,128)S(1)} %copy-done.10, f32[288,256]{1,0:T(8,128)S(1)} %collective-permute-done.11.refs_2_, f32[192,256]{1,0:T(8,128)S(1)} %collective-permute-done.17.refs_3_, ...), custom_call_target="tpu_custom_call" | custom-call | flops 905969664 | bytes 5505024 | tf_op jit(solution)/shard_map/merge/pallas_call | solution.py:277
  (36 shorter events, 0.1 us)
Async XLA Ops:
  6.5 230.7 %reduce-scatter.2.cloned.1.call-start = ((), (), s32[]{:S(2)}) async-start(), calls=%async_computation.1 | async-start | bytes 3932160 | tf_op jit(solution)/shard_map/reduce_scatter | solution.py:363
  6.5 0.7 copy-start
  7.2 1.9 copy-start.2
  9.1 2.9 %copy-start.3 = (bf16[768,2048]{1,0:T(8,128)(2,1)S(1)}, bf16[768,2048]{1,0:T(8,128)(2,1)}, u32[]{:S(2)}) copy-start(bf16[768,2048]{1,0:T(8,128)(2,1)} %tok_ref.5) | copy-start | bytes 9437188
  18.3 1.0 copy-start.5
  19.3 29.0 %collective-permute-start.7 = (bf16[288,2048]{1,0:T(8,128)(2,1)S(1)}, bf16[288,2048]{1,0:T(8,128)(2,1)S(1)}, u32[]{:S(2)}, u32[]{:S(2)}) collective-permute-start(bf16[288,2048]{1,0:T(8,128)(2,1)S(1)} %get-tuple-element.64), channel_id=1, source_target_pairs={{0,4},{4,0},{8,12},{12,8},{1,5},{5,1},{9,13},{13,9},{2,6},{6,2},{1... | collective-permute-start | bytes 3538952 | tf_op jit(solution)/shard_map/ppermute | solution.py:287
  56.0 3.9 %copy-start.1 = (s32[768,1]{0,1:T(1,128)S(1)}, s32[768,1]{0,1:T(1,128)}, u32[]{:S(2)}) copy-start(s32[768,1]{0,1:T(1,128)} %param.13) | copy-start | bytes 9220
  56.1 136.4 %collective-permute-start.12 = (bf16[192,2048]{1,0:T(8,128)(2,1)S(1)}, bf16[192,2048]{1,0:T(8,128)(2,1)}, u32[]{:S(2)}, u32[]{:S(2)}) collective-permute-start(bf16[192,2048]{1,0:T(8,128)(2,1)S(1)} %get-tuple-element.72), channel_id=1, source_target_pairs={{0,12},{4,8},{8,4},{12,0},{1,13},{5,9},{9,5},{13,1},{2,14},{6,10},... | collective-permute-start | bytes 2359304 | tf_op jit(solution)/shard_map/ppermute | solution.py:287
  59.9 132.6 %collective-permute-start.13 = (bf16[192,2048]{1,0:T(8,128)(2,1)S(1)}, bf16[192,2048]{1,0:T(8,128)(2,1)}, u32[]{:S(2)}, u32[]{:S(2)}) collective-permute-start(bf16[192,2048]{1,0:T(8,128)(2,1)S(1)} %get-tuple-element.73), channel_id=1, source_target_pairs={{0,8},{4,12},{8,0},{12,4},{1,9},{5,13},{9,1},{13,5},{2,10},{6,14},... | collective-permute-start | bytes 2359304 | tf_op jit(solution)/shard_map/ppermute | solution.py:287
  154.4 1.3 copy-start.6
  155.7 22.7 %copy-start.12 = (f32[24]{0:T(128)S(1)}, f32[24]{0:T(128)}, u32[]{:S(2)}) copy-start(f32[24]{0:T(128)} %param.12) | copy-start | bytes 292
  168.9 6.3 %collective-permute-start.10 = (f32[288,128]{1,0:T(8,128)}, f32[288,128]{1,0:T(8,128)S(1)}, u32[]{:S(2)}, u32[]{:S(2)}) collective-permute-start(f32[288,128]{1,0:T(8,128)} %get-tuple-element.67), channel_id=1, source_target_pairs={{0,3},{1,2},{2,1},{3,0},{4,7},{5,6},{6,5},{7,4},{8,11},{9,10},{10,... | collective-permute-start | bytes 442376 | tf_op jit(solution)/shard_map/ppermute | solution.py:287
  168.9 9.5 %collective-permute-start.9 = (f32[288,128]{1,0:T(8,128)}, f32[288,128]{1,0:T(8,128)S(1)}, u32[]{:S(2)}, u32[]{:S(2)}) collective-permute-start(f32[288,128]{1,0:T(8,128)} %get-tuple-element.67), channel_id=1, source_target_pairs={{0,2},{1,3},{2,0},{3,1},{4,6},{5,7},{6,4},{7,5},{8,10},{9,11},{10,... | collective-permute-start | bytes 442376 | tf_op jit(solution)/shard_map/ppermute | solution.py:287
  170.4 4.8 %collective-permute-start.8 = (f32[288,128]{1,0:T(8,128)}, f32[288,128]{1,0:T(8,128)S(1)}, u32[]{:S(2)}, u32[]{:S(2)}) collective-permute-start(f32[288,128]{1,0:T(8,128)} %get-tuple-element.66.refs_0_), channel_id=1, source_target_pairs={{0,1},{1,0},{2,3},{3,2},{4,5},{5,4},{6,7},{7,6},{8,9},{9,8},{10,11... | collective-permute-start | bytes 442376 | tf_op jit(solution)/shard_map/ppermute | solution.py:287
  184.0 30.7 %collective-permute-start.19 = (bf16[48,2048]{1,0:T(8,128)(2,1)S(1)}, bf16[48,2048]{1,0:T(8,128)(2,1)S(1)}, u32[]{:S(2)}, u32[]{:S(2)}) collective-permute-start(bf16[48,2048]{1,0:T(8,128)(2,1)S(1)} %get-tuple-element.78), channel_id=1, source_target_pairs={{0,12},{4,8},{8,4},{12,0},{1,13},{5,9},{9,5},{13,1},{2,14},{6,10},... | collective-permute-start | bytes 589832 | tf_op jit(solution)/shard_map/ppermute | solution.py:287
  185.3 29.4 %collective-permute-start.20 = (bf16[48,2048]{1,0:T(8,128)(2,1)S(1)}, bf16[48,2048]{1,0:T(8,128)(2,1)S(1)}, u32[]{:S(2)}, u32[]{:S(2)}) collective-permute-start(bf16[48,2048]{1,0:T(8,128)(2,1)S(1)} %get-tuple-element.79), channel_id=1, source_target_pairs={{0,8},{4,12},{8,0},{12,4},{1,9},{5,13},{9,1},{13,5},{2,10},{6,14},... | collective-permute-start | bytes 589832 | tf_op jit(solution)/shard_map/ppermute | solution.py:287
  192.4 17.4 %copy-start.7 = (bf16[24,64,256]{2,1,0:T(8,128)(2,1)S(1)}, bf16[24,64,256]{2,1,0:T(8,128)(2,1)}, u32[]{:S(2)}) copy-start(bf16[24,64,256]{2,1,0:T(8,128)(2,1)} %param.11) | copy-start | bytes 2359300
  203.6 6.3 %collective-permute-start.15 = (f32[192,128]{1,0:T(8,128)S(1)}, f32[192,128]{1,0:T(8,128)S(1)}, u32[]{:S(2)}, u32[]{:S(2)}) collective-permute-start(f32[192,128]{1,0:T(8,128)S(1)} %get-tuple-element.75), channel_id=1, source_target_pairs={{0,2},{1,3},{2,0},{3,1},{4,6},{5,7},{6,4},{7,5},{8,10},{9,11},{10,... | collective-permute-start | bytes 294920 | tf_op jit(solution)/shard_map/ppermute | solution.py:287
  203.6 6.2 %collective-permute-start.16 = (f32[192,128]{1,0:T(8,128)S(1)}, f32[192,128]{1,0:T(8,128)S(1)}, u32[]{:S(2)}, u32[]{:S(2)}) collective-permute-start(f32[192,128]{1,0:T(8,128)S(1)} %get-tuple-element.75), channel_id=1, source_target_pairs={{0,3},{1,2},{2,1},{3,0},{4,7},{5,6},{6,5},{7,4},{8,11},{9,10},{10,... | collective-permute-start | bytes 294920 | tf_op jit(solution)/shard_map/ppermute | solution.py:287
  204.8 2.0 collective-permute-start.14
  206.7 30.5 %collective-permute-start.11 = (f32[288,256]{1,0:T(8,128)S(1)}, f32[288,256]{1,0:T(8,128)S(1)}, u32[]{:S(2)}, u32[]{:S(2)}) collective-permute-start(f32[288,256]{1,0:T(8,128)S(1)} %get-tuple-element.71), channel_id=1, source_target_pairs={{0,4},{4,0},{8,12},{12,8},{1,5},{5,1},{9,13},{13,9},{2,6},{6,2},{1... | collective-permute-start | bytes 884744 | tf_op jit(solution)/shard_map/ppermute | solution.py:287
  211.0 26.2 %collective-permute-start.17 = (f32[192,256]{1,0:T(8,128)S(1)}, f32[192,256]{1,0:T(8,128)S(1)}, u32[]{:S(2)}, u32[]{:S(2)}) collective-permute-start(f32[192,256]{1,0:T(8,128)S(1)} %get-tuple-element.76.refs_2_), channel_id=1, source_target_pairs={{0,12},{4,8},{8,4},{12,0},{1,13},{5,9},{9,5},{13,1},{2,14},{6,10},... | collective-permute-start | bytes 589832 | tf_op jit(solution)/shard_map/ppermute | solution.py:287
  212.9 24.3 %copy-start.10 = (f32[768,256]{1,0:T(8,128)S(1)}, f32[768,256]{1,0:T(8,128)}, u32[]{:S(2)}) copy-start(f32[768,256]{1,0:T(8,128)} %get-tuple-element.112.refs_2_.refs_1_) | copy-start | bytes 2359300
  212.9 24.3 %collective-permute-start.18 = (f32[192,256]{1,0:T(8,128)S(1)}, f32[192,256]{1,0:T(8,128)S(1)}, u32[]{:S(2)}, u32[]{:S(2)}) collective-permute-start(f32[192,256]{1,0:T(8,128)S(1)} %get-tuple-element.77), channel_id=1, source_target_pairs={{0,8},{4,12},{8,0},{12,4},{1,9},{5,13},{9,1},{13,5},{2,10},{6,14},... | collective-permute-start | bytes 589832 | tf_op jit(solution)/shard_map/ppermute | solution.py:287
  217.7 1.6 collective-permute-start.21
  218.1 3.8 %collective-permute-start.22 = (f32[48,128]{1,0:T(8,128)S(1)}, f32[48,128]{1,0:T(8,128)S(1)}, u32[]{:S(2)}, u32[]{:S(2)}) collective-permute-start(f32[48,128]{1,0:T(8,128)S(1)} %get-tuple-element.81), channel_id=1, source_target_pairs={{0,2},{1,3},{2,0},{3,1},{4,6},{5,7},{6,4},{7,5},{8,10},{9,11},{10,... | collective-permute-start | bytes 73736 | tf_op jit(solution)/shard_map/ppermute | solution.py:287
  219.3 3.3 %collective-permute-start.23 = (f32[48,128]{1,0:T(8,128)S(1)}, f32[48,128]{1,0:T(8,128)S(1)}, u32[]{:S(2)}, u32[]{:S(2)}) collective-permute-start(f32[48,128]{1,0:T(8,128)S(1)} %get-tuple-element.81), channel_id=1, source_target_pairs={{0,3},{1,2},{2,1},{3,0},{4,7},{5,6},{6,5},{7,4},{8,11},{9,10},{10,... | collective-permute-start | bytes 73736 | tf_op jit(solution)/shard_map/ppermute | solution.py:287
  223.1 6.5 %collective-permute-start.24 = (f32[48,256]{1,0:T(8,128)S(1)}, f32[48,256]{1,0:T(8,128)S(1)}, u32[]{:S(2)}, u32[]{:S(2)}) collective-permute-start(f32[48,256]{1,0:T(8,128)S(1)} %get-tuple-element.82), channel_id=1, source_target_pairs={{0,12},{4,8},{8,4},{12,0},{1,13},{5,9},{9,5},{13,1},{2,14},{6,10},... | collective-permute-start | bytes 147464 | tf_op jit(solution)/shard_map/ppermute | solution.py:287
  224.5 12.7 %collective-permute-start.25 = (f32[48,256]{1,0:T(8,128)S(1)}, f32[48,256]{1,0:T(8,128)S(1)}, u32[]{:S(2)}, u32[]{:S(2)}) collective-permute-start(f32[48,256]{1,0:T(8,128)S(1)} %get-tuple-element.83), channel_id=1, source_target_pairs={{0,8},{4,12},{8,0},{12,4},{1,9},{5,13},{9,1},{13,5},{2,10},{6,14},... | collective-permute-start | bytes 147464 | tf_op jit(solution)/shard_map/ppermute | solution.py:287
  237.2 1.1 copy-start.4
Sparse Core Ops, SparseCore 0:
  56.2 39.3 reduce-scatter.1

commit v3 on v2

--- a/solution.py
+++ b/solution.py
@@ -32,83 +32,116 @@
     return total
 
 
-def move_rows(pieces, cap, slot, tok_ref, outs):
-    for (block, first, count), out in zip(pieces, outs):
-        at = block * cap + first + lax.broadcasted_iota(I32, (count, slot.shape[1]), 0)
-        place = jnp.where(at == slot, 1.0, 0.0).astype(BF16)
+def as_column(line):
+    size = line.shape[1]
+    here = lax.broadcasted_iota(I32, (size, size), 0) == lax.broadcasted_iota(I32, (size, size), 1)
+    return jnp.sum(jnp.where(here, line, 0), axis=1, keepdims=True)
+
+
+def route_kernel(owners, owned, cap, me_ref, row_ref, slot_ref, target_ref):
+    rows = row_ref.shape[1]
+    id_row = row_ref[...]
+    key_row = id_row * rows + lax.broadcasted_iota(I32, (1, rows), 1)
+    key_col = as_column(key_row)
+    own_row = owner_of(id_row, owners, owned)
+    before = (key_col < key_row) & (key_col >= own_row * (owned * rows))
+    rank = jnp.sum(jnp.where(before, 1, 0), axis=0, keepdims=True)
+    found = (own_row ^ me_ref[0]) * cap + rank
+    slot_ref[...] = found
+    target_ref[...] = as_column(found)
+
+
+def route(ids_row, me, owners, owned, cap):
+    rows = ids_row.shape[1]
+    return pl.pallas_call(
+        functools.partial(route_kernel, owners, owned, cap),
+        in_specs=[
+            pl.BlockSpec(memory_space=pltpu.SMEM),
+            pl.BlockSpec(memory_space=pltpu.VMEM),
+        ],
+        out_shape=[jax.ShapeDtypeStruct((1, rows), I32), jax.ShapeDtypeStruct((rows, 1), I32)],
+        compiler_params=PARAMS,
+        cost_estimate=cost(rows, rows, 8),
+        name="route",
+    )(me, ids_row)
+
+
+def sort_kernel(cap, pieces, waits, slot_ref, tok_ref, *refs):
+    for (block, first, count), out in zip(pieces, refs[waits:]):
+        at = block * cap + first + lax.broadcasted_iota(I32, (count, slot_ref.shape[1]), 0)
+        place = jnp.where(at == slot_ref[...], 1.0, 0.0).astype(BF16)
         out[...] = jnp.dot(place, tok_ref[...], preferred_element_type=F32).astype(BF16)
 
 
-def head_kernel(owners, owned, cap, pieces, me_ref, row_ref, tok_ref, *refs):
-    outs, slot_ref, slot = refs[: len(pieces)], refs[-2], refs[-1]
-    rows = row_ref.shape[1]
-
-    @pl.when(pl.program_id(0) == 0)
-    def _():
-        id_row = row_ref[...]
-        key_row = id_row * rows + lax.broadcasted_iota(I32, (1, rows), 1)
-        down = lax.broadcasted_iota(I32, (rows, rows), 0)
-        across = lax.broadcasted_iota(I32, (rows, rows), 1)
-        key_col = jnp.sum(jnp.where(down == across, key_row, 0), axis=1, keepdims=True)
-        own_row = owner_of(id_row, owners, owned)
-        before = (key_col < key_row) & (key_col >= own_row * (owned * rows))
-        rank = jnp.sum(jnp.where(before, 1, 0), axis=0, keepdims=True)
-        found = (own_row ^ me_ref[0]) * cap + rank
-        slot[...] = found
-        slot_ref[...] = found
-
-    move_rows(pieces, cap, slot[...], tok_ref, outs)
-
-
-def rest_kernel(cap, pieces, slot_ref, tok_ref, *refs):
-    outs, target_ref = refs[: len(pieces)], refs[-1]
-    rows = slot_ref.shape[1]
-
-    @pl.when(pl.program_id(0) == 0)
-    def _():
-        down = lax.broadcasted_iota(I32, (rows, rows), 0)
-        across = lax.broadcasted_iota(I32, (rows, rows), 1)
-        target_ref[...] = jnp.sum(
-            jnp.where(down == across, slot_ref[...], 0), axis=1, keepdims=True
-        )
-
-    move_rows(pieces, cap, slot_ref[...], tok_ref, outs)
-
-
-def sort_rows(tokens, ids_row, me, owners, owned, cap, first, rest):
+def sort_rows(tokens, slot, cap, pieces, later_than=()):
     rows, width = tokens.shape
     step = min(512, width)
-    line = pl.BlockSpec((1, rows), lambda i: (0, 0))
-    strip = pl.BlockSpec((rows, step), lambda i: (0, i))
-
-    def outs(pieces):
-        specs = [pl.BlockSpec((count, step), lambda i: (0, i)) for _, _, count in pieces]
-        return specs, [jax.ShapeDtypeStruct((count, width), BF16) for _, _, count in pieces]
-
-    specs, shapes = outs(first)
-    *sent, slot = pl.pallas_call(
-        functools.partial(head_kernel, owners, owned, cap, first),
+    return pl.pallas_call(
+        functools.partial(sort_kernel, cap, pieces, len(later_than)),
         grid=(width // step,),
-        in_specs=[pl.BlockSpec(memory_space=pltpu.SMEM), line, strip],
-        out_specs=specs + [line],
-        out_shape=shapes + [jax.ShapeDtypeStruct((1, rows), I32)],
-        scratch_shapes=[pltpu.VMEM((1, rows), I32)],
-        compiler_params=PARAMS,
-        cost_estimate=cost(sum(c for _, _, c in first), rows, width),
-        name="sort_first",
-    )(me, ids_row, tokens)
-    specs, shapes = outs(rest)
-    *others, target = pl.pallas_call(
-        functools.partial(rest_kernel, cap, rest),
-        grid=(width // step,),
-        in_specs=[line, strip],
-        out_specs=specs + [pl.BlockSpec((rows, 1), lambda i: (0, 0))],
-        out_shape=shapes + [jax.ShapeDtypeStruct((rows, 1), I32)],
-        compiler_params=PARAMS,
-        cost_estimate=cost(sum(c for _, _, c in rest), rows, width),
-        name="sort_rest",
-    )(slot, tokens)
-    return sent, others, target
+        in_specs=[
+            pl.BlockSpec((1, rows), lambda i: (0, 0)),
+            pl.BlockSpec((rows, step), lambda i: (0, i)),
+        ]
+        + [ANYWHERE] * len(later_than),
+        out_specs=[pl.BlockSpec((count, step), lambda i: (0, i)) for _, _, count in pieces],
+        out_shape=[jax.ShapeDtypeStruct((count, width), BF16) for _, _, count in pieces],
+        compiler_params=PARAMS,
+        cost_estimate=cost(sum(c for _, _, c in pieces), rows, width),
+        name="sort",
+    )(slot, tokens, *later_than)
+
+
+def name_kernel(owners, owned, sets, here_ref, *refs):
+    lines, outs, plan_ref, most_ref = refs[:owners], refs[owners:-2], refs[-2], refs[-1]
+    me, half = here_ref[0], here_ref[1]
+    held = -(-owned // 8) * 8
+    owner = lax.broadcasted_iota(I32, (-(-owners // 8) * 8, 1), 0)
+    adapter = lax.broadcasted_iota(I32, (held, 1), 0)
+    diagonal = adapter == lax.broadcasted_iota(I32, (held, 128), 1)
+    used = lax.broadcasted_iota(I32, (1, 128), 1) < owned
+    most = jnp.zeros(owner.shape, I32)
+    ends = []
+    for j, line in enumerate(lines):
+        ids = line[...]
+        chosen = jnp.where(owner_of(ids, owners, owned) == owner, 1, 0)
+        count = jnp.sum(chosen, axis=1, keepdims=True)
+        far = (me ^ j ^ owner >= 2) & (owner < owners)
+        most = jnp.maximum(most, jnp.where(far, count, 0))
+        mine = ids - me * owned
+        upto = jnp.sum(jnp.where((mine >= 0) & (mine <= adapter), 1, 0), axis=1, keepdims=True)
+        across = jnp.sum(jnp.where(diagonal, upto, 0), axis=0, keepdims=True)
+        ends.append(jnp.where(used, across, 1 << 20))
+    most_ref[...] = jnp.broadcast_to(jnp.max(most, axis=0, keepdims=True), most_ref.shape)
+    for k, (pieces, out) in enumerate(zip(sets, outs)):
+        begin, low, high = 0, owned - 1, 0
+        for block, first, count in pieces:
+            at = first + lax.broadcasted_iota(I32, (count, 1), 0)
+            names = jnp.sum(jnp.where(ends[block] <= at, 1, 0), axis=1, keepdims=True)
+            out[begin : begin + count, :] = names
+            low = jnp.minimum(low, jnp.min(names))
+            high = jnp.maximum(high, jnp.max(jnp.where(names < owned, names, 0)))
+            begin += count
+        plan_ref[3 * k] = low
+        plan_ref[3 * k + 1] = jnp.maximum(low, high)
+        plan_ref[3 * k + 2] = half
+
+
+def name_rows(lines, here, owned, sets):
+    totals = [sum(c for _, _, c in pieces) for pieces in sets]
+    on_chip, scalars = (pl.BlockSpec(memory_space=m) for m in (pltpu.VMEM, pltpu.SMEM))
+    *names, plan, most = pl.pallas_call(
+        functools.partial(name_kernel, len(lines), owned, sets),
+        in_specs=[scalars] + [on_chip] * len(lines),
+        out_specs=[on_chip] * len(sets) + [scalars, on_chip],
+        out_shape=[jax.ShapeDtypeStruct((t, 1), I32) for t in totals]
+        + [jax.ShapeDtypeStruct((3 * len(sets),), I32), jax.ShapeDtypeStruct((1, 128), I32)],
+        compiler_params=PARAMS,
+        cost_estimate=cost(sum(totals), owned, 8),
+        name="name_rows",
+    )(here, *lines)
+    plans = [plan[3 * k : 3 * k + 3] for k in range(len(sets))]
+    return names, plans, most
 
 
 def base_kernel(tok_ref, weight_ref, _, out_ref):
@@ -173,14 +206,12 @@
         other_ref[...] = jnp.where(second, keys, values)
 
 
-def shrink(blocks, names, down, half, later_than=()):
+def shrink(blocks, names, plan, down, later_than=()):
     sizes = tuple(b.shape[0] for b in blocks)
     total = sum(sizes)
     owned, rank2, width = down.shape
     group = next(g for g in (4, 3, 2, 1) if owned % g == 0)
     fine = next(g for g in (2, 3, 1) if group % g == 0)
-    low = jnp.minimum(jnp.min(names), owned - 1)
-    high = jnp.maximum(jnp.max(jnp.where(names < owned, names, 0)), low)
     line = jax.ShapeDtypeStruct((total // 2, 2 * ADAPTER_RANK), F32)
     return pl.pallas_call(
         functools.partial(shrink_kernel, sizes, group, fine, len(later_than)),
@@ -203,7 +234,7 @@
         compiler_params=PARAMS,
         cost_estimate=cost(total, width, owned * rank2),
         name="shrink",
-    )(jnp.stack([low, high, half]).astype(I32), names.reshape(-1, 1), down, *blocks, *later_than)
+    )(plan, names, down, *blocks, *later_than)
 
 
 def split(x, terms):
@@ -249,7 +280,7 @@
         compiler_params=PARAMS,
         cost_estimate=cost(sum(sizes), up.shape[0], columns, 3),
         name="expand",
-    )(names.reshape(-1, 1), scale, up, *lines)
+    )(names, scale, up, *lines)
 
 
 def merge_kernel(begins, parts, target_ref, *refs):
@@ -308,90 +339,85 @@
     half = (lax.axis_index(feature_axes) >= sharers // 2).astype(I32)
     cap = up_to_16(owned * TOKEN_LIMIT)
 
+    own, near = (0, 0, cap), (1, 0, cap)
     if owners == 4:
         usual = up_to_16(cap * 5 // 6)
         most = up_to_16(usual * 4 // 5)
-        near = [(1, 0, cap)]
         far = [[(3, 0, most), (2, 0, most)], [(3, most, usual - most), (2, most, usual - most)]]
         extra = [(3, usual, cap - usual), (2, usual, cap - usual)]
     else:
-        usual, near, extra = cap, [(1, 0, cap)], []
-        far = [[(j, 0, cap) for j in range(2, owners)]]
-    head = far[0]
-    own = (0, 0, cap)
+        usual, far, extra = cap, [[(j, 0, cap) for j in range(2, owners)]], []
 
     ids_row = token_adapter_index.reshape(1, rows)
-    ids_all = lax.all_gather(ids_row, ("parts", "dp"), axis=0, tiled=True)
-    rest = near + [p for s in far[1:] for p in s] + extra + [own]
-    sent_first, sent_rest, target = sort_rows(
-        tokens, ids_row, me.reshape(1), owners, owned, cap, head, rest
-    )
-    packed = dict(zip(head + rest, sent_first + sent_rest))
-    received = {p: swap(packed[p], "dp", owners, p[0]) for s in [near, *far] for p in s}
-
-    group_of = lax.axis_index("parts") * owners
-    sources = group_of + (me ^ jnp.arange(owners, dtype=I32))
-    everyone = jnp.arange(ids_all.shape[0], dtype=I32)
-    chosen = sources[:, None, None] == everyone[None, :, None]
-    heard = jnp.sum(jnp.where(chosen, ids_all[None], 0), axis=1, dtype=I32) - me * owned
-    adapters = jnp.arange(owned, dtype=I32)
-    upto = jnp.sum(
-        (heard[:, None, :] >= 0) & (heard[:, None, :] <= adapters[None, :, None]), axis=2, dtype=I32
-    )
-    at = jnp.arange(cap, dtype=I32)
-    which = jnp.sum(upto[:, None, :] <= at[None, :, None], axis=2, dtype=I32)
+    ids_heard = [ids_row] + [swap(ids_row, "dp", owners, j) for j in range(1, owners)]
+    slot, target = route(ids_row, me.reshape(1), owners, owned, cap)
+    early = sort_rows(tokens, slot, cap, far[0], tuple(ids_heard[1:]))
+    later = [near] + [p for s in far[1:] for p in s] + [own] + extra
+    packed = dict(zip(far[0] + later, early + sort_rows(tokens, slot, cap, later, early[:1])))
+    sent = [p for s in far for p in s] + [near]
+    received = {p: swap(packed[p], "dp", owners, p[0]) for p in sent}
+
+    sets = [[own, near]] + far + ([extra] if extra else [])
+    here = jnp.stack([me.astype(I32), half])
+    names, plans, largest = name_rows(ids_heard, here, owned, sets)
 
     if owned % 2:
         adapter_up_weight = jnp.pad(adapter_up_weight, ((0, 1), (0, 0), (0, 0)))
     up = adapter_up_weight.reshape(-1, adapter_up_weight.shape[2])
     scale = adapter_scale.reshape(1, owned)
 
-    def shares(pieces, blocks, later_than):
-        names = jnp.concatenate([which[b, f : f + c] for b, f, c in pieces])
-        mine, other = shrink(blocks, names, adapter_down_weight, half, later_than)
+    def deltas_of(blocks, names, plan, down, up, scale, later_than):
+        mine, other = shrink(blocks, names, plan, down, later_than)
         lines = [mine] + [
             swap(mine if d < sharers // 2 else other, feature_axes, sharers, d)
             for d in range(1, sharers)
         ]
-        return expand(lines, names, scale, up, tuple(c for _, _, c in pieces))
+        return expand(lines, names, scale, up, tuple(b.shape[0] for b in blocks))
+
+    def send_back(pieces, deltas):
+        return [swap(d, "dp", owners, p[0]) for p, d in zip(pieces, deltas)]
 
     def begins(pieces):
         return [b * cap + f for b, f, _ in pieces]
 
-    arrived = received[near[0]]
-    base_part = base_product(tokens, key_value_weight, arrived)
+    weights = (adapter_down_weight, up, scale)
+    base_part = base_product(tokens, key_value_weight, packed[own])
     base = lax.psum_scatter(base_part, feature_axes, scatter_dimension=1, tiled=True)
-    at_hand = [own] + near
-    deltas = shares(at_hand, [packed[own]] + [received[p] for p in near], (base_part,))
-    total = jnp.zeros((rows, up.shape[1]), F32)
-    total = merge([total], target, begins([own]), deltas[:1], F32)
-
-    if extra:
-        counts = jnp.sum(
-            (ids_all[:, None, :] >= owned * jnp.arange(owners, dtype=I32)[None, :, None])
-            & (ids_all[:, None, :] < owned * (1 + jnp.arange(owners, dtype=I32))[None, :, None]),
-            axis=2,
-            dtype=I32,
-        )
-        away = (everyone[:, None] % owners) ^ jnp.arange(owners, dtype=I32)[None, :]
-        more = jnp.max(jnp.where(away >= 2, counts, 0)) > usual
-
-        def with_extra(so_far):
-            blocks = [swap(packed[p], "dp", owners, p[0]) for p in extra]
-            found = shares(extra, blocks, ())
-            back = [swap(d, "dp", owners, p[0]) for p, d in zip(extra, found)]
-            return merge([so_far], target, begins(extra), back, F32)
-
-        total = lax.cond(more, with_extra, lambda so_far: so_far, total)
-
-    last = total
-    returned = [swap(d, "dp", owners, p[0]) for p, d in zip(near, deltas[1:])]
-    for pieces in far:
-        deltas = shares(pieces, [received[p] for p in pieces], (last,))
-        returned += [swap(d, "dp", owners, p[0]) for p, d in zip(pieces, deltas)]
-        last = deltas[0]
-    pieces = near + [p for s in far for p in s]
-    return merge([base, total], target, begins(pieces), returned, BF16)
+    blocks = [packed[own], received[near]]
+    deltas = deltas_of(blocks, names[0], plans[0], *weights, (base_part,))
+    returned = [deltas[0]] + send_back([near], deltas[1:])
+    done = [own, near]
+    for k, pieces in enumerate(far):
+        blocks = [received[p] for p in pieces]
+        deltas = deltas_of(blocks, names[1 + k], plans[1 + k], *weights, (deltas[0],))
+        returned += send_back(pieces, deltas)
+        done += pieces
+
+    def finish(base, target, returned, *_):
+        return merge([base], target, begins(done), returned, BF16)
+
+    if not extra:
+        return finish(base, target, returned)
+
+    def finish_with_extra(base, target, returned, blocks, names, plan, weights):
+        blocks = send_back(extra, blocks)
+        deltas = send_back(extra, deltas_of(blocks, names, plan, *weights, ()))
+        return merge([base], target, begins(done + extra), returned + deltas, BF16)
+
+    for d in range(1, lax.axis_size("parts")):
+        largest = jnp.maximum(largest, swap(largest, "parts", lax.axis_size("parts"), d))
+    return lax.cond(
+        largest[0, 0] > usual,
+        finish_with_extra,
+        finish,
+        base,
+        target,
+        returned,
+        [packed[p] for p in extra],
+        names[-1],
+        plans[-1],
+        weights,
+    )
 
 
 def solution(mesh):

time: 249 us -> 168 us (0.67)
  blocking collectives: 89.2 us -> 0 us
  waiting for transfers between devices: 47.8 us -> 63 us
  starting transfers between devices: 23.4 us -> 31.4 us
  other arithmetic: 6.57 us -> 0.08 us
  between operations: 19.9 us -> 13.7 us
    all_gather x1 -> x0, blocking collectives: 89.2 us -> none  [local(): ids_all = lax.all_gather(ids_row, ('parts', 'dp'), axis=0, tiled=True)]
    ppermute x19 -> x23, waiting for transfers between devices: 47.8 us -> 63 us  [swap(): return lax.ppermute(x, axes, [(i, i ^ distance) for i in range(size)])]
    ppermute x19 -> x23, starting transfers between devices: 23.4 us -> 31.4 us  [swap(): return lax.ppermute(x, axes, [(i, i ^ distance) for i in range(size)])]
    pallas_call x2 -> x4, Pallas kernels: 9.15 us -> 12.4 us  [the longest x2 9.07 us: sort_rows(): pl.pallas_call(functools.partial(sort_kernel, cap, pieces, len(later_than...]
    reduce_max x4 -> x0, other arithmetic: 2.8 us -> none  [the longest x3 2.16 us: shrink(): high = jnp.maximum(jnp.max(jnp.where(names < owned, names, 0)), low)]
    pallas_call x2 -> x1, Pallas kernels: 5.71 us -> 3.18 us  [merge(): pl.pallas_call(functools.partial(merge_kernel, tuple(begins), len(parts))...]
    unnamed x20 -> x32, local copies, waits for them, and re-layouts: 6.02 us -> 5.66 us
  transfers between devices with their start and end apart: 20 -> 24, of which waited for: 8 -> 10; matrix products, arithmetic and copies ran while one was open for 3% -> 0% of each run, Pallas kernels for 14% -> 20%
where the time goes in v3:
time: 168 us; the launch traced here: 167 us
  waiting for transfers between devices  63 us (38%)
  Pallas kernels  52.9 us (31%)
  starting transfers between devices  31.4 us (19%)
  between operations  13.7 us (8%)
  local copies, waits for them, and re-layouts  5.74 us (3%)
    ppermute x23, waiting for transfers between devices, swap(): return lax.ppermute(x, axes, [(i, i ^ distance) for i in range(size)])  63 us
    ppermute x23, starting transfers between devices, swap(): return lax.ppermute(x, axes, [(i, i ^ distance) for i in range(size)])  31.4 us
    pallas_call x3, Pallas kernels, shrink(): pl.pallas_call(functools.partial(shrink_kernel, sizes, group, fine, len(l...  26.2 us
    pallas_call x2, Pallas kernels, sort_rows(): pl.pallas_call(functools.partial(sort_kernel, cap, pieces, len(later_than...  9.07 us
    pallas_call x1, Pallas kernels, base_product(): pl.pallas_call(base_kernel, grid=(columns // step,), in_specs=[pl.BlockSp...  7.75 us
    unnamed x32, local copies, waits for them, and re-layouts  5.66 us
    pallas_call x3, Pallas kernels, expand(): pl.pallas_call(functools.partial(expand_kernel, sizes, len(lines)), out_s...  3.41 us
  transfers between devices with their start and end apart: 24, of which 10 were waited for; matrix products, arithmetic and copies ran while one was open for 0% of the time, Pallas kernels for 20%

profile of v3, /device:TPU:0, one launch (start us, length us, event | category | flops | bytes accessed | tf_op | source)
XLA Modules:
  0.0 167.1 jit_solution(8499136155389972226)
XLA Ops:
  6.5 5.0 %collective-permute-start.9 = (s32[1,768]{1,0:T(1,128)}, s32[1,768]{1,0:T(1,128)S(1)}, u32[]{:S(2)}, u32[]{:S(2)}) collective-permute-start(s32[1,768]{1,0:T(1,128)} %bitcast.7), channel_id=1, source_target_pairs={{0,12},{4,8},{8,4},{12,0},{1,13},{5,9},{9,5},{13,1},{2,14},{6,10},... | collective-permute-start | bytes 9224 | tf_op jit(solution)/shard_map/ppermute | solution.py:318
  11.6 0.6 collective-permute-start.7
  12.2 0.7 copy-done
  12.9 1.6 route.1
  14.5 0.0 collective-permute-done.9.refs_3_.refs_2_
  14.5 1.8 %collective-permute-done.8.refs_2_.refs_1_ = s32[1,768]{1,0:T(1,128)S(1)} collective-permute-done((s32[1,768]{1,0:T(1,128)}, s32[1,768]{1,0:T(1,128)S(1)}, u32[]{:S(2)}, u32[]{:S(2)}) %collective-permute-start.8) | collective-permute-done | bytes 3104 | tf_op jit(solution)/shard_map/ppermute | solution.py:318
  16.3 0.0 collective-permute-done.7.refs_1_.refs_0_
  16.3 1.9 %copy-done.2 = bf16[768,2048]{1,0:T(8,128)(2,1)S(1)} copy-done((bf16[768,2048]{1,0:T(8,128)(2,1)S(1)}, bf16[768,2048]{1,0:T(8,128)(2,1)}, u32[]{:S(2)}) %copy-start.2) | copy-done | bytes 3145752
  18.2 2.3 %sort.2 = (bf16[192,2048]{1,0:T(8,128)(2,1)S(1)}, bf16[192,2048]{1,0:T(8,128)(2,1)S(1)}) custom-call(s32[1,768]{1,0:T(1,128)S(1)} %get-tuple-element.112.slot_ref, bf16[768,2048]{1,0:T(8,128)(2,1)S(1)} %copy-done.2, s32[1,768]{1,0:T(1,128)S(1)} %collective-permute-done.7.refs_1_.refs_0_, s32[1,768]{1,0:T(1,128)S(1)} %collective-permute-done.8.refs_2_.refs_1_, ...), custom_call_target="tpu_custom_call" | custom-call | flops 1207959552 | bytes 6881280 | tf_op jit(solution)/shard_map/sort/pallas_call | solution.py:79
  20.5 6.8 %sort.3 = (bf16[288,2048]{1,0:T(8,128)(2,1)S(1)}, bf16[48,2048]{1,0:T(8,128)(2,1)S(1)}, bf16[48,2048]{1,0:T(8,128)(2,1)S(1)}, bf16[288,2048]{1,0:T(8,128)(2,1)S(...) custom-call(s32[1,768]{1,0:T(1,128)S(1)} %get-tuple-element.112.slot_ref, bf16[768,2048]{1,0:T(8,128)(2,1)} %tok_ref.5, ...), custom_call_target="tpu_custom_call" | custom-call | flops 2415919104 | bytes 10616832 | tf_op jit(solution)/shard_map/sort/pallas_call | solution.py:79
  27.3 7.7 %base.1.refs_2_ = f32[768,1024]{1,0:T(8,128)} custom-call(bf16[768,2048]{1,0:T(8,128)(2,1)} %tok_ref.5, bf16[2048,1024]{1,0:T(8,128)(2,1)} %weight_ref.1, bf16[288,2048]{1,0:T(8,128)(2,1)S(1)} %get-tuple-element.114._.refs_0_), custom_call_target="tpu_custom_call" | custom-call | flops 3221225472 | bytes 10485760 | tf_op jit(solution)/shard_map/base/pallas_call | solution.py:154
  35.0 1.0 copy-done.4
  36.0 0.0 reduce-scatter.2.cloned.1.call-update
  36.1 0.1 collective-permute-start.11
  36.1 0.1 pad_add_fusion.here_ref
  36.2 3.5 %collective-permute-start.16 = (bf16[192,2048]{1,0:T(8,128)(2,1)S(1)}, bf16[192,2048]{1,0:T(8,128)(2,1)S(1)}, u32[]{:S(2)}, u32[]{:S(2)}) collective-permute-start(bf16[192,2048]{1,0:T(8,128)(2,1)S(1)} %get-tuple-element.113.refs_0_), channel_id=1, source_target_pairs={{0,12},{4,8},{8,4},{12,0},{1,13},{5,9},{9,5},{13,1},{2,14},{6,10},... | collective-permute-start | bytes 2359304 | tf_op jit(solution)/shard_map/ppermute | solution.py:318
  39.7 0.0 collective-permute-start.17
  39.7 1.7 %name_rows.1 = (s32[576,1]{1,0:T(8,128)S(1)}, s32[384,1]{1,0:T(8,128)S(1)}, s32[96,1]{1,0:T(8,128)S(1)}, s32[96,1]{1,0:T(8,128)}, s32[12]{0:T(128)S(1)}, /*index=5*/s32[1,128]{1,0:T(1,128)S(1)}) custom-call(s32[2]{0:T(128)S(1)} %pad_add_fusion.here_ref, s32[1,768]{1,0:T(1,128)S(1)} %bitcast.11, s32[1,768]{1,0:T(1,128)S(1)} %collective-permute-done.7.refs_1_.refs_0_, ...), custom_call_target="tpu_custom_call" | custom-call | flops 442368 | bytes 92544 | tf_op jit(solution)/shard_map/name_rows/pallas_call | solution.py:133
  41.4 0.1 fusion
  41.5 46.2 %collective-permute-done.11.refs_1_ = bf16[288,2048]{1,0:T(8,128)(2,1)S(1)} collective-permute-done((bf16[288,2048]{1,0:T(8,128)(2,1)S(1)}, bf16[288,2048]{1,0:T(8,128)(2,1)S(1)}, u32[]{:S(2)}, u32[]{:S(2)}) %collective-permute-start.11) | collective-permute-done | bytes 1179680 | tf_op jit(solution)/shard_map/ppermute | solution.py:318
  87.7 1.3 copy-done.5
  88.9 12.5 %shrink.5 = (f32[288,128]{1,0:T(8,128)S(1)}, f32[288,128]{1,0:T(8,128)S(1)}) custom-call(s32[3]{0:T(128)S(1)} %get-tuple-element.141.plan_ref, s32[576,1]{1,0:T(8,128)S(1)} %get-tuple-element.115.which_ref, bf16[24,128,2048]{2,1,0:T(8,128)(2,1)} %down_ref.5, bf16[288,2048]{1,0:T(8,128)(2,1)S(1)} %copy-done.5, ...), custom_call_target="tpu_custom_call" | custom-call | flops 7247757312 | bytes 22020096 | tf_op jit(solution)/shard_map/shrink/pallas_call | solution.py:216
  101.4 0.1 collective-permute-start.12
  101.5 1.6 collective-permute-start.14
  103.1 0.5 collective-permute-start.13
  103.7 1.2 collective-permute-start.23
  104.8 2.5 %collective-permute-done.14.refs_3_ = f32[288,128]{1,0:T(8,128)S(1)} collective-permute-done((f32[288,128]{1,0:T(8,128)S(1)}, f32[288,128]{1,0:T(8,128)S(1)}, u32[]{:S(2)}, u32[]{:S(2)}) %collective-permute-start.14) | collective-permute-done | bytes 147488 | tf_op jit(solution)/shard_map/ppermute | solution.py:318
  107.3 3.6 %collective-permute-done.13.refs_2_ = f32[288,128]{1,0:T(8,128)S(1)} collective-permute-done((f32[288,128]{1,0:T(8,128)S(1)}, f32[288,128]{1,0:T(8,128)S(1)}, u32[]{:S(2)}, u32[]{:S(2)}) %collective-permute-start.13) | collective-permute-done | bytes 147488 | tf_op jit(solution)/shard_map/ppermute | solution.py:318
  110.9 1.6 expand.5
  112.6 0.0 collective-permute-done.17.refs_1_
  112.6 10.7 %shrink.6 = (f32[192,128]{1,0:T(8,128)S(1)}, f32[192,128]{1,0:T(8,128)S(1)}) custom-call(s32[3]{0:T(128)S(1)} %get-tuple-element.140.plan_ref, s32[384,1]{1,0:T(8,128)S(1)} %get-tuple-element.122.which_ref, bf16[24,128,2048]{2,1,0:T(8,128)(2,1)} %down_ref.5, bf16[192,2048]{1,0:T(8,128)(2,1)S(1)} %collective-permute-done.16.refs_0_, ...), custom_call_target="tpu_custom_call" | custom-call | flops 4831838208 | bytes 18874368 | tf_op jit(solution)/shard_map/shrink/pallas_call | solution.py:216
  123.3 0.1 collective-permute-start.18
  123.4 1.6 collective-permute-start.20
  125.0 0.5 collective-permute-start.19
  125.5 3.8 %collective-permute-start.15 = (f32[288,256]{1,0:T(8,128)S(1)}, f32[288,256]{1,0:T(8,128)S(1)}, u32[]{:S(2)}, u32[]{:S(2)}) collective-permute-start(f32[288,256]{1,0:T(8,128)S(1)} %get-tuple-element.121), channel_id=1, source_target_pairs={{0,4},{4,0},{8,12},{12,8},{1,5},{5,1},{9,13},{13,9},{2,6},{6,2},{1... | collective-permute-start | bytes 884744 | tf_op jit(solution)/shard_map/ppermute | solution.py:318
  129.3 0.0 collective-permute-done.20.refs_3_
  129.3 1.4 collective-permute-done.19.refs_2_
  130.6 1.2 expand.6
  131.8 2.0 %collective-permute-start.22 = (f32[192,256]{1,0:T(8,128)S(1)}, f32[192,256]{1,0:T(8,128)S(1)}, u32[]{:S(2)}, u32[]{:S(2)}) collective-permute-start(f32[192,256]{1,0:T(8,128)S(1)} %get-tuple-element.127), channel_id=1, source_target_pairs={{0,8},{4,12},{8,0},{12,4},{1,9},{5,13},{9,1},{13,5},{2,10},{6,14},... | collective-permute-start | bytes 589832 | tf_op jit(solution)/shard_map/ppermute | solution.py:318
  133.8 4.6 %collective-permute-start.21 = (f32[192,256]{1,0:T(8,128)S(1)}, f32[192,256]{1,0:T(8,128)S(1)}, u32[]{:S(2)}, u32[]{:S(2)}) collective-permute-start(f32[192,256]{1,0:T(8,128)S(1)} %get-tuple-element.126.refs_2_), channel_id=1, source_target_pairs={{0,12},{4,8},{8,4},{12,0},{1,13},{5,9},{9,5},{13,1},{2,14},{6,10},... | collective-permute-start | bytes 589832 | tf_op jit(solution)/shard_map/ppermute | solution.py:318
  138.5 0.0 collective-permute-done.23.refs_0_
  138.5 0.0 collective-permute-done.24.refs_1_
  138.5 0.0 copy-start.16
  138.5 3.0 %shrink.7 = (f32[48,128]{1,0:T(8,128)S(1)}, f32[48,128]{1,0:T(8,128)S(1)}) custom-call(s32[3]{0:T(128)S(1)} %get-tuple-element.139.plan_ref, s32[96,1]{1,0:T(8,128)S(1)} %get-tuple-element.128.which_ref, bf16[24,128,2048]{2,1,0:T(8,128)(2,1)} %down_ref.5, bf16[48,2048]{1,0:T(8,128)(2,1)S(1)} %collective-permute-done.23.refs_0_, ...), custom_call_target="tpu_custom_call" | custom-call | flops 1207959552 | bytes 14155776 | tf_op jit(solution)/shard_map/shrink/pallas_call | solution.py:216
  141.5 0.1 collective-permute-start.25
  141.6 1.6 collective-permute-start.27
  143.2 0.0 collective-permute-done.25.refs_1_
  143.2 1.1 collective-permute-start.26
  144.3 0.6 collective-permute-done.27.refs_3_
  144.9 1.5 collective-permute-start.10
  146.5 0.6 collective-permute-done.26.refs_2_
  147.0 0.6 expand.7
  147.6 0.1 collective-permute-start.28
  147.7 0.8 collective-permute-done.10
  148.5 1.9 %collective-permute-start.29 = (f32[48,256]{1,0:T(8,128)S(1)}, f32[48,256]{1,0:T(8,128)S(1)}, u32[]{:S(2)}, u32[]{:S(2)}) collective-permute-start(f32[48,256]{1,0:T(8,128)S(1)} %get-tuple-element.134), channel_id=1, source_target_pairs={{0,8},{4,12},{8,0},{12,4},{1,9},{5,13},{9,1},{13,5},{2,10},{6,14},... | collective-permute-start | bytes 147464 | tf_op jit(solution)/shard_map/ppermute | solution.py:318
  150.5 3.5 %collective-permute-done.28 = f32[48,256]{1,0:T(8,128)S(1)} collective-permute-done((f32[48,256]{1,0:T(8,128)S(1)}, f32[48,256]{1,0:T(8,128)S(1)}, u32[]{:S(2)}, u32[]{:S(2)}) %collective-permute-start.28) | collective-permute-done | bytes 49184 | tf_op jit(solution)/shard_map/ppermute | solution.py:318
  154.0 2.1 %collective-permute-done.29 = f32[48,256]{1,0:T(8,128)S(1)} collective-permute-done((f32[48,256]{1,0:T(8,128)S(1)}, f32[48,256]{1,0:T(8,128)S(1)}, u32[]{:S(2)}, u32[]{:S(2)}) %collective-permute-start.29) | collective-permute-done | bytes 49184 | tf_op jit(solution)/shard_map/ppermute | solution.py:318
  156.1 0.0 collective-permute-done.15
  156.1 0.0 collective-permute-done.22
  156.1 0.0 reduce-scatter.2.cloned.1.call-done
  156.2 3.4 %conditional.1 = (bf16[768,256]{1,0:T(8,128)(2,1)S(1)}) conditional(s32[]{:T(128)} %bitcast.3, (s32[768,1]{1,0:T(8,128)S(1)}, f32[768,256]{1,0:T(8,128)}, f32[288,256]{1,0:T(8,128)S(1)}, f32[288,256]{1,0:T(8,128)S(1)}, f32[192,256]{1,0:T(8,128)S(1)}, /*index=5*/f32[192,256]{1,0:T(8,128)S(1)}, f32[48,256]{1,0:T(8,128)S(1)}, ...), branch_computations={%region_1.0_spmd, %region_2.0_spmd} | conditional | flops 2793406464 | bytes 30794124 | solution.py:409
  156.3 3.2 %merge.2 = bf16[768,256]{1,0:T(8,128)(2,1)S(1)} custom-call(s32[768,1]{1,0:T(8,128)S(1)} %get-tuple-element.55.target_ref, f32[768,256]{1,0:T(8,128)} %get-tuple-element.56.refs_0_, f32[288,256]{1,0:T(8,128)S(1)} %get-tuple-element.57.refs_1_, f32[288,256]{1,0:T(8,128)S(1)} %get-tuple-element.58.refs_2_, f32[192,256]{1,0:T(8,128)S(1)} %get-tuple-element.59.refs_3_, ...), custom_call_target="tpu_custom_call" | custom-call | flops 1245708288 | bytes 7274496 | tf_op jit(solution)/shard_map/cond/branch_0_fun/merge/pallas_call | solution.py:308
  159.5 0.0 copy-start.15
  159.6 0.7 copy-done.15
  (33 shorter events, 0.1 us)
Async XLA Ops:
  6.5 149.6 %reduce-scatter.2.cloned.1.call-start = ((), (), s32[]{:S(2)}) async-start(), calls=%async_computation.1 | async-start | bytes 3932160 | tf_op jit(solution)/shard_map/reduce_scatter | solution.py:385
  6.5 8.0 %collective-permute-start.9 = (s32[1,768]{1,0:T(1,128)}, s32[1,768]{1,0:T(1,128)S(1)}, u32[]{:S(2)}, u32[]{:S(2)}) collective-permute-start(s32[1,768]{1,0:T(1,128)} %bitcast.7), channel_id=1, source_target_pairs={{0,12},{4,8},{8,4},{12,0},{1,13},{5,9},{9,5},{13,1},{2,14},{6,10},... | collective-permute-start | bytes 9224 | tf_op jit(solution)/shard_map/ppermute | solution.py:318
  11.6 4.7 %collective-permute-start.8 = (s32[1,768]{1,0:T(1,128)}, s32[1,768]{1,0:T(1,128)S(1)}, u32[]{:S(2)}, u32[]{:S(2)}) collective-permute-start(s32[1,768]{1,0:T(1,128)} %bitcast.8), channel_id=1, source_target_pairs={{0,8},{4,12},{8,0},{12,4},{1,9},{5,13},{9,1},{13,5},{2,10},{6,14},... | collective-permute-start | bytes 9224 | tf_op jit(solution)/shard_map/ppermute | solution.py:318
  11.6 4.7 %collective-permute-start.7 = (s32[1,768]{1,0:T(1,128)}, s32[1,768]{1,0:T(1,128)S(1)}, u32[]{:S(2)}, u32[]{:S(2)}) collective-permute-start(s32[1,768]{1,0:T(1,128)} %bitcast.9), channel_id=1, source_target_pairs={{0,4},{4,0},{8,12},{12,8},{1,5},{5,1},{9,13},{13,9},{2,6},{6,2},{1... | collective-permute-start | bytes 9224 | tf_op jit(solution)/shard_map/ppermute | solution.py:318
  12.2 0.7 copy-start
  16.3 1.9 %copy-start.2 = (bf16[768,2048]{1,0:T(8,128)(2,1)S(1)}, bf16[768,2048]{1,0:T(8,128)(2,1)}, u32[]{:S(2)}) copy-start(bf16[768,2048]{1,0:T(8,128)(2,1)} %tok_ref.5) | copy-start | bytes 9437188
  20.5 6.8 %copy-start.3 = (bf16[192,2048]{1,0:T(8,128)(2,1)}, bf16[192,2048]{1,0:T(8,128)(2,1)S(1)}, u32[]{:S(2)}) copy-start(bf16[192,2048]{1,0:T(8,128)(2,1)S(1)} %get-tuple-element.123) | copy-start | bytes 2359300
  35.0 1.0 copy-start.4
  36.0 3.7 %copy-start.1 = (s32[768,1]{0,1:T(1,128)S(1)}, s32[768,1]{0,1:T(1,128)}, u32[]{:S(2)}) copy-start(s32[768,1]{0,1:T(1,128)} %param.13) | copy-start | bytes 9220
  36.1 51.6 %collective-permute-start.11 = (bf16[288,2048]{1,0:T(8,128)(2,1)S(1)}, bf16[288,2048]{1,0:T(8,128)(2,1)S(1)}, u32[]{:S(2)}, u32[]{:S(2)}) collective-permute-start(bf16[288,2048]{1,0:T(8,128)(2,1)S(1)} %get-tuple-element.117), channel_id=1, source_target_pairs={{0,4},{4,0},{8,12},{12,8},{1,5},{5,1},{9,13},{13,9},{2,6},{6,2},{1... | collective-permute-start | bytes 3538952 | tf_op jit(solution)/shard_map/ppermute | solution.py:318
  36.2 76.4 %collective-permute-start.16 = (bf16[192,2048]{1,0:T(8,128)(2,1)S(1)}, bf16[192,2048]{1,0:T(8,128)(2,1)S(1)}, u32[]{:S(2)}, u32[]{:S(2)}) collective-permute-start(bf16[192,2048]{1,0:T(8,128)(2,1)S(1)} %get-tuple-element.113.refs_0_), channel_id=1, source_target_pairs={{0,12},{4,8},{8,4},{12,0},{1,13},{5,9},{9,5},{13,1},{2,14},{6,10},... | collective-permute-start | bytes 2359304 | tf_op jit(solution)/shard_map/ppermute | solution.py:318
  39.7 72.9 %collective-permute-start.17 = (bf16[192,2048]{1,0:T(8,128)(2,1)}, bf16[192,2048]{1,0:T(8,128)(2,1)S(1)}, u32[]{:S(2)}, u32[]{:S(2)}) collective-permute-start(bf16[192,2048]{1,0:T(8,128)(2,1)} %copy-done.3), channel_id=1, source_target_pairs={{0,8},{4,12},{8,0},{12,4},{1,9},{5,13},{9,1},{13,5},{2,10},{6,14},... | collective-permute-start | bytes 2359304 | tf_op jit(solution)/shard_map/ppermute | solution.py:318
  41.4 60.0 %copy-start.9 = (s32[12]{0:T(128)}, s32[12]{0:T(128)S(1)}, u32[]{:S(2)}) copy-start(s32[12]{0:T(128)S(1)} %get-tuple-element.116) | copy-start | bytes 148
  87.7 1.3 copy-start.5
  88.9 22.0 %copy-start.6 = (bf16[24,64,256]{2,1,0:T(8,128)(2,1)S(1)}, bf16[24,64,256]{2,1,0:T(8,128)(2,1)}, u32[]{:S(2)}) copy-start(bf16[24,64,256]{2,1,0:T(8,128)(2,1)} %param.11) | copy-start | bytes 2359300
  88.9 22.0 %copy-start.11 = (f32[24]{0:T(128)S(1)}, f32[24]{0:T(128)}, u32[]{:S(2)}) copy-start(f32[24]{0:T(128)} %param.12) | copy-start | bytes 292
  101.4 2.2 %collective-permute-start.12 = (f32[288,128]{1,0:T(8,128)S(1)}, f32[288,128]{1,0:T(8,128)S(1)}, u32[]{:S(2)}, u32[]{:S(2)}) collective-permute-start(f32[288,128]{1,0:T(8,128)S(1)} %get-tuple-element.118.refs_0_), channel_id=1, source_target_pairs={{0,1},{1,0},{2,3},{3,2},{4,5},{5,4},{6,7},{7,6},{8,9},{9,8},{10,11... | collective-permute-start | bytes 442376 | tf_op jit(solution)/shard_map/ppermute | solution.py:318
  101.5 5.8 %collective-permute-start.14 = (f32[288,128]{1,0:T(8,128)S(1)}, f32[288,128]{1,0:T(8,128)S(1)}, u32[]{:S(2)}, u32[]{:S(2)}) collective-permute-start(f32[288,128]{1,0:T(8,128)S(1)} %get-tuple-element.119), channel_id=1, source_target_pairs={{0,3},{1,2},{2,1},{3,0},{4,7},{5,6},{6,5},{7,4},{8,11},{9,10},{10,... | collective-permute-start | bytes 442376 | tf_op jit(solution)/shard_map/ppermute | solution.py:318
  103.1 7.8 %collective-permute-start.13 = (f32[288,128]{1,0:T(8,128)S(1)}, f32[288,128]{1,0:T(8,128)S(1)}, u32[]{:S(2)}, u32[]{:S(2)}) collective-permute-start(f32[288,128]{1,0:T(8,128)S(1)} %get-tuple-element.119), channel_id=1, source_target_pairs={{0,2},{1,3},{2,0},{3,1},{4,6},{5,7},{6,4},{7,5},{8,10},{9,11},{10,... | collective-permute-start | bytes 442376 | tf_op jit(solution)/shard_map/ppermute | solution.py:318
  103.7 34.8 %collective-permute-start.23 = (bf16[48,2048]{1,0:T(8,128)(2,1)S(1)}, bf16[48,2048]{1,0:T(8,128)(2,1)S(1)}, u32[]{:S(2)}, u32[]{:S(2)}) collective-permute-start(bf16[48,2048]{1,0:T(8,128)(2,1)S(1)} %get-tuple-element.129), channel_id=1, source_target_pairs={{0,12},{4,8},{8,4},{12,0},{1,13},{5,9},{9,5},{13,1},{2,14},{6,10},... | collective-permute-start | bytes 589832 | tf_op jit(solution)/shard_map/ppermute | solution.py:318
  107.3 31.1 %collective-permute-start.24 = (bf16[48,2048]{1,0:T(8,128)(2,1)S(1)}, bf16[48,2048]{1,0:T(8,128)(2,1)S(1)}, u32[]{:S(2)}, u32[]{:S(2)}) collective-permute-start(bf16[48,2048]{1,0:T(8,128)(2,1)S(1)} %get-tuple-element.130), channel_id=1, source_target_pairs={{0,8},{4,12},{8,0},{12,4},{1,9},{5,13},{9,1},{13,5},{2,10},{6,14},... | collective-permute-start | bytes 589832 | tf_op jit(solution)/shard_map/ppermute | solution.py:318
  123.3 2.2 %collective-permute-start.18 = (f32[192,128]{1,0:T(8,128)S(1)}, f32[192,128]{1,0:T(8,128)S(1)}, u32[]{:S(2)}, u32[]{:S(2)}) collective-permute-start(f32[192,128]{1,0:T(8,128)S(1)} %get-tuple-element.124.refs_0_), channel_id=1, source_target_pairs={{0,1},{1,0},{2,3},{3,2},{4,5},{5,4},{6,7},{7,6},{8,9},{9,8},{10,11... | collective-permute-start | bytes 294920 | tf_op jit(solution)/shard_map/ppermute | solution.py:318
  123.4 5.9 %collective-permute-start.20 = (f32[192,128]{1,0:T(8,128)S(1)}, f32[192,128]{1,0:T(8,128)S(1)}, u32[]{:S(2)}, u32[]{:S(2)}) collective-permute-start(f32[192,128]{1,0:T(8,128)S(1)} %get-tuple-element.125), channel_id=1, source_target_pairs={{0,3},{1,2},{2,1},{3,0},{4,7},{5,6},{6,5},{7,4},{8,11},{9,10},{10,... | collective-permute-start | bytes 294920 | tf_op jit(solution)/shard_map/ppermute | solution.py:318
  125.0 5.7 %collective-permute-start.19 = (f32[192,128]{1,0:T(8,128)S(1)}, f32[192,128]{1,0:T(8,128)S(1)}, u32[]{:S(2)}, u32[]{:S(2)}) collective-permute-start(f32[192,128]{1,0:T(8,128)S(1)} %get-tuple-element.125), channel_id=1, source_target_pairs={{0,2},{1,3},{2,0},{3,1},{4,6},{5,7},{6,4},{7,5},{8,10},{9,11},{10,... | collective-permute-start | bytes 294920 | tf_op jit(solution)/shard_map/ppermute | solution.py:318
  125.5 30.5 %collective-permute-start.15 = (f32[288,256]{1,0:T(8,128)S(1)}, f32[288,256]{1,0:T(8,128)S(1)}, u32[]{:S(2)}, u32[]{:S(2)}) collective-permute-start(f32[288,256]{1,0:T(8,128)S(1)} %get-tuple-element.121), channel_id=1, source_target_pairs={{0,4},{4,0},{8,12},{12,8},{1,5},{5,1},{9,13},{13,9},{2,6},{6,2},{1... | collective-permute-start | bytes 884744 | tf_op jit(solution)/shard_map/ppermute | solution.py:318
  131.8 24.2 %collective-permute-start.22 = (f32[192,256]{1,0:T(8,128)S(1)}, f32[192,256]{1,0:T(8,128)S(1)}, u32[]{:S(2)}, u32[]{:S(2)}) collective-permute-start(f32[192,256]{1,0:T(8,128)S(1)} %get-tuple-element.127), channel_id=1, source_target_pairs={{0,8},{4,12},{8,0},{12,4},{1,9},{5,13},{9,1},{13,5},{2,10},{6,14},... | collective-permute-start | bytes 589832 | tf_op jit(solution)/shard_map/ppermute | solution.py:318
  133.8 22.2 %collective-permute-start.21 = (f32[192,256]{1,0:T(8,128)S(1)}, f32[192,256]{1,0:T(8,128)S(1)}, u32[]{:S(2)}, u32[]{:S(2)}) collective-permute-start(f32[192,256]{1,0:T(8,128)S(1)} %get-tuple-element.126.refs_2_), channel_id=1, source_target_pairs={{0,12},{4,8},{8,4},{12,0},{1,13},{5,9},{9,5},{13,1},{2,14},{6,10},... | collective-permute-start | bytes 589832 | tf_op jit(solution)/shard_map/ppermute | solution.py:318
  138.5 17.6 %copy-start.7 = (bf16[24,64,256]{2,1,0:T(8,128)(2,1)S(1)}, bf16[24,64,256]{2,1,0:T(8,128)(2,1)}, u32[]{:S(2)}) copy-start(bf16[24,64,256]{2,1,0:T(8,128)(2,1)} %param.11) | copy-start | bytes 2359300
  138.5 17.6 %copy-start.8 = (s32[96,1]{1,0:T(8,128)S(1)}, s32[96,1]{1,0:T(8,128)}, u32[]{:S(2)}) copy-start(s32[96,1]{1,0:T(8,128)} %get-tuple-element.137) | copy-start | bytes 1156
  138.5 17.6 %copy-start.10 = (s32[12]{0:T(128)S(1)}, s32[12]{0:T(128)}, u32[]{:S(2)}) copy-start(s32[12]{0:T(128)} %copy-done.9) | copy-start | bytes 148
  138.5 17.6 %copy-start.13 = (bf16[48,2048]{1,0:T(8,128)(2,1)S(1)}, bf16[48,2048]{1,0:T(8,128)(2,1)}, u32[]{:S(2)}) copy-start(bf16[48,2048]{1,0:T(8,128)(2,1)} %get-tuple-element.135) | copy-start | bytes 589828
  138.5 17.6 %copy-start.14 = (bf16[48,2048]{1,0:T(8,128)(2,1)S(1)}, bf16[48,2048]{1,0:T(8,128)(2,1)}, u32[]{:S(2)}) copy-start(bf16[48,2048]{1,0:T(8,128)(2,1)} %get-tuple-element.136) | copy-start | bytes 589828
  138.5 17.6 %copy-start.16 = (s32[768,1]{1,0:T(8,128)S(1)}, s32[768,1]{1,0:T(8,128)}, u32[]{:S(2)}) copy-start(s32[768,1]{1,0:T(8,128)} %get-tuple-element.111) | copy-start | bytes 9220
  141.5 1.7 %collective-permute-start.25 = (f32[48,128]{1,0:T(8,128)S(1)}, f32[48,128]{1,0:T(8,128)S(1)}, u32[]{:S(2)}, u32[]{:S(2)}) collective-permute-start(f32[48,128]{1,0:T(8,128)S(1)} %get-tuple-element.131.refs_0_), channel_id=1, source_target_pairs={{0,1},{1,0},{2,3},{3,2},{4,5},{5,4},{6,7},{7,6},{8,9},{9,8},{10,11... | collective-permute-start | bytes 73736 | tf_op jit(solution)/shard_map/ppermute | solution.py:318
  141.6 3.3 %collective-permute-start.27 = (f32[48,128]{1,0:T(8,128)S(1)}, f32[48,128]{1,0:T(8,128)S(1)}, u32[]{:S(2)}, u32[]{:S(2)}) collective-permute-start(f32[48,128]{1,0:T(8,128)S(1)} %get-tuple-element.132), channel_id=1, source_target_pairs={{0,3},{1,2},{2,1},{3,0},{4,7},{5,6},{6,5},{7,4},{8,11},{9,10},{10,... | collective-permute-start | bytes 73736 | tf_op jit(solution)/shard_map/ppermute | solution.py:318
  143.2 3.8 %collective-permute-start.26 = (f32[48,128]{1,0:T(8,128)S(1)}, f32[48,128]{1,0:T(8,128)S(1)}, u32[]{:S(2)}, u32[]{:S(2)}) collective-permute-start(f32[48,128]{1,0:T(8,128)S(1)} %get-tuple-element.132), channel_id=1, source_target_pairs={{0,2},{1,3},{2,0},{3,1},{4,6},{5,7},{6,4},{7,5},{8,10},{9,11},{10,... | collective-permute-start | bytes 73736 | tf_op jit(solution)/shard_map/ppermute | solution.py:318
  144.9 3.5 %collective-permute-start.10 = (s32[1,128]{1,0:T(1,128)S(1)}, s32[1,128]{1,0:T(1,128)S(1)}, u32[]{:S(2)}, u32[]{:S(2)}) collective-permute-start(s32[1,128]{1,0:T(1,128)S(1)} %get-tuple-element.110), channel_id=1, source_target_pairs={{0,16},{16,0},{1,17},{17,1},{2,18},{18,2},{3,19},{19,3},{4,20},{20... | collective-permute-start | bytes 1544 | tf_op jit(solution)/shard_map/ppermute | solution.py:318
  147.6 6.4 %collective-permute-start.28 = (f32[48,256]{1,0:T(8,128)S(1)}, f32[48,256]{1,0:T(8,128)S(1)}, u32[]{:S(2)}, u32[]{:S(2)}) collective-permute-start(f32[48,256]{1,0:T(8,128)S(1)} %get-tuple-element.133), channel_id=1, source_target_pairs={{0,12},{4,8},{8,4},{12,0},{1,13},{5,9},{9,5},{13,1},{2,14},{6,10},... | collective-permute-start | bytes 147464 | tf_op jit(solution)/shard_map/ppermute | solution.py:318
  148.5 7.6 %collective-permute-start.29 = (f32[48,256]{1,0:T(8,128)S(1)}, f32[48,256]{1,0:T(8,128)S(1)}, u32[]{:S(2)}, u32[]{:S(2)}) collective-permute-start(f32[48,256]{1,0:T(8,128)S(1)} %get-tuple-element.134), channel_id=1, source_target_pairs={{0,8},{4,12},{8,0},{12,4},{1,9},{5,13},{9,1},{13,5},{2,10},{6,14},... | collective-permute-start | bytes 147464 | tf_op jit(solution)/shard_map/ppermute | solution.py:318
  159.5 0.7 copy-start.15
Sparse Core Ops, SparseCore 0:
  36.2 37.6 reduce-scatter.1

commit v4 on v3

--- a/solution.py
+++ b/solution.py
@@ -14,15 +14,9 @@
 BF16 = jnp.bfloat16
 I32 = jnp.int32
 ANYWHERE = pl.BlockSpec(memory_space=pl.ANY)
+LIGHT = pl.CostEstimate(flops=1, transcendentals=0, bytes_accessed=1)
+HEAVY = pl.CostEstimate(flops=26 * 10**9, transcendentals=0, bytes_accessed=1)
 PARAMS = pltpu.CompilerParams(vmem_limit_bytes=VMEM_LIMIT)
-
-
-def cost(rows, depth, columns, terms=1):
-    return pl.CostEstimate(
-        flops=2 * rows * depth * columns * terms,
-        transcendentals=0,
-        bytes_accessed=2 * terms * (rows + columns) * depth + 4 * rows * columns,
-    )
 
 
 def owner_of(ids, owners, owned):
@@ -61,16 +55,28 @@
         ],
         out_shape=[jax.ShapeDtypeStruct((1, rows), I32), jax.ShapeDtypeStruct((rows, 1), I32)],
         compiler_params=PARAMS,
-        cost_estimate=cost(rows, rows, 8),
+        cost_estimate=LIGHT,
         name="route",
     )(me, ids_row)
 
 
 def sort_kernel(cap, pieces, waits, slot_ref, tok_ref, *refs):
-    for (block, first, count), out in zip(pieces, refs[waits:]):
-        at = block * cap + first + lax.broadcasted_iota(I32, (count, slot_ref.shape[1]), 0)
-        place = jnp.where(at == slot_ref[...], 1.0, 0.0).astype(BF16)
-        out[...] = jnp.dot(place, tok_ref[...], preferred_element_type=F32).astype(BF16)
+    outs, place = refs[waits:-1], refs[-1]
+
+    @pl.when(pl.program_id(0) == 0)
+    def _():
+        begin = 0
+        for block, first, count in pieces:
+            at = block * cap + first + lax.broadcasted_iota(I32, (count, slot_ref.shape[1]), 0)
+            found = jnp.where(at == slot_ref[...], 1.0, 0.0).astype(BF16)
+            place[begin : begin + count, :] = found
+            begin += count
+
+    moved = jnp.dot(place[...], tok_ref[...], preferred_element_type=F32).astype(BF16)
+    begin = 0
+    for (_, _, count), out in zip(pieces, outs):
+        out[...] = moved[begin : begin + count, :]
+        begin += count
 
 
 def sort_rows(tokens, slot, cap, pieces, later_than=()):
@@ -86,8 +92,9 @@
         + [ANYWHERE] * len(later_than),
         out_specs=[pl.BlockSpec((count, step), lambda i: (0, i)) for _, _, count in pieces],
         out_shape=[jax.ShapeDtypeStruct((count, width), BF16) for _, _, count in pieces],
-        compiler_params=PARAMS,
-        cost_estimate=cost(sum(c for _, _, c in pieces), rows, width),
+        scratch_shapes=[pltpu.VMEM((sum(c for _, _, c in pieces), rows), BF16)],
+        compiler_params=PARAMS,
+        cost_estimate=LIGHT,
         name="sort",
     )(slot, tokens, *later_than)
 
@@ -137,7 +144,7 @@
         out_shape=[jax.ShapeDtypeStruct((t, 1), I32) for t in totals]
         + [jax.ShapeDtypeStruct((3 * len(sets),), I32), jax.ShapeDtypeStruct((1, 128), I32)],
         compiler_params=PARAMS,
-        cost_estimate=cost(sum(totals), owned, 8),
+        cost_estimate=LIGHT,
         name="name_rows",
     )(here, *lines)
     plans = [plan[3 * k : 3 * k + 3] for k in range(len(sets))]
@@ -162,7 +169,7 @@
         out_specs=pl.BlockSpec((rows, step), lambda i: (0, i)),
         out_shape=jax.ShapeDtypeStruct((rows, columns), F32),
         compiler_params=PARAMS,
-        cost_estimate=cost(rows, width, columns),
+        cost_estimate=LIGHT,
         name="base",
     )(tokens, weight, later_than)
 
@@ -206,7 +213,7 @@
         other_ref[...] = jnp.where(second, keys, values)
 
 
-def shrink(blocks, names, plan, down, later_than=()):
+def shrink(blocks, names, plan, down, later_than=(), cost=LIGHT):
     sizes = tuple(b.shape[0] for b in blocks)
     total = sum(sizes)
     owned, rank2, width = down.shape
@@ -232,7 +239,7 @@
         ),
         out_shape=[line, line],
         compiler_params=PARAMS,
-        cost_estimate=cost(total, width, owned * rank2),
+        cost_estimate=cost,
         name="shrink",
     )(plan, names, down, *blocks, *later_than)
 
@@ -245,15 +252,18 @@
     return parts + [x]
 
 
-def expand_kernel(sizes, heard, which_ref, scale_ref, up_ref, *refs):
+def expand_kernel(groups, sizes, heard, which_ref, scale_ref, up_ref, *refs):
     lines, outs = refs[:heard], refs[heard:]
     total = lines[0][...]
     for line in lines[1:]:
         total = total + line[...]
-    upper, lower = total[:, :ADAPTER_RANK], total[:, ADAPTER_RANK:]
-    twice = jnp.concatenate(
-        [jnp.concatenate([upper, upper], axis=1), jnp.concatenate([lower, lower], axis=1)], axis=0
-    )
+    twice, begin = [], 0
+    for count in groups:
+        lines = total[begin : begin + count, :]
+        for side in (lines[:, :ADAPTER_RANK], lines[:, ADAPTER_RANK:]):
+            twice.append(jnp.concatenate([side, side], axis=1))
+        begin += count
+    twice = jnp.concatenate(twice, axis=0)
     which = which_ref[...]
     parity = jnp.where(lax.broadcasted_iota(I32, (1, 2 * ADAPTER_RANK), 1) >= ADAPTER_RANK, 1, 0)
     pairs = up_ref.shape[0] // (2 * ADAPTER_RANK)
@@ -272,13 +282,13 @@
         begin += size
 
 
-def expand(lines, names, scale, up, sizes):
+def expand(lines, groups, names, scale, up, sizes):
     columns = up.shape[1]
     return pl.pallas_call(
-        functools.partial(expand_kernel, sizes, len(lines)),
+        functools.partial(expand_kernel, groups, sizes, len(lines)),
         out_shape=[jax.ShapeDtypeStruct((s, columns), F32) for s in sizes],
         compiler_params=PARAMS,
-        cost_estimate=cost(sum(sizes), up.shape[0], columns, 3),
+        cost_estimate=LIGHT,
         name="expand",
     )(names, scale, up, *lines)
 
@@ -309,7 +319,7 @@
         functools.partial(merge_kernel, tuple(begins), len(parts)),
         out_shape=jax.ShapeDtypeStruct(parts[0].shape, kind),
         compiler_params=PARAMS,
-        cost_estimate=cost(parts[0].shape[0], sum(b.shape[0] for b in blocks), parts[0].shape[1], 3),
+        cost_estimate=LIGHT,
         name="merge",
     )(target, *parts, *blocks)
 
@@ -339,25 +349,29 @@
     half = (lax.axis_index(feature_axes) >= sharers // 2).astype(I32)
     cap = up_to_16(owned * TOKEN_LIMIT)
 
-    own, near = (0, 0, cap), (1, 0, cap)
+    own = (0, 0, cap)
     if owners == 4:
         usual = up_to_16(cap * 5 // 6)
         most = up_to_16(usual * 4 // 5)
-        far = [[(3, 0, most), (2, 0, most)], [(3, most, usual - most), (2, most, usual - most)]]
+        near = (1, 0, up_to_16(cap // 3))
+        far = [
+            [(3, 0, most), (2, 0, most), (1, near[2], cap - near[2])],
+            [(3, most, usual - most), (2, most, usual - most)],
+        ]
         extra = [(3, usual, cap - usual), (2, usual, cap - usual)]
     else:
-        usual, far, extra = cap, [[(j, 0, cap) for j in range(2, owners)]], []
+        usual, near, far = cap, (1, 0, cap), [[(j, 0, cap) for j in range(2, owners)]]
+        extra = []
 
     ids_row = token_adapter_index.reshape(1, rows)
     ids_heard = [ids_row] + [swap(ids_row, "dp", owners, j) for j in range(1, owners)]
     slot, target = route(ids_row, me.reshape(1), owners, owned, cap)
-    early = sort_rows(tokens, slot, cap, far[0], tuple(ids_heard[1:]))
-    later = [near] + [p for s in far[1:] for p in s] + [own] + extra
-    packed = dict(zip(far[0] + later, early + sort_rows(tokens, slot, cap, later, early[:1])))
-    sent = [p for s in far for p in s] + [near]
+    sent = [near] + [p for s in far for p in s]
+    packed = dict(zip(sent, sort_rows(tokens, slot, cap, sent, tuple(ids_heard[1:]))))
     received = {p: swap(packed[p], "dp", owners, p[0]) for p in sent}
-
-    sets = [[own, near]] + far + ([extra] if extra else [])
+    packed |= zip([own] + extra, sort_rows(tokens, slot, cap, [own] + extra, (received[near],)))
+
+    sets = [[own], [near], [own, near]] + far + ([extra] if extra else [])
     here = jnp.stack([me.astype(I32), half])
     names, plans, largest = name_rows(ids_heard, here, owned, sets)
 
@@ -366,13 +380,16 @@
     up = adapter_up_weight.reshape(-1, adapter_up_weight.shape[2])
     scale = adapter_scale.reshape(1, owned)
 
-    def deltas_of(blocks, names, plan, down, up, scale, later_than):
-        mine, other = shrink(blocks, names, plan, down, later_than)
-        lines = [mine] + [
+    def exchange(mine, other):
+        return [mine] + [
             swap(mine if d < sharers // 2 else other, feature_axes, sharers, d)
             for d in range(1, sharers)
         ]
-        return expand(lines, names, scale, up, tuple(b.shape[0] for b in blocks))
+
+    def deltas_of(blocks, names, plan, down, up, scale, later_than, cost=LIGHT):
+        mine, other = shrink(blocks, names, plan, down, later_than, cost)
+        sizes = tuple(b.shape[0] for b in blocks)
+        return expand(exchange(mine, other), (mine.shape[0],), names, scale, up, sizes)
 
     def send_back(pieces, deltas):
         return [swap(d, "dp", owners, p[0]) for p, d in zip(pieces, deltas)]
@@ -381,15 +398,19 @@
         return [b * cap + f for b, f, _ in pieces]
 
     weights = (adapter_down_weight, up, scale)
-    base_part = base_product(tokens, key_value_weight, packed[own])
+    base_part = base_product(tokens, key_value_weight, received[near])
     base = lax.psum_scatter(base_part, feature_axes, scatter_dimension=1, tiled=True)
-    blocks = [packed[own], received[near]]
-    deltas = deltas_of(blocks, names[0], plans[0], *weights, (base_part,))
+    first = shrink([packed[own]], names[0], plans[0], adapter_down_weight, (base_part,))
+    second = shrink([received[near]], names[1], plans[1], adapter_down_weight, tuple(first[:1]))
+    lines = exchange(*(jnp.concatenate(pair, axis=0) for pair in zip(first, second)))
+    sizes = (cap, near[2])
+    deltas = expand(lines, tuple(c // 2 for c in sizes), names[2], scale, up, sizes)
     returned = [deltas[0]] + send_back([near], deltas[1:])
     done = [own, near]
     for k, pieces in enumerate(far):
         blocks = [received[p] for p in pieces]
-        deltas = deltas_of(blocks, names[1 + k], plans[1 + k], *weights, (deltas[0],))
+        cost = HEAVY if k and pieces is far[-1] else LIGHT
+        deltas = deltas_of(blocks, names[3 + k], plans[3 + k], *weights, (deltas[0],), cost)
         returned += send_back(pieces, deltas)
         done += pieces
 

time: 168 us -> 184 us (1.095)
  waiting for transfers between devices: 63 us -> 73.6 us
  Pallas kernels: 52.9 us -> 57.6 us
    ppermute x23 -> x25, waiting for transfers between devices: 63 us -> 73.6 us  [swap(): return lax.ppermute(x, axes, [(i, i ^ distance) for i in range(size)])]
    pallas_call x3 -> x4, Pallas kernels: 26.2 us -> 31.8 us  [shrink(): pl.pallas_call(functools.partial(shrink_kernel, sizes, group, fine, len(l...]
    unnamed x32 -> x40, local copies, waits for them, and re-layouts: 5.66 us -> 6.24 us
    ppermute x23 -> x25, starting transfers between devices: 31.4 us -> 31.6 us  [swap(): return lax.ppermute(x, axes, [(i, i ^ distance) for i in range(size)])]
  transfers between devices with their start and end apart: 24 -> 26, of which waited for: 10 -> 13; matrix products, arithmetic and copies ran while one was open for 0% -> 0% of each run, Pallas kernels for 20% -> 23%
where the time goes in v4:
time: 184 us; the launch traced here: 183 us
  waiting for transfers between devices  73.6 us (40%)
  Pallas kernels  57.6 us (31%)
  starting transfers between devices  31.6 us (17%)
  between operations  13.8 us (8%)
  local copies, waits for them, and re-layouts  6.32 us (3%)
    ppermute x25, waiting for transfers between devices, swap(): return lax.ppermute(x, axes, [(i, i ^ distance) for i in range(size)])  73.6 us
    pallas_call x4, Pallas kernels, shrink(): pl.pallas_call(functools.partial(shrink_kernel, sizes, group, fine, len(l...  31.8 us
    ppermute x25, starting transfers between devices, swap(): return lax.ppermute(x, axes, [(i, i ^ distance) for i in range(size)])  31.6 us
    pallas_call x2, Pallas kernels, sort_rows(): pl.pallas_call(functools.partial(sort_kernel, cap, pieces, len(later_than...  8.14 us
    pallas_call x1, Pallas kernels, base_product(): pl.pallas_call(base_kernel, grid=(columns // step,), in_specs=[pl.BlockSp...  7.75 us
    unnamed x40, local copies, waits for them, and re-layouts  6.24 us
  transfers between devices with their start and end apart: 26, of which 13 were waited for; matrix products, arithmetic and copies ran while one was open for 0% of the time, Pallas kernels for 23%

profile of v4, /device:TPU:0, one launch (start us, length us, event | category | flops | bytes accessed | tf_op | source)
XLA Modules:
  0.0 183.1 jit_solution(17861281797248910219)
XLA Ops:
  6.5 5.0 %collective-permute-start.9 = (s32[1,768]{1,0:T(1,128)}, s32[1,768]{1,0:T(1,128)S(1)}, u32[]{:S(2)}, u32[]{:S(2)}) collective-permute-start(s32[1,768]{1,0:T(1,128)} %bitcast.7), channel_id=1, source_target_pairs={{0,12},{4,8},{8,4},{12,0},{1,13},{5,9},{9,5},{13,1},{2,14},{6,10},... | collective-permute-start | bytes 9224 | tf_op jit(solution)/shard_map/ppermute | solution.py:328
  11.6 0.6 collective-permute-start.7
  12.2 0.7 copy-done.1
  12.9 1.6 route.1
  14.5 0.0 collective-permute-done.9.refs_3_.refs_2_
  14.5 1.8 collective-permute-done.8.refs_2_.refs_1_
  16.3 5.1 %sort.2 = (bf16[96,2048]{1,0:T(8,128)(2,1)S(1)}, bf16[192,2048]{1,0:T(8,128)(2,1)S(1)}, bf16[192,2048]{1,0:T(8,128)(2,1)S(1)}, bf16[192,2048]{1,0:T(8,128)(2,1)S...) custom-call(s32[1,768]{1,0:T(1,128)S(1)} %get-tuple-element.124.slot_ref, bf16[768,2048]{1,0:T(8,128)(2,1)} %tok_ref.5, ...), custom_call_target="tpu_custom_call" | custom-call | flops 1 | bytes 1 | tf_op jit(solution)/shard_map/sort/pallas_call | solution.py:85
  21.4 0.9 copy-done.3
  22.3 0.9 copy-done.4
  23.2 0.9 copy-done.5
  24.1 0.7 copy-done.6
  24.7 0.7 copy-done.8
  25.4 9.4 %collective-permute-done.11._.refs_0_ = bf16[96,2048]{1,0:T(8,128)(2,1)S(1)} collective-permute-done((bf16[96,2048]{1,0:T(8,128)(2,1)S(1)}, bf16[96,2048]{1,0:T(8,128)(2,1)S(1)}, u32[]{:S(2)}, u32[]{:S(2)}) %collective-permute-start.11) | collective-permute-done | bytes 393248 | tf_op jit(solution)/shard_map/ppermute | solution.py:328
  34.8 7.8 %base.1.refs_1_ = f32[768,1024]{1,0:T(8,128)} custom-call(bf16[768,2048]{1,0:T(8,128)(2,1)} %tok_ref.5, bf16[2048,1024]{1,0:T(8,128)(2,1)} %weight_ref.1, bf16[96,2048]{1,0:T(8,128)(2,1)S(1)} %collective-permute-done.11._.refs_0_), custom_call_target="tpu_custom_call" | custom-call | flops 1 | bytes 1 | tf_op jit(solution)/shard_map/base/pallas_call | solution.py:161
  42.6 0.0 reduce-scatter.2.cloned.1.call-update
  42.6 0.1 pad_add_fusion.here_ref
  42.7 2.6 %collective-permute-start.16 = (bf16[192,2048]{1,0:T(8,128)(2,1)}, bf16[192,2048]{1,0:T(8,128)(2,1)S(1)}, u32[]{:S(2)}, u32[]{:S(2)}) collective-permute-start(bf16[192,2048]{1,0:T(8,128)(2,1)} %copy-done.5), channel_id=1, source_target_pairs={{0,12},{4,8},{8,4},{12,0},{1,13},{5,9},{9,5},{13,1},{2,14},{6,10},... | collective-permute-start | bytes 2359304 | tf_op jit(solution)/shard_map/ppermute | solution.py:328
  45.4 1.8 collective-permute-start.18
  47.1 0.7 copy-done.2
  47.8 1.7 name_rows.1
  49.5 0.1 fusion
  49.6 3.1 %sort.3 = (bf16[288,2048]{1,0:T(8,128)(2,1)S(1)}, bf16[48,2048]{1,0:T(8,128)(2,1)}, bf16[48,2048]{1,0:T(8,128)(2,1)}) custom-call(s32[1,768]{1,0:T(1,128)S(1)} %get-tuple-element.124.slot_ref, bf16[768,2048]{1,0:T(8,128)(2,1)S(1)} %copy-done, bf16[96,2048]{1,0:T(8,128)(2,1)S(1)} %collective-permute-done.11._.refs_0_), custom_call_target="tpu_custom_call" | custom-call | flops 1 | bytes 1 | tf_op jit(solution)/shard_map/sort/pallas_call | solution.py:85
  52.7 10.4 %shrink.6 = (f32[144,128]{1,0:T(8,128)S(1)}, f32[144,128]{1,0:T(8,128)S(1)}) custom-call(s32[3]{0:T(128)S(1)} %get-tuple-element.160.plan_ref, s32[288,1]{1,0:T(8,128)S(1)} %get-tuple-element.128.which_ref, bf16[24,128,2048]{2,1,0:T(8,128)(2,1)} %down_ref.7, bf16[288,2048]{1,0:T(8,128)(2,1)S(1)} %get-tuple-element.129.refs_0_, f32[768,1024]{1,0:T(8,128)} %base.1.refs_1_), custom_call_target="tpu_custom_call" | custom-call | flops 1 | bytes 1 | tf_op jit(solution)/shard_map/shrink/pallas_call | solution.py:223
  63.1 0.0 copy-start.10
  63.1 0.0 copy-start.15
  63.1 5.9 %shrink.7 = (f32[48,128]{1,0:T(8,128)S(1)}, f32[48,128]{1,0:T(8,128)S(1)}) custom-call(s32[3]{0:T(128)S(1)} %get-tuple-element.159.plan_ref, s32[96,1]{1,0:T(8,128)S(1)} %get-tuple-element.131.which_ref, bf16[24,128,2048]{2,1,0:T(8,128)(2,1)} %down_ref.7, bf16[96,2048]{1,0:T(8,128)(2,1)S(1)} %collective-permute-done.11._.refs_0_, ...), custom_call_target="tpu_custom_call" | custom-call | flops 1 | bytes 1 | tf_op jit(solution)/shard_map/shrink/pallas_call | solution.py:223
  69.0 0.1 collective-permute-start.12
  69.1 1.5 collective-permute-start.14
  70.6 1.1 collective-permute-start.13
  71.7 4.4 %collective-permute-done.14.refs_3_ = f32[192,128]{1,0:T(8,128)S(1)} collective-permute-done((f32[192,128]{1,0:T(8,128)S(1)}, f32[192,128]{1,0:T(8,128)S(1)}, u32[]{:S(2)}, u32[]{:S(2)}) %collective-permute-start.14) | collective-permute-done | bytes 98336 | tf_op jit(solution)/shard_map/ppermute | solution.py:328
  76.2 3.3 %collective-permute-start.25 = (bf16[48,2048]{1,0:T(8,128)(2,1)S(1)}, bf16[48,2048]{1,0:T(8,128)(2,1)S(1)}, u32[]{:S(2)}, u32[]{:S(2)}) collective-permute-start(bf16[48,2048]{1,0:T(8,128)(2,1)S(1)} %copy-done.9), channel_id=1, source_target_pairs={{0,12},{4,8},{8,4},{12,0},{1,13},{5,9},{9,5},{13,1},{2,14},{6,10},... | collective-permute-start | bytes 589832 | tf_op jit(solution)/shard_map/ppermute | solution.py:328
  79.5 1.5 collective-permute-done.13.refs_2_
  81.0 0.8 collective-permute-start.26
  81.8 1.2 expand.5
  83.0 37.8 %collective-permute-done.17.refs_1_ = bf16[192,2048]{1,0:T(8,128)(2,1)S(1)} collective-permute-done((bf16[192,2048]{1,0:T(8,128)(2,1)}, bf16[192,2048]{1,0:T(8,128)(2,1)S(1)}, u32[]{:S(2)}, u32[]{:S(2)}) %collective-permute-start.17) | collective-permute-done | bytes 786464 | tf_op jit(solution)/shard_map/ppermute | solution.py:328
  120.8 12.5 %shrink.8 = (f32[288,128]{1,0:T(8,128)S(1)}, f32[288,128]{1,0:T(8,128)S(1)}) custom-call(s32[3]{0:T(128)S(1)} %get-tuple-element.158.plan_ref, s32[576,1]{1,0:T(8,128)S(1)} %get-tuple-element.137.which_ref, bf16[24,128,2048]{2,1,0:T(8,128)(2,1)} %down_ref.7, bf16[192,2048]{1,0:T(8,128)(2,1)S(1)} %collective-permute-done.16.refs_0_, ...), custom_call_target="tpu_custom_call" | custom-call | flops 1 | bytes 1 | tf_op jit(solution)/shard_map/shrink/pallas_call | solution.py:223
  133.3 0.1 collective-permute-start.19
  133.4 1.6 collective-permute-start.21
  135.0 0.5 collective-permute-start.20
  135.5 0.5 collective-permute-start.15
  136.0 3.2 %collective-permute-done.21.refs_3_ = f32[288,128]{1,0:T(8,128)S(1)} collective-permute-done((f32[288,128]{1,0:T(8,128)S(1)}, f32[288,128]{1,0:T(8,128)S(1)}, u32[]{:S(2)}, u32[]{:S(2)}) %collective-permute-start.21) | collective-permute-done | bytes 147488 | tf_op jit(solution)/shard_map/ppermute | solution.py:328
  139.2 3.6 %collective-permute-done.20.refs_2_ = f32[288,128]{1,0:T(8,128)S(1)} collective-permute-done((f32[288,128]{1,0:T(8,128)S(1)}, f32[288,128]{1,0:T(8,128)S(1)}, u32[]{:S(2)}, u32[]{:S(2)}) %collective-permute-start.20) | collective-permute-done | bytes 147488 | tf_op jit(solution)/shard_map/ppermute | solution.py:328
  142.8 1.6 expand.6
  144.4 0.1 collective-permute-start.23
  144.5 3.8 %collective-permute-start.24 = (f32[192,256]{1,0:T(8,128)S(1)}, f32[192,256]{1,0:T(8,128)S(1)}, u32[]{:S(2)}, u32[]{:S(2)}) collective-permute-start(f32[192,256]{1,0:T(8,128)S(1)} %get-tuple-element.145), channel_id=1, source_target_pairs={{0,4},{4,0},{8,12},{12,8},{1,5},{5,1},{9,13},{13,9},{2,6},{6,2},{1... | collective-permute-start | bytes 589832 | tf_op jit(solution)/shard_map/ppermute | solution.py:328
  148.3 0.6 collective-permute-start.22
  148.9 3.0 %shrink.9 = (f32[48,128]{1,0:T(8,128)S(1)}, f32[48,128]{1,0:T(8,128)S(1)}) custom-call(s32[3]{0:T(128)S(1)} %get-tuple-element.157.plan_ref, s32[96,1]{1,0:T(8,128)S(1)} %get-tuple-element.146.which_ref, bf16[24,128,2048]{2,1,0:T(8,128)(2,1)} %down_ref.7, bf16[48,2048]{1,0:T(8,128)(2,1)S(1)} %collective-permute-done.25.refs_0_, ...), custom_call_target="tpu_custom_call" | custom-call | flops 25999998976 | bytes 1 | tf_op jit(solution)/shard_map/shrink/pallas_call | solution.py:223
  151.9 0.1 collective-permute-start.27
  152.0 1.2 collective-permute-done.27.refs_1_
  153.2 1.3 collective-permute-start.29
  154.5 2.0 %collective-permute-done.29.refs_3_ = f32[48,128]{1,0:T(8,128)S(1)} collective-permute-done((f32[48,128]{1,0:T(8,128)S(1)}, f32[48,128]{1,0:T(8,128)S(1)}, u32[]{:S(2)}, u32[]{:S(2)}) %collective-permute-start.29) | collective-permute-done | bytes 24608 | tf_op jit(solution)/shard_map/ppermute | solution.py:328
  156.4 1.5 collective-permute-start.28
  157.9 2.3 %collective-permute-done.28.refs_2_ = f32[48,128]{1,0:T(8,128)S(1)} collective-permute-done((f32[48,128]{1,0:T(8,128)S(1)}, f32[48,128]{1,0:T(8,128)S(1)}, u32[]{:S(2)}, u32[]{:S(2)}) %collective-permute-start.28) | collective-permute-done | bytes 24608 | tf_op jit(solution)/shard_map/ppermute | solution.py:328
  160.3 1.5 collective-permute-start.10
  161.8 0.6 expand.7
  162.3 1.5 collective-permute-done.10
  163.8 3.2 %collective-permute-start.30 = (f32[48,256]{1,0:T(8,128)S(1)}, f32[48,256]{1,0:T(8,128)S(1)}, u32[]{:S(2)}, u32[]{:S(2)}) collective-permute-start(f32[48,256]{1,0:T(8,128)S(1)} %get-tuple-element.151), channel_id=1, source_target_pairs={{0,12},{4,8},{8,4},{12,0},{1,13},{5,9},{9,5},{13,1},{2,14},{6,10},... | collective-permute-start | bytes 147464 | tf_op jit(solution)/shard_map/ppermute | solution.py:328
  167.1 2.6 %collective-permute-done.30 = f32[48,256]{1,0:T(8,128)S(1)} collective-permute-done((f32[48,256]{1,0:T(8,128)S(1)}, f32[48,256]{1,0:T(8,128)S(1)}, u32[]{:S(2)}, u32[]{:S(2)}) %collective-permute-start.30) | collective-permute-done | bytes 49184 | tf_op jit(solution)/shard_map/ppermute | solution.py:328
  169.7 2.3 %collective-permute-done.31 = f32[48,256]{1,0:T(8,128)S(1)} collective-permute-done((f32[48,256]{1,0:T(8,128)S(1)}, f32[48,256]{1,0:T(8,128)S(1)}, u32[]{:S(2)}, u32[]{:S(2)}) %collective-permute-start.31) | collective-permute-done | bytes 49184 | tf_op jit(solution)/shard_map/ppermute | solution.py:328
  172.0 0.0 reduce-scatter.2.cloned.1.call-done
  172.1 3.4 %conditional.1 = (bf16[768,256]{1,0:T(8,128)(2,1)S(1)}) conditional(s32[]{:T(128)} %bitcast.3, (s32[768,1]{1,0:T(8,128)S(1)}, f32[768,256]{1,0:T(8,128)}, f32[288,256]{1,0:T(8,128)S(1)}, f32[96,256]{1,0:T(8,128)S(1)}, f32[192,256]{1,0:T(8,128)S(1)}, /*index=5*/f32[192,256]{1,0:T(8,128)S(1)}, f32[192,256]{1,0:T(8,128)S(1)}, f32[48,256]{1,0:T(8,128)S(1)}, ...), branch_computations={%region_1.0_spmd, %region_2.0_spmd} | conditional | flops 3 | bytes 5407063 | solution.py:430
  172.1 3.2 %merge.2 = bf16[768,256]{1,0:T(8,128)(2,1)S(1)} custom-call(s32[768,1]{1,0:T(8,128)S(1)} %get-tuple-element.59.target_ref, f32[768,256]{1,0:T(8,128)} %get-tuple-element.60.refs_0_, f32[288,256]{1,0:T(8,128)S(1)} %get-tuple-element.61.refs_1_, f32[96,256]{1,0:T(8,128)S(1)} %get-tuple-element.62.refs_2_, f32[192,256]{1,0:T(8,128)S(1)} %get-tuple-element.63.refs_3_, ...), custom_call_target="tpu_custom_call" | custom-call | flops 1 | bytes 1 | tf_op jit(solution)/shard_map/cond/branch_0_fun/merge/pallas_call | solution.py:318
  175.5 0.0 copy-start.13
  175.5 0.7 copy-done.13
  (48 shorter events, 0.1 us)
Async XLA Ops:
  6.5 165.5 %reduce-scatter.2.cloned.1.call-start = ((), (), s32[]{:S(2)}) async-start(), calls=%async_computation.1 | async-start | bytes 3932160 | tf_op jit(solution)/shard_map/reduce_scatter | solution.py:402
  6.5 8.0 %collective-permute-start.9 = (s32[1,768]{1,0:T(1,128)}, s32[1,768]{1,0:T(1,128)S(1)}, u32[]{:S(2)}, u32[]{:S(2)}) collective-permute-start(s32[1,768]{1,0:T(1,128)} %bitcast.7), channel_id=1, source_target_pairs={{0,12},{4,8},{8,4},{12,0},{1,13},{5,9},{9,5},{13,1},{2,14},{6,10},... | collective-permute-start | bytes 9224 | tf_op jit(solution)/shard_map/ppermute | solution.py:328
  11.6 4.7 %collective-permute-start.8 = (s32[1,768]{1,0:T(1,128)}, s32[1,768]{1,0:T(1,128)S(1)}, u32[]{:S(2)}, u32[]{:S(2)}) collective-permute-start(s32[1,768]{1,0:T(1,128)} %bitcast.8), channel_id=1, source_target_pairs={{0,8},{4,12},{8,0},{12,4},{1,9},{5,13},{9,1},{13,5},{2,10},{6,14},... | collective-permute-start | bytes 9224 | tf_op jit(solution)/shard_map/ppermute | solution.py:328
  11.6 4.7 %collective-permute-start.7 = (s32[1,768]{1,0:T(1,128)}, s32[1,768]{1,0:T(1,128)S(1)}, u32[]{:S(2)}, u32[]{:S(2)}) collective-permute-start(s32[1,768]{1,0:T(1,128)} %bitcast.9), channel_id=1, source_target_pairs={{0,4},{4,0},{8,12},{12,8},{1,5},{5,1},{9,13},{13,9},{2,6},{6,2},{1... | collective-permute-start | bytes 9224 | tf_op jit(solution)/shard_map/ppermute | solution.py:328
  12.2 0.7 copy-start.1
  21.4 0.9 copy-start.3
  22.3 0.9 copy-start.4
  23.2 0.9 copy-start.5
  24.1 0.7 copy-start.6
  24.7 0.7 copy-start.8
  25.4 9.4 %collective-permute-start.11 = (bf16[96,2048]{1,0:T(8,128)(2,1)S(1)}, bf16[96,2048]{1,0:T(8,128)(2,1)S(1)}, u32[]{:S(2)}, u32[]{:S(2)}) collective-permute-start(bf16[96,2048]{1,0:T(8,128)(2,1)S(1)} %get-tuple-element.125), channel_id=1, source_target_pairs={{0,4},{4,0},{8,12},{12,8},{1,5},{5,1},{9,13},{13,9},{2,6},{6,2},{1... | collective-permute-start | bytes 1179656 | tf_op jit(solution)/shard_map/ppermute | solution.py:328
  42.6 7.0 %copy-start = (bf16[768,2048]{1,0:T(8,128)(2,1)S(1)}, bf16[768,2048]{1,0:T(8,128)(2,1)}, u32[]{:S(2)}) copy-start(bf16[768,2048]{1,0:T(8,128)(2,1)} %tok_ref.5) | copy-start | bytes 9437188
  42.7 40.3 %collective-permute-start.16 = (bf16[192,2048]{1,0:T(8,128)(2,1)}, bf16[192,2048]{1,0:T(8,128)(2,1)S(1)}, u32[]{:S(2)}, u32[]{:S(2)}) collective-permute-start(bf16[192,2048]{1,0:T(8,128)(2,1)} %copy-done.5), channel_id=1, source_target_pairs={{0,12},{4,8},{8,4},{12,0},{1,13},{5,9},{9,5},{13,1},{2,14},{6,10},... | collective-permute-start | bytes 2359304 | tf_op jit(solution)/shard_map/ppermute | solution.py:328
  45.4 75.5 %collective-permute-start.17 = (bf16[192,2048]{1,0:T(8,128)(2,1)}, bf16[192,2048]{1,0:T(8,128)(2,1)S(1)}, u32[]{:S(2)}, u32[]{:S(2)}) collective-permute-start(bf16[192,2048]{1,0:T(8,128)(2,1)} %copy-done.4), channel_id=1, source_target_pairs={{0,8},{4,12},{8,0},{12,4},{1,9},{5,13},{9,1},{13,5},{2,10},{6,14},... | collective-permute-start | bytes 2359304 | tf_op jit(solution)/shard_map/ppermute | solution.py:328
  45.4 75.5 %collective-permute-start.18 = (bf16[192,2048]{1,0:T(8,128)(2,1)}, bf16[192,2048]{1,0:T(8,128)(2,1)S(1)}, u32[]{:S(2)}, u32[]{:S(2)}) collective-permute-start(bf16[192,2048]{1,0:T(8,128)(2,1)} %copy-done.3), channel_id=1, source_target_pairs={{0,4},{4,0},{8,12},{12,8},{1,5},{5,1},{9,13},{13,9},{2,6},{6,2},{1... | collective-permute-start | bytes 2359304 | tf_op jit(solution)/shard_map/ppermute | solution.py:328
  47.1 0.7 copy-start.2
  49.5 13.6 %copy-start.16 = (s32[18]{0:T(128)}, s32[18]{0:T(128)S(1)}, u32[]{:S(2)}) copy-start(s32[18]{0:T(128)S(1)} %get-tuple-element.127) | copy-start | bytes 220
  63.1 13.1 %copy-start.9 = (bf16[48,2048]{1,0:T(8,128)(2,1)S(1)}, bf16[48,2048]{1,0:T(8,128)(2,1)}, u32[]{:S(2)}) copy-start(bf16[48,2048]{1,0:T(8,128)(2,1)} %copy-done.8) | copy-start | bytes 589828
  63.1 17.9 %copy-start.7 = (bf16[48,2048]{1,0:T(8,128)(2,1)S(1)}, bf16[48,2048]{1,0:T(8,128)(2,1)}, u32[]{:S(2)}) copy-start(bf16[48,2048]{1,0:T(8,128)(2,1)} %copy-done.6) | copy-start | bytes 589828
  63.1 18.7 %copy-start.10 = (bf16[24,64,256]{2,1,0:T(8,128)(2,1)S(1)}, bf16[24,64,256]{2,1,0:T(8,128)(2,1)}, u32[]{:S(2)}) copy-start(bf16[24,64,256]{2,1,0:T(8,128)(2,1)} %param.11) | copy-start | bytes 2359300
  63.1 18.7 %copy-start.15 = (f32[24]{0:T(128)S(1)}, f32[24]{0:T(128)}, u32[]{:S(2)}) copy-start(f32[24]{0:T(128)} %param.12) | copy-start | bytes 292
  69.0 1.6 collective-permute-start.12
  69.1 7.0 %collective-permute-start.14 = (f32[192,128]{1,0:T(8,128)S(1)}, f32[192,128]{1,0:T(8,128)S(1)}, u32[]{:S(2)}, u32[]{:S(2)}) collective-permute-start(f32[192,128]{1,0:T(8,128)S(1)} %constant_dynamic-update-slice_fusion.2), channel_id=1, source_target_pairs={{0,3},{1,2},{2,1},{3,0},{4,7},{5,6},{6,5},{7,4},{8,11},{9,10},{10,... | collective-permute-start | bytes 294920 | tf_op jit(solution)/shard_map/ppermute | solution.py:328
  70.6 10.4 %collective-permute-start.13 = (f32[192,128]{1,0:T(8,128)S(1)}, f32[192,128]{1,0:T(8,128)S(1)}, u32[]{:S(2)}, u32[]{:S(2)}) collective-permute-start(f32[192,128]{1,0:T(8,128)S(1)} %constant_dynamic-update-slice_fusion.2), channel_id=1, source_target_pairs={{0,2},{1,3},{2,0},{3,1},{4,6},{5,7},{6,4},{7,5},{8,10},{9,11},{10,... | collective-permute-start | bytes 294920 | tf_op jit(solution)/shard_map/ppermute | solution.py:328
  76.2 72.1 %collective-permute-start.25 = (bf16[48,2048]{1,0:T(8,128)(2,1)S(1)}, bf16[48,2048]{1,0:T(8,128)(2,1)S(1)}, u32[]{:S(2)}, u32[]{:S(2)}) collective-permute-start(bf16[48,2048]{1,0:T(8,128)(2,1)S(1)} %copy-done.9), channel_id=1, source_target_pairs={{0,12},{4,8},{8,4},{12,0},{1,13},{5,9},{9,5},{13,1},{2,14},{6,10},... | collective-permute-start | bytes 589832 | tf_op jit(solution)/shard_map/ppermute | solution.py:328
  81.0 67.9 %collective-permute-start.26 = (bf16[48,2048]{1,0:T(8,128)(2,1)S(1)}, bf16[48,2048]{1,0:T(8,128)(2,1)S(1)}, u32[]{:S(2)}, u32[]{:S(2)}) collective-permute-start(bf16[48,2048]{1,0:T(8,128)(2,1)S(1)} %copy-done.7), channel_id=1, source_target_pairs={{0,8},{4,12},{8,0},{12,4},{1,9},{5,13},{9,1},{13,5},{2,10},{6,14},... | collective-permute-start | bytes 589832 | tf_op jit(solution)/shard_map/ppermute | solution.py:328
  133.3 2.2 %collective-permute-start.19 = (f32[288,128]{1,0:T(8,128)S(1)}, f32[288,128]{1,0:T(8,128)S(1)}, u32[]{:S(2)}, u32[]{:S(2)}) collective-permute-start(f32[288,128]{1,0:T(8,128)S(1)} %get-tuple-element.141.refs_0_), channel_id=1, source_target_pairs={{0,1},{1,0},{2,3},{3,2},{4,5},{5,4},{6,7},{7,6},{8,9},{9,8},{10,11... | collective-permute-start | bytes 442376 | tf_op jit(solution)/shard_map/ppermute | solution.py:328
  133.4 5.8 %collective-permute-start.21 = (f32[288,128]{1,0:T(8,128)S(1)}, f32[288,128]{1,0:T(8,128)S(1)}, u32[]{:S(2)}, u32[]{:S(2)}) collective-permute-start(f32[288,128]{1,0:T(8,128)S(1)} %get-tuple-element.142), channel_id=1, source_target_pairs={{0,3},{1,2},{2,1},{3,0},{4,7},{5,6},{6,5},{7,4},{8,11},{9,10},{10,... | collective-permute-start | bytes 442376 | tf_op jit(solution)/shard_map/ppermute | solution.py:328
  135.0 7.8 %collective-permute-start.20 = (f32[288,128]{1,0:T(8,128)S(1)}, f32[288,128]{1,0:T(8,128)S(1)}, u32[]{:S(2)}, u32[]{:S(2)}) collective-permute-start(f32[288,128]{1,0:T(8,128)S(1)} %get-tuple-element.142), channel_id=1, source_target_pairs={{0,2},{1,3},{2,0},{3,1},{4,6},{5,7},{6,4},{7,5},{8,10},{9,11},{10,... | collective-permute-start | bytes 442376 | tf_op jit(solution)/shard_map/ppermute | solution.py:328
  135.5 31.5 %collective-permute-start.15 = (f32[96,256]{1,0:T(8,128)S(1)}, f32[96,256]{1,0:T(8,128)S(1)}, u32[]{:S(2)}, u32[]{:S(2)}) collective-permute-start(f32[96,256]{1,0:T(8,128)S(1)} %get-tuple-element.136), channel_id=1, source_target_pairs={{0,4},{4,0},{8,12},{12,8},{1,5},{5,1},{9,13},{13,9},{2,6},{6,2},{1... | collective-permute-start | bytes 294920 | tf_op jit(solution)/shard_map/ppermute | solution.py:328
  144.4 27.6 %collective-permute-start.23 = (f32[192,256]{1,0:T(8,128)S(1)}, f32[192,256]{1,0:T(8,128)S(1)}, u32[]{:S(2)}, u32[]{:S(2)}) collective-permute-start(f32[192,256]{1,0:T(8,128)S(1)} %get-tuple-element.144), channel_id=1, source_target_pairs={{0,8},{4,12},{8,0},{12,4},{1,9},{5,13},{9,1},{13,5},{2,10},{6,14},... | collective-permute-start | bytes 589832 | tf_op jit(solution)/shard_map/ppermute | solution.py:328
  144.5 27.5 %collective-permute-start.24 = (f32[192,256]{1,0:T(8,128)S(1)}, f32[192,256]{1,0:T(8,128)S(1)}, u32[]{:S(2)}, u32[]{:S(2)}) collective-permute-start(f32[192,256]{1,0:T(8,128)S(1)} %get-tuple-element.145), channel_id=1, source_target_pairs={{0,4},{4,0},{8,12},{12,8},{1,5},{5,1},{9,13},{13,9},{2,6},{6,2},{1... | collective-permute-start | bytes 589832 | tf_op jit(solution)/shard_map/ppermute | solution.py:328
  148.3 23.7 %collective-permute-start.22 = (f32[192,256]{1,0:T(8,128)S(1)}, f32[192,256]{1,0:T(8,128)S(1)}, u32[]{:S(2)}, u32[]{:S(2)}) collective-permute-start(f32[192,256]{1,0:T(8,128)S(1)} %get-tuple-element.143.refs_2_), channel_id=1, source_target_pairs={{0,12},{4,8},{8,4},{12,0},{1,13},{5,9},{9,5},{13,1},{2,14},{6,10},... | collective-permute-start | bytes 589832 | tf_op jit(solution)/shard_map/ppermute | solution.py:328
  148.9 23.2 %copy-start.12 = (s32[768,1]{1,0:T(8,128)S(1)}, s32[768,1]{1,0:T(8,128)}, u32[]{:S(2)}) copy-start(s32[768,1]{1,0:T(8,128)} %get-tuple-element.123) | copy-start | bytes 9220
  148.9 23.2 %copy-start.14 = (s32[96,1]{1,0:T(8,128)S(1)}, s32[96,1]{1,0:T(8,128)}, u32[]{:S(2)}) copy-start(s32[96,1]{1,0:T(8,128)} %get-tuple-element.155) | copy-start | bytes 1156
  148.9 23.2 %copy-start.17 = (s32[18]{0:T(128)S(1)}, s32[18]{0:T(128)}, u32[]{:S(2)}) copy-start(s32[18]{0:T(128)} %copy-done.16) | copy-start | bytes 220
  148.9 23.2 %copy-start.18 = (bf16[48,2048]{1,0:T(8,128)(2,1)S(1)}, bf16[48,2048]{1,0:T(8,128)(2,1)}, u32[]{:S(2)}) copy-start(bf16[48,2048]{1,0:T(8,128)(2,1)} %get-tuple-element.153) | copy-start | bytes 589828
  148.9 23.2 %copy-start.19 = (bf16[48,2048]{1,0:T(8,128)(2,1)S(1)}, bf16[48,2048]{1,0:T(8,128)(2,1)}, u32[]{:S(2)}) copy-start(bf16[48,2048]{1,0:T(8,128)(2,1)} %get-tuple-element.154) | copy-start | bytes 589828
  151.9 1.3 collective-permute-start.27
  153.2 3.3 %collective-permute-start.29 = (f32[48,128]{1,0:T(8,128)S(1)}, f32[48,128]{1,0:T(8,128)S(1)}, u32[]{:S(2)}, u32[]{:S(2)}) collective-permute-start(f32[48,128]{1,0:T(8,128)S(1)} %get-tuple-element.150), channel_id=1, source_target_pairs={{0,3},{1,2},{2,1},{3,0},{4,7},{5,6},{6,5},{7,4},{8,11},{9,10},{10,... | collective-permute-start | bytes 73736 | tf_op jit(solution)/shard_map/ppermute | solution.py:328
  156.4 3.8 %collective-permute-start.28 = (f32[48,128]{1,0:T(8,128)S(1)}, f32[48,128]{1,0:T(8,128)S(1)}, u32[]{:S(2)}, u32[]{:S(2)}) collective-permute-start(f32[48,128]{1,0:T(8,128)S(1)} %get-tuple-element.150), channel_id=1, source_target_pairs={{0,2},{1,3},{2,0},{3,1},{4,6},{5,7},{6,4},{7,5},{8,10},{9,11},{10,... | collective-permute-start | bytes 73736 | tf_op jit(solution)/shard_map/ppermute | solution.py:328
  160.3 3.5 %collective-permute-start.10 = (s32[1,128]{1,0:T(1,128)S(1)}, s32[1,128]{1,0:T(1,128)S(1)}, u32[]{:S(2)}, u32[]{:S(2)}) collective-permute-start(s32[1,128]{1,0:T(1,128)S(1)} %get-tuple-element.122), channel_id=1, source_target_pairs={{0,16},{16,0},{1,17},{17,1},{2,18},{18,2},{3,19},{19,3},{4,20},{20... | collective-permute-start | bytes 1544 | tf_op jit(solution)/shard_map/ppermute | solution.py:328
  163.8 5.9 %collective-permute-start.30 = (f32[48,256]{1,0:T(8,128)S(1)}, f32[48,256]{1,0:T(8,128)S(1)}, u32[]{:S(2)}, u32[]{:S(2)}) collective-permute-start(f32[48,256]{1,0:T(8,128)S(1)} %get-tuple-element.151), channel_id=1, source_target_pairs={{0,12},{4,8},{8,4},{12,0},{1,13},{5,9},{9,5},{13,1},{2,14},{6,10},... | collective-permute-start | bytes 147464 | tf_op jit(solution)/shard_map/ppermute | solution.py:328
  167.0 5.0 %collective-permute-start.31 = (f32[48,256]{1,0:T(8,128)S(1)}, f32[48,256]{1,0:T(8,128)S(1)}, u32[]{:S(2)}, u32[]{:S(2)}) collective-permute-start(f32[48,256]{1,0:T(8,128)S(1)} %get-tuple-element.152), channel_id=1, source_target_pairs={{0,8},{4,12},{8,0},{12,4},{1,9},{5,13},{9,1},{13,5},{2,10},{6,14},... | collective-permute-start | bytes 147464 | tf_op jit(solution)/shard_map/ppermute | solution.py:328
  175.5 0.7 copy-start.13
Sparse Core Ops, SparseCore 0:
  42.7 42.4 reduce-scatter.1

commit v5 on v4

--- a/solution.py
+++ b/solution.py
@@ -9,14 +9,17 @@
 
 ADAPTER_RANK = 64
 TOKEN_LIMIT = 12
-VMEM_LIMIT = 48 * 1024 * 1024
+VMEM_LIMIT = 28 * 1024 * 1024
 F32 = jnp.float32
 BF16 = jnp.bfloat16
 I32 = jnp.int32
 ANYWHERE = pl.BlockSpec(memory_space=pl.ANY)
-LIGHT = pl.CostEstimate(flops=1, transcendentals=0, bytes_accessed=1)
-HEAVY = pl.CostEstimate(flops=26 * 10**9, transcendentals=0, bytes_accessed=1)
+COST = pl.CostEstimate(flops=10**9, transcendentals=0, bytes_accessed=1)
 PARAMS = pltpu.CompilerParams(vmem_limit_bytes=VMEM_LIMIT)
+
+
+def up_to_16(count):
+    return -(-count // 16) * 16
 
 
 def owner_of(ids, owners, owned):
@@ -55,7 +58,7 @@
         ],
         out_shape=[jax.ShapeDtypeStruct((1, rows), I32), jax.ShapeDtypeStruct((rows, 1), I32)],
         compiler_params=PARAMS,
-        cost_estimate=LIGHT,
+        cost_estimate=COST,
         name="route",
     )(me, ids_row)
 
@@ -94,13 +97,13 @@
         out_shape=[jax.ShapeDtypeStruct((count, width), BF16) for _, _, count in pieces],
         scratch_shapes=[pltpu.VMEM((sum(c for _, _, c in pieces), rows), BF16)],
         compiler_params=PARAMS,
-        cost_estimate=LIGHT,
+        cost_estimate=COST,
         name="sort",
     )(slot, tokens, *later_than)
 
 
 def name_kernel(owners, owned, sets, here_ref, *refs):
-    lines, outs, plan_ref, most_ref = refs[:owners], refs[owners:-2], refs[-2], refs[-1]
+    lines, outs, (ends_ref, plan_ref, most_ref) = refs[:owners], refs[owners:-3], refs[-3:]
     me, half = here_ref[0], here_ref[1]
     held = -(-owned // 8) * 8
     owner = lax.broadcasted_iota(I32, (-(-owners // 8) * 8, 1), 0)
@@ -119,6 +122,7 @@
         upto = jnp.sum(jnp.where((mine >= 0) & (mine <= adapter), 1, 0), axis=1, keepdims=True)
         across = jnp.sum(jnp.where(diagonal, upto, 0), axis=0, keepdims=True)
         ends.append(jnp.where(used, across, 1 << 20))
+        ends_ref[j : j + 1, :] = ends[j]
     most_ref[...] = jnp.broadcast_to(jnp.max(most, axis=0, keepdims=True), most_ref.shape)
     for k, (pieces, out) in enumerate(zip(sets, outs)):
         begin, low, high = 0, owned - 1, 0
@@ -137,18 +141,22 @@
 def name_rows(lines, here, owned, sets):
     totals = [sum(c for _, _, c in pieces) for pieces in sets]
     on_chip, scalars = (pl.BlockSpec(memory_space=m) for m in (pltpu.VMEM, pltpu.SMEM))
-    *names, plan, most = pl.pallas_call(
+    *names, ends, plan, most = pl.pallas_call(
         functools.partial(name_kernel, len(lines), owned, sets),
         in_specs=[scalars] + [on_chip] * len(lines),
-        out_specs=[on_chip] * len(sets) + [scalars, on_chip],
+        out_specs=[on_chip] * len(sets) + [on_chip, scalars, on_chip],
         out_shape=[jax.ShapeDtypeStruct((t, 1), I32) for t in totals]
-        + [jax.ShapeDtypeStruct((3 * len(sets),), I32), jax.ShapeDtypeStruct((1, 128), I32)],
-        compiler_params=PARAMS,
-        cost_estimate=LIGHT,
+        + [
+            jax.ShapeDtypeStruct((len(lines), 128), I32),
+            jax.ShapeDtypeStruct((3 * len(sets),), I32),
+            jax.ShapeDtypeStruct((1, 128), I32),
+        ],
+        compiler_params=PARAMS,
+        cost_estimate=COST,
         name="name_rows",
     )(here, *lines)
     plans = [plan[3 * k : 3 * k + 3] for k in range(len(sets))]
-    return names, plans, most
+    return names, ends, plans, most
 
 
 def base_kernel(tok_ref, weight_ref, _, out_ref):
@@ -169,43 +177,55 @@
         out_specs=pl.BlockSpec((rows, step), lambda i: (0, i)),
         out_shape=jax.ShapeDtypeStruct((rows, columns), F32),
         compiler_params=PARAMS,
-        cost_estimate=LIGHT,
+        cost_estimate=COST,
         name="base",
     )(tokens, weight, later_than)
 
 
-def shrink_kernel(sizes, group, fine, waits, plan_ref, which_ref, down_ref, *refs):
-    blocks, (mine_ref, other_ref, rows, acc) = refs[: len(sizes)], refs[len(sizes) + waits :]
+def shrink_kernel(pieces, group, fine, plan_ref, ends_ref, which_ref, down_ref, *refs):
+    blocks, (mine_ref, other_ref, acc) = refs[: len(pieces)], refs[-3:]
     step, rank2 = pl.program_id(0), 2 * ADAPTER_RANK
     low, high, second = plan_ref[0], plan_ref[1], plan_ref[2] == 1
     begin = (low // group + step) * group
 
     @pl.when(step == 0)
     def _():
-        at = 0
-        for size, block in zip(sizes, blocks):
-            rows[at : at + size, :] = block[...]
-            at += size
         acc[...] = jnp.zeros_like(acc)
 
     for f in range(0, group, fine):
 
         @pl.when((begin + f <= high) & (begin + f + fine > low))
         def _(f=f):
+            adapter = begin + f
+            windows, spans, at = [], [], 0
+            for (block, first, size), rows in zip(pieces, blocks):
+                span = min(up_to_16(fine * TOKEN_LIMIT + 15), size)
+                ahead = ends_ref[block, jnp.maximum(adapter - 1, 0)]
+                start = jnp.where(adapter > 0, ahead, 0) - first
+                start = jnp.minimum(jnp.maximum(start, 0), size - span) // 16 * 16
+                windows.append(rows[pl.ds(pl.multiple_of(start, 16), span), :])
+                spans.append((pl.ds(pl.multiple_of(at + start, 16), span), span))
+                at += size
             factors = down_ref[f : f + fine].reshape(fine * rank2, down_ref.shape[2])
             product = lax.dot_general(
-                rows[...], factors, (((1,), (1,)), ((), ())), preferred_element_type=F32
+                jnp.concatenate(windows, axis=0),
+                factors,
+                (((1,), (1,)), ((), ())),
+                preferred_element_type=F32,
             )
-            which = which_ref[...] - (begin + f)
-            found = acc[...]
-            for q in range(fine):
-                part = product[:, q * rank2 : (q + 1) * rank2]
-                found = found + jnp.where(which == q, part, 0.0)
-            acc[...] = found
+            at = 0
+            for here, span in spans:
+                which = which_ref[here, :] - adapter
+                found = acc[here, :]
+                for q in range(fine):
+                    part = product[at : at + span, q * rank2 : (q + 1) * rank2]
+                    found = found + jnp.where(which == q, part, 0.0)
+                acc[here, :] = found
+                at += span
 
     @pl.when(step == pl.num_programs(0) - 1)
     def _():
-        total = sum(sizes)
+        total = acc.shape[0]
         upper, lower = acc[: total // 2, :], acc[total // 2 :, :]
         keys = jnp.concatenate([upper[:, :ADAPTER_RANK], lower[:, :ADAPTER_RANK]], axis=1)
         values = jnp.concatenate([upper[:, ADAPTER_RANK:], lower[:, ADAPTER_RANK:]], axis=1)
@@ -213,35 +233,35 @@
         other_ref[...] = jnp.where(second, keys, values)
 
 
-def shrink(blocks, names, plan, down, later_than=(), cost=LIGHT):
-    sizes = tuple(b.shape[0] for b in blocks)
-    total = sum(sizes)
+def shrink(pieces, blocks, names, ends, plan, down, later_than=()):
+    total = sum(b.shape[0] for b in blocks)
     owned, rank2, width = down.shape
     group = next(g for g in (4, 3, 2, 1) if owned % g == 0)
     fine = next(g for g in (2, 3, 1) if group % g == 0)
     line = jax.ShapeDtypeStruct((total // 2, 2 * ADAPTER_RANK), F32)
     return pl.pallas_call(
-        functools.partial(shrink_kernel, sizes, group, fine, len(later_than)),
+        functools.partial(shrink_kernel, pieces, group, fine),
         grid_spec=pltpu.PrefetchScalarGridSpec(
             num_scalar_prefetch=1,
             grid=(owned // group,),
             in_specs=[
+                pl.BlockSpec(memory_space=pltpu.SMEM),
                 pl.BlockSpec((total, 1), lambda i, p: (0, 0)),
                 pl.BlockSpec(
                     (group, rank2, width),
                     lambda i, p: (jnp.minimum(p[0] // group + i, p[1] // group), 0, 0),
                 ),
             ]
-            + [pl.BlockSpec((s, width), lambda i, p: (0, 0)) for s in sizes]
+            + [pl.BlockSpec(b.shape, lambda i, p: (0, 0)) for b in blocks]
             + [ANYWHERE] * len(later_than),
             out_specs=[pl.BlockSpec((total // 2, rank2), lambda i, p: (0, 0))] * 2,
-            scratch_shapes=[pltpu.VMEM((total, width), BF16), pltpu.VMEM((total, rank2), F32)],
+            scratch_shapes=[pltpu.VMEM((total, rank2), F32)],
         ),
         out_shape=[line, line],
         compiler_params=PARAMS,
-        cost_estimate=cost,
+        cost_estimate=COST,
         name="shrink",
-    )(plan, names, down, *blocks, *later_than)
+    )(plan, ends, names, down, *blocks, *later_than)
 
 
 def split(x, terms):
@@ -288,7 +308,7 @@
         functools.partial(expand_kernel, groups, sizes, len(lines)),
         out_shape=[jax.ShapeDtypeStruct((s, columns), F32) for s in sizes],
         compiler_params=PARAMS,
-        cost_estimate=LIGHT,
+        cost_estimate=COST,
         name="expand",
     )(names, scale, up, *lines)
 
@@ -319,17 +339,13 @@
         functools.partial(merge_kernel, tuple(begins), len(parts)),
         out_shape=jax.ShapeDtypeStruct(parts[0].shape, kind),
         compiler_params=PARAMS,
-        cost_estimate=LIGHT,
+        cost_estimate=COST,
         name="merge",
     )(target, *parts, *blocks)
 
 
 def swap(x, axes, size, distance):
     return lax.ppermute(x, axes, [(i, i ^ distance) for i in range(size)])
-
-
-def up_to_16(count):
-    return -(-count // 16) * 16
 
 
 def local(
@@ -349,47 +365,45 @@
     half = (lax.axis_index(feature_axes) >= sharers // 2).astype(I32)
     cap = up_to_16(owned * TOKEN_LIMIT)
 
-    own = (0, 0, cap)
+    own, near = (0, 0, cap), (1, 0, cap)
     if owners == 4:
         usual = up_to_16(cap * 5 // 6)
         most = up_to_16(usual * 4 // 5)
-        near = (1, 0, up_to_16(cap // 3))
-        far = [
-            [(3, 0, most), (2, 0, most), (1, near[2], cap - near[2])],
-            [(3, most, usual - most), (2, most, usual - most)],
-        ]
+        far = [[(3, 0, most), (2, 0, most)], [(3, most, usual - most), (2, most, usual - most)]]
         extra = [(3, usual, cap - usual), (2, usual, cap - usual)]
     else:
-        usual, near, far = cap, (1, 0, cap), [[(j, 0, cap) for j in range(2, owners)]]
-        extra = []
+        usual, far, extra = cap, [[(j, 0, cap) for j in range(2, owners)]], []
 
     ids_row = token_adapter_index.reshape(1, rows)
     ids_heard = [ids_row] + [swap(ids_row, "dp", owners, j) for j in range(1, owners)]
     slot, target = route(ids_row, me.reshape(1), owners, owned, cap)
-    sent = [near] + [p for s in far for p in s]
+    sent = [p for s in far for p in s] + [near]
     packed = dict(zip(sent, sort_rows(tokens, slot, cap, sent, tuple(ids_heard[1:]))))
     received = {p: swap(packed[p], "dp", owners, p[0]) for p in sent}
-    packed |= zip([own] + extra, sort_rows(tokens, slot, cap, [own] + extra, (received[near],)))
 
     sets = [[own], [near], [own, near]] + far + ([extra] if extra else [])
     here = jnp.stack([me.astype(I32), half])
-    names, plans, largest = name_rows(ids_heard, here, owned, sets)
+    names, ends, plans, largest = name_rows(ids_heard, here, owned, sets)
 
     if owned % 2:
         adapter_up_weight = jnp.pad(adapter_up_weight, ((0, 1), (0, 0), (0, 0)))
     up = adapter_up_weight.reshape(-1, adapter_up_weight.shape[2])
     scale = adapter_scale.reshape(1, owned)
 
-    def exchange(mine, other):
+    def exchange(mine, other, steps=2):
+        if sharers == 4 and steps == 2:
+            mine = mine + swap(other, "tensor", 2, 1)
+            return [mine, swap(mine, "sub", 2, 1)]
         return [mine] + [
             swap(mine if d < sharers // 2 else other, feature_axes, sharers, d)
             for d in range(1, sharers)
         ]
 
-    def deltas_of(blocks, names, plan, down, up, scale, later_than, cost=LIGHT):
-        mine, other = shrink(blocks, names, plan, down, later_than, cost)
+    def deltas_of(pieces, blocks, names, ends, plan, down, up, scale, later_than, steps=2):
+        mine, other = shrink(pieces, blocks, names, ends, plan, down, later_than)
         sizes = tuple(b.shape[0] for b in blocks)
-        return expand(exchange(mine, other), (mine.shape[0],), names, scale, up, sizes)
+        lines = exchange(mine, other, steps)
+        return expand(lines, (mine.shape[0],), names, scale, up, sizes)
 
     def send_back(pieces, deltas):
         return [swap(d, "dp", owners, p[0]) for p, d in zip(pieces, deltas)]
@@ -398,19 +412,23 @@
         return [b * cap + f for b, f, _ in pieces]
 
     weights = (adapter_down_weight, up, scale)
-    base_part = base_product(tokens, key_value_weight, received[near])
+    base_part = base_product(tokens, key_value_weight, packed[near])
     base = lax.psum_scatter(base_part, feature_axes, scatter_dimension=1, tiled=True)
-    first = shrink([packed[own]], names[0], plans[0], adapter_down_weight, (base_part,))
-    second = shrink([received[near]], names[1], plans[1], adapter_down_weight, tuple(first[:1]))
-    lines = exchange(*(jnp.concatenate(pair, axis=0) for pair in zip(first, second)))
-    sizes = (cap, near[2])
-    deltas = expand(lines, tuple(c // 2 for c in sizes), names[2], scale, up, sizes)
+    packed |= zip([own] + extra, sort_rows(tokens, slot, cap, [own] + extra, (base_part,)))
+    down = adapter_down_weight
+    first = shrink([own], [packed[own]], names[0], ends, plans[0], down)
+    second = shrink(
+        [near], [received[near]], names[1], ends, plans[1], down, tuple(first[:1])
+    )
+    lines = exchange(*(jnp.concatenate(pair, axis=0) for pair in zip(first, second)), steps=1)
+    deltas = expand(lines, (cap // 2, cap // 2), names[2], scale, up, (cap, cap))
     returned = [deltas[0]] + send_back([near], deltas[1:])
     done = [own, near]
     for k, pieces in enumerate(far):
         blocks = [received[p] for p in pieces]
-        cost = HEAVY if k and pieces is far[-1] else LIGHT
-        deltas = deltas_of(blocks, names[3 + k], plans[3 + k], *weights, (deltas[0],), cost)
+        deltas = deltas_of(
+            pieces, blocks, names[3 + k], ends, plans[3 + k], *weights, (deltas[0],), 1 + (pieces is far[-1])
+        )
         returned += send_back(pieces, deltas)
         done += pieces
 
@@ -420,9 +438,10 @@
     if not extra:
         return finish(base, target, returned)
 
-    def finish_with_extra(base, target, returned, blocks, names, plan, weights):
+    def finish_with_extra(base, target, returned, blocks, names, ends, plan, weights):
         blocks = send_back(extra, blocks)
-        deltas = send_back(extra, deltas_of(blocks, names, plan, *weights, ()))
+        deltas = deltas_of(extra, blocks, names, ends, plan, *weights, ())
+        deltas = send_back(extra, deltas)
         return merge([base], target, begins(done + extra), returned + deltas, BF16)
 
     for d in range(1, lax.axis_size("parts")):
@@ -436,6 +455,7 @@
         returned,
         [packed[p] for p in extra],
         names[-1],
+        ends,
         plans[-1],
         weights,
     )

time: 184 us -> 160 us (0.87)
  Pallas kernels: 57.6 us -> 48.8 us
  starting transfers between devices: 31.6 us -> 24.9 us
  waiting for transfers between devices: 73.6 us -> 67.5 us
  local copies, waits for them, and re-layouts: 6.32 us -> 4.47 us
    ppermute x25 -> x22, starting transfers between devices: 31.6 us -> 24.9 us  [swap(): return lax.ppermute(x, axes, [(i, i ^ distance) for i in range(size)])]
    ppermute x25 -> x22, waiting for transfers between devices: 73.6 us -> 67.5 us  [swap(): return lax.ppermute(x, axes, [(i, i ^ distance) for i in range(size)])]
    pallas_call x4, Pallas kernels: 31.8 us -> 26.6 us  [shrink(): pl.pallas_call(functools.partial(shrink_kernel, pieces, group, fine), gri...]
    pallas_call x1, Pallas kernels: 7.75 us -> 5.51 us  [base_product(): pl.pallas_call(base_kernel, grid=(columns // step,), in_specs=[pl.BlockSp...]
    unnamed x40 -> x34, local copies, waits for them, and re-layouts: 6.24 us -> 4.38 us
  transfers between devices with their start and end apart: 26 -> 23, of which waited for: 13 -> 9; matrix products, arithmetic and copies ran while one was open for 0% -> 0% of each run, Pallas kernels for 23% -> 23%
where the time goes in v5:
time: 160 us
  waiting for transfers between devices  67.5 us (42%)
  Pallas kernels  48.8 us (30%)
  starting transfers between devices  24.9 us (16%)
  between operations  13.7 us (9%)
  local copies, waits for them, and re-layouts  4.47 us (3%)
    ppermute x22, waiting for transfers between devices, swap(): return lax.ppermute(x, axes, [(i, i ^ distance) for i in range(size)])  67.5 us
    pallas_call x4, Pallas kernels, shrink(): pl.pallas_call(functools.partial(shrink_kernel, pieces, group, fine), gri...  26.6 us
    ppermute x22, starting transfers between devices, swap(): return lax.ppermute(x, axes, [(i, i ^ distance) for i in range(size)])  24.9 us
    pallas_call x2, Pallas kernels, sort_rows(): pl.pallas_call(functools.partial(sort_kernel, cap, pieces, len(later_than...  6.86 us
    pallas_call x1, Pallas kernels, base_product(): pl.pallas_call(base_kernel, grid=(columns // step,), in_specs=[pl.BlockSp...  5.51 us
    unnamed x34, local copies, waits for them, and re-layouts  4.38 us
    pallas_call x3, Pallas kernels, expand(): pl.pallas_call(functools.partial(expand_kernel, groups, sizes, len(lines)...  3.41 us
  transfers between devices with their start and end apart: 23, of which 9 were waited for; matrix products, arithmetic and copies ran while one was open for 0% of the time, Pallas kernels for 23%

profile of v5, /device:TPU:0, one launch (start us, length us, event | category | flops | bytes accessed | tf_op | source)
XLA Modules:
  0.0 159.7 jit_solution(10057649929015879654)
XLA Ops:
  6.5 3.0 %collective-permute-start.6 = (s32[1,768]{1,0:T(1,128)}, s32[1,768]{1,0:T(1,128)S(1)}, u32[]{:S(2)}, u32[]{:S(2)}) collective-permute-start(s32[1,768]{1,0:T(1,128)} %bitcast.7), channel_id=1, source_target_pairs={{0,4},{4,0},{8,12},{12,8},{1,5},{5,1},{9,13},{13,9},{2,6},{6,2},{1... | collective-permute-start | bytes 9224 | tf_op jit(solution)/shard_map/ppermute | solution.py:348
  9.6 2.6 %collective-permute-start.7 = (s32[1,768]{1,0:T(1,128)}, s32[1,768]{1,0:T(1,128)S(1)}, u32[]{:S(2)}, u32[]{:S(2)}) collective-permute-start(s32[1,768]{1,0:T(1,128)} %bitcast.8), channel_id=1, source_target_pairs={{0,8},{4,12},{8,0},{12,4},{1,9},{5,13},{9,1},{13,5},{2,10},{6,14},... | collective-permute-start | bytes 9224 | tf_op jit(solution)/shard_map/ppermute | solution.py:348
  12.2 0.0 collective-permute-start.8
  12.2 0.7 copy-done.5
  12.9 1.6 %route.1 = (s32[1,768]{1,0:T(1,128)S(1)}, s32[768,1]{1,0:T(8,128)}) custom-call(s32[1]{0:T(128)} %bitcast.me_ref, s32[1,768]{1,0:T(1,128)S(1)} %bitcast.10), custom_call_target="tpu_custom_call" | custom-call | flops 1000000000 | bytes 1 | tf_op jit(solution)/shard_map/route/pallas_call | solution.py:53
  14.5 0.0 collective-permute-done.6.refs_1_.refs_0_
  14.5 0.0 collective-permute-done.7.refs_2_.refs_1_
  14.5 3.2 %collective-permute-done.8.refs_3_.refs_2_ = s32[1,768]{1,0:T(1,128)S(1)} collective-permute-done((s32[1,768]{1,0:T(1,128)}, s32[1,768]{1,0:T(1,128)S(1)}, u32[]{:S(2)}, u32[]{:S(2)}) %collective-permute-start.8) | collective-permute-done | bytes 3104 | tf_op jit(solution)/shard_map/ppermute | solution.py:348
  17.8 3.8 %sort.2 = (bf16[192,2048]{1,0:T(8,128)(2,1)S(1)}, bf16[192,2048]{1,0:T(8,128)(2,1)S(1)}, bf16[48,2048]{1,0:T(8,128)(2,1)S(1)}, bf16[48,2048]{1,0:T(8,128)(2,1)S(1)}, bf16[288,2048]{1,0:T(8,128)(2,1)S(1)}) custom-call(s32[1,768]{1,0:T(1,128)S(1)} %get-tuple-element.120.slot_ref, bf16[768,2048]{1,0:T(8,128)(2,1)S(1)} %copy-done, ...), custom_call_target="tpu_custom_call" | custom-call | flops 1000000000 | bytes 1 | tf_op jit(solution)/shard_map/sort/pallas_call | solution.py:88
  21.6 0.9 copy-done.3
  22.4 0.9 copy-done.4
  23.4 5.5 %base.1.refs_0_ = f32[768,1024]{1,0:T(8,128)} custom-call(bf16[768,2048]{1,0:T(8,128)(2,1)S(1)} %copy-done, bf16[2048,1024]{1,0:T(8,128)(2,1)S(1)} %copy-done.1, bf16[288,2048]{1,0:T(8,128)(2,1)S(1)} %get-tuple-element.121._), custom_call_target="tpu_custom_call" | custom-call | flops 1000000000 | bytes 1 | tf_op jit(solution)/shard_map/base/pallas_call | solution.py:169
  28.9 1.0 copy-done.2
  29.9 0.0 reduce-scatter.2.cloned.1.call-update
  29.9 0.1 collective-permute-start.10
  30.0 0.1 pad_add_fusion.here_ref
  30.1 0.6 collective-permute-start.15
  30.7 2.9 %collective-permute-start.16 = (bf16[192,2048]{1,0:T(8,128)(2,1)}, bf16[192,2048]{1,0:T(8,128)(2,1)S(1)}, u32[]{:S(2)}, u32[]{:S(2)}) collective-permute-start(bf16[192,2048]{1,0:T(8,128)(2,1)} %copy-done.3), channel_id=1, source_target_pairs={{0,8},{4,12},{8,0},{12,4},{1,9},{5,13},{9,1},{13,5},{2,10},{6,14},... | collective-permute-start | bytes 2359304 | tf_op jit(solution)/shard_map/ppermute | solution.py:348
  33.6 3.1 %sort.3 = (bf16[288,2048]{1,0:T(8,128)(2,1)S(1)}, bf16[48,2048]{1,0:T(8,128)(2,1)}, bf16[48,2048]{1,0:T(8,128)(2,1)}) custom-call(s32[1,768]{1,0:T(1,128)S(1)} %get-tuple-element.120.slot_ref, bf16[768,2048]{1,0:T(8,128)(2,1)S(1)} %copy-done, f32[768,1024]{1,0:T(8,128)} %base.1.refs_0_), custom_call_target="tpu_custom_call" | custom-call | flops 1000000000 | bytes 1 | tf_op jit(solution)/shard_map/sort/pallas_call | solution.py:88
  36.6 1.7 %name_rows.1 = (s32[288,1]{1,0:T(8,128)S(1)}, s32[288,1]{1,0:T(8,128)S(1)}, s32[576,1]{1,0:T(8,128)S(1)}, s32[384,1]{1,0:T(8,128)S(1)}, s32[96,1]{1,0:T(8,128)S(...) custom-call(s32[2]{0:T(128)S(1)} %pad_add_fusion.here_ref, ...), custom_call_target="tpu_custom_call" | custom-call | flops 1000000000 | bytes 1 | tf_op jit(solution)/shard_map/name_rows/pallas_call | solution.py:144
  38.4 0.1 fusion
  38.4 10.1 %shrink.6 = (f32[144,128]{1,0:T(8,128)S(1)}, f32[144,128]{1,0:T(8,128)S(1)}) custom-call(s32[3]{0:T(128)S(1)} %get-tuple-element.155.plan_ref, s32[4,128]{1,0:T(4,128)S(1)} %get-tuple-element.124.ends_ref, s32[288,1]{1,0:T(8,128)S(1)} %get-tuple-element.125.which_ref, bf16[24,128,2048]{2,1,0:T(8,128)(2,1)} %down_ref.7, ...), custom_call_target="tpu_custom_call" | custom-call | flops 1000000000 | bytes 1 | tf_op jit(solution)/shard_map/shrink/pallas_call | solution.py:242
  48.6 31.5 %collective-permute-done.10.refs_0_ = bf16[288,2048]{1,0:T(8,128)(2,1)} collective-permute-done((bf16[288,2048]{1,0:T(8,128)(2,1)}, bf16[288,2048]{1,0:T(8,128)(2,1)}, u32[]{:S(2)}, u32[]{:S(2)}) %collective-permute-start.10) | collective-permute-done | bytes 1179680 | tf_op jit(solution)/shard_map/ppermute | solution.py:348
  80.1 0.0 copy-start.7
  80.1 0.0 copy-start.11
  80.1 7.4 %shrink.7 = (f32[144,128]{1,0:T(8,128)S(1)}, f32[144,128]{1,0:T(8,128)S(1)}) custom-call(s32[3]{0:T(128)S(1)} %get-tuple-element.154.plan_ref, s32[4,128]{1,0:T(4,128)S(1)} %get-tuple-element.124.ends_ref, s32[288,1]{1,0:T(8,128)S(1)} %get-tuple-element.128.which_ref, bf16[24,128,2048]{2,1,0:T(8,128)(2,1)S(1)} %bitcast.13, ...), custom_call_target="tpu_custom_call" | custom-call | flops 1000000000 | bytes 1 | tf_op jit(solution)/shard_map/shrink/pallas_call | solution.py:242
  87.6 1.6 collective-permute-start.12
  89.1 0.0 collective-permute-start.13
  89.1 0.6 collective-permute-start.11
  89.8 3.7 %collective-permute-done.12.refs_2_ = f32[288,128]{1,0:T(8,128)S(1)} collective-permute-done((f32[288,128]{1,0:T(8,128)S(1)}, f32[288,128]{1,0:T(8,128)S(1)}, u32[]{:S(2)}, u32[]{:S(2)}) %collective-permute-start.12) | collective-permute-done | bytes 147488 | tf_op jit(solution)/shard_map/ppermute | solution.py:348
  93.4 2.4 %collective-permute-start.22 = (bf16[48,2048]{1,0:T(8,128)(2,1)S(1)}, bf16[48,2048]{1,0:T(8,128)(2,1)S(1)}, u32[]{:S(2)}, u32[]{:S(2)}) collective-permute-start(bf16[48,2048]{1,0:T(8,128)(2,1)S(1)} %get-tuple-element.142), channel_id=1, source_target_pairs={{0,12},{4,8},{8,4},{12,0},{1,13},{5,9},{9,5},{13,1},{2,14},{6,10},... | collective-permute-start | bytes 589832 | tf_op jit(solution)/shard_map/ppermute | solution.py:348
  95.8 0.0 collective-permute-done.13.refs_3_
  95.8 0.0 collective-permute-start.23
  95.8 0.0 collective-permute-done.11.refs_1_
  95.9 1.7 %expand.5 = (f32[288,256]{1,0:T(8,128)S(1)}, f32[288,256]{1,0:T(8,128)S(1)}) custom-call(s32[576,1]{1,0:T(8,128)S(1)} %get-tuple-element.122.which_ref, f32[1,24]{1,0:T(1,128)S(1)} %bitcast.18, bf16[1536,256]{1,0:T(8,128)(2,1)S(1)} %bitcast.14, f32[288,128]{1,0:T(8,128)S(1)} %constant_dynamic-update-slice_fusion.refs_0_, ...), custom_call_target="tpu_custom_call" | custom-call | flops 1000000000 | bytes 1 | tf_op jit(solution)/shard_map/expand/pallas_call | solution.py:307
  97.5 0.0 collective-permute-done.15.refs_0_
  97.5 13.7 %collective-permute-done.16.refs_1_ = bf16[192,2048]{1,0:T(8,128)(2,1)S(1)} collective-permute-done((bf16[192,2048]{1,0:T(8,128)(2,1)}, bf16[192,2048]{1,0:T(8,128)(2,1)S(1)}, u32[]{:S(2)}, u32[]{:S(2)}) %collective-permute-start.16) | collective-permute-done | bytes 786464 | tf_op jit(solution)/shard_map/ppermute | solution.py:348
  111.2 7.1 %shrink.8 = (f32[192,128]{1,0:T(8,128)S(1)}, f32[192,128]{1,0:T(8,128)S(1)}) custom-call(s32[3]{0:T(128)S(1)} %get-tuple-element.153.plan_ref, s32[4,128]{1,0:T(4,128)S(1)} %get-tuple-element.124.ends_ref, s32[384,1]{1,0:T(8,128)S(1)} %get-tuple-element.134.which_ref, bf16[24,128,2048]{2,1,0:T(8,128)(2,1)S(1)} %bitcast.13, ...), custom_call_target="tpu_custom_call" | custom-call | flops 1000000000 | bytes 1 | tf_op jit(solution)/shard_map/shrink/pallas_call | solution.py:242
  118.3 0.1 collective-permute-start.17
  118.4 1.6 collective-permute-start.18
  120.0 0.3 collective-permute-start.19
  120.3 0.0 collective-permute-done.17.refs_1_
  120.3 0.0 collective-permute-start.14
  120.3 3.8 %collective-permute-done.18.refs_2_ = f32[192,128]{1,0:T(8,128)S(1)} collective-permute-done((f32[192,128]{1,0:T(8,128)S(1)}, f32[192,128]{1,0:T(8,128)S(1)}, u32[]{:S(2)}, u32[]{:S(2)}) %collective-permute-start.18) | collective-permute-done | bytes 98336 | tf_op jit(solution)/shard_map/ppermute | solution.py:348
  124.1 1.2 collective-permute-done.19.refs_3_
  125.3 1.2 expand.6
  126.5 1.0 collective-permute-start.20
  127.4 2.0 %shrink.9 = (f32[48,128]{1,0:T(8,128)S(1)}, f32[48,128]{1,0:T(8,128)S(1)}) custom-call(s32[3]{0:T(128)S(1)} %get-tuple-element.152.plan_ref, s32[4,128]{1,0:T(4,128)S(1)} %get-tuple-element.124.ends_ref, s32[96,1]{1,0:T(8,128)S(1)} %get-tuple-element.141.which_ref, bf16[24,128,2048]{2,1,0:T(8,128)(2,1)S(1)} %bitcast.13, ...), custom_call_target="tpu_custom_call" | custom-call | flops 1000000000 | bytes 1 | tf_op jit(solution)/shard_map/shrink/pallas_call | solution.py:242
  129.4 0.0 copy-start.13
  129.4 1.6 collective-permute-start.24
  131.0 2.3 %collective-permute-done.24 = f32[48,128]{1,0:T(8,128)S(1)} collective-permute-done((f32[48,128]{1,0:T(8,128)S(1)}, f32[48,128]{1,0:T(8,128)S(1)}, u32[]{:S(2)}, u32[]{:S(2)}) %collective-permute-start.24) | collective-permute-done | bytes 24608 | tf_op jit(solution)/shard_map/ppermute | solution.py:348
  133.3 1.6 collective-permute-start.9
  134.9 0.6 expand.7
  135.5 3.5 %collective-permute-start.26 = (f32[48,256]{1,0:T(8,128)S(1)}, f32[48,256]{1,0:T(8,128)S(1)}, u32[]{:S(2)}, u32[]{:S(2)}) collective-permute-start(f32[48,256]{1,0:T(8,128)S(1)} %get-tuple-element.146), channel_id=1, source_target_pairs={{0,12},{4,8},{8,4},{12,0},{1,13},{5,9},{9,5},{13,1},{2,14},{6,10},... | collective-permute-start | bytes 147464 | tf_op jit(solution)/shard_map/ppermute | solution.py:348
  138.9 0.0 collective-permute-done.9
  138.9 1.6 %collective-permute-start.27 = (f32[48,256]{1,0:T(8,128)S(1)}, f32[48,256]{1,0:T(8,128)S(1)}, u32[]{:S(2)}, u32[]{:S(2)}) collective-permute-start(f32[48,256]{1,0:T(8,128)S(1)} %get-tuple-element.147), channel_id=1, source_target_pairs={{0,8},{4,12},{8,0},{12,4},{1,9},{5,13},{9,1},{13,5},{2,10},{6,14},... | collective-permute-start | bytes 147464 | tf_op jit(solution)/shard_map/ppermute | solution.py:348
  140.6 0.8 collective-permute-done.26
  141.4 7.2 %collective-permute-done.27 = f32[48,256]{1,0:T(8,128)S(1)} collective-permute-done((f32[48,256]{1,0:T(8,128)S(1)}, f32[48,256]{1,0:T(8,128)S(1)}, u32[]{:S(2)}, u32[]{:S(2)}) %collective-permute-start.27) | collective-permute-done | bytes 49184 | tf_op jit(solution)/shard_map/ppermute | solution.py:348
  148.7 0.0 collective-permute-done.21
  148.7 0.0 reduce-scatter.2.cloned.1.call-done
  148.7 3.4 %conditional.1 = (bf16[768,256]{1,0:T(8,128)(2,1)S(1)}) conditional(s32[]{:T(128)} %bitcast.3, (s32[768,1]{1,0:T(8,128)S(1)}, f32[768,256]{1,0:T(8,128)}, f32[288,256]{1,0:T(8,128)S(1)}, f32[288,256]{1,0:T(8,128)S(1)}, f32[192,256]{1,0:T(8,128)S(1)}, /*index=5*/f32[192,256]{1,0:T(8,128)S(1)}, f32[48,256]{1,0:T(8,128)S(1)}, ...), branch_computations={%region_1.0_spmd, %region_2.0_spmd} | conditional | flops 3000006144 | bytes 5407079 | solution.py:449
  148.9 3.2 %merge.2 = bf16[768,256]{1,0:T(8,128)(2,1)S(1)} custom-call(s32[768,1]{1,0:T(8,128)S(1)} %get-tuple-element.57.target_ref, f32[768,256]{1,0:T(8,128)} %get-tuple-element.58.refs_0_, f32[288,256]{1,0:T(8,128)S(1)} %get-tuple-element.59.refs_1_, f32[288,256]{1,0:T(8,128)S(1)} %get-tuple-element.60.refs_2_, f32[192,256]{1,0:T(8,128)S(1)} %get-tuple-element.61.refs_3_, ...), custom_call_target="tpu_custom_call" | custom-call | flops 1000000000 | bytes 1 | tf_op jit(solution)/shard_map/cond/branch_0_fun/merge/pallas_call | solution.py:338
  152.1 0.0 copy-start.12
  152.1 0.7 copy-done.12
  (38 shorter events, 0.1 us)
Async XLA Ops:
  6.5 11.2 %copy-start = (bf16[768,2048]{1,0:T(8,128)(2,1)S(1)}, bf16[768,2048]{1,0:T(8,128)(2,1)}, u32[]{:S(2)}) copy-start(bf16[768,2048]{1,0:T(8,128)(2,1)} %tok_ref.5) | copy-start | bytes 9437188
  6.5 142.2 %reduce-scatter.2.cloned.1.call-start = ((), (), s32[]{:S(2)}) async-start(), calls=%async_computation.1 | async-start | bytes 3932160 | tf_op jit(solution)/shard_map/reduce_scatter | solution.py:416
  6.5 8.0 %collective-permute-start.6 = (s32[1,768]{1,0:T(1,128)}, s32[1,768]{1,0:T(1,128)S(1)}, u32[]{:S(2)}, u32[]{:S(2)}) collective-permute-start(s32[1,768]{1,0:T(1,128)} %bitcast.7), channel_id=1, source_target_pairs={{0,4},{4,0},{8,12},{12,8},{1,5},{5,1},{9,13},{13,9},{2,6},{6,2},{1... | collective-permute-start | bytes 9224 | tf_op jit(solution)/shard_map/ppermute | solution.py:348
  9.6 5.0 %collective-permute-start.7 = (s32[1,768]{1,0:T(1,128)}, s32[1,768]{1,0:T(1,128)S(1)}, u32[]{:S(2)}, u32[]{:S(2)}) collective-permute-start(s32[1,768]{1,0:T(1,128)} %bitcast.8), channel_id=1, source_target_pairs={{0,8},{4,12},{8,0},{12,4},{1,9},{5,13},{9,1},{13,5},{2,10},{6,14},... | collective-permute-start | bytes 9224 | tf_op jit(solution)/shard_map/ppermute | solution.py:348
  12.2 5.6 %collective-permute-start.8 = (s32[1,768]{1,0:T(1,128)}, s32[1,768]{1,0:T(1,128)S(1)}, u32[]{:S(2)}, u32[]{:S(2)}) collective-permute-start(s32[1,768]{1,0:T(1,128)} %bitcast.9), channel_id=1, source_target_pairs={{0,12},{4,8},{8,4},{12,0},{1,13},{5,9},{9,5},{13,1},{2,14},{6,10},... | collective-permute-start | bytes 9224 | tf_op jit(solution)/shard_map/ppermute | solution.py:348
  12.2 0.8 copy-start.5
  12.9 10.5 %copy-start.1 = (bf16[2048,1024]{1,0:T(8,128)(2,1)S(1)}, bf16[2048,1024]{1,0:T(8,128)(2,1)}, u32[]{:S(2)}) copy-start(bf16[2048,1024]{1,0:T(8,128)(2,1)} %weight_ref.1) | copy-start | bytes 12582916
  21.5 0.9 copy-start.3
  22.4 0.9 copy-start.4
  28.9 1.0 copy-start.2
  29.9 50.2 %collective-permute-start.10 = (bf16[288,2048]{1,0:T(8,128)(2,1)}, bf16[288,2048]{1,0:T(8,128)(2,1)}, u32[]{:S(2)}, u32[]{:S(2)}) collective-permute-start(bf16[288,2048]{1,0:T(8,128)(2,1)} %copy-done.2), channel_id=1, source_target_pairs={{0,4},{4,0},{8,12},{12,8},{1,5},{5,1},{9,13},{13,9},{2,6},{6,2},{1... | collective-permute-start | bytes 3538952 | tf_op jit(solution)/shard_map/ppermute | solution.py:348
  30.1 67.4 %collective-permute-start.15 = (bf16[192,2048]{1,0:T(8,128)(2,1)}, bf16[192,2048]{1,0:T(8,128)(2,1)S(1)}, u32[]{:S(2)}, u32[]{:S(2)}) collective-permute-start(bf16[192,2048]{1,0:T(8,128)(2,1)} %copy-done.4), channel_id=1, source_target_pairs={{0,12},{4,8},{8,4},{12,0},{1,13},{5,9},{9,5},{13,1},{2,14},{6,10},... | collective-permute-start | bytes 2359304 | tf_op jit(solution)/shard_map/ppermute | solution.py:348
  30.7 5.9 %copy-start.6 = (s32[768,1]{0,1:T(1,128)S(1)}, s32[768,1]{0,1:T(1,128)}, u32[]{:S(2)}) copy-start(s32[768,1]{0,1:T(1,128)} %param.13) | copy-start | bytes 9220
  30.7 80.6 %collective-permute-start.16 = (bf16[192,2048]{1,0:T(8,128)(2,1)}, bf16[192,2048]{1,0:T(8,128)(2,1)S(1)}, u32[]{:S(2)}, u32[]{:S(2)}) collective-permute-start(bf16[192,2048]{1,0:T(8,128)(2,1)} %copy-done.3), channel_id=1, source_target_pairs={{0,8},{4,12},{8,0},{12,4},{1,9},{5,13},{9,1},{13,5},{2,10},{6,14},... | collective-permute-start | bytes 2359304 | tf_op jit(solution)/shard_map/ppermute | solution.py:348
  33.6 46.5 %slice-start = ((s8[12582912]{0:T(1024)(128)(4,1)}), s8[4194304]{0:T(1024)(128)(4,1)S(1)}, s32[]{:S(2)}) async-start(s8[12582912]{0:T(1024)(128)(4,1)} %bitcast.12), calls=%async_computation.2 | async-start | bytes 8388608
  36.6 43.5 %slice-start.1 = ((s8[12582912]{0:T(1024)(128)(4,1)}), s8[4194304]{0:T(1024)(128)(4,1)S(1)}, s32[]{:S(2)}) async-start(s8[12582912]{0:T(1024)(128)(4,1)} %bitcast.12), calls=%async_computation.3 | async-start | bytes 8388608
  38.4 41.7 %slice-start.2 = ((s8[12582912]{0:T(1024)(128)(4,1)}), s8[4194304]{0:T(1024)(128)(4,1)S(1)}, s32[]{:S(2)}) async-start(s8[12582912]{0:T(1024)(128)(4,1)} %bitcast.12), calls=%async_computation.4 | async-start | bytes 8388608
  80.1 15.7 %copy-start.7 = (bf16[24,64,256]{2,1,0:T(8,128)(2,1)S(1)}, bf16[24,64,256]{2,1,0:T(8,128)(2,1)}, u32[]{:S(2)}) copy-start(bf16[24,64,256]{2,1,0:T(8,128)(2,1)} %param.11) | copy-start | bytes 2359300
  80.1 15.7 %copy-start.11 = (f32[24]{0:T(128)S(1)}, f32[24]{0:T(128)}, u32[]{:S(2)}) copy-start(f32[24]{0:T(128)} %param.12) | copy-start | bytes 292
  87.6 5.9 %collective-permute-start.12 = (f32[288,128]{1,0:T(8,128)S(1)}, f32[288,128]{1,0:T(8,128)S(1)}, u32[]{:S(2)}, u32[]{:S(2)}) collective-permute-start(f32[288,128]{1,0:T(8,128)S(1)} %constant_dynamic-update-slice_fusion.2), channel_id=1, source_target_pairs={{0,2},{1,3},{2,0},{3,1},{4,6},{5,7},{6,4},{7,5},{8,10},{9,11},{10,... | collective-permute-start | bytes 442376 | tf_op jit(solution)/shard_map/ppermute | solution.py:348
  89.1 6.7 %collective-permute-start.13 = (f32[288,128]{1,0:T(8,128)S(1)}, f32[288,128]{1,0:T(8,128)S(1)}, u32[]{:S(2)}, u32[]{:S(2)}) collective-permute-start(f32[288,128]{1,0:T(8,128)S(1)} %constant_dynamic-update-slice_fusion.2), channel_id=1, source_target_pairs={{0,3},{1,2},{2,1},{3,0},{4,7},{5,6},{6,5},{7,4},{8,11},{9,10},{10,... | collective-permute-start | bytes 442376 | tf_op jit(solution)/shard_map/ppermute | solution.py:348
  89.1 6.7 %collective-permute-start.11 = (f32[288,128]{1,0:T(8,128)S(1)}, f32[288,128]{1,0:T(8,128)S(1)}, u32[]{:S(2)}, u32[]{:S(2)}) collective-permute-start(f32[288,128]{1,0:T(8,128)S(1)} %constant_dynamic-update-slice_fusion.refs_0_), channel_id=1, source_target_pairs={{0,1},{1,0},{2,3},{3,2},{4,5},{5,4},{6,7},{7,6},{8,9},{9,8},{10,11... | collective-permute-start | bytes 442376 | tf_op jit(solution)/shard_map/ppermute | solution.py:348
  93.4 34.0 %collective-permute-start.22 = (bf16[48,2048]{1,0:T(8,128)(2,1)S(1)}, bf16[48,2048]{1,0:T(8,128)(2,1)S(1)}, u32[]{:S(2)}, u32[]{:S(2)}) collective-permute-start(bf16[48,2048]{1,0:T(8,128)(2,1)S(1)} %get-tuple-element.142), channel_id=1, source_target_pairs={{0,12},{4,8},{8,4},{12,0},{1,13},{5,9},{9,5},{13,1},{2,14},{6,10},... | collective-permute-start | bytes 589832 | tf_op jit(solution)/shard_map/ppermute | solution.py:348
  95.8 31.6 %collective-permute-start.23 = (bf16[48,2048]{1,0:T(8,128)(2,1)S(1)}, bf16[48,2048]{1,0:T(8,128)(2,1)S(1)}, u32[]{:S(2)}, u32[]{:S(2)}) collective-permute-start(bf16[48,2048]{1,0:T(8,128)(2,1)S(1)} %get-tuple-element.143), channel_id=1, source_target_pairs={{0,8},{4,12},{8,0},{12,4},{1,9},{5,13},{9,1},{13,5},{2,10},{6,14},... | collective-permute-start | bytes 589832 | tf_op jit(solution)/shard_map/ppermute | solution.py:348
  118.3 1.9 %collective-permute-start.17 = (f32[192,128]{1,0:T(8,128)S(1)}, f32[192,128]{1,0:T(8,128)S(1)}, u32[]{:S(2)}, u32[]{:S(2)}) collective-permute-start(f32[192,128]{1,0:T(8,128)S(1)} %get-tuple-element.137.refs_0_), channel_id=1, source_target_pairs={{0,1},{1,0},{2,3},{3,2},{4,5},{5,4},{6,7},{7,6},{8,9},{9,8},{10,11... | collective-permute-start | bytes 294920 | tf_op jit(solution)/shard_map/ppermute | solution.py:348
  118.4 5.7 %collective-permute-start.18 = (f32[192,128]{1,0:T(8,128)S(1)}, f32[192,128]{1,0:T(8,128)S(1)}, u32[]{:S(2)}, u32[]{:S(2)}) collective-permute-start(f32[192,128]{1,0:T(8,128)S(1)} %get-tuple-element.138), channel_id=1, source_target_pairs={{0,2},{1,3},{2,0},{3,1},{4,6},{5,7},{6,4},{7,5},{8,10},{9,11},{10,... | collective-permute-start | bytes 294920 | tf_op jit(solution)/shard_map/ppermute | solution.py:348
  120.0 5.3 %collective-permute-start.19 = (f32[192,128]{1,0:T(8,128)S(1)}, f32[192,128]{1,0:T(8,128)S(1)}, u32[]{:S(2)}, u32[]{:S(2)}) collective-permute-start(f32[192,128]{1,0:T(8,128)S(1)} %get-tuple-element.138), channel_id=1, source_target_pairs={{0,3},{1,2},{2,1},{3,0},{4,7},{5,6},{6,5},{7,4},{8,11},{9,10},{10,... | collective-permute-start | bytes 294920 | tf_op jit(solution)/shard_map/ppermute | solution.py:348
  120.3 28.4 %collective-permute-start.14 = (f32[288,256]{1,0:T(8,128)S(1)}, f32[288,256]{1,0:T(8,128)S(1)}, u32[]{:S(2)}, u32[]{:S(2)}) collective-permute-start(f32[288,256]{1,0:T(8,128)S(1)} %get-tuple-element.133), channel_id=1, source_target_pairs={{0,4},{4,0},{8,12},{12,8},{1,5},{5,1},{9,13},{13,9},{2,6},{6,2},{1... | collective-permute-start | bytes 884744 | tf_op jit(solution)/shard_map/ppermute | solution.py:348
  126.5 22.2 %collective-permute-start.20 = (f32[192,256]{1,0:T(8,128)S(1)}, f32[192,256]{1,0:T(8,128)S(1)}, u32[]{:S(2)}, u32[]{:S(2)}) collective-permute-start(f32[192,256]{1,0:T(8,128)S(1)} %get-tuple-element.139.refs_2_), channel_id=1, source_target_pairs={{0,12},{4,8},{8,4},{12,0},{1,13},{5,9},{9,5},{13,1},{2,14},{6,10},... | collective-permute-start | bytes 589832 | tf_op jit(solution)/shard_map/ppermute | solution.py:348
  127.4 21.3 %collective-permute-start.21 = (f32[192,256]{1,0:T(8,128)S(1)}, f32[192,256]{1,0:T(8,128)S(1)}, u32[]{:S(2)}, u32[]{:S(2)}) collective-permute-start(f32[192,256]{1,0:T(8,128)S(1)} %get-tuple-element.140), channel_id=1, source_target_pairs={{0,8},{4,12},{8,0},{12,4},{1,9},{5,13},{9,1},{13,5},{2,10},{6,14},... | collective-permute-start | bytes 589832 | tf_op jit(solution)/shard_map/ppermute | solution.py:348
  129.4 19.3 %copy-start.9 = (bf16[48,2048]{1,0:T(8,128)(2,1)S(1)}, bf16[48,2048]{1,0:T(8,128)(2,1)}, u32[]{:S(2)}) copy-start(bf16[48,2048]{1,0:T(8,128)(2,1)} %get-tuple-element.148) | copy-start | bytes 589828
  129.4 19.3 %copy-start.10 = (bf16[48,2048]{1,0:T(8,128)(2,1)S(1)}, bf16[48,2048]{1,0:T(8,128)(2,1)}, u32[]{:S(2)}) copy-start(bf16[48,2048]{1,0:T(8,128)(2,1)} %get-tuple-element.149) | copy-start | bytes 589828
  129.4 19.3 %copy-start.13 = (s32[768,1]{1,0:T(8,128)S(1)}, s32[768,1]{1,0:T(8,128)}, u32[]{:S(2)}) copy-start(s32[768,1]{1,0:T(8,128)} %get-tuple-element.119) | copy-start | bytes 9220
  129.4 3.9 %collective-permute-start.24 = (f32[48,128]{1,0:T(8,128)S(1)}, f32[48,128]{1,0:T(8,128)S(1)}, u32[]{:S(2)}, u32[]{:S(2)}) collective-permute-start(f32[48,128]{1,0:T(8,128)S(1)} %get-tuple-element.145), channel_id=1, source_target_pairs={{0,2},{2,0},{1,3},{3,1},{4,6},{6,4},{5,7},{7,5},{8,10},{10,8},{9,1... | collective-permute-start | bytes 73736 | tf_op jit(solution)/shard_map/ppermute | solution.py:348
  133.3 1.6 collective-permute-start.25
  133.3 5.6 %collective-permute-start.9 = (s32[1,128]{1,0:T(1,128)S(1)}, s32[1,128]{1,0:T(1,128)S(1)}, u32[]{:S(2)}, u32[]{:S(2)}) collective-permute-start(s32[1,128]{1,0:T(1,128)S(1)} %get-tuple-element.118), channel_id=1, source_target_pairs={{0,16},{16,0},{1,17},{17,1},{2,18},{18,2},{3,19},{19,3},{4,20},{20... | collective-permute-start | bytes 1544 | tf_op jit(solution)/shard_map/ppermute | solution.py:348
  135.5 6.0 %collective-permute-start.26 = (f32[48,256]{1,0:T(8,128)S(1)}, f32[48,256]{1,0:T(8,128)S(1)}, u32[]{:S(2)}, u32[]{:S(2)}) collective-permute-start(f32[48,256]{1,0:T(8,128)S(1)} %get-tuple-element.146), channel_id=1, source_target_pairs={{0,12},{4,8},{8,4},{12,0},{1,13},{5,9},{9,5},{13,1},{2,14},{6,10},... | collective-permute-start | bytes 147464 | tf_op jit(solution)/shard_map/ppermute | solution.py:348
  138.9 9.7 %collective-permute-start.27 = (f32[48,256]{1,0:T(8,128)S(1)}, f32[48,256]{1,0:T(8,128)S(1)}, u32[]{:S(2)}, u32[]{:S(2)}) collective-permute-start(f32[48,256]{1,0:T(8,128)S(1)} %get-tuple-element.147), channel_id=1, source_target_pairs={{0,8},{4,12},{8,0},{12,4},{1,9},{5,13},{9,1},{13,5},{2,10},{6,14},... | collective-permute-start | bytes 147464 | tf_op jit(solution)/shard_map/ppermute | solution.py:348
  152.1 0.7 copy-start.12
Sparse Core Ops, SparseCore 0:
  30.0 36.1 reduce-scatter.1

commit v6 on v5

--- a/solution.py
+++ b/solution.py
@@ -116,7 +116,7 @@
         ids = line[...]
         chosen = jnp.where(owner_of(ids, owners, owned) == owner, 1, 0)
         count = jnp.sum(chosen, axis=1, keepdims=True)
-        far = (me ^ j ^ owner >= 2) & (owner < owners)
+        far = (me ^ j ^ owner >= 1) & (owner < owners)
         most = jnp.maximum(most, jnp.where(far, count, 0))
         mine = ids - me * owned
         upto = jnp.sum(jnp.where((mine >= 0) & (mine <= adapter), 1, 0), axis=1, keepdims=True)
@@ -298,39 +298,87 @@
     delta = delta * gain
     begin = 0
     for size, out in zip(sizes, outs):
-        out[...] = delta[begin : begin + size, :]
+        piece = delta[begin : begin + size, :]
+        if out.dtype == F32:
+            out[...] = piece
+        else:
+            code_rows(piece, out)
         begin += size
 
 
-def expand(lines, groups, names, scale, up, sizes):
+def code_rows(x, out_ref):
+    rows, columns = x.shape
+    largest = jnp.maximum(jnp.max(jnp.abs(x), axis=1, keepdims=True), 2.0**-105)
+    power = jnp.floor(jnp.log2(largest)) - 14.0
+    power = power + jnp.where(largest * power_of_two(-power) > 32767.0, 1.0, 0.0)
+    coded = jnp.round(x * power_of_two(-power))
+    coded = jnp.minimum(jnp.maximum(coded, -32767.0), 32767.0)
+    out_ref[:rows, :] = coded.astype(I32).astype(jnp.int16)
+    down = lax.broadcasted_iota(I32, (rows, columns), 0)
+    across = lax.broadcasted_iota(I32, (rows, columns), 1)
+    line = jnp.sum(jnp.where(down == across, power, 0.0), axis=0, keepdims=True)
+    line = jnp.broadcast_to(line, (16, columns)).astype(I32)
+    out_ref[rows:, :] = line.astype(jnp.int16)
+
+
+def power_of_two(power):
+    return jnp.exp2(power).astype(BF16).astype(F32)
+
+
+def expand(lines, groups, names, scale, up, sizes, kept=0):
     columns = up.shape[1]
+    shapes = [
+        jax.ShapeDtypeStruct((s, columns), F32)
+        if i < kept
+        else jax.ShapeDtypeStruct((s + 16, columns), jnp.int16)
+        for i, s in enumerate(sizes)
+    ]
     return pl.pallas_call(
         functools.partial(expand_kernel, groups, sizes, len(lines)),
-        out_shape=[jax.ShapeDtypeStruct((s, columns), F32) for s in sizes],
+        out_shape=shapes,
         compiler_params=PARAMS,
         cost_estimate=COST,
         name="expand",
     )(names, scale, up, *lines)
 
 
+def place_kernel(begin, target_ref, rows_ref, out_ref):
+    at = begin + lax.broadcasted_iota(I32, (1, rows_ref.shape[0]), 1)
+    place = jnp.where(target_ref[...] == at, 1.0, 0.0).astype(BF16)
+    total = None
+    for term in split(rows_ref[...], 3):
+        moved = jnp.dot(place, term.astype(BF16), preferred_element_type=F32)
+        total = moved if total is None else total + moved
+    out_ref[...] = total
+
+
+def place_rows(target, begin, rows):
+    return pl.pallas_call(
+        functools.partial(place_kernel, begin),
+        out_shape=jax.ShapeDtypeStruct((target.shape[0], rows.shape[1]), F32),
+        compiler_params=PARAMS,
+        cost_estimate=COST,
+        name="place",
+    )(target, rows)
+
+
 def merge_kernel(begins, parts, target_ref, *refs):
     blocks, out_ref = refs[parts:-1], refs[-1]
-    returned = jnp.concatenate([b[...] for b in blocks], axis=0)
-    target = target_ref[...]
-    place = jnp.concatenate(
-        [
-            jnp.where(
-                target == begin + lax.broadcasted_iota(I32, (1, block.shape[0]), 1), 1.0, 0.0
-            ).astype(BF16)
-            for begin, block in zip(begins, blocks)
-        ],
-        axis=1,
-    )
-    total = refs[0][...]
-    for part in refs[1:parts]:
+    spots, powers, highs, lows = [], [], [], []
+    for begin, block in zip(begins, blocks):
+        count = block.shape[0] - 16
+        spots.append(begin + lax.broadcasted_iota(I32, (1, count), 1))
+        powers.append(block[count:, :].astype(I32)[:1, :count])
+        coded = block[:count, :].astype(I32)
+        high = (coded + 128) >> 8
+        highs.append(high.astype(F32).astype(BF16))
+        lows.append((coded - high * 256).astype(F32).astype(BF16))
+    spot, power = jnp.concatenate(spots, axis=1), jnp.concatenate(powers, axis=1)
+    place = jnp.where(target_ref[...] == spot, jnp.exp2(power.astype(F32)), 0.0).astype(BF16)
+    total = jnp.dot(place, jnp.concatenate(highs, axis=0), preferred_element_type=F32) * 256.0
+    total = total + jnp.dot(place, jnp.concatenate(lows, axis=0), preferred_element_type=F32)
+    for part in refs[:parts]:
         total = total + part[...]
-    for term in split(returned, 3):
-        total = total + jnp.dot(place, term.astype(BF16), preferred_element_type=F32)
     out_ref[...] = total.astype(out_ref.dtype)
 
 
@@ -368,9 +416,10 @@
     own, near = (0, 0, cap), (1, 0, cap)
     if owners == 4:
         usual = up_to_16(cap * 5 // 6)
+        near = (1, 0, usual)
         most = up_to_16(usual * 4 // 5)
         far = [[(3, 0, most), (2, 0, most)], [(3, most, usual - most), (2, most, usual - most)]]
-        extra = [(3, usual, cap - usual), (2, usual, cap - usual)]
+        extra = [(j, usual, cap - usual) for j in (3, 2, 1)]
     else:
         usual, far, extra = cap, [[(j, 0, cap) for j in range(2, owners)]], []
 
@@ -379,6 +428,8 @@
     slot, target = route(ids_row, me.reshape(1), owners, owned, cap)
     sent = [p for s in far for p in s] + [near]
     packed = dict(zip(sent, sort_rows(tokens, slot, cap, sent, tuple(ids_heard[1:]))))
+    base_part = base_product(tokens, key_value_weight, packed[near])
+    base = lax.psum_scatter(base_part, feature_axes, scatter_dimension=1, tiled=True)
     received = {p: swap(packed[p], "dp", owners, p[0]) for p in sent}
 
     sets = [[own], [near], [own, near]] + far + ([extra] if extra else [])
@@ -412,8 +463,6 @@
         return [b * cap + f for b, f, _ in pieces]
 
     weights = (adapter_down_weight, up, scale)
-    base_part = base_product(tokens, key_value_weight, packed[near])
-    base = lax.psum_scatter(base_part, feature_axes, scatter_dimension=1, tiled=True)
     packed |= zip([own] + extra, sort_rows(tokens, slot, cap, [own] + extra, (base_part,)))
     down = adapter_down_weight
     first = shrink([own], [packed[own]], names[0], ends, plans[0], down)
@@ -421,28 +470,30 @@
         [near], [received[near]], names[1], ends, plans[1], down, tuple(first[:1])
     )
     lines = exchange(*(jnp.concatenate(pair, axis=0) for pair in zip(first, second)), steps=1)
-    deltas = expand(lines, (cap // 2, cap // 2), names[2], scale, up, (cap, cap))
-    returned = [deltas[0]] + send_back([near], deltas[1:])
-    done = [own, near]
+    sizes = (own[2], near[2])
+    deltas = expand(lines, tuple(c // 2 for c in sizes), names[2], scale, up, sizes, kept=1)
+    parts = [base, place_rows(target, own[0] * cap, deltas[0])]
+    returned = send_back([near], deltas[1:])
+    done = [near]
     for k, pieces in enumerate(far):
         blocks = [received[p] for p in pieces]
         deltas = deltas_of(
-            pieces, blocks, names[3 + k], ends, plans[3 + k], *weights, (deltas[0],), 1 + (pieces is far[-1])
+            pieces, blocks, names[3 + k], ends, plans[3 + k], *weights, (deltas[0], parts[1]), 1 + (pieces is far[-1])
         )
         returned += send_back(pieces, deltas)
         done += pieces
 
-    def finish(base, target, returned, *_):
-        return merge([base], target, begins(done), returned, BF16)
+    def finish(parts, target, returned, *_):
+        return merge(parts, target, begins(done), returned, BF16)
 
     if not extra:
-        return finish(base, target, returned)
-
-    def finish_with_extra(base, target, returned, blocks, names, ends, plan, weights):
+        return finish(parts, target, returned)
+
+    def finish_with_extra(parts, target, returned, blocks, names, ends, plan, weights):
         blocks = send_back(extra, blocks)
         deltas = deltas_of(extra, blocks, names, ends, plan, *weights, ())
         deltas = send_back(extra, deltas)
-        return merge([base], target, begins(done + extra), returned + deltas, BF16)
+        return merge(parts, target, begins(done + extra), returned + deltas, BF16)
 
     for d in range(1, lax.axis_size("parts")):
         largest = jnp.maximum(largest, swap(largest, "parts", lax.axis_size("parts"), d))
@@ -450,7 +501,7 @@
         largest[0, 0] > usual,
         finish_with_extra,
         finish,
-        base,
+        parts,
         target,
         returned,
         [packed[p] for p in extra],

time: 160 us -> 158 us (0.988)
    unnamed x34 -> x36, local copies, waits for them, and re-layouts: 4.38 us -> 4.27 us
  transfers between devices with their start and end apart: 23 -> 23, of which waited for: 9 -> 10; matrix products, arithmetic and copies ran while one was open for 0% -> 0% of each run, Pallas kernels for 23% -> 24%
where the time goes in v6:
time: 158 us
  waiting for transfers between devices  66 us (42%)
  Pallas kernels  48.5 us (31%)
  starting transfers between devices  25.2 us (16%)
  between operations  13.8 us (9%)
  local copies, waits for them, and re-layouts  4.36 us (3%)
    ppermute x22, waiting for transfers between devices, swap(): return lax.ppermute(x, axes, [(i, i ^ distance) for i in range(size)])  66 us
    pallas_call x4, Pallas kernels, shrink(): pl.pallas_call(functools.partial(shrink_kernel, pieces, group, fine), gri...  26.3 us
    ppermute x22, starting transfers between devices, swap(): return lax.ppermute(x, axes, [(i, i ^ distance) for i in range(size)])  25.2 us
    pallas_call x2, Pallas kernels, sort_rows(): pl.pallas_call(functools.partial(sort_kernel, cap, pieces, len(later_than...  6.87 us
    pallas_call x1, Pallas kernels, base_product(): pl.pallas_call(base_kernel, grid=(columns // step,), in_specs=[pl.BlockSp...  5.49 us
    unnamed x36, local copies, waits for them, and re-layouts  4.27 us
    pallas_call x3, Pallas kernels, expand(): pl.pallas_call(functools.partial(expand_kernel, groups, sizes, len(lines)...  3.68 us
  transfers between devices with their start and end apart: 23, of which 10 were waited for; matrix products, arithmetic and copies ran while one was open for 0% of the time, Pallas kernels for 24%

profile of v6, /device:TPU:0, one launch (start us, length us, event | category | flops | bytes accessed | tf_op | source)
XLA Modules:
  0.0 158.1 jit_solution(8613467213186121342)
XLA Ops:
  6.5 5.0 %collective-permute-start.10 = (s32[1,768]{1,0:T(1,128)}, s32[1,768]{1,0:T(1,128)S(1)}, u32[]{:S(2)}, u32[]{:S(2)}) collective-permute-start(s32[1,768]{1,0:T(1,128)} %bitcast.7), channel_id=1, source_target_pairs={{0,12},{4,8},{8,4},{12,0},{1,13},{5,9},{9,5},{13,1},{2,14},{6,10},... | collective-permute-start | bytes 9224 | tf_op jit(solution)/shard_map/ppermute | solution.py:396
  11.6 0.0 collective-permute-start.8
  11.6 0.6 collective-permute-start.9
  12.2 0.7 copy-done.5
  12.9 1.6 %route.1 = (s32[1,768]{1,0:T(1,128)S(1)}, s32[768,1]{1,0:T(8,128)}) custom-call(s32[1]{0:T(128)} %bitcast.me_ref, s32[1,768]{1,0:T(1,128)S(1)} %bitcast.10), custom_call_target="tpu_custom_call" | custom-call | flops 1000000000 | bytes 1 | tf_op jit(solution)/shard_map/route/pallas_call | solution.py:53
  14.5 0.0 collective-permute-done.10.refs_3_.refs_2_
  14.5 0.9 collective-permute-done.8.refs_1_.refs_0_
  15.4 0.9 collective-permute-done.9.refs_2_.refs_1_
  16.3 3.6 %sort.2 = (bf16[192,2048]{1,0:T(8,128)(2,1)S(1)}, bf16[192,2048]{1,0:T(8,128)(2,1)S(1)}, bf16[48,2048]{1,0:T(8,128)(2,1)S(1)}, bf16[48,2048]{1,0:T(8,128)(2,1)S(1)}, bf16[240,2048]{1,0:T(8,128)(2,1)S(1)}) custom-call(s32[1,768]{1,0:T(1,128)S(1)} %get-tuple-element.125.slot_ref, bf16[768,2048]{1,0:T(8,128)(2,1)S(1)} %copy-done, ...), custom_call_target="tpu_custom_call" | custom-call | flops 1000000000 | bytes 1 | tf_op jit(solution)/shard_map/sort/pallas_call | solution.py:88
  19.9 0.9 copy-done.3
  20.8 0.9 copy-done.4
  21.7 5.5 %base.1.refs_0_ = f32[768,1024]{1,0:T(8,128)} custom-call(bf16[768,2048]{1,0:T(8,128)(2,1)S(1)} %copy-done, bf16[2048,1024]{1,0:T(8,128)(2,1)S(1)} %copy-done.1, bf16[240,2048]{1,0:T(8,128)(2,1)S(1)} %get-tuple-element.126._), custom_call_target="tpu_custom_call" | custom-call | flops 1000000000 | bytes 1 | tf_op jit(solution)/shard_map/base/pallas_call | solution.py:169
  27.2 1.0 copy-done.2
  28.2 0.0 reduce-scatter.2.cloned.1.call-update
  28.2 2.1 %collective-permute-start.12 = (bf16[240,2048]{1,0:T(8,128)(2,1)}, bf16[240,2048]{1,0:T(8,128)(2,1)}, u32[]{:S(2)}, u32[]{:S(2)}) collective-permute-start(bf16[240,2048]{1,0:T(8,128)(2,1)} %copy-done.2), channel_id=1, source_target_pairs={{0,4},{4,0},{8,12},{12,8},{1,5},{5,1},{9,13},{13,9},{2,6},{6,2},{1... | collective-permute-start | bytes 2949128 | tf_op jit(solution)/shard_map/ppermute | solution.py:396
  30.3 0.1 pad_add_fusion.here_ref
  30.4 0.0 collective-permute-start.17
  30.4 1.5 collective-permute-start.18
  31.9 3.2 %sort.3 = (bf16[288,2048]{1,0:T(8,128)(2,1)S(1)}, bf16[48,2048]{1,0:T(8,128)(2,1)}, bf16[48,2048]{1,0:T(8,128)(2,1)}, bf16[48,2048]{1,0:T(8,128)(2,1)}) custom-call(s32[1,768]{1,0:T(1,128)S(1)} %get-tuple-element.125.slot_ref, bf16[768,2048]{1,0:T(8,128)(2,1)S(1)} %copy-done, f32[768,1024]{1,0:T(8,128)} %base.1.refs_0_), custom_call_target="tpu_custom_call" | custom-call | flops 1000000000 | bytes 1 | tf_op jit(solution)/shard_map/sort/pallas_call | solution.py:88
  35.1 1.7 %name_rows.1 = (s32[288,1]{1,0:T(8,128)S(1)}, s32[240,1]{1,0:T(8,128)S(1)}, s32[528,1]{1,0:T(8,128)S(1)}, s32[384,1]{1,0:T(8,128)S(1)}, s32[96,1]{1,0:T(8,128)S(...) custom-call(s32[2]{0:T(128)S(1)} %pad_add_fusion.here_ref, ...), custom_call_target="tpu_custom_call" | custom-call | flops 1000000000 | bytes 1 | tf_op jit(solution)/shard_map/name_rows/pallas_call | solution.py:144
  36.8 0.1 fusion
  36.9 10.0 %shrink.6 = (f32[144,128]{1,0:T(8,128)S(1)}, f32[144,128]{1,0:T(8,128)S(1)}) custom-call(s32[3]{0:T(128)S(1)} %get-tuple-element.161.plan_ref, s32[4,128]{1,0:T(4,128)S(1)} %get-tuple-element.129.ends_ref, s32[288,1]{1,0:T(8,128)S(1)} %get-tuple-element.130.which_ref, bf16[24,128,2048]{2,1,0:T(8,128)(2,1)} %down_ref.7, ...), custom_call_target="tpu_custom_call" | custom-call | flops 1000000000 | bytes 1 | tf_op jit(solution)/shard_map/shrink/pallas_call | solution.py:242
  46.9 24.5 %collective-permute-done.12.refs_0_ = bf16[240,2048]{1,0:T(8,128)(2,1)} collective-permute-done((bf16[240,2048]{1,0:T(8,128)(2,1)}, bf16[240,2048]{1,0:T(8,128)(2,1)}, u32[]{:S(2)}, u32[]{:S(2)}) %collective-permute-start.12) | collective-permute-done | bytes 983072 | tf_op jit(solution)/shard_map/ppermute | solution.py:396
  71.4 0.0 copy-start.7
  71.5 0.0 copy-start.12
  71.5 7.3 %shrink.7 = (f32[120,128]{1,0:T(8,128)S(1)}, f32[120,128]{1,0:T(8,128)S(1)}) custom-call(s32[3]{0:T(128)S(1)} %get-tuple-element.160.plan_ref, s32[4,128]{1,0:T(4,128)S(1)} %get-tuple-element.129.ends_ref, s32[240,1]{1,0:T(8,128)S(1)} %get-tuple-element.133.which_ref, bf16[24,128,2048]{2,1,0:T(8,128)(2,1)S(1)} %bitcast.13, ...), custom_call_target="tpu_custom_call" | custom-call | flops 1000000000 | bytes 1 | tf_op jit(solution)/shard_map/shrink/pallas_call | solution.py:242
  78.8 0.0 copy-start.14
  78.8 1.6 collective-permute-start.14
  80.4 0.6 collective-permute-start.13
  81.0 3.4 %collective-permute-done.14.refs_2_ = f32[264,128]{1,0:T(8,128)S(1)} collective-permute-done((f32[264,128]{1,0:T(8,128)S(1)}, f32[264,128]{1,0:T(8,128)S(1)}, u32[]{:S(2)}, u32[]{:S(2)}) %collective-permute-start.14) | collective-permute-done | bytes 135200 | tf_op jit(solution)/shard_map/ppermute | solution.py:396
  84.4 2.7 %collective-permute-start.24 = (bf16[48,2048]{1,0:T(8,128)(2,1)S(1)}, bf16[48,2048]{1,0:T(8,128)(2,1)S(1)}, u32[]{:S(2)}, u32[]{:S(2)}) collective-permute-start(bf16[48,2048]{1,0:T(8,128)(2,1)S(1)} %get-tuple-element.147), channel_id=1, source_target_pairs={{0,12},{4,8},{8,4},{12,0},{1,13},{5,9},{9,5},{13,1},{2,14},{6,10},... | collective-permute-start | bytes 589832 | tf_op jit(solution)/shard_map/ppermute | solution.py:396
  87.1 0.0 collective-permute-start.25
  87.1 0.0 collective-permute-done.13.refs_1_
  87.1 1.7 %expand.5 = (f32[288,256]{1,0:T(8,128)S(1)}, s16[256,256]{1,0:T(8,128)(2,1)S(1)}) custom-call(s32[528,1]{1,0:T(8,128)S(1)} %get-tuple-element.127.which_ref, f32[1,24]{1,0:T(1,128)S(1)} %bitcast.18, bf16[1536,256]{1,0:T(8,128)(2,1)S(1)} %bitcast.14, f32[264,128]{1,0:T(8,128)S(1)} %constant_dynamic-update-slice_fusion.refs_0_, ...), custom_call_target="tpu_custom_call" | custom-call | flops 1000000000 | bytes 1 | tf_op jit(solution)/shard_map/expand/pallas_call | solution.py:336
  88.8 0.8 place.1.refs_3_
  89.7 19.8 %collective-permute-done.18.refs_1_ = bf16[192,2048]{1,0:T(8,128)(2,1)S(1)} collective-permute-done((bf16[192,2048]{1,0:T(8,128)(2,1)}, bf16[192,2048]{1,0:T(8,128)(2,1)S(1)}, u32[]{:S(2)}, u32[]{:S(2)}) %collective-permute-start.18) | collective-permute-done | bytes 786464 | tf_op jit(solution)/shard_map/ppermute | solution.py:396
  109.5 7.1 %shrink.8 = (f32[192,128]{1,0:T(8,128)S(1)}, f32[192,128]{1,0:T(8,128)S(1)}) custom-call(s32[3]{0:T(128)S(1)} %get-tuple-element.159.plan_ref, s32[4,128]{1,0:T(4,128)S(1)} %get-tuple-element.129.ends_ref, s32[384,1]{1,0:T(8,128)S(1)} %get-tuple-element.139.which_ref, bf16[24,128,2048]{2,1,0:T(8,128)(2,1)S(1)} %bitcast.13, ...), custom_call_target="tpu_custom_call" | custom-call | flops 1000000000 | bytes 1 | tf_op jit(solution)/shard_map/shrink/pallas_call | solution.py:242
  116.6 0.1 collective-permute-start.19
  116.7 1.6 collective-permute-start.20
  118.2 0.3 collective-permute-start.21
  118.5 3.8 %collective-permute-done.20.refs_2_ = f32[192,128]{1,0:T(8,128)S(1)} collective-permute-done((f32[192,128]{1,0:T(8,128)S(1)}, f32[192,128]{1,0:T(8,128)S(1)}, u32[]{:S(2)}, u32[]{:S(2)}) %collective-permute-start.20) | collective-permute-done | bytes 98336 | tf_op jit(solution)/shard_map/ppermute | solution.py:396
  122.3 1.2 collective-permute-done.21.refs_3_
  123.5 1.3 expand.6
  124.9 2.0 %shrink.9 = (f32[48,128]{1,0:T(8,128)S(1)}, f32[48,128]{1,0:T(8,128)S(1)}) custom-call(s32[3]{0:T(128)S(1)} %get-tuple-element.158.plan_ref, s32[4,128]{1,0:T(4,128)S(1)} %get-tuple-element.129.ends_ref, s32[96,1]{1,0:T(8,128)S(1)} %get-tuple-element.146.which_ref, bf16[24,128,2048]{2,1,0:T(8,128)(2,1)S(1)} %bitcast.13, ...), custom_call_target="tpu_custom_call" | custom-call | flops 1000000000 | bytes 1 | tf_op jit(solution)/shard_map/shrink/pallas_call | solution.py:242
  126.9 1.6 collective-permute-start.26
  128.4 2.3 %collective-permute-done.26 = f32[48,128]{1,0:T(8,128)S(1)} collective-permute-done((f32[48,128]{1,0:T(8,128)S(1)}, f32[48,128]{1,0:T(8,128)S(1)}, u32[]{:S(2)}, u32[]{:S(2)}) %collective-permute-start.26) | collective-permute-done | bytes 24608 | tf_op jit(solution)/shard_map/ppermute | solution.py:396
  130.8 0.0 collective-permute-start.27
  130.8 0.1 collective-permute-start.16
  130.9 1.6 %collective-permute-start.11 = (s32[1,128]{1,0:T(1,128)S(1)}, s32[1,128]{1,0:T(1,128)S(1)}, u32[]{:S(2)}, u32[]{:S(2)}) collective-permute-start(s32[1,128]{1,0:T(1,128)S(1)} %get-tuple-element.123), channel_id=1, source_target_pairs={{0,16},{16,0},{1,17},{17,1},{2,18},{18,2},{3,19},{19,3},{4,20},{20... | collective-permute-start | bytes 1544 | tf_op jit(solution)/shard_map/ppermute | solution.py:396
  132.5 2.0 %collective-permute-start.22 = (s16[208,256]{1,0:T(8,128)(2,1)S(1)}, s16[208,256]{1,0:T(8,128)(2,1)S(1)}, u32[]{:S(2)}, u32[]{:S(2)}) collective-permute-start(s16[208,256]{1,0:T(8,128)(2,1)S(1)} %get-tuple-element.144.refs_2_), channel_id=1, source_target_pairs={{0,12},{4,8},{8,4},{12,0},{1,13},{5,9},{9,5},{13,1},{2,14},{6,10},... | collective-permute-start | bytes 319496 | tf_op jit(solution)/shard_map/ppermute | solution.py:396
  134.5 1.4 collective-permute-start.23
  135.9 0.0 collective-permute-done.27.refs_1_
  135.9 0.7 expand.7
  136.6 2.1 %collective-permute-start.28 = (s16[64,256]{1,0:T(8,128)(2,1)S(1)}, s16[64,256]{1,0:T(8,128)(2,1)S(1)}, u32[]{:S(2)}, u32[]{:S(2)}) collective-permute-start(s16[64,256]{1,0:T(8,128)(2,1)S(1)} %get-tuple-element.151), channel_id=1, source_target_pairs={{0,12},{4,8},{8,4},{12,0},{1,13},{5,9},{9,5},{13,1},{2,14},{6,10},... | collective-permute-start | bytes 98312 | tf_op jit(solution)/shard_map/ppermute | solution.py:396
  138.6 0.5 collective-permute-start.29
  139.1 0.0 collective-permute-done.16
  139.1 3.5 %collective-permute-done.28 = s16[64,256]{1,0:T(8,128)(2,1)S(1)} collective-permute-done((s16[64,256]{1,0:T(8,128)(2,1)S(1)}, s16[64,256]{1,0:T(8,128)(2,1)S(1)}, u32[]{:S(2)}, u32[]{:S(2)}) %collective-permute-start.28) | collective-permute-done | bytes 32800 | tf_op jit(solution)/shard_map/ppermute | solution.py:396
  142.7 5.6 %collective-permute-done.29 = s16[64,256]{1,0:T(8,128)(2,1)S(1)} collective-permute-done((s16[64,256]{1,0:T(8,128)(2,1)S(1)}, s16[64,256]{1,0:T(8,128)(2,1)S(1)}, u32[]{:S(2)}, u32[]{:S(2)}) %collective-permute-start.29) | collective-permute-done | bytes 32800 | tf_op jit(solution)/shard_map/ppermute | solution.py:396
  148.3 0.0 collective-permute-done.23
  148.3 0.0 reduce-scatter.2.cloned.1.call-done
  148.3 2.2 %conditional.1 = (bf16[768,256]{1,0:T(8,128)(2,1)S(1)}) conditional(s32[]{:T(128)} %bitcast.3, (s32[768,1]{1,0:T(8,128)S(1)}, f32[768,256]{1,0:T(8,128)}, f32[768,256]{1,0:T(8,128)S(1)}, s16[256,256]{1,0:T(8,128)(2,1)S(1)}, s16[208,256]{1,0:T(8,128)(2,1)S(1)}, /*index=5*/s16[208,256]{1,0:T(8,128)(2,1)S(1)}, s16[64,256]{1,0:T(8,128)(2,1)S(1)}, ...), branch_computations={%region_1.0_spmd, %region_2.0_spmd} | conditional | flops 3000009216 | bytes 6328759 | solution.py:500
  148.5 2.0 %merge.2 = bf16[768,256]{1,0:T(8,128)(2,1)S(1)} custom-call(s32[768,1]{1,0:T(8,128)S(1)} %get-tuple-element.59.target_ref, f32[768,256]{1,0:T(8,128)} %get-tuple-element.60.refs_0_, f32[768,256]{1,0:T(8,128)S(1)} %get-tuple-element.61.refs_1_, s16[256,256]{1,0:T(8,128)(2,1)S(1)} %get-tuple-element.62.refs_2_, s16[208,256]{1,0:T(8,128)(2,1)S(1)} %get-tuple-element.63.refs_3_, ...), custom_call_target="tpu_custom_call" | custom-call | flops 1000000000 | bytes 1 | tf_op jit(solution)/shard_map/cond/branch_0_fun/merge/pallas_call | solution.py:386
  150.5 0.0 copy-start.13
  150.5 0.7 copy-done.13
  (41 shorter events, 0.1 us)
Async XLA Ops:
  6.5 9.8 %copy-start = (bf16[768,2048]{1,0:T(8,128)(2,1)S(1)}, bf16[768,2048]{1,0:T(8,128)(2,1)}, u32[]{:S(2)}) copy-start(bf16[768,2048]{1,0:T(8,128)(2,1)} %tok_ref.5) | copy-start | bytes 9437188
  6.5 141.7 %reduce-scatter.2.cloned.1.call-start = ((), (), s32[]{:S(2)}) async-start(), calls=%async_computation.1 | async-start | bytes 3932160 | tf_op jit(solution)/shard_map/reduce_scatter | solution.py:432
  6.5 8.0 %collective-permute-start.10 = (s32[1,768]{1,0:T(1,128)}, s32[1,768]{1,0:T(1,128)S(1)}, u32[]{:S(2)}, u32[]{:S(2)}) collective-permute-start(s32[1,768]{1,0:T(1,128)} %bitcast.7), channel_id=1, source_target_pairs={{0,12},{4,8},{8,4},{12,0},{1,13},{5,9},{9,5},{13,1},{2,14},{6,10},... | collective-permute-start | bytes 9224 | tf_op jit(solution)/shard_map/ppermute | solution.py:396
  11.6 3.8 %collective-permute-start.8 = (s32[1,768]{1,0:T(1,128)}, s32[1,768]{1,0:T(1,128)S(1)}, u32[]{:S(2)}, u32[]{:S(2)}) collective-permute-start(s32[1,768]{1,0:T(1,128)} %bitcast.8), channel_id=1, source_target_pairs={{0,4},{4,0},{8,12},{12,8},{1,5},{5,1},{9,13},{13,9},{2,6},{6,2},{1... | collective-permute-start | bytes 9224 | tf_op jit(solution)/shard_map/ppermute | solution.py:396
  11.6 4.7 %collective-permute-start.9 = (s32[1,768]{1,0:T(1,128)}, s32[1,768]{1,0:T(1,128)S(1)}, u32[]{:S(2)}, u32[]{:S(2)}) collective-permute-start(s32[1,768]{1,0:T(1,128)} %bitcast.9), channel_id=1, source_target_pairs={{0,8},{4,12},{8,0},{12,4},{1,9},{5,13},{9,1},{13,5},{2,10},{6,14},... | collective-permute-start | bytes 9224 | tf_op jit(solution)/shard_map/ppermute | solution.py:396
  12.2 0.7 copy-start.5
  12.9 8.9 %copy-start.1 = (bf16[2048,1024]{1,0:T(8,128)(2,1)S(1)}, bf16[2048,1024]{1,0:T(8,128)(2,1)}, u32[]{:S(2)}) copy-start(bf16[2048,1024]{1,0:T(8,128)(2,1)} %weight_ref.1) | copy-start | bytes 12582916
  19.9 0.9 copy-start.3
  20.8 0.9 copy-start.4
  27.2 1.0 copy-start.2
  28.2 43.2 %collective-permute-start.12 = (bf16[240,2048]{1,0:T(8,128)(2,1)}, bf16[240,2048]{1,0:T(8,128)(2,1)}, u32[]{:S(2)}, u32[]{:S(2)}) collective-permute-start(bf16[240,2048]{1,0:T(8,128)(2,1)} %copy-done.2), channel_id=1, source_target_pairs={{0,4},{4,0},{8,12},{12,8},{1,5},{5,1},{9,13},{13,9},{2,6},{6,2},{1... | collective-permute-start | bytes 2949128 | tf_op jit(solution)/shard_map/ppermute | solution.py:396
  30.4 59.3 %collective-permute-start.17 = (bf16[192,2048]{1,0:T(8,128)(2,1)}, bf16[192,2048]{1,0:T(8,128)(2,1)S(1)}, u32[]{:S(2)}, u32[]{:S(2)}) collective-permute-start(bf16[192,2048]{1,0:T(8,128)(2,1)} %copy-done.4), channel_id=1, source_target_pairs={{0,12},{4,8},{8,4},{12,0},{1,13},{5,9},{9,5},{13,1},{2,14},{6,10},... | collective-permute-start | bytes 2359304 | tf_op jit(solution)/shard_map/ppermute | solution.py:396
  30.4 4.7 %copy-start.6 = (s32[768,1]{0,1:T(1,128)S(1)}, s32[768,1]{0,1:T(1,128)}, u32[]{:S(2)}) copy-start(s32[768,1]{0,1:T(1,128)} %param.13) | copy-start | bytes 9220
  30.4 79.1 %collective-permute-start.18 = (bf16[192,2048]{1,0:T(8,128)(2,1)}, bf16[192,2048]{1,0:T(8,128)(2,1)S(1)}, u32[]{:S(2)}, u32[]{:S(2)}) collective-permute-start(bf16[192,2048]{1,0:T(8,128)(2,1)} %copy-done.3), channel_id=1, source_target_pairs={{0,8},{4,12},{8,0},{12,4},{1,9},{5,13},{9,1},{13,5},{2,10},{6,14},... | collective-permute-start | bytes 2359304 | tf_op jit(solution)/shard_map/ppermute | solution.py:396
  31.9 39.6 %slice-start = ((s8[12582912]{0:T(1024)(128)(4,1)}), s8[4194304]{0:T(1024)(128)(4,1)S(1)}, s32[]{:S(2)}) async-start(s8[12582912]{0:T(1024)(128)(4,1)} %bitcast.12), calls=%async_computation.2 | async-start | bytes 8388608
  35.1 36.3 %slice-start.1 = ((s8[12582912]{0:T(1024)(128)(4,1)}), s8[4194304]{0:T(1024)(128)(4,1)S(1)}, s32[]{:S(2)}) async-start(s8[12582912]{0:T(1024)(128)(4,1)} %bitcast.12), calls=%async_computation.3 | async-start | bytes 8388608
  36.9 34.5 %slice-start.2 = ((s8[12582912]{0:T(1024)(128)(4,1)}), s8[4194304]{0:T(1024)(128)(4,1)S(1)}, s32[]{:S(2)}) async-start(s8[12582912]{0:T(1024)(128)(4,1)} %bitcast.12), calls=%async_computation.4 | async-start | bytes 8388608
  71.4 15.7 %copy-start.7 = (bf16[24,64,256]{2,1,0:T(8,128)(2,1)S(1)}, bf16[24,64,256]{2,1,0:T(8,128)(2,1)}, u32[]{:S(2)}) copy-start(bf16[24,64,256]{2,1,0:T(8,128)(2,1)} %param.11) | copy-start | bytes 2359300
  71.5 15.7 %copy-start.12 = (f32[24]{0:T(128)S(1)}, f32[24]{0:T(128)}, u32[]{:S(2)}) copy-start(f32[24]{0:T(128)} %param.12) | copy-start | bytes 292
  78.8 10.0 %copy-start.14 = (s32[768,1]{1,0:T(8,128)S(1)}, s32[768,1]{1,0:T(8,128)}, u32[]{:S(2)}) copy-start(s32[768,1]{1,0:T(8,128)} %get-tuple-element.124.target_ref) | copy-start | bytes 9220
  78.8 5.6 %collective-permute-start.14 = (f32[264,128]{1,0:T(8,128)S(1)}, f32[264,128]{1,0:T(8,128)S(1)}, u32[]{:S(2)}, u32[]{:S(2)}) collective-permute-start(f32[264,128]{1,0:T(8,128)S(1)} %constant_dynamic-update-slice_fusion.2), channel_id=1, source_target_pairs={{0,2},{1,3},{2,0},{3,1},{4,6},{5,7},{6,4},{7,5},{8,10},{9,11},{10,... | collective-permute-start | bytes 405512 | tf_op jit(solution)/shard_map/ppermute | solution.py:396
  80.4 6.7 %collective-permute-start.15 = (f32[264,128]{1,0:T(8,128)S(1)}, f32[264,128]{1,0:T(8,128)S(1)}, u32[]{:S(2)}, u32[]{:S(2)}) collective-permute-start(f32[264,128]{1,0:T(8,128)S(1)} %constant_dynamic-update-slice_fusion.2), channel_id=1, source_target_pairs={{0,3},{1,2},{2,1},{3,0},{4,7},{5,6},{6,5},{7,4},{8,11},{9,10},{10,... | collective-permute-start | bytes 405512 | tf_op jit(solution)/shard_map/ppermute | solution.py:396
  80.4 6.7 %collective-permute-start.13 = (f32[264,128]{1,0:T(8,128)S(1)}, f32[264,128]{1,0:T(8,128)S(1)}, u32[]{:S(2)}, u32[]{:S(2)}) collective-permute-start(f32[264,128]{1,0:T(8,128)S(1)} %constant_dynamic-update-slice_fusion.refs_0_), channel_id=1, source_target_pairs={{0,1},{1,0},{2,3},{3,2},{4,5},{5,4},{6,7},{7,6},{8,9},{9,8},{10,11... | collective-permute-start | bytes 405512 | tf_op jit(solution)/shard_map/ppermute | solution.py:396
  84.4 40.4 %collective-permute-start.24 = (bf16[48,2048]{1,0:T(8,128)(2,1)S(1)}, bf16[48,2048]{1,0:T(8,128)(2,1)S(1)}, u32[]{:S(2)}, u32[]{:S(2)}) collective-permute-start(bf16[48,2048]{1,0:T(8,128)(2,1)S(1)} %get-tuple-element.147), channel_id=1, source_target_pairs={{0,12},{4,8},{8,4},{12,0},{1,13},{5,9},{9,5},{13,1},{2,14},{6,10},... | collective-permute-start | bytes 589832 | tf_op jit(solution)/shard_map/ppermute | solution.py:396
  87.1 37.8 %collective-permute-start.25 = (bf16[48,2048]{1,0:T(8,128)(2,1)S(1)}, bf16[48,2048]{1,0:T(8,128)(2,1)S(1)}, u32[]{:S(2)}, u32[]{:S(2)}) collective-permute-start(bf16[48,2048]{1,0:T(8,128)(2,1)S(1)} %get-tuple-element.148), channel_id=1, source_target_pairs={{0,8},{4,12},{8,0},{12,4},{1,9},{5,13},{9,1},{13,5},{2,10},{6,14},... | collective-permute-start | bytes 589832 | tf_op jit(solution)/shard_map/ppermute | solution.py:396
  116.6 1.9 %collective-permute-start.19 = (f32[192,128]{1,0:T(8,128)S(1)}, f32[192,128]{1,0:T(8,128)S(1)}, u32[]{:S(2)}, u32[]{:S(2)}) collective-permute-start(f32[192,128]{1,0:T(8,128)S(1)} %get-tuple-element.142.refs_0_), channel_id=1, source_target_pairs={{0,1},{1,0},{2,3},{3,2},{4,5},{5,4},{6,7},{7,6},{8,9},{9,8},{10,11... | collective-permute-start | bytes 294920 | tf_op jit(solution)/shard_map/ppermute | solution.py:396
  116.7 5.7 %collective-permute-start.20 = (f32[192,128]{1,0:T(8,128)S(1)}, f32[192,128]{1,0:T(8,128)S(1)}, u32[]{:S(2)}, u32[]{:S(2)}) collective-permute-start(f32[192,128]{1,0:T(8,128)S(1)} %get-tuple-element.143), channel_id=1, source_target_pairs={{0,2},{1,3},{2,0},{3,1},{4,6},{5,7},{6,4},{7,5},{8,10},{9,11},{10,... | collective-permute-start | bytes 294920 | tf_op jit(solution)/shard_map/ppermute | solution.py:396
  118.2 5.3 %collective-permute-start.21 = (f32[192,128]{1,0:T(8,128)S(1)}, f32[192,128]{1,0:T(8,128)S(1)}, u32[]{:S(2)}, u32[]{:S(2)}) collective-permute-start(f32[192,128]{1,0:T(8,128)S(1)} %get-tuple-element.143), channel_id=1, source_target_pairs={{0,3},{1,2},{2,1},{3,0},{4,7},{5,6},{6,5},{7,4},{8,11},{9,10},{10,... | collective-permute-start | bytes 294920 | tf_op jit(solution)/shard_map/ppermute | solution.py:396
  126.9 21.4 %copy-start.9 = (bf16[48,2048]{1,0:T(8,128)(2,1)S(1)}, bf16[48,2048]{1,0:T(8,128)(2,1)}, u32[]{:S(2)}) copy-start(bf16[48,2048]{1,0:T(8,128)(2,1)} %get-tuple-element.153) | copy-start | bytes 589828
  126.9 21.4 %copy-start.10 = (bf16[48,2048]{1,0:T(8,128)(2,1)S(1)}, bf16[48,2048]{1,0:T(8,128)(2,1)}, u32[]{:S(2)}) copy-start(bf16[48,2048]{1,0:T(8,128)(2,1)} %get-tuple-element.154) | copy-start | bytes 589828
  126.9 21.4 %copy-start.11 = (bf16[48,2048]{1,0:T(8,128)(2,1)S(1)}, bf16[48,2048]{1,0:T(8,128)(2,1)}, u32[]{:S(2)}) copy-start(bf16[48,2048]{1,0:T(8,128)(2,1)} %get-tuple-element.155) | copy-start | bytes 589828
  126.9 3.9 %collective-permute-start.26 = (f32[48,128]{1,0:T(8,128)S(1)}, f32[48,128]{1,0:T(8,128)S(1)}, u32[]{:S(2)}, u32[]{:S(2)}) collective-permute-start(f32[48,128]{1,0:T(8,128)S(1)} %get-tuple-element.150), channel_id=1, source_target_pairs={{0,2},{2,0},{1,3},{3,1},{4,6},{6,4},{5,7},{7,5},{8,10},{10,8},{9,1... | collective-permute-start | bytes 73736 | tf_op jit(solution)/shard_map/ppermute | solution.py:396
  130.8 5.1 %collective-permute-start.27 = (f32[48,128]{1,0:T(8,128)S(1)}, f32[48,128]{1,0:T(8,128)S(1)}, u32[]{:S(2)}, u32[]{:S(2)}) collective-permute-start(f32[48,128]{1,0:T(8,128)S(1)} %add.12.refs_0_), channel_id=1, source_target_pairs={{0,1},{1,0},{2,3},{3,2},{4,5},{5,4},{6,7},{7,6},{8,9},{9,8},{10,11... | collective-permute-start | bytes 73736 | tf_op jit(solution)/shard_map/ppermute | solution.py:396
  130.8 8.3 %collective-permute-start.16 = (s16[256,256]{1,0:T(8,128)(2,1)S(1)}, s16[256,256]{1,0:T(8,128)(2,1)S(1)}, u32[]{:S(2)}, u32[]{:S(2)}) collective-permute-start(s16[256,256]{1,0:T(8,128)(2,1)S(1)} %get-tuple-element.138), channel_id=1, source_target_pairs={{0,4},{4,0},{8,12},{12,8},{1,5},{5,1},{9,13},{13,9},{2,6},{6,2},{1... | collective-permute-start | bytes 393224 | tf_op jit(solution)/shard_map/ppermute | solution.py:396
  130.9 7.8 %collective-permute-start.11 = (s32[1,128]{1,0:T(1,128)S(1)}, s32[1,128]{1,0:T(1,128)S(1)}, u32[]{:S(2)}, u32[]{:S(2)}) collective-permute-start(s32[1,128]{1,0:T(1,128)S(1)} %get-tuple-element.123), channel_id=1, source_target_pairs={{0,16},{16,0},{1,17},{17,1},{2,18},{18,2},{3,19},{19,3},{4,20},{20... | collective-permute-start | bytes 1544 | tf_op jit(solution)/shard_map/ppermute | solution.py:396
  132.5 15.8 %collective-permute-start.22 = (s16[208,256]{1,0:T(8,128)(2,1)S(1)}, s16[208,256]{1,0:T(8,128)(2,1)S(1)}, u32[]{:S(2)}, u32[]{:S(2)}) collective-permute-start(s16[208,256]{1,0:T(8,128)(2,1)S(1)} %get-tuple-element.144.refs_2_), channel_id=1, source_target_pairs={{0,12},{4,8},{8,4},{12,0},{1,13},{5,9},{9,5},{13,1},{2,14},{6,10},... | collective-permute-start | bytes 319496 | tf_op jit(solution)/shard_map/ppermute | solution.py:396
  134.5 13.8 %collective-permute-start.23 = (s16[208,256]{1,0:T(8,128)(2,1)S(1)}, s16[208,256]{1,0:T(8,128)(2,1)S(1)}, u32[]{:S(2)}, u32[]{:S(2)}) collective-permute-start(s16[208,256]{1,0:T(8,128)(2,1)S(1)} %get-tuple-element.145), channel_id=1, source_target_pairs={{0,8},{4,12},{8,0},{12,4},{1,9},{5,13},{9,1},{13,5},{2,10},{6,14},... | collective-permute-start | bytes 319496 | tf_op jit(solution)/shard_map/ppermute | solution.py:396
  136.6 6.1 %collective-permute-start.28 = (s16[64,256]{1,0:T(8,128)(2,1)S(1)}, s16[64,256]{1,0:T(8,128)(2,1)S(1)}, u32[]{:S(2)}, u32[]{:S(2)}) collective-permute-start(s16[64,256]{1,0:T(8,128)(2,1)S(1)} %get-tuple-element.151), channel_id=1, source_target_pairs={{0,12},{4,8},{8,4},{12,0},{1,13},{5,9},{9,5},{13,1},{2,14},{6,10},... | collective-permute-start | bytes 98312 | tf_op jit(solution)/shard_map/ppermute | solution.py:396
  138.6 9.6 %collective-permute-start.29 = (s16[64,256]{1,0:T(8,128)(2,1)S(1)}, s16[64,256]{1,0:T(8,128)(2,1)S(1)}, u32[]{:S(2)}, u32[]{:S(2)}) collective-permute-start(s16[64,256]{1,0:T(8,128)(2,1)S(1)} %get-tuple-element.152), channel_id=1, source_target_pairs={{0,8},{4,12},{8,0},{12,4},{1,9},{5,13},{9,1},{13,5},{2,10},{6,14},... | collective-permute-start | bytes 98312 | tf_op jit(solution)/shard_map/ppermute | solution.py:396
  150.5 0.7 copy-start.13
Sparse Core Ops, SparseCore 0:
  28.3 37.6 reduce-scatter.1

commit v7 on v6

--- a/solution.py
+++ b/solution.py
@@ -417,22 +417,25 @@
     if owners == 4:
         usual = up_to_16(cap * 5 // 6)
         near = (1, 0, usual)
-        most = up_to_16(usual * 4 // 5)
-        far = [[(3, 0, most), (2, 0, most)], [(3, most, usual - most), (2, most, usual - most)]]
+        far, last = [(3, 0, usual)], [(2, 0, usual)]
         extra = [(j, usual, cap - usual) for j in (3, 2, 1)]
     else:
-        usual, far, extra = cap, [[(j, 0, cap) for j in range(2, owners)]], []
+        usual, far, last, extra = cap, [], [(j, 0, cap) for j in range(2, owners)], []
 
     ids_row = token_adapter_index.reshape(1, rows)
     ids_heard = [ids_row] + [swap(ids_row, "dp", owners, j) for j in range(1, owners)]
     slot, target = route(ids_row, me.reshape(1), owners, owned, cap)
-    sent = [p for s in far for p in s] + [near]
+    sent = far + [near]
     packed = dict(zip(sent, sort_rows(tokens, slot, cap, sent, tuple(ids_heard[1:]))))
+    received = {p: swap(packed[p], "dp", owners, p[0]) for p in sent}
     base_part = base_product(tokens, key_value_weight, packed[near])
     base = lax.psum_scatter(base_part, feature_axes, scatter_dimension=1, tiled=True)
-    received = {p: swap(packed[p], "dp", owners, p[0]) for p in sent}
-
-    sets = [[own], [near], [own, near]] + far + ([extra] if extra else [])
+    packed |= zip([own] + extra, sort_rows(tokens, slot, cap, [own] + extra, (base_part,)))
+    packed |= zip(last, sort_rows(tokens, slot, cap, last, (received[near],)))
+    received |= {p: swap(packed[p], "dp", owners, p[0]) for p in last}
+
+    early = [own, near] + far
+    sets = [[p] for p in early] + [early, last] + ([extra] if extra else [])
     here = jnp.stack([me.astype(I32), half])
     names, ends, plans, largest = name_rows(ids_heard, here, owned, sets)
 
@@ -464,24 +467,25 @@
 
     weights = (adapter_down_weight, up, scale)
     packed |= zip([own] + extra, sort_rows(tokens, slot, cap, [own] + extra, (base_part,)))
-    down = adapter_down_weight
-    first = shrink([own], [packed[own]], names[0], ends, plans[0], down)
-    second = shrink(
-        [near], [received[near]], names[1], ends, plans[1], down, tuple(first[:1])
+    shares, waits = [], ()
+    for k, p in enumerate(early):
+        rows_here = received.get(p, packed[p])
+        shares.append(
+            shrink([p], [rows_here], names[k], ends, plans[k], adapter_down_weight, waits)
+        )
+        waits = (shares[-1][0], packed[last[0]])
+    lines = exchange(*(jnp.concatenate(pair, axis=0) for pair in zip(*shares)), steps=1)
+    sizes = tuple(p[2] for p in early)
+    here = len(early)
+    deltas = expand(lines, tuple(c // 2 for c in sizes), names[here], scale, up, sizes, kept=1)
+    parts = [base, place_rows(target, own[0] * cap, deltas[0])]
+    returned = send_back(early[1:], deltas[1:])
+    blocks = [received[p] for p in last]
+    deltas = deltas_of(
+        last, blocks, names[here + 1], ends, plans[here + 1], *weights, (deltas[0], parts[1])
     )
-    lines = exchange(*(jnp.concatenate(pair, axis=0) for pair in zip(first, second)), steps=1)
-    sizes = (own[2], near[2])
-    deltas = expand(lines, tuple(c // 2 for c in sizes), names[2], scale, up, sizes, kept=1)
-    parts = [base, place_rows(target, own[0] * cap, deltas[0])]
-    returned = send_back([near], deltas[1:])
-    done = [near]
-    for k, pieces in enumerate(far):
-        blocks = [received[p] for p in pieces]
-        deltas = deltas_of(
-            pieces, blocks, names[3 + k], ends, plans[3 + k], *weights, (deltas[0], parts[1]), 1 + (pieces is far[-1])
-        )
-        returned += send_back(pieces, deltas)
-        done += pieces
+    returned += send_back(last, deltas)
+    done = early[1:] + last
 
     def finish(parts, target, returned, *_):
         return merge(parts, target, begins(done), returned, BF16)

time: 158 us -> 150 us (0.949)
  starting transfers between devices: 25.2 us -> 17.9 us
  waiting for transfers between devices: 66 us -> 59.8 us
  Pallas kernels: 48.5 us -> 54.4 us
    ppermute x22 -> x15, starting transfers between devices: 25.2 us -> 17.9 us  [swap(): return lax.ppermute(x, axes, [(i, i ^ distance) for i in range(size)])]
    ppermute x22 -> x15, waiting for transfers between devices: 66 us -> 59.8 us  [swap(): return lax.ppermute(x, axes, [(i, i ^ distance) for i in range(size)])]
    pallas_call x4, Pallas kernels: 26.3 us -> 31.8 us  [shrink(): pl.pallas_call(functools.partial(shrink_kernel, pieces, group, fine), gri...]
    pallas_call x2 -> x3, Pallas kernels: 6.87 us -> 7.74 us  [sort_rows(): pl.pallas_call(functools.partial(sort_kernel, cap, pieces, len(later_than...]
    unnamed x36 -> x33, local copies, waits for them, and re-layouts: 4.27 us -> 3.45 us
    pallas_call x3 -> x2, Pallas kernels: 3.68 us -> 3.24 us  [expand(): pl.pallas_call(functools.partial(expand_kernel, groups, sizes, len(lines)...]
  transfers between devices with their start and end apart: 23 -> 16, of which waited for: 10 -> 11; matrix products, arithmetic and copies ran while one was open for 0% -> 0% of each run, Pallas kernels for 24% -> 30%
where the time goes in v7:
time: 150 us
  waiting for transfers between devices  59.8 us (40%)
  Pallas kernels  54.4 us (36%)
  starting transfers between devices  17.9 us (12%)
  between operations  13.7 us (9%)
  local copies, waits for them, and re-layouts  3.53 us (2%)
    ppermute x15, waiting for transfers between devices, swap(): return lax.ppermute(x, axes, [(i, i ^ distance) for i in range(size)])  59.8 us
    pallas_call x4, Pallas kernels, shrink(): pl.pallas_call(functools.partial(shrink_kernel, pieces, group, fine), gri...  31.8 us
    ppermute x15, starting transfers between devices, swap(): return lax.ppermute(x, axes, [(i, i ^ distance) for i in range(size)])  17.9 us
    pallas_call x3, Pallas kernels, sort_rows(): pl.pallas_call(functools.partial(sort_kernel, cap, pieces, len(later_than...  7.74 us
    pallas_call x1, Pallas kernels, base_product(): pl.pallas_call(base_kernel, grid=(columns // step,), in_specs=[pl.BlockSp...  5.5 us
    unnamed x33, local copies, waits for them, and re-layouts  3.45 us
    pallas_call x2, Pallas kernels, expand(): pl.pallas_call(functools.partial(expand_kernel, groups, sizes, len(lines)...  3.24 us
  transfers between devices with their start and end apart: 16, of which 11 were waited for; matrix products, arithmetic and copies ran while one was open for 0% of the time, Pallas kernels for 30%

profile of v7, /device:TPU:0, one launch (start us, length us, event | category | flops | bytes accessed | tf_op | source)
XLA Modules:
  0.0 149.6 jit_solution(1140226255428109267)
XLA Ops:
  6.5 0.0 reduce-scatter.2.cloned.1.call-start
  6.5 5.0 %collective-permute-start.10 = (s32[1,768]{1,0:T(1,128)}, s32[1,768]{1,0:T(1,128)S(1)}, u32[]{:S(2)}, u32[]{:S(2)}) collective-permute-start(s32[1,768]{1,0:T(1,128)} %bitcast.7), channel_id=1, source_target_pairs={{0,12},{4,8},{8,4},{12,0},{1,13},{5,9},{9,5},{13,1},{2,14},{6,10},... | collective-permute-start | bytes 9224 | tf_op jit(solution)/shard_map/ppermute | solution.py:396
  11.6 0.0 collective-permute-start.8
  11.6 0.6 collective-permute-start.9
  12.2 0.7 copy-done.4
  12.9 1.6 %route.1 = (s32[1,768]{1,0:T(1,128)S(1)}, s32[768,1]{1,0:T(8,128)}) custom-call(s32[1]{0:T(128)} %bitcast.me_ref, s32[1,768]{1,0:T(1,128)S(1)} %bitcast.10), custom_call_target="tpu_custom_call" | custom-call | flops 1000000000 | bytes 1 | tf_op jit(solution)/shard_map/route/pallas_call | solution.py:53
  14.5 0.0 collective-permute-done.10.refs_3_.refs_2_
  14.5 0.9 collective-permute-done.8.refs_1_.refs_0_
  15.4 0.9 collective-permute-done.9.refs_2_.refs_1_
  16.3 0.0 copy-done
  16.3 2.7 %sort.3 = (bf16[240,2048]{1,0:T(8,128)(2,1)S(1)}, bf16[240,2048]{1,0:T(8,128)(2,1)S(1)}) custom-call(s32[1,768]{1,0:T(1,128)S(1)} %get-tuple-element.107.slot_ref, bf16[768,2048]{1,0:T(8,128)(2,1)S(1)} %copy-done, s32[1,768]{1,0:T(1,128)S(1)} %collective-permute-done.8.refs_1_.refs_0_, s32[1,768]{1,0:T(1,128)S(1)} %collective-permute-done.9.refs_2_.refs_1_, ...), custom_call_target="tpu_custom_call" | custom-call | flops 1000000000 | bytes 1 | tf_op jit(solution)/shard_map/sort/pallas_call | solution.py:88
  19.0 0.0 copy-start.3
  19.0 0.9 copy-done.3
  20.0 0.0 copy-done.1
  20.0 5.5 %base.1.refs_0_ = f32[768,1024]{1,0:T(8,128)} custom-call(bf16[768,2048]{1,0:T(8,128)(2,1)S(1)} %copy-done, bf16[2048,1024]{1,0:T(8,128)(2,1)S(1)} %copy-done.1, bf16[240,2048]{1,0:T(8,128)(2,1)S(1)} %get-tuple-element.108._), custom_call_target="tpu_custom_call" | custom-call | flops 1000000000 | bytes 1 | tf_op jit(solution)/shard_map/base/pallas_call | solution.py:169
  25.5 1.0 copy-done.2
  26.5 0.0 reduce-scatter.2.cloned.1.call-update
  26.5 2.1 %collective-permute-start.12 = (bf16[240,2048]{1,0:T(8,128)(2,1)}, bf16[240,2048]{1,0:T(8,128)(2,1)}, u32[]{:S(2)}, u32[]{:S(2)}) collective-permute-start(bf16[240,2048]{1,0:T(8,128)(2,1)} %copy-done.2), channel_id=1, source_target_pairs={{0,4},{4,0},{8,12},{12,8},{1,5},{5,1},{9,13},{13,9},{2,6},{6,2},{1... | collective-permute-start | bytes 2949128 | tf_op jit(solution)/shard_map/ppermute | solution.py:396
  28.6 0.1 collective-permute-start.13
  28.7 0.1 pad_add_fusion.here_ref
  28.7 3.2 %sort.4 = (bf16[288,2048]{1,0:T(8,128)(2,1)S(1)}, bf16[48,2048]{1,0:T(8,128)(2,1)S(1)}, bf16[48,2048]{1,0:T(8,128)(2,1)}, bf16[48,2048]{1,0:T(8,128)(2,1)}) custom-call(s32[1,768]{1,0:T(1,128)S(1)} %get-tuple-element.107.slot_ref, bf16[768,2048]{1,0:T(8,128)(2,1)S(1)} %copy-done, f32[768,1024]{1,0:T(8,128)} %base.1.refs_0_), custom_call_target="tpu_custom_call" | custom-call | flops 1000000000 | bytes 1 | tf_op jit(solution)/shard_map/sort/pallas_call | solution.py:88
  32.0 0.0 copy-done.5
  32.0 1.7 %name_rows.1 = (s32[288,1]{1,0:T(8,128)S(1)}, s32[240,1]{1,0:T(8,128)S(1)}, s32[240,1]{1,0:T(8,128)S(1)}, s32[768,1]{1,0:T(8,128)S(1)}, s32[240,1]{1,0:T(8,128)S...) custom-call(s32[2]{0:T(128)S(1)} %pad_add_fusion.here_ref, ...), custom_call_target="tpu_custom_call" | custom-call | flops 1000000000 | bytes 1 | tf_op jit(solution)/shard_map/name_rows/pallas_call | solution.py:144
  33.7 0.1 fusion
  33.8 10.5 %shrink.6 = (f32[144,128]{1,0:T(8,128)S(1)}, f32[144,128]{1,0:T(8,128)S(1)}) custom-call(s32[3]{0:T(128)S(1)} %get-tuple-element.137.plan_ref, s32[4,128]{1,0:T(4,128)S(1)} %get-tuple-element.111.ends_ref, s32[288,1]{1,0:T(8,128)S(1)} %get-tuple-element.112.which_ref, bf16[24,128,2048]{2,1,0:T(8,128)(2,1)} %down_ref.7, ...), custom_call_target="tpu_custom_call" | custom-call | flops 1000000000 | bytes 1 | tf_op jit(solution)/shard_map/shrink/pallas_call | solution.py:242
  44.3 6.8 %collective-permute-done.12.refs_0_ = bf16[240,2048]{1,0:T(8,128)(2,1)} collective-permute-done((bf16[240,2048]{1,0:T(8,128)(2,1)}, bf16[240,2048]{1,0:T(8,128)(2,1)}, u32[]{:S(2)}, u32[]{:S(2)}) %collective-permute-start.12) | collective-permute-done | bytes 983072 | tf_op jit(solution)/shard_map/ppermute | solution.py:396
  51.1 1.8 %sort.5.refs_2_ = bf16[240,2048]{1,0:T(8,128)(2,1)S(1)} custom-call(s32[1,768]{1,0:T(1,128)S(1)} %get-tuple-element.107.slot_ref, bf16[768,2048]{1,0:T(8,128)(2,1)S(1)} %copy-done, bf16[240,2048]{1,0:T(8,128)(2,1)} %collective-permute-done.12.refs_0_), custom_call_target="tpu_custom_call" | custom-call | flops 1000000000 | bytes 1 | tf_op jit(solution)/shard_map/sort/pallas_call | solution.py:88
  52.9 1.1 collective-permute-start.19
  54.0 0.0 slice-done
  54.0 0.0 slice-done.1
  54.0 0.0 slice-done.2
  54.0 7.3 %shrink.7 = (f32[120,128]{1,0:T(8,128)S(1)}, f32[120,128]{1,0:T(8,128)S(1)}) custom-call(s32[3]{0:T(128)S(1)} %get-tuple-element.136.plan_ref, s32[4,128]{1,0:T(4,128)S(1)} %get-tuple-element.111.ends_ref, s32[240,1]{1,0:T(8,128)S(1)} %get-tuple-element.115.which_ref, bf16[24,128,2048]{2,1,0:T(8,128)(2,1)S(1)} %bitcast.13, ...), custom_call_target="tpu_custom_call" | custom-call | flops 1000000000 | bytes 1 | tf_op jit(solution)/shard_map/shrink/pallas_call | solution.py:242
  61.3 11.4 %collective-permute-done.13.refs_0_ = bf16[240,2048]{1,0:T(8,128)(2,1)} collective-permute-done((bf16[240,2048]{1,0:T(8,128)(2,1)}, bf16[240,2048]{1,0:T(8,128)(2,1)}, u32[]{:S(2)}, u32[]{:S(2)}) %collective-permute-start.13) | collective-permute-done | bytes 983072 | tf_op jit(solution)/shard_map/ppermute | solution.py:396
  72.7 7.3 %shrink.8 = (f32[120,128]{1,0:T(8,128)S(1)}, f32[120,128]{1,0:T(8,128)S(1)}) custom-call(s32[3]{0:T(128)S(1)} %get-tuple-element.135.plan_ref, s32[4,128]{1,0:T(4,128)S(1)} %get-tuple-element.111.ends_ref, s32[240,1]{1,0:T(8,128)S(1)} %get-tuple-element.117.which_ref, bf16[24,128,2048]{2,1,0:T(8,128)(2,1)S(1)} %bitcast.13, ...), custom_call_target="tpu_custom_call" | custom-call | flops 1000000000 | bytes 1 | tf_op jit(solution)/shard_map/shrink/pallas_call | solution.py:242
  80.0 0.0 copy-start.12
  80.1 1.8 %collective-permute-start.15 = (f32[384,128]{1,0:T(8,128)S(1)}, f32[384,128]{1,0:T(8,128)S(1)}, u32[]{:S(2)}, u32[]{:S(2)}) collective-permute-start(f32[384,128]{1,0:T(8,128)S(1)} %constant_dynamic-update-slice_fusion.3), channel_id=1, source_target_pairs={{0,2},{1,3},{2,0},{3,1},{4,6},{5,7},{6,4},{7,5},{8,10},{9,11},{10,... | collective-permute-start | bytes 589832 | tf_op jit(solution)/shard_map/ppermute | solution.py:396
  81.8 0.0 collective-permute-start.16
  81.9 0.5 collective-permute-start.14
  82.4 4.5 %collective-permute-done.15.refs_2_ = f32[384,128]{1,0:T(8,128)S(1)} collective-permute-done((f32[384,128]{1,0:T(8,128)S(1)}, f32[384,128]{1,0:T(8,128)S(1)}, u32[]{:S(2)}, u32[]{:S(2)}) %collective-permute-start.15) | collective-permute-done | bytes 196640 | tf_op jit(solution)/shard_map/ppermute | solution.py:396
  86.9 2.1 %collective-permute-done.16.refs_3_ = f32[384,128]{1,0:T(8,128)S(1)} collective-permute-done((f32[384,128]{1,0:T(8,128)S(1)}, f32[384,128]{1,0:T(8,128)S(1)}, u32[]{:S(2)}, u32[]{:S(2)}) %collective-permute-start.16) | collective-permute-done | bytes 196640 | tf_op jit(solution)/shard_map/ppermute | solution.py:396
  89.0 0.0 collective-permute-done.14.refs_1_
  89.1 0.0 copy-done.6
  89.1 0.0 copy-done.10
  89.1 2.3 %expand.4 = (f32[288,256]{1,0:T(8,128)S(1)}, s16[256,256]{1,0:T(8,128)(2,1)S(1)}, s16[256,256]{1,0:T(8,128)(2,1)S(1)}) custom-call(s32[768,1]{1,0:T(8,128)S(1)} %get-tuple-element.109.which_ref, f32[1,24]{1,0:T(1,128)S(1)} %bitcast.17, bf16[1536,256]{1,0:T(8,128)(2,1)S(1)} %bitcast.14, f32[384,128]{1,0:T(8,128)S(1)} %constant_dynamic-update-slice_fusion.refs_0_, ...), custom_call_target="tpu_custom_call" | custom-call | flops 1000000000 | bytes 1 | tf_op jit(solution)/shard_map/expand/pallas_call | solution.py:336
  91.4 0.8 place.1.refs_2_
  92.2 21.0 %collective-permute-done.19.refs_0_ = bf16[240,2048]{1,0:T(8,128)(2,1)S(1)} collective-permute-done((bf16[240,2048]{1,0:T(8,128)(2,1)S(1)}, bf16[240,2048]{1,0:T(8,128)(2,1)S(1)}, u32[]{:S(2)}, u32[]{:S(2)}) %collective-permute-start.19) | collective-permute-done | bytes 983072 | tf_op jit(solution)/shard_map/ppermute | solution.py:396
  113.3 6.7 %shrink.9 = (f32[120,128]{1,0:T(8,128)S(1)}, f32[120,128]{1,0:T(8,128)S(1)}) custom-call(s32[3]{0:T(128)S(1)} %get-tuple-element.134.plan_ref, s32[4,128]{1,0:T(4,128)S(1)} %get-tuple-element.111.ends_ref, s32[240,1]{1,0:T(8,128)S(1)} %get-tuple-element.126.which_ref, bf16[24,128,2048]{2,1,0:T(8,128)(2,1)S(1)} %bitcast.13, ...), custom_call_target="tpu_custom_call" | custom-call | flops 1000000000 | bytes 1 | tf_op jit(solution)/shard_map/shrink/pallas_call | solution.py:242
  120.0 1.6 %collective-permute-start.20 = (f32[120,128]{1,0:T(8,128)S(1)}, f32[120,128]{1,0:T(8,128)S(1)}, u32[]{:S(2)}, u32[]{:S(2)}) collective-permute-start(f32[120,128]{1,0:T(8,128)S(1)} %get-tuple-element.128), channel_id=1, source_target_pairs={{0,2},{2,0},{1,3},{3,1},{4,6},{6,4},{5,7},{7,5},{8,10},{10,8},{9,1... | collective-permute-start | bytes 184328 | tf_op jit(solution)/shard_map/ppermute | solution.py:396
  121.5 2.7 %collective-permute-done.20 = f32[120,128]{1,0:T(8,128)S(1)} collective-permute-done((f32[120,128]{1,0:T(8,128)S(1)}, f32[120,128]{1,0:T(8,128)S(1)}, u32[]{:S(2)}, u32[]{:S(2)}) %collective-permute-start.20) | collective-permute-done | bytes 61472 | tf_op jit(solution)/shard_map/ppermute | solution.py:396
  124.3 0.1 collective-permute-start.21
  124.3 0.1 collective-permute-start.17
  124.4 2.6 %collective-permute-start.18 = (s16[256,256]{1,0:T(8,128)(2,1)S(1)}, s16[256,256]{1,0:T(8,128)(2,1)S(1)}, u32[]{:S(2)}, u32[]{:S(2)}) collective-permute-start(s16[256,256]{1,0:T(8,128)(2,1)S(1)} %get-tuple-element.125), channel_id=1, source_target_pairs={{0,12},{4,8},{8,4},{12,0},{1,13},{5,9},{9,5},{13,1},{2,14},{6,10},... | collective-permute-start | bytes 393224 | tf_op jit(solution)/shard_map/ppermute | solution.py:396
  127.0 0.0 collective-permute-done.21.refs_1_
  127.0 0.9 expand.5
  128.0 0.9 collective-permute-start.22
  128.9 1.5 %collective-permute-start.11 = (s32[1,128]{1,0:T(1,128)S(1)}, s32[1,128]{1,0:T(1,128)S(1)}, u32[]{:S(2)}, u32[]{:S(2)}) collective-permute-start(s32[1,128]{1,0:T(1,128)S(1)} %get-tuple-element.105), channel_id=1, source_target_pairs={{0,16},{16,0},{1,17},{17,1},{2,18},{18,2},{3,19},{19,3},{4,20},{20... | collective-permute-start | bytes 1544 | tf_op jit(solution)/shard_map/ppermute | solution.py:396
  130.4 2.0 %collective-permute-done.11 = s32[1,128]{1,0:T(1,128)S(1)} collective-permute-done((s32[1,128]{1,0:T(1,128)S(1)}, s32[1,128]{1,0:T(1,128)S(1)}, u32[]{:S(2)}, u32[]{:S(2)}) %collective-permute-start.11) | collective-permute-done | bytes 544 | tf_op jit(solution)/shard_map/ppermute | solution.py:396
  132.5 0.0 collective-permute-done.17
  132.5 1.7 %collective-permute-done.18 = s16[256,256]{1,0:T(8,128)(2,1)S(1)} collective-permute-done((s16[256,256]{1,0:T(8,128)(2,1)S(1)}, s16[256,256]{1,0:T(8,128)(2,1)S(1)}, u32[]{:S(2)}, u32[]{:S(2)}) %collective-permute-start.18) | collective-permute-done | bytes 131104 | tf_op jit(solution)/shard_map/ppermute | solution.py:396
  134.2 5.7 %collective-permute-done.22 = s16[256,256]{1,0:T(8,128)(2,1)S(1)} collective-permute-done((s16[256,256]{1,0:T(8,128)(2,1)S(1)}, s16[256,256]{1,0:T(8,128)(2,1)S(1)}, u32[]{:S(2)}, u32[]{:S(2)}) %collective-permute-start.22) | collective-permute-done | bytes 131104 | tf_op jit(solution)/shard_map/ppermute | solution.py:396
  139.9 2.2 %conditional.1 = (bf16[768,256]{1,0:T(8,128)(2,1)S(1)}) conditional(s32[]{:T(128)} %bitcast.3, (s32[768,1]{1,0:T(8,128)S(1)}, f32[768,256]{1,0:T(8,128)}, f32[768,256]{1,0:T(8,128)S(1)}, s16[256,256]{1,0:T(8,128)(2,1)S(1)}, s16[256,256]{1,0:T(8,128)(2,1)S(1)}, /*index=5*/s16[256,256]{1,0:T(8,128)(2,1)S(1)}) %tuple.28, (s32[18]{0:T(128)S(1)}, ...), branch_computations={%region_1.0_spmd, %region_2.0_spmd} | conditional | flops 3000009216 | bytes 6328759 | solution.py:504
  139.9 2.0 %merge.2 = bf16[768,256]{1,0:T(8,128)(2,1)S(1)} custom-call(s32[768,1]{1,0:T(8,128)S(1)} %get-tuple-element.51.target_ref, f32[768,256]{1,0:T(8,128)} %get-tuple-element.52.refs_0_, f32[768,256]{1,0:T(8,128)S(1)} %get-tuple-element.53.refs_1_, s16[256,256]{1,0:T(8,128)(2,1)S(1)} %get-tuple-element.54.refs_2_, s16[256,256]{1,0:T(8,128)(2,1)S(1)} %get-tuple-element.55.refs_3_, ...), custom_call_target="tpu_custom_call" | custom-call | flops 1000000000 | bytes 1 | tf_op jit(solution)/shard_map/cond/branch_0_fun/merge/pallas_call | solution.py:386
  142.0 0.0 copy-start.11
  142.0 0.7 copy-done.11
  (24 shorter events, 0.1 us)
Async XLA Ops:
  6.5 9.8 %copy-start = (bf16[768,2048]{1,0:T(8,128)(2,1)S(1)}, bf16[768,2048]{1,0:T(8,128)(2,1)}, u32[]{:S(2)}) copy-start(bf16[768,2048]{1,0:T(8,128)(2,1)} %tok_ref.7) | copy-start | bytes 9437188
  6.5 133.3 %reduce-scatter.2.cloned.1.call-start = ((), (), s32[]{:S(2)}) async-start(), calls=%async_computation.1 | async-start | bytes 3932160 | tf_op jit(solution)/shard_map/reduce_scatter | solution.py:432
  6.5 8.0 %collective-permute-start.10 = (s32[1,768]{1,0:T(1,128)}, s32[1,768]{1,0:T(1,128)S(1)}, u32[]{:S(2)}, u32[]{:S(2)}) collective-permute-start(s32[1,768]{1,0:T(1,128)} %bitcast.7), channel_id=1, source_target_pairs={{0,12},{4,8},{8,4},{12,0},{1,13},{5,9},{9,5},{13,1},{2,14},{6,10},... | collective-permute-start | bytes 9224 | tf_op jit(solution)/shard_map/ppermute | solution.py:396
  11.6 3.8 %collective-permute-start.8 = (s32[1,768]{1,0:T(1,128)}, s32[1,768]{1,0:T(1,128)S(1)}, u32[]{:S(2)}, u32[]{:S(2)}) collective-permute-start(s32[1,768]{1,0:T(1,128)} %bitcast.8), channel_id=1, source_target_pairs={{0,4},{4,0},{8,12},{12,8},{1,5},{5,1},{9,13},{13,9},{2,6},{6,2},{1... | collective-permute-start | bytes 9224 | tf_op jit(solution)/shard_map/ppermute | solution.py:396
  11.6 4.7 %collective-permute-start.9 = (s32[1,768]{1,0:T(1,128)}, s32[1,768]{1,0:T(1,128)S(1)}, u32[]{:S(2)}, u32[]{:S(2)}) collective-permute-start(s32[1,768]{1,0:T(1,128)} %bitcast.9), channel_id=1, source_target_pairs={{0,8},{4,12},{8,0},{12,4},{1,9},{5,13},{9,1},{13,5},{2,10},{6,14},... | collective-permute-start | bytes 9224 | tf_op jit(solution)/shard_map/ppermute | solution.py:396
  12.2 0.7 copy-start.4
  12.9 7.1 %copy-start.1 = (bf16[2048,1024]{1,0:T(8,128)(2,1)S(1)}, bf16[2048,1024]{1,0:T(8,128)(2,1)}, u32[]{:S(2)}) copy-start(bf16[2048,1024]{1,0:T(8,128)(2,1)} %weight_ref.1) | copy-start | bytes 12582916
  19.0 0.9 copy-start.3
  25.5 1.0 copy-start.2
  26.5 24.6 %collective-permute-start.12 = (bf16[240,2048]{1,0:T(8,128)(2,1)}, bf16[240,2048]{1,0:T(8,128)(2,1)}, u32[]{:S(2)}, u32[]{:S(2)}) collective-permute-start(bf16[240,2048]{1,0:T(8,128)(2,1)} %copy-done.2), channel_id=1, source_target_pairs={{0,4},{4,0},{8,12},{12,8},{1,5},{5,1},{9,13},{13,9},{2,6},{6,2},{1... | collective-permute-start | bytes 2949128 | tf_op jit(solution)/shard_map/ppermute | solution.py:396
  28.6 44.2 %collective-permute-start.13 = (bf16[240,2048]{1,0:T(8,128)(2,1)}, bf16[240,2048]{1,0:T(8,128)(2,1)}, u32[]{:S(2)}, u32[]{:S(2)}) collective-permute-start(bf16[240,2048]{1,0:T(8,128)(2,1)} %copy-done.3), channel_id=1, source_target_pairs={{0,12},{4,8},{8,4},{12,0},{1,13},{5,9},{9,5},{13,1},{2,14},{6,10},... | collective-permute-start | bytes 2949128 | tf_op jit(solution)/shard_map/ppermute | solution.py:396
  28.7 3.2 %copy-start.5 = (s32[768,1]{0,1:T(1,128)S(1)}, s32[768,1]{0,1:T(1,128)}, u32[]{:S(2)}) copy-start(s32[768,1]{0,1:T(1,128)} %param.13) | copy-start | bytes 9220
  32.0 22.1 %slice-start = ((s8[12582912]{0:T(1024)(128)(4,1)}), s8[4194304]{0:T(1024)(128)(4,1)S(1)}, s32[]{:S(2)}) async-start(s8[12582912]{0:T(1024)(128)(4,1)} %bitcast.12), calls=%async_computation.2 | async-start | bytes 8388608
  33.7 20.3 %slice-start.1 = ((s8[12582912]{0:T(1024)(128)(4,1)}), s8[4194304]{0:T(1024)(128)(4,1)S(1)}, s32[]{:S(2)}) async-start(s8[12582912]{0:T(1024)(128)(4,1)} %bitcast.12), calls=%async_computation.3 | async-start | bytes 8388608
  33.8 20.3 %slice-start.2 = ((s8[12582912]{0:T(1024)(128)(4,1)}), s8[4194304]{0:T(1024)(128)(4,1)S(1)}, s32[]{:S(2)}) async-start(s8[12582912]{0:T(1024)(128)(4,1)} %bitcast.12), calls=%async_computation.4 | async-start | bytes 8388608
  52.9 60.4 %collective-permute-start.19 = (bf16[240,2048]{1,0:T(8,128)(2,1)S(1)}, bf16[240,2048]{1,0:T(8,128)(2,1)S(1)}, u32[]{:S(2)}, u32[]{:S(2)}) collective-permute-start(bf16[240,2048]{1,0:T(8,128)(2,1)S(1)} %sort.5.refs_2_), channel_id=1, source_target_pairs={{0,8},{4,12},{8,0},{12,4},{1,9},{5,13},{9,1},{13,5},{2,10},{6,14},... | collective-permute-start | bytes 2949128 | tf_op jit(solution)/shard_map/ppermute | solution.py:396
  72.7 16.3 %copy-start.6 = (bf16[24,64,256]{2,1,0:T(8,128)(2,1)S(1)}, bf16[24,64,256]{2,1,0:T(8,128)(2,1)}, u32[]{:S(2)}) copy-start(bf16[24,64,256]{2,1,0:T(8,128)(2,1)} %param.11) | copy-start | bytes 2359300
  72.7 16.3 %copy-start.10 = (f32[24]{0:T(128)S(1)}, f32[24]{0:T(128)}, u32[]{:S(2)}) copy-start(f32[24]{0:T(128)} %param.12) | copy-start | bytes 292
  80.0 11.3 %copy-start.12 = (s32[768,1]{1,0:T(8,128)S(1)}, s32[768,1]{1,0:T(8,128)}, u32[]{:S(2)}) copy-start(s32[768,1]{1,0:T(8,128)} %get-tuple-element.106.target_ref) | copy-start | bytes 9220
  80.1 6.8 %collective-permute-start.15 = (f32[384,128]{1,0:T(8,128)S(1)}, f32[384,128]{1,0:T(8,128)S(1)}, u32[]{:S(2)}, u32[]{:S(2)}) collective-permute-start(f32[384,128]{1,0:T(8,128)S(1)} %constant_dynamic-update-slice_fusion.3), channel_id=1, source_target_pairs={{0,2},{1,3},{2,0},{3,1},{4,6},{5,7},{6,4},{7,5},{8,10},{9,11},{10,... | collective-permute-start | bytes 589832 | tf_op jit(solution)/shard_map/ppermute | solution.py:396
  81.8 7.2 %collective-permute-start.16 = (f32[384,128]{1,0:T(8,128)S(1)}, f32[384,128]{1,0:T(8,128)S(1)}, u32[]{:S(2)}, u32[]{:S(2)}) collective-permute-start(f32[384,128]{1,0:T(8,128)S(1)} %constant_dynamic-update-slice_fusion.3), channel_id=1, source_target_pairs={{0,3},{1,2},{2,1},{3,0},{4,7},{5,6},{6,5},{7,4},{8,11},{9,10},{10,... | collective-permute-start | bytes 589832 | tf_op jit(solution)/shard_map/ppermute | solution.py:396
  81.9 7.2 %collective-permute-start.14 = (f32[384,128]{1,0:T(8,128)S(1)}, f32[384,128]{1,0:T(8,128)S(1)}, u32[]{:S(2)}, u32[]{:S(2)}) collective-permute-start(f32[384,128]{1,0:T(8,128)S(1)} %constant_dynamic-update-slice_fusion.refs_0_), channel_id=1, source_target_pairs={{0,1},{1,0},{2,3},{3,2},{4,5},{5,4},{6,7},{7,6},{8,9},{9,8},{10,11... | collective-permute-start | bytes 589832 | tf_op jit(solution)/shard_map/ppermute | solution.py:396
  119.9 19.9 %copy-start.8 = (bf16[48,2048]{1,0:T(8,128)(2,1)S(1)}, bf16[48,2048]{1,0:T(8,128)(2,1)}, u32[]{:S(2)}) copy-start(bf16[48,2048]{1,0:T(8,128)(2,1)} %get-tuple-element.130) | copy-start | bytes 589828
  120.0 19.9 %copy-start.9 = (bf16[48,2048]{1,0:T(8,128)(2,1)S(1)}, bf16[48,2048]{1,0:T(8,128)(2,1)}, u32[]{:S(2)}) copy-start(bf16[48,2048]{1,0:T(8,128)(2,1)} %get-tuple-element.131) | copy-start | bytes 589828
  120.0 4.3 %collective-permute-start.20 = (f32[120,128]{1,0:T(8,128)S(1)}, f32[120,128]{1,0:T(8,128)S(1)}, u32[]{:S(2)}, u32[]{:S(2)}) collective-permute-start(f32[120,128]{1,0:T(8,128)S(1)} %get-tuple-element.128), channel_id=1, source_target_pairs={{0,2},{2,0},{1,3},{3,1},{4,6},{6,4},{5,7},{7,5},{8,10},{10,8},{9,1... | collective-permute-start | bytes 184328 | tf_op jit(solution)/shard_map/ppermute | solution.py:396
  124.3 2.8 %collective-permute-start.21 = (f32[120,128]{1,0:T(8,128)S(1)}, f32[120,128]{1,0:T(8,128)S(1)}, u32[]{:S(2)}, u32[]{:S(2)}) collective-permute-start(f32[120,128]{1,0:T(8,128)S(1)} %add.12.refs_0_), channel_id=1, source_target_pairs={{0,1},{1,0},{2,3},{3,2},{4,5},{5,4},{6,7},{7,6},{8,9},{9,8},{10,11... | collective-permute-start | bytes 184328 | tf_op jit(solution)/shard_map/ppermute | solution.py:396
  124.3 8.2 %collective-permute-start.17 = (s16[256,256]{1,0:T(8,128)(2,1)S(1)}, s16[256,256]{1,0:T(8,128)(2,1)S(1)}, u32[]{:S(2)}, u32[]{:S(2)}) collective-permute-start(s16[256,256]{1,0:T(8,128)(2,1)S(1)} %get-tuple-element.124), channel_id=1, source_target_pairs={{0,4},{4,0},{8,12},{12,8},{1,5},{5,1},{9,13},{13,9},{2,6},{6,2},{1... | collective-permute-start | bytes 393224 | tf_op jit(solution)/shard_map/ppermute | solution.py:396
  124.4 9.8 %collective-permute-start.18 = (s16[256,256]{1,0:T(8,128)(2,1)S(1)}, s16[256,256]{1,0:T(8,128)(2,1)S(1)}, u32[]{:S(2)}, u32[]{:S(2)}) collective-permute-start(s16[256,256]{1,0:T(8,128)(2,1)S(1)} %get-tuple-element.125), channel_id=1, source_target_pairs={{0,12},{4,8},{8,4},{12,0},{1,13},{5,9},{9,5},{13,1},{2,14},{6,10},... | collective-permute-start | bytes 393224 | tf_op jit(solution)/shard_map/ppermute | solution.py:396
  128.0 11.9 %collective-permute-start.22 = (s16[256,256]{1,0:T(8,128)(2,1)S(1)}, s16[256,256]{1,0:T(8,128)(2,1)S(1)}, u32[]{:S(2)}, u32[]{:S(2)}) collective-permute-start(s16[256,256]{1,0:T(8,128)(2,1)S(1)} %expand.5), channel_id=1, source_target_pairs={{0,8},{4,12},{8,0},{12,4},{1,9},{5,13},{9,1},{13,5},{2,10},{6,14},... | collective-permute-start | bytes 393224 | tf_op jit(solution)/shard_map/ppermute | solution.py:396
  128.9 3.5 %collective-permute-start.11 = (s32[1,128]{1,0:T(1,128)S(1)}, s32[1,128]{1,0:T(1,128)S(1)}, u32[]{:S(2)}, u32[]{:S(2)}) collective-permute-start(s32[1,128]{1,0:T(1,128)S(1)} %get-tuple-element.105), channel_id=1, source_target_pairs={{0,16},{16,0},{1,17},{17,1},{2,18},{18,2},{3,19},{19,3},{4,20},{20... | collective-permute-start | bytes 1544 | tf_op jit(solution)/shard_map/ppermute | solution.py:396
  142.0 0.7 copy-start.11
Sparse Core Ops, SparseCore 0:
  26.6 37.6 reduce-scatter.1

commit v8 on v7

--- a/solution.py
+++ b/solution.py
@@ -14,7 +14,7 @@
 BF16 = jnp.bfloat16
 I32 = jnp.int32
 ANYWHERE = pl.BlockSpec(memory_space=pl.ANY)
-COST = pl.CostEstimate(flops=10**9, transcendentals=0, bytes_accessed=1)
+COST = pl.CostEstimate(flops=1, transcendentals=0, bytes_accessed=1)
 PARAMS = pltpu.CompilerParams(vmem_limit_bytes=VMEM_LIMIT)
 
 
@@ -175,7 +175,7 @@
             ANYWHERE,
         ],
         out_specs=pl.BlockSpec((rows, step), lambda i: (0, i)),
-        out_shape=jax.ShapeDtypeStruct((rows, columns), F32),
+        out_shape=pltpu.HBM((rows, columns), F32),
         compiler_params=PARAMS,
         cost_estimate=COST,
         name="base",
@@ -272,8 +272,8 @@
     return parts + [x]
 
 
-def expand_kernel(groups, sizes, heard, which_ref, scale_ref, up_ref, *refs):
-    lines, outs = refs[:heard], refs[heard:]
+def expand_kernel(groups, sizes, heard, waits, which_ref, scale_ref, up_ref, *refs):
+    lines, outs = refs[:heard], refs[heard + waits :]
     total = lines[0][...]
     for line in lines[1:]:
         total = total + line[...]
@@ -325,7 +325,7 @@
     return jnp.exp2(power).astype(BF16).astype(F32)
 
 
-def expand(lines, groups, names, scale, up, sizes, kept=0):
+def expand(lines, groups, names, scale, up, sizes, kept=0, later_than=()):
     columns = up.shape[1]
     shapes = [
         jax.ShapeDtypeStruct((s, columns), F32)
@@ -334,12 +334,14 @@
         for i, s in enumerate(sizes)
     ]
     return pl.pallas_call(
-        functools.partial(expand_kernel, groups, sizes, len(lines)),
+        functools.partial(expand_kernel, groups, sizes, len(lines), len(later_than)),
+        in_specs=[pl.BlockSpec(memory_space=pltpu.VMEM)] * (3 + len(lines))
+        + [ANYWHERE] * len(later_than),
         out_shape=shapes,
         compiler_params=PARAMS,
         cost_estimate=COST,
         name="expand",
-    )(names, scale, up, *lines)
+    )(names, scale, up, *lines, *later_than)
 
 
 def place_kernel(begin, target_ref, rows_ref, out_ref):
@@ -417,10 +419,11 @@
     if owners == 4:
         usual = up_to_16(cap * 5 // 6)
         near = (1, 0, usual)
-        far, last = [(3, 0, usual)], [(2, 0, usual)]
+        first = up_to_16(usual * 3 // 5)
+        far, last = [(3, 0, usual)], [[(2, 0, first)], [(2, first, usual - first)]]
         extra = [(j, usual, cap - usual) for j in (3, 2, 1)]
     else:
-        usual, far, last, extra = cap, [], [(j, 0, cap) for j in range(2, owners)], []
+        usual, far, last, extra = cap, [], [[(j, 0, cap) for j in range(2, owners)]], []
 
     ids_row = token_adapter_index.reshape(1, rows)
     ids_heard = [ids_row] + [swap(ids_row, "dp", owners, j) for j in range(1, owners)]
@@ -431,11 +434,12 @@
     base_part = base_product(tokens, key_value_weight, packed[near])
     base = lax.psum_scatter(base_part, feature_axes, scatter_dimension=1, tiled=True)
     packed |= zip([own] + extra, sort_rows(tokens, slot, cap, [own] + extra, (base_part,)))
-    packed |= zip(last, sort_rows(tokens, slot, cap, last, (received[near],)))
-    received |= {p: swap(packed[p], "dp", owners, p[0]) for p in last}
+    gated = [p for pieces in last for p in pieces]
+    packed |= zip(gated, sort_rows(tokens, slot, cap, gated, (received[near],)))
+    received |= {p: swap(packed[p], "dp", owners, p[0]) for p in gated}
 
     early = [own, near] + far
-    sets = [[p] for p in early] + [early, last] + ([extra] if extra else [])
+    sets = [[p] for p in early] + [early] + last + ([extra] if extra else [])
     here = jnp.stack([me.astype(I32), half])
     names, ends, plans, largest = name_rows(ids_heard, here, owned, sets)
 
@@ -453,10 +457,10 @@
             for d in range(1, sharers)
         ]
 
-    def deltas_of(pieces, blocks, names, ends, plan, down, up, scale, later_than, steps=2):
+    def deltas_of(pieces, blocks, names, ends, plan, down, up, scale, later_than):
         mine, other = shrink(pieces, blocks, names, ends, plan, down, later_than)
         sizes = tuple(b.shape[0] for b in blocks)
-        lines = exchange(mine, other, steps)
+        lines = exchange(mine, other)
         return expand(lines, (mine.shape[0],), names, scale, up, sizes)
 
     def send_back(pieces, deltas):
@@ -473,19 +477,22 @@
         shares.append(
             shrink([p], [rows_here], names[k], ends, plans[k], adapter_down_weight, waits)
         )
-        waits = (shares[-1][0], packed[last[0]])
+        waits = (shares[-1][0], packed[gated[0]])
     lines = exchange(*(jnp.concatenate(pair, axis=0) for pair in zip(*shares)), steps=1)
     sizes = tuple(p[2] for p in early)
     here = len(early)
     deltas = expand(lines, tuple(c // 2 for c in sizes), names[here], scale, up, sizes, kept=1)
     parts = [base, place_rows(target, own[0] * cap, deltas[0])]
     returned = send_back(early[1:], deltas[1:])
-    blocks = [received[p] for p in last]
-    deltas = deltas_of(
-        last, blocks, names[here + 1], ends, plans[here + 1], *weights, (deltas[0], parts[1])
-    )
-    returned += send_back(last, deltas)
-    done = early[1:] + last
+    done = early[1:]
+    for k, pieces in enumerate(last):
+        blocks = [received[p] for p in pieces]
+        waits = (deltas[0], parts[1])
+        deltas = deltas_of(
+            pieces, blocks, names[here + 1 + k], ends, plans[here + 1 + k], *weights, waits
+        )
+        returned += send_back(pieces, deltas)
+        done += pieces
 
     def finish(parts, target, returned, *_):
         return merge(parts, target, begins(done), returned, BF16)

time: 150 us -> 148 us (0.987)
  waiting for transfers between devices: 59.8 us -> 27.9 us
  starting transfers between devices: 17.9 us -> 39.8 us
  local copies, waits for them, and re-layouts: 3.53 us -> 9.95 us
  Pallas kernels: 54.4 us -> 56 us
    ppermute x15 -> x19, waiting for transfers between devices: 59.8 us -> 27.9 us  [swap(): return lax.ppermute(x, axes, [(i, i ^ distance) for i in range(size)])]
    ppermute x15 -> x19, starting transfers between devices: 17.9 us -> 39.8 us  [swap(): return lax.ppermute(x, axes, [(i, i ^ distance) for i in range(size)])]
    unnamed x33 -> x45, local copies, waits for them, and re-layouts: 3.45 us -> 9.86 us
    pallas_call x4 -> x5, Pallas kernels: 31.8 us -> 33.7 us  [shrink(): pl.pallas_call(functools.partial(shrink_kernel, pieces, group, fine), gri...]
    pallas_call x2 -> x3, Pallas kernels: 3.24 us -> 3.69 us  [expand(): pl.pallas_call(functools.partial(expand_kernel, groups, sizes, len(lines)...]
  transfers between devices with their start and end apart: 16 -> 20, of which waited for: 11 -> 10; matrix products, arithmetic and copies ran while one was open for 0% -> 0% of each run, Pallas kernels for 30% -> 31%
where the time goes in v8:
time: 148 us
  Pallas kernels  56 us (38%)
  starting transfers between devices  39.8 us (27%)
  waiting for transfers between devices  27.9 us (19%)
  between operations  13.8 us (9%)
  local copies, waits for them, and re-layouts  9.95 us (7%)
    ppermute x19, starting transfers between devices, swap(): return lax.ppermute(x, axes, [(i, i ^ distance) for i in range(size)])  39.8 us
    pallas_call x5, Pallas kernels, shrink(): pl.pallas_call(functools.partial(shrink_kernel, pieces, group, fine), gri...  33.7 us
    ppermute x19, waiting for transfers between devices, swap(): return lax.ppermute(x, axes, [(i, i ^ distance) for i in range(size)])  27.9 us
    unnamed x45, local copies, waits for them, and re-layouts  9.86 us
    pallas_call x3, Pallas kernels, sort_rows(): pl.pallas_call(functools.partial(sort_kernel, cap, pieces, len(later_than...  7.77 us
    pallas_call x1, Pallas kernels, base_product(): pl.pallas_call(base_kernel, grid=(columns // step,), in_specs=[pl.BlockSp...  5.48 us
    pallas_call x3, Pallas kernels, expand(): pl.pallas_call(functools.partial(expand_kernel, groups, sizes, len(lines)...  3.69 us
  transfers between devices with their start and end apart: 20, of which 10 were waited for; matrix products, arithmetic and copies ran while one was open for 0% of the time, Pallas kernels for 31%

profile of v8, /device:TPU:0, one launch (start us, length us, event | category | flops | bytes accessed | tf_op | source)
XLA Modules:
  0.0 147.8 jit_solution(3390129475443788189)
XLA Ops:
  6.5 5.0 %collective-permute-start.10 = (s32[1,768]{1,0:T(1,128)}, s32[1,768]{1,0:T(1,128)S(1)}, u32[]{:S(2)}, u32[]{:S(2)}) collective-permute-start(s32[1,768]{1,0:T(1,128)} %bitcast.7), channel_id=1, source_target_pairs={{0,12},{4,8},{8,4},{12,0},{1,13},{5,9},{9,5},{13,1},{2,14},{6,10},... | collective-permute-start | bytes 9224 | tf_op jit(solution)/shard_map/ppermute | solution.py:398
  11.6 0.0 collective-permute-start.8
  11.6 0.6 collective-permute-start.9
  12.2 0.7 copy-done.5
  12.9 0.9 route.1
  13.7 0.0 collective-permute-done.10.refs_3_.refs_2_
  13.8 1.6 %collective-permute-done.8.refs_1_.refs_0_ = s32[1,768]{1,0:T(1,128)S(1)} collective-permute-done((s32[1,768]{1,0:T(1,128)}, s32[1,768]{1,0:T(1,128)S(1)}, u32[]{:S(2)}, u32[]{:S(2)}) %collective-permute-start.8) | collective-permute-done | bytes 3104 | tf_op jit(solution)/shard_map/ppermute | solution.py:398
  15.4 0.9 collective-permute-done.9.refs_2_.refs_1_
  16.3 1.9 %copy-done = bf16[768,2048]{1,0:T(8,128)(2,1)S(1)} copy-done((bf16[768,2048]{1,0:T(8,128)(2,1)S(1)}, bf16[768,2048]{1,0:T(8,128)(2,1)}, u32[]{:S(2)}) %copy-start) | copy-done | bytes 3145752
  18.2 2.7 %sort.3 = (bf16[240,2048]{1,0:T(8,128)(2,1)S(1)}, bf16[240,2048]{1,0:T(8,128)(2,1)S(1)}) custom-call(s32[1,768]{1,0:T(1,128)S(1)} %get-tuple-element.118.slot_ref, bf16[768,2048]{1,0:T(8,128)(2,1)S(1)} %copy-done, s32[1,768]{1,0:T(1,128)S(1)} %collective-permute-done.8.refs_1_.refs_0_, s32[1,768]{1,0:T(1,128)S(1)} %collective-permute-done.9.refs_2_.refs_1_, ...), custom_call_target="tpu_custom_call" | custom-call | flops 1 | bytes 1 | tf_op jit(solution)/shard_map/sort/pallas_call | solution.py:88
  20.9 0.9 copy-done.7
  21.9 2.2 %copy-done.3 = bf16[2048,1024]{1,0:T(8,128)(2,1)S(1)} copy-done((bf16[2048,1024]{1,0:T(8,128)(2,1)S(1)}, bf16[2048,1024]{1,0:T(8,128)(2,1)}, u32[]{:S(2)}) %copy-start.3) | copy-done | bytes 4194328
  24.1 5.5 %base.1.refs_0_ = f32[768,1024]{1,0:T(8,128)} custom-call(bf16[768,2048]{1,0:T(8,128)(2,1)S(1)} %copy-done.1, bf16[2048,1024]{1,0:T(8,128)(2,1)S(1)} %copy-done.3, bf16[240,2048]{1,0:T(8,128)(2,1)S(1)} %get-tuple-element.119._), custom_call_target="tpu_custom_call" | custom-call | flops 1 | bytes 1 | tf_op jit(solution)/shard_map/base/pallas_call | solution.py:169
  29.5 1.0 copy-done.4
  30.5 0.0 reduce-scatter.2.cloned.1.call-update
  30.5 2.1 %collective-permute-start.12 = (bf16[240,2048]{1,0:T(8,128)(2,1)}, bf16[240,2048]{1,0:T(8,128)(2,1)}, u32[]{:S(2)}, u32[]{:S(2)}) collective-permute-start(bf16[240,2048]{1,0:T(8,128)(2,1)} %copy-done.4), channel_id=1, source_target_pairs={{0,4},{4,0},{8,12},{12,8},{1,5},{5,1},{9,13},{13,9},{2,6},{6,2},{1... | collective-permute-start | bytes 2949128 | tf_op jit(solution)/shard_map/ppermute | solution.py:398
  32.6 0.0 collective-permute-start.13
  32.6 0.1 pad_add_fusion.here_ref
  32.7 1.9 %copy-done.2 = f32[768,1024]{1,0:T(8,128)S(1)} copy-done((f32[768,1024]{1,0:T(8,128)S(1)}, f32[768,1024]{1,0:T(8,128)}, u32[]{:S(2)}) %copy-start.2) | copy-done | bytes 3145752
  34.6 3.2 %sort.4 = (bf16[288,2048]{1,0:T(8,128)(2,1)S(1)}, bf16[48,2048]{1,0:T(8,128)(2,1)}, bf16[48,2048]{1,0:T(8,128)(2,1)}, bf16[48,2048]{1,0:T(8,128)(2,1)}) custom-call(s32[1,768]{1,0:T(1,128)S(1)} %get-tuple-element.118.slot_ref, bf16[768,2048]{1,0:T(8,128)(2,1)S(1)} %copy-done.1, f32[768,1024]{1,0:T(8,128)S(1)} %copy-done.2), custom_call_target="tpu_custom_call" | custom-call | flops 1 | bytes 1 | tf_op jit(solution)/shard_map/sort/pallas_call | solution.py:88
  37.8 1.7 %name_rows.1 = (s32[288,1]{1,0:T(8,128)S(1)}, s32[240,1]{1,0:T(8,128)S(1)}, s32[240,1]{1,0:T(8,128)S(1)}, s32[768,1]{1,0:T(8,128)S(1)}, s32[144,1]{1,0:T(8,128)S...) custom-call(s32[2]{0:T(128)S(1)} %pad_add_fusion.here_ref, ...), custom_call_target="tpu_custom_call" | custom-call | flops 1 | bytes 1 | tf_op jit(solution)/shard_map/name_rows/pallas_call | solution.py:144
  39.6 0.1 fusion
  39.6 0.4 copy-done.13
  40.1 10.5 %shrink.7 = (f32[144,128]{1,0:T(8,128)S(1)}, f32[144,128]{1,0:T(8,128)S(1)}) custom-call(s32[3]{0:T(128)S(1)} %get-tuple-element.154.plan_ref, s32[4,128]{1,0:T(4,128)S(1)} %get-tuple-element.122.ends_ref, s32[288,1]{1,0:T(8,128)S(1)} %get-tuple-element.123.which_ref, bf16[24,128,2048]{2,1,0:T(8,128)(2,1)} %down_ref.9, ...), custom_call_target="tpu_custom_call" | custom-call | flops 1 | bytes 1 | tf_op jit(solution)/shard_map/shrink/pallas_call | solution.py:242
  50.6 4.7 %collective-permute-done.12.refs_0_ = bf16[240,2048]{1,0:T(8,128)(2,1)} collective-permute-done((bf16[240,2048]{1,0:T(8,128)(2,1)}, bf16[240,2048]{1,0:T(8,128)(2,1)}, u32[]{:S(2)}, u32[]{:S(2)}) %collective-permute-start.12) | collective-permute-done | bytes 983072 | tf_op jit(solution)/shard_map/ppermute | solution.py:398
  55.3 1.8 %sort.5 = (bf16[144,2048]{1,0:T(8,128)(2,1)S(1)}, bf16[96,2048]{1,0:T(8,128)(2,1)S(1)}) custom-call(s32[1,768]{1,0:T(1,128)S(1)} %get-tuple-element.118.slot_ref, bf16[768,2048]{1,0:T(8,128)(2,1)S(1)} %copy-done.1, bf16[240,2048]{1,0:T(8,128)(2,1)} %collective-permute-done.12.refs_0_), custom_call_target="tpu_custom_call" | custom-call | flops 1 | bytes 1 | tf_op jit(solution)/shard_map/sort/pallas_call | solution.py:88
  57.1 1.0 collective-permute-start.19
  58.1 7.3 %shrink.8 = (f32[120,128]{1,0:T(8,128)S(1)}, f32[120,128]{1,0:T(8,128)S(1)}) custom-call(s32[3]{0:T(128)S(1)} %get-tuple-element.153.plan_ref, s32[4,128]{1,0:T(4,128)S(1)} %get-tuple-element.122.ends_ref, s32[240,1]{1,0:T(8,128)S(1)} %get-tuple-element.126.which_ref, bf16[24,128,2048]{2,1,0:T(8,128)(2,1)S(1)} %bitcast.13, ...), custom_call_target="tpu_custom_call" | custom-call | flops 1 | bytes 1 | tf_op jit(solution)/shard_map/shrink/pallas_call | solution.py:242
  65.4 11.3 %collective-permute-done.13.refs_0_ = bf16[240,2048]{1,0:T(8,128)(2,1)} collective-permute-done((bf16[240,2048]{1,0:T(8,128)(2,1)}, bf16[240,2048]{1,0:T(8,128)(2,1)}, u32[]{:S(2)}, u32[]{:S(2)}) %collective-permute-start.13) | collective-permute-done | bytes 983072 | tf_op jit(solution)/shard_map/ppermute | solution.py:398
  76.8 7.3 %shrink.9 = (f32[120,128]{1,0:T(8,128)S(1)}, f32[120,128]{1,0:T(8,128)S(1)}) custom-call(s32[3]{0:T(128)S(1)} %get-tuple-element.152.plan_ref, s32[4,128]{1,0:T(4,128)S(1)} %get-tuple-element.122.ends_ref, s32[240,1]{1,0:T(8,128)S(1)} %get-tuple-element.129.which_ref, bf16[24,128,2048]{2,1,0:T(8,128)(2,1)S(1)} %bitcast.13, ...), custom_call_target="tpu_custom_call" | custom-call | flops 1 | bytes 1 | tf_op jit(solution)/shard_map/shrink/pallas_call | solution.py:242
  84.1 1.8 %collective-permute-start.15 = (f32[384,128]{1,0:T(8,128)S(1)}, f32[384,128]{1,0:T(8,128)S(1)}, u32[]{:S(2)}, u32[]{:S(2)}) collective-permute-start(f32[384,128]{1,0:T(8,128)S(1)} %constant_dynamic-update-slice_fusion.3), channel_id=1, source_target_pairs={{0,2},{1,3},{2,0},{3,1},{4,6},{5,7},{6,4},{7,5},{8,10},{9,11},{10,... | collective-permute-start | bytes 589832 | tf_op jit(solution)/shard_map/ppermute | solution.py:398
  85.9 0.0 collective-permute-start.16
  85.9 11.5 %collective-permute-start.23 = (bf16[96,2048]{1,0:T(8,128)(2,1)S(1)}, bf16[96,2048]{1,0:T(8,128)(2,1)S(1)}, u32[]{:S(2)}, u32[]{:S(2)}) collective-permute-start(bf16[96,2048]{1,0:T(8,128)(2,1)S(1)} %get-tuple-element.142), channel_id=1, source_target_pairs={{0,8},{4,12},{8,0},{12,4},{1,9},{5,13},{9,1},{13,5},{2,10},{6,14},... | collective-permute-start | bytes 1179656 | tf_op jit(solution)/shard_map/ppermute | solution.py:398
  97.4 0.4 collective-permute-start.14
  97.8 0.0 collective-permute-done.15.refs_2_
  97.8 1.1 collective-permute-done.14.refs_1_
  98.9 2.3 %expand.5 = (f32[288,256]{1,0:T(8,128)S(1)}, s16[256,256]{1,0:T(8,128)(2,1)S(1)}, s16[256,256]{1,0:T(8,128)(2,1)S(1)}) custom-call(s32[768,1]{1,0:T(8,128)S(1)} %get-tuple-element.120.which_ref, f32[1,24]{1,0:T(1,128)S(1)} %bitcast.18, bf16[1536,256]{1,0:T(8,128)(2,1)S(1)} %bitcast.14, f32[384,128]{1,0:T(8,128)S(1)} %constant_dynamic-update-slice_fusion.refs_0_, ...), custom_call_target="tpu_custom_call" | custom-call | flops 1 | bytes 1 | tf_op jit(solution)/shard_map/expand/pallas_call | solution.py:336
  101.2 0.8 place.1.refs_2_
  102.1 0.0 collective-permute-done.19.refs_0_
  102.1 5.8 %shrink.10 = (f32[72,128]{1,0:T(8,128)S(1)}, f32[72,128]{1,0:T(8,128)S(1)}) custom-call(s32[3]{0:T(128)S(1)} %get-tuple-element.151.plan_ref, s32[4,128]{1,0:T(4,128)S(1)} %get-tuple-element.122.ends_ref, s32[144,1]{1,0:T(8,128)S(1)} %get-tuple-element.138.which_ref, bf16[24,128,2048]{2,1,0:T(8,128)(2,1)S(1)} %bitcast.13, ...), custom_call_target="tpu_custom_call" | custom-call | flops 1 | bytes 1 | tf_op jit(solution)/shard_map/shrink/pallas_call | solution.py:242
  107.9 9.3 %collective-permute-start.20 = (f32[72,128]{1,0:T(8,128)S(1)}, f32[72,128]{1,0:T(8,128)S(1)}, u32[]{:S(2)}, u32[]{:S(2)}) collective-permute-start(f32[72,128]{1,0:T(8,128)S(1)} %get-tuple-element.140), channel_id=1, source_target_pairs={{0,2},{2,0},{1,3},{3,1},{4,6},{6,4},{5,7},{7,5},{8,10},{10,8},{9,1... | collective-permute-start | bytes 110600 | tf_op jit(solution)/shard_map/ppermute | solution.py:398
  117.2 1.9 %collective-permute-done.20 = f32[72,128]{1,0:T(8,128)S(1)} collective-permute-done((f32[72,128]{1,0:T(8,128)S(1)}, f32[72,128]{1,0:T(8,128)S(1)}, u32[]{:S(2)}, u32[]{:S(2)}) %collective-permute-start.20) | collective-permute-done | bytes 36896 | tf_op jit(solution)/shard_map/ppermute | solution.py:398
  119.2 0.0 collective-permute-start.21
  119.2 0.3 collective-permute-start.17
  119.5 0.7 collective-permute-start.18
  120.2 0.2 collective-permute-done.21.refs_1_
  120.4 0.7 expand.6.refs_1_
  121.1 0.0 copy-start.16
  121.2 2.8 %shrink.11 = (f32[48,128]{1,0:T(8,128)S(1)}, f32[48,128]{1,0:T(8,128)S(1)}) custom-call(s32[3]{0:T(128)S(1)} %get-tuple-element.150.plan_ref, s32[4,128]{1,0:T(4,128)S(1)} %get-tuple-element.122.ends_ref, s32[96,1]{1,0:T(8,128)S(1)} %get-tuple-element.141.which_ref, bf16[24,128,2048]{2,1,0:T(8,128)(2,1)S(1)} %bitcast.13, ...), custom_call_target="tpu_custom_call" | custom-call | flops 1 | bytes 1 | tf_op jit(solution)/shard_map/shrink/pallas_call | solution.py:242
  123.9 2.1 %collective-permute-start.24 = (f32[48,128]{1,0:T(8,128)S(1)}, f32[48,128]{1,0:T(8,128)S(1)}, u32[]{:S(2)}, u32[]{:S(2)}) collective-permute-start(f32[48,128]{1,0:T(8,128)S(1)} %get-tuple-element.144), channel_id=1, source_target_pairs={{0,2},{2,0},{1,3},{3,1},{4,6},{6,4},{5,7},{7,5},{8,10},{10,8},{9,1... | collective-permute-start | bytes 73736 | tf_op jit(solution)/shard_map/ppermute | solution.py:398
  126.0 1.8 %collective-permute-done.24 = f32[48,128]{1,0:T(8,128)S(1)} collective-permute-done((f32[48,128]{1,0:T(8,128)S(1)}, f32[48,128]{1,0:T(8,128)S(1)}, u32[]{:S(2)}, u32[]{:S(2)}) %collective-permute-start.24) | collective-permute-done | bytes 24608 | tf_op jit(solution)/shard_map/ppermute | solution.py:398
  127.9 2.8 %collective-permute-start.22 = (s16[160,256]{1,0:T(8,128)(2,1)S(1)}, s16[160,256]{1,0:T(8,128)(2,1)S(1)}, u32[]{:S(2)}, u32[]{:S(2)}) collective-permute-start(s16[160,256]{1,0:T(8,128)(2,1)S(1)} %expand.6.refs_1_), channel_id=1, source_target_pairs={{0,8},{4,12},{8,0},{12,4},{1,9},{5,13},{9,1},{13,5},{2,10},{6,14},... | collective-permute-start | bytes 245768 | tf_op jit(solution)/shard_map/ppermute | solution.py:398
  130.7 0.0 collective-permute-done.25.refs_1_
  130.7 0.7 expand.7
  131.4 1.2 collective-permute-start.26
  132.6 1.1 collective-permute-start.11
  133.7 2.4 %collective-permute-done.11 = s32[1,128]{1,0:T(1,128)S(1)} collective-permute-done((s32[1,128]{1,0:T(1,128)S(1)}, s32[1,128]{1,0:T(1,128)S(1)}, u32[]{:S(2)}, u32[]{:S(2)}) %collective-permute-start.11) | collective-permute-done | bytes 544 | tf_op jit(solution)/shard_map/ppermute | solution.py:398
  136.2 0.0 collective-permute-done.18
  136.2 0.0 collective-permute-done.22
  136.2 1.8 %collective-permute-done.26 = s16[112,256]{1,0:T(8,128)(2,1)S(1)} collective-permute-done((s16[112,256]{1,0:T(8,128)(2,1)S(1)}, s16[112,256]{1,0:T(8,128)(2,1)S(1)}, u32[]{:S(2)}, u32[]{:S(2)}) %collective-permute-start.26) | collective-permute-done | bytes 57376 | tf_op jit(solution)/shard_map/ppermute | solution.py:398
  138.0 2.2 %conditional.1 = (bf16[768,256]{1,0:T(8,128)(2,1)S(1)}) conditional(s32[]{:T(128)} %bitcast.3, (s32[768,1]{1,0:T(8,128)S(1)}, f32[768,256]{1,0:T(8,128)}, f32[768,256]{1,0:T(8,128)S(1)}, s16[256,256]{1,0:T(8,128)(2,1)S(1)}, s16[256,256]{1,0:T(8,128)(2,1)S(1)}, /*index=5*/s16[160,256]{1,0:T(8,128)(2,1)S(1)}, s16[112,256]{1,0:T(8,128)(2,1)S(1)}) %tuple.11, ...), branch_computations={%region_1.0_spmd, %region_2.0_spmd} | conditional | flops 9219 | bytes 6304127 | solution.py:511
  138.2 2.0 %merge.2 = bf16[768,256]{1,0:T(8,128)(2,1)S(1)} custom-call(s32[768,1]{1,0:T(8,128)S(1)} %get-tuple-element.55.target_ref, f32[768,256]{1,0:T(8,128)} %get-tuple-element.56.refs_0_, f32[768,256]{1,0:T(8,128)S(1)} %get-tuple-element.57.refs_1_, s16[256,256]{1,0:T(8,128)(2,1)S(1)} %get-tuple-element.58.refs_2_, s16[256,256]{1,0:T(8,128)(2,1)S(1)} %get-tuple-element.59.refs_3_, ...), custom_call_target="tpu_custom_call" | custom-call | flops 1 | bytes 1 | tf_op jit(solution)/shard_map/cond/branch_0_fun/merge/pallas_call | solution.py:388
  140.2 0.0 copy-start.10
  140.2 0.7 copy-done.10
  (47 shorter events, 0.1 us)
Async XLA Ops:
  6.5 131.4 %reduce-scatter.2.cloned.1.call-start = ((), (), s32[]{:S(2)}) async-start(), calls=%async_computation.1 | async-start | bytes 3932160 | tf_op jit(solution)/shard_map/reduce_scatter | solution.py:435
  6.5 7.2 %collective-permute-start.10 = (s32[1,768]{1,0:T(1,128)}, s32[1,768]{1,0:T(1,128)S(1)}, u32[]{:S(2)}, u32[]{:S(2)}) collective-permute-start(s32[1,768]{1,0:T(1,128)} %bitcast.7), channel_id=1, source_target_pairs={{0,12},{4,8},{8,4},{12,0},{1,13},{5,9},{9,5},{13,1},{2,14},{6,10},... | collective-permute-start | bytes 9224 | tf_op jit(solution)/shard_map/ppermute | solution.py:398
  11.6 3.8 %collective-permute-start.8 = (s32[1,768]{1,0:T(1,128)}, s32[1,768]{1,0:T(1,128)S(1)}, u32[]{:S(2)}, u32[]{:S(2)}) collective-permute-start(s32[1,768]{1,0:T(1,128)} %bitcast.8), channel_id=1, source_target_pairs={{0,4},{4,0},{8,12},{12,8},{1,5},{5,1},{9,13},{13,9},{2,6},{6,2},{1... | collective-permute-start | bytes 9224 | tf_op jit(solution)/shard_map/ppermute | solution.py:398
  11.6 4.7 %collective-permute-start.9 = (s32[1,768]{1,0:T(1,128)}, s32[1,768]{1,0:T(1,128)S(1)}, u32[]{:S(2)}, u32[]{:S(2)}) collective-permute-start(s32[1,768]{1,0:T(1,128)} %bitcast.9), channel_id=1, source_target_pairs={{0,8},{4,12},{8,0},{12,4},{1,9},{5,13},{9,1},{13,5},{2,10},{6,14},... | collective-permute-start | bytes 9224 | tf_op jit(solution)/shard_map/ppermute | solution.py:398
  12.2 0.7 copy-start.5
  16.3 1.9 %copy-start = (bf16[768,2048]{1,0:T(8,128)(2,1)S(1)}, bf16[768,2048]{1,0:T(8,128)(2,1)}, u32[]{:S(2)}) copy-start(bf16[768,2048]{1,0:T(8,128)(2,1)} %tok_ref.7) | copy-start | bytes 9437188
  18.2 3.7 %copy-start.1 = (bf16[768,2048]{1,0:T(8,128)(2,1)S(1)}, bf16[768,2048]{1,0:T(8,128)(2,1)}, u32[]{:S(2)}) copy-start(bf16[768,2048]{1,0:T(8,128)(2,1)} %tok_ref.7) | copy-start | bytes 9437188
  20.9 1.0 copy-start.7
  21.9 2.2 %copy-start.3 = (bf16[2048,1024]{1,0:T(8,128)(2,1)S(1)}, bf16[2048,1024]{1,0:T(8,128)(2,1)}, u32[]{:S(2)}) copy-start(bf16[2048,1024]{1,0:T(8,128)(2,1)} %weight_ref.1) | copy-start | bytes 12582916
  29.5 1.0 copy-start.4
  30.5 24.7 %collective-permute-start.12 = (bf16[240,2048]{1,0:T(8,128)(2,1)}, bf16[240,2048]{1,0:T(8,128)(2,1)}, u32[]{:S(2)}, u32[]{:S(2)}) collective-permute-start(bf16[240,2048]{1,0:T(8,128)(2,1)} %copy-done.4), channel_id=1, source_target_pairs={{0,4},{4,0},{8,12},{12,8},{1,5},{5,1},{9,13},{13,9},{2,6},{6,2},{1... | collective-permute-start | bytes 2949128 | tf_op jit(solution)/shard_map/ppermute | solution.py:398
  32.6 44.2 %collective-permute-start.13 = (bf16[240,2048]{1,0:T(8,128)(2,1)}, bf16[240,2048]{1,0:T(8,128)(2,1)}, u32[]{:S(2)}, u32[]{:S(2)}) collective-permute-start(bf16[240,2048]{1,0:T(8,128)(2,1)} %copy-done.7), channel_id=1, source_target_pairs={{0,12},{4,8},{8,4},{12,0},{1,13},{5,9},{9,5},{13,1},{2,14},{6,10},... | collective-permute-start | bytes 2949128 | tf_op jit(solution)/shard_map/ppermute | solution.py:398
  32.7 1.9 %copy-start.2 = (f32[768,1024]{1,0:T(8,128)S(1)}, f32[768,1024]{1,0:T(8,128)}, u32[]{:S(2)}) copy-start(f32[768,1024]{1,0:T(8,128)} %base.1.refs_0_) | copy-start | bytes 9437188
  34.6 3.2 %copy-start.6 = (s32[768,1]{0,1:T(1,128)S(1)}, s32[768,1]{0,1:T(1,128)}, u32[]{:S(2)}) copy-start(s32[768,1]{0,1:T(1,128)} %param.13) | copy-start | bytes 9220
  34.6 23.5 %slice-start = ((s8[12582912]{0:T(1024)(128)(4,1)}), s8[4194304]{0:T(1024)(128)(4,1)S(1)}, s32[]{:S(2)}) async-start(s8[12582912]{0:T(1024)(128)(4,1)} %bitcast.12), calls=%async_computation.2 | async-start | bytes 8388608
  39.5 0.5 copy-start.13
  39.5 81.6 %copy-start.12 = (s32[4,128]{1,0:T(4,128)}, s32[4,128]{1,0:T(4,128)S(1)}, u32[]{:S(2)}) copy-start(s32[4,128]{1,0:T(4,128)S(1)} %get-tuple-element.122.ends_ref) | copy-start | bytes 6148
  40.1 18.0 %slice-start.1 = ((s8[12582912]{0:T(1024)(128)(4,1)}), s8[4194304]{0:T(1024)(128)(4,1)S(1)}, s32[]{:S(2)}) async-start(s8[12582912]{0:T(1024)(128)(4,1)} %bitcast.12), calls=%async_computation.3 | async-start | bytes 8388608
  40.1 18.0 %slice-start.2 = ((s8[12582912]{0:T(1024)(128)(4,1)}), s8[4194304]{0:T(1024)(128)(4,1)S(1)}, s32[]{:S(2)}) async-start(s8[12582912]{0:T(1024)(128)(4,1)} %bitcast.12), calls=%async_computation.4 | async-start | bytes 8388608
  57.1 44.9 %collective-permute-start.19 = (bf16[144,2048]{1,0:T(8,128)(2,1)S(1)}, bf16[144,2048]{1,0:T(8,128)(2,1)S(1)}, u32[]{:S(2)}, u32[]{:S(2)}) collective-permute-start(bf16[144,2048]{1,0:T(8,128)(2,1)S(1)} %get-tuple-element.127.refs_2_), channel_id=1, source_target_pairs={{0,8},{4,12},{8,0},{12,4},{1,9},{5,13},{9,1},{13,5},{2,10},{6,14},... | collective-permute-start | bytes 1769480 | tf_op jit(solution)/shard_map/ppermute | solution.py:398
  76.8 22.1 %copy-start.8 = (bf16[24,64,256]{2,1,0:T(8,128)(2,1)S(1)}, bf16[24,64,256]{2,1,0:T(8,128)(2,1)}, u32[]{:S(2)}) copy-start(bf16[24,64,256]{2,1,0:T(8,128)(2,1)} %param.11) | copy-start | bytes 2359300
  76.8 22.1 %copy-start.15 = (f32[24]{0:T(128)S(1)}, f32[24]{0:T(128)}, u32[]{:S(2)}) copy-start(f32[24]{0:T(128)} %param.12) | copy-start | bytes 292
  84.1 13.6 %collective-permute-start.15 = (f32[384,128]{1,0:T(8,128)S(1)}, f32[384,128]{1,0:T(8,128)S(1)}, u32[]{:S(2)}, u32[]{:S(2)}) collective-permute-start(f32[384,128]{1,0:T(8,128)S(1)} %constant_dynamic-update-slice_fusion.3), channel_id=1, source_target_pairs={{0,2},{1,3},{2,0},{3,1},{4,6},{5,7},{6,4},{7,5},{8,10},{9,11},{10,... | collective-permute-start | bytes 589832 | tf_op jit(solution)/shard_map/ppermute | solution.py:398
  85.9 11.9 %collective-permute-start.16 = (f32[384,128]{1,0:T(8,128)S(1)}, f32[384,128]{1,0:T(8,128)S(1)}, u32[]{:S(2)}, u32[]{:S(2)}) collective-permute-start(f32[384,128]{1,0:T(8,128)S(1)} %constant_dynamic-update-slice_fusion.3), channel_id=1, source_target_pairs={{0,3},{1,2},{2,1},{3,0},{4,7},{5,6},{6,5},{7,4},{8,11},{9,10},{10,... | collective-permute-start | bytes 589832 | tf_op jit(solution)/shard_map/ppermute | solution.py:398
  85.9 35.2 %collective-permute-start.23 = (bf16[96,2048]{1,0:T(8,128)(2,1)S(1)}, bf16[96,2048]{1,0:T(8,128)(2,1)S(1)}, u32[]{:S(2)}, u32[]{:S(2)}) collective-permute-start(bf16[96,2048]{1,0:T(8,128)(2,1)S(1)} %get-tuple-element.142), channel_id=1, source_target_pairs={{0,8},{4,12},{8,0},{12,4},{1,9},{5,13},{9,1},{13,5},{2,10},{6,14},... | collective-permute-start | bytes 1179656 | tf_op jit(solution)/shard_map/ppermute | solution.py:398
  97.4 1.5 %collective-permute-start.14 = (f32[384,128]{1,0:T(8,128)S(1)}, f32[384,128]{1,0:T(8,128)S(1)}, u32[]{:S(2)}, u32[]{:S(2)}) collective-permute-start(f32[384,128]{1,0:T(8,128)S(1)} %constant_dynamic-update-slice_fusion.refs_0_), channel_id=1, source_target_pairs={{0,1},{1,0},{2,3},{3,2},{4,5},{5,4},{6,7},{7,6},{8,9},{9,8},{10,11... | collective-permute-start | bytes 589832 | tf_op jit(solution)/shard_map/ppermute | solution.py:398
  107.9 11.3 %collective-permute-start.20 = (f32[72,128]{1,0:T(8,128)S(1)}, f32[72,128]{1,0:T(8,128)S(1)}, u32[]{:S(2)}, u32[]{:S(2)}) collective-permute-start(f32[72,128]{1,0:T(8,128)S(1)} %get-tuple-element.140), channel_id=1, source_target_pairs={{0,2},{2,0},{1,3},{3,1},{4,6},{6,4},{5,7},{7,5},{8,10},{10,8},{9,1... | collective-permute-start | bytes 110600 | tf_op jit(solution)/shard_map/ppermute | solution.py:398
  119.2 1.2 collective-permute-start.21
  119.2 17.0 %collective-permute-start.17 = (s16[256,256]{1,0:T(8,128)(2,1)S(1)}, s16[256,256]{1,0:T(8,128)(2,1)S(1)}, u32[]{:S(2)}, u32[]{:S(2)}) collective-permute-start(s16[256,256]{1,0:T(8,128)(2,1)S(1)} %get-tuple-element.136), channel_id=1, source_target_pairs={{0,4},{4,0},{8,12},{12,8},{1,5},{5,1},{9,13},{13,9},{2,6},{6,2},{1... | collective-permute-start | bytes 393224 | tf_op jit(solution)/shard_map/ppermute | solution.py:398
  119.5 16.7 %collective-permute-start.18 = (s16[256,256]{1,0:T(8,128)(2,1)S(1)}, s16[256,256]{1,0:T(8,128)(2,1)S(1)}, u32[]{:S(2)}, u32[]{:S(2)}) collective-permute-start(s16[256,256]{1,0:T(8,128)(2,1)S(1)} %get-tuple-element.137), channel_id=1, source_target_pairs={{0,12},{4,8},{8,4},{12,0},{1,13},{5,9},{9,5},{13,1},{2,14},{6,10},... | collective-permute-start | bytes 393224 | tf_op jit(solution)/shard_map/ppermute | solution.py:398
  121.1 16.9 %copy-start.11 = (s32[144,1]{1,0:T(8,128)S(1)}, s32[144,1]{1,0:T(8,128)}, u32[]{:S(2)}) copy-start(s32[144,1]{1,0:T(8,128)} %get-tuple-element.148) | copy-start | bytes 1732
  121.1 16.8 %copy-start.14 = (s32[21]{0:T(128)S(1)}, s32[21]{0:T(128)}, u32[]{:S(2)}) copy-start(s32[21]{0:T(128)} %copy-done.13) | copy-start | bytes 256
  121.1 16.8 %copy-start.16 = (bf16[48,2048]{1,0:T(8,128)(2,1)S(1)}, bf16[48,2048]{1,0:T(8,128)(2,1)}, u32[]{:S(2)}) copy-start(bf16[48,2048]{1,0:T(8,128)(2,1)} %get-tuple-element.145) | copy-start | bytes 589828
  121.1 16.8 %copy-start.17 = (bf16[48,2048]{1,0:T(8,128)(2,1)S(1)}, bf16[48,2048]{1,0:T(8,128)(2,1)}, u32[]{:S(2)}) copy-start(bf16[48,2048]{1,0:T(8,128)(2,1)} %get-tuple-element.146) | copy-start | bytes 589828
  121.1 16.8 %copy-start.18 = (bf16[48,2048]{1,0:T(8,128)(2,1)S(1)}, bf16[48,2048]{1,0:T(8,128)(2,1)}, u32[]{:S(2)}) copy-start(bf16[48,2048]{1,0:T(8,128)(2,1)} %get-tuple-element.147) | copy-start | bytes 589828
  123.9 3.9 %collective-permute-start.24 = (f32[48,128]{1,0:T(8,128)S(1)}, f32[48,128]{1,0:T(8,128)S(1)}, u32[]{:S(2)}, u32[]{:S(2)}) collective-permute-start(f32[48,128]{1,0:T(8,128)S(1)} %get-tuple-element.144), channel_id=1, source_target_pairs={{0,2},{2,0},{1,3},{3,1},{4,6},{6,4},{5,7},{7,5},{8,10},{10,8},{9,1... | collective-permute-start | bytes 73736 | tf_op jit(solution)/shard_map/ppermute | solution.py:398
  127.8 2.9 %collective-permute-start.25 = (f32[48,128]{1,0:T(8,128)S(1)}, f32[48,128]{1,0:T(8,128)S(1)}, u32[]{:S(2)}, u32[]{:S(2)}) collective-permute-start(f32[48,128]{1,0:T(8,128)S(1)} %add.16.refs_0_), channel_id=1, source_target_pairs={{0,1},{1,0},{2,3},{3,2},{4,5},{5,4},{6,7},{7,6},{8,9},{9,8},{10,11... | collective-permute-start | bytes 73736 | tf_op jit(solution)/shard_map/ppermute | solution.py:398
  127.9 8.3 %collective-permute-start.22 = (s16[160,256]{1,0:T(8,128)(2,1)S(1)}, s16[160,256]{1,0:T(8,128)(2,1)S(1)}, u32[]{:S(2)}, u32[]{:S(2)}) collective-permute-start(s16[160,256]{1,0:T(8,128)(2,1)S(1)} %expand.6.refs_1_), channel_id=1, source_target_pairs={{0,8},{4,12},{8,0},{12,4},{1,9},{5,13},{9,1},{13,5},{2,10},{6,14},... | collective-permute-start | bytes 245768 | tf_op jit(solution)/shard_map/ppermute | solution.py:398
  131.4 6.6 %collective-permute-start.26 = (s16[112,256]{1,0:T(8,128)(2,1)S(1)}, s16[112,256]{1,0:T(8,128)(2,1)S(1)}, u32[]{:S(2)}, u32[]{:S(2)}) collective-permute-start(s16[112,256]{1,0:T(8,128)(2,1)S(1)} %expand.7), channel_id=1, source_target_pairs={{0,8},{4,12},{8,0},{12,4},{1,9},{5,13},{9,1},{13,5},{2,10},{6,14},... | collective-permute-start | bytes 172040 | tf_op jit(solution)/shard_map/ppermute | solution.py:398
  132.6 3.5 %collective-permute-start.11 = (s32[1,128]{1,0:T(1,128)S(1)}, s32[1,128]{1,0:T(1,128)S(1)}, u32[]{:S(2)}, u32[]{:S(2)}) collective-permute-start(s32[1,128]{1,0:T(1,128)S(1)} %get-tuple-element.116), channel_id=1, source_target_pairs={{0,16},{16,0},{1,17},{17,1},{2,18},{18,2},{3,19},{19,3},{4,20},{20... | collective-permute-start | bytes 1544 | tf_op jit(solution)/shard_map/ppermute | solution.py:398
  140.2 0.7 copy-start.10
Sparse Core Ops, SparseCore 0:
  30.7 37.6 reduce-scatter.1

commit v9 on v8

--- a/solution.py
+++ b/solution.py
@@ -9,7 +9,7 @@
 
 ADAPTER_RANK = 64
 TOKEN_LIMIT = 12
-VMEM_LIMIT = 28 * 1024 * 1024
+VMEM_LIMIT = 16 * 1024 * 1024
 F32 = jnp.float32
 BF16 = jnp.bfloat16
 I32 = jnp.int32
@@ -159,7 +159,8 @@
     return names, ends, plans, most
 
 
-def base_kernel(tok_ref, weight_ref, _, out_ref):
+def base_kernel(tok_ref, weight_ref, _, out_ref, done_ref):
+    done_ref[...] = jnp.zeros_like(done_ref)
     out_ref[...] = jnp.dot(tok_ref[...], weight_ref[...], preferred_element_type=F32)
 
 
@@ -174,8 +175,14 @@
             pl.BlockSpec((width, step), lambda i: (0, i)),
             ANYWHERE,
         ],
-        out_specs=pl.BlockSpec((rows, step), lambda i: (0, i)),
-        out_shape=pltpu.HBM((rows, columns), F32),
+        out_specs=[
+            pl.BlockSpec((rows, step), lambda i: (0, i)),
+            pl.BlockSpec((8, 128), lambda i: (0, 0)),
+        ],
+        out_shape=[
+            jax.ShapeDtypeStruct((rows, columns), F32),
+            jax.ShapeDtypeStruct((8, 128), F32),
+        ],
         compiler_params=PARAMS,
         cost_estimate=COST,
         name="base",
@@ -431,9 +438,9 @@
     sent = far + [near]
     packed = dict(zip(sent, sort_rows(tokens, slot, cap, sent, tuple(ids_heard[1:]))))
     received = {p: swap(packed[p], "dp", owners, p[0]) for p in sent}
-    base_part = base_product(tokens, key_value_weight, packed[near])
+    base_part, base_done = base_product(tokens, key_value_weight, packed[near])
     base = lax.psum_scatter(base_part, feature_axes, scatter_dimension=1, tiled=True)
-    packed |= zip([own] + extra, sort_rows(tokens, slot, cap, [own] + extra, (base_part,)))
+    packed |= zip([own] + extra, sort_rows(tokens, slot, cap, [own] + extra, (base_done,)))
     gated = [p for pieces in last for p in pieces]
     packed |= zip(gated, sort_rows(tokens, slot, cap, gated, (received[near],)))
     received |= {p: swap(packed[p], "dp", owners, p[0]) for p in gated}
@@ -470,7 +477,9 @@
         return [b * cap + f for b, f, _ in pieces]
 
     weights = (adapter_down_weight, up, scale)
-    packed |= zip([own] + extra, sort_rows(tokens, slot, cap, [own] + extra, (base_part,)))
+    packed |= zip([own] + extra, sort_rows(tokens, slot, cap, [own] + extra, (base_done,)))
+    for d in range(1, lax.axis_size("parts")):
+        largest = jnp.maximum(largest, swap(largest, "parts", lax.axis_size("parts"), d))
     shares, waits = [], ()
     for k, p in enumerate(early):
         rows_here = received.get(p, packed[p])
@@ -487,7 +496,7 @@
     done = early[1:]
     for k, pieces in enumerate(last):
         blocks = [received[p] for p in pieces]
-        waits = (deltas[0], parts[1])
+        waits = (deltas[0], parts[1], largest)
         deltas = deltas_of(
             pieces, blocks, names[here + 1 + k], ends, plans[here + 1 + k], *weights, waits
         )
@@ -506,8 +515,6 @@
         deltas = send_back(extra, deltas)
         return merge(parts, target, begins(done + extra), returned + deltas, BF16)
 
-    for d in range(1, lax.axis_size("parts")):
-        largest = jnp.maximum(largest, swap(largest, "parts", lax.axis_size("parts"), d))
     return lax.cond(
         largest[0, 0] > usual,
         finish_with_extra,

time: 148 us -> 152 us (1.027)
  waiting for transfers between devices: 27.9 us -> 47.1 us
  starting transfers between devices: 39.8 us -> 23.1 us
  Pallas kernels: 56 us -> 58.2 us
    ppermute x19, waiting for transfers between devices: 27.9 us -> 47.1 us  [swap(): return lax.ppermute(x, axes, [(i, i ^ distance) for i in range(size)])]
    ppermute x19, starting transfers between devices: 39.8 us -> 23.1 us  [swap(): return lax.ppermute(x, axes, [(i, i ^ distance) for i in range(size)])]
    pallas_call x5, Pallas kernels: 33.7 us -> 35.7 us  [shrink(): pl.pallas_call(functools.partial(shrink_kernel, pieces, group, fine), gri...]
    unnamed x45 -> x39, local copies, waits for them, and re-layouts: 9.86 us -> 8.59 us
  transfers between devices with their start and end apart: 20 -> 20, of which waited for: 10 -> 8; matrix products, arithmetic and copies ran while one was open for 0% -> 0% of each run, Pallas kernels for 31% -> 32%
where the time goes in v9:
time: 152 us; the launch traced here: 151 us
  Pallas kernels  58.2 us (38%)
  waiting for transfers between devices  47.1 us (31%)
  starting transfers between devices  23.1 us (15%)
  between operations  13.8 us (9%)
  local copies, waits for them, and re-layouts  8.67 us (6%)
    ppermute x19, waiting for transfers between devices, swap(): return lax.ppermute(x, axes, [(i, i ^ distance) for i in range(size)])  47.1 us
    pallas_call x5, Pallas kernels, shrink(): pl.pallas_call(functools.partial(shrink_kernel, pieces, group, fine), gri...  35.7 us
    ppermute x19, starting transfers between devices, swap(): return lax.ppermute(x, axes, [(i, i ^ distance) for i in range(size)])  23.1 us
    unnamed x39, local copies, waits for them, and re-layouts  8.59 us
    pallas_call x3, Pallas kernels, sort_rows(): pl.pallas_call(functools.partial(sort_kernel, cap, pieces, len(later_than...  7.82 us
    pallas_call x1, Pallas kernels, base_product(): pl.pallas_call(base_kernel, grid=(columns // step,), in_specs=[pl.BlockSp...  4.75 us
    pallas_call x3, Pallas kernels, expand(): pl.pallas_call(functools.partial(expand_kernel, groups, sizes, len(lines)...  3.7 us
  transfers between devices with their start and end apart: 20, of which 8 were waited for; matrix products, arithmetic and copies ran while one was open for 0% of the time, Pallas kernels for 32%

profile of v9, /device:TPU:0, one launch (start us, length us, event | category | flops | bytes accessed | tf_op | source)
XLA Modules:
  0.0 151.0 jit_solution(1116980810038193491)
XLA Ops:
  6.5 3.0 %collective-permute-start.8 = (s32[1,768]{1,0:T(1,128)}, s32[1,768]{1,0:T(1,128)S(1)}, u32[]{:S(2)}, u32[]{:S(2)}) collective-permute-start(s32[1,768]{1,0:T(1,128)} %bitcast.7), channel_id=1, source_target_pairs={{0,4},{4,0},{8,12},{12,8},{1,5},{5,1},{9,13},{13,9},{2,6},{6,2},{1... | collective-permute-start | bytes 9224 | tf_op jit(solution)/shard_map/ppermute | solution.py:405
  9.6 2.6 %collective-permute-start.9 = (s32[1,768]{1,0:T(1,128)}, s32[1,768]{1,0:T(1,128)S(1)}, u32[]{:S(2)}, u32[]{:S(2)}) collective-permute-start(s32[1,768]{1,0:T(1,128)} %bitcast.8), channel_id=1, source_target_pairs={{0,8},{4,12},{8,0},{12,4},{1,9},{5,13},{9,1},{13,5},{2,10},{6,14},... | collective-permute-start | bytes 9224 | tf_op jit(solution)/shard_map/ppermute | solution.py:405
  12.2 0.0 collective-permute-start.10
  12.2 0.7 copy-done.5
  12.9 1.6 %route.1 = (s32[1,768]{1,0:T(1,128)S(1)}, s32[768,1]{1,0:T(8,128)}) custom-call(s32[1]{0:T(128)} %bitcast.me_ref, s32[1,768]{1,0:T(1,128)S(1)} %bitcast.10), custom_call_target="tpu_custom_call" | custom-call | flops 1 | bytes 1 | tf_op jit(solution)/shard_map/route/pallas_call | solution.py:53
  14.5 0.0 collective-permute-done.9.refs_2_.refs_1_
  14.5 3.2 %collective-permute-done.10.refs_3_.refs_2_ = s32[1,768]{1,0:T(1,128)S(1)} collective-permute-done((s32[1,768]{1,0:T(1,128)}, s32[1,768]{1,0:T(1,128)S(1)}, u32[]{:S(2)}, u32[]{:S(2)}) %collective-permute-start.10) | collective-permute-done | bytes 3104 | tf_op jit(solution)/shard_map/ppermute | solution.py:405
  17.8 1.9 %copy-done = bf16[768,2048]{1,0:T(8,128)(2,1)S(1)} copy-done((bf16[768,2048]{1,0:T(8,128)(2,1)S(1)}, bf16[768,2048]{1,0:T(8,128)(2,1)}, u32[]{:S(2)}) %copy-start) | copy-done | bytes 3145752
  19.6 2.7 %sort.3 = (bf16[240,2048]{1,0:T(8,128)(2,1)S(1)}, bf16[240,2048]{1,0:T(8,128)(2,1)S(1)}) custom-call(s32[1,768]{1,0:T(1,128)S(1)} %get-tuple-element.120.slot_ref, bf16[768,2048]{1,0:T(8,128)(2,1)S(1)} %copy-done, s32[1,768]{1,0:T(1,128)S(1)} %collective-permute-done.8.refs_1_.refs_0_, s32[1,768]{1,0:T(1,128)S(1)} %collective-permute-done.9.refs_2_.refs_1_, ...), custom_call_target="tpu_custom_call" | custom-call | flops 1 | bytes 1 | tf_op jit(solution)/shard_map/sort/pallas_call | solution.py:88
  22.4 0.9 copy-done.7
  23.3 2.5 %copy-done.2 = bf16[2048,1024]{1,0:T(8,128)(2,1)S(1)} copy-done((bf16[2048,1024]{1,0:T(8,128)(2,1)S(1)}, bf16[2048,1024]{1,0:T(8,128)(2,1)}, u32[]{:S(2)}) %copy-start.2) | copy-done | bytes 4194328
  25.9 4.8 %base.1 = (f32[768,1024]{1,0:T(8,128)S(1)}, f32[8,128]{1,0:T(8,128)S(1)}) custom-call(bf16[768,2048]{1,0:T(8,128)(2,1)S(1)} %copy-done.1, bf16[2048,1024]{1,0:T(8,128)(2,1)S(1)} %copy-done.2, bf16[240,2048]{1,0:T(8,128)(2,1)S(1)} %get-tuple-element.121._), custom_call_target="tpu_custom_call" | custom-call | flops 1 | bytes 1 | tf_op jit(solution)/shard_map/base/pallas_call | solution.py:170
  30.7 1.6 %copy-done.3 = f32[768,1024]{1,0:T(8,128)} copy-done((f32[768,1024]{1,0:T(8,128)}, f32[768,1024]{1,0:T(8,128)S(1)}, u32[]{:S(2)}) %copy-start.3) | copy-done | bytes 3145752
  32.3 0.0 reduce-scatter.2.cloned.1.call-update
  32.3 0.1 collective-permute-start.12
  32.4 0.7 collective-permute-start.13
  33.0 0.1 pad_add_fusion.here_ref
  33.1 1.7 %name_rows.1 = (s32[288,1]{1,0:T(8,128)S(1)}, s32[240,1]{1,0:T(8,128)S(1)}, s32[240,1]{1,0:T(8,128)S(1)}, s32[768,1]{1,0:T(8,128)S(1)}, s32[144,1]{1,0:T(8,128)S...) custom-call(s32[2]{0:T(128)S(1)} %pad_add_fusion.here_ref, ...), custom_call_target="tpu_custom_call" | custom-call | flops 1 | bytes 1 | tf_op jit(solution)/shard_map/name_rows/pallas_call | solution.py:144
  34.8 1.6 %collective-permute-start.11 = (s32[1,128]{1,0:T(1,128)S(1)}, s32[1,128]{1,0:T(1,128)S(1)}, u32[]{:S(2)}, u32[]{:S(2)}) collective-permute-start(s32[1,128]{1,0:T(1,128)S(1)} %get-tuple-element.118), channel_id=1, source_target_pairs={{0,16},{16,0},{1,17},{17,1},{2,18},{18,2},{3,19},{19,3},{4,20},{20... | collective-permute-start | bytes 1544 | tf_op jit(solution)/shard_map/ppermute | solution.py:405
  36.4 3.3 %sort.4 = (bf16[288,2048]{1,0:T(8,128)(2,1)S(1)}, bf16[48,2048]{1,0:T(8,128)(2,1)}, bf16[48,2048]{1,0:T(8,128)(2,1)}, bf16[48,2048]{1,0:T(8,128)(2,1)}) custom-call(s32[1,768]{1,0:T(1,128)S(1)} %get-tuple-element.120.slot_ref, bf16[768,2048]{1,0:T(8,128)(2,1)S(1)} %copy-done.1, f32[8,128]{1,0:T(8,128)S(1)} %get-tuple-element.127.refs_0_), custom_call_target="tpu_custom_call" | custom-call | flops 1 | bytes 1 | tf_op jit(solution)/shard_map/sort/pallas_call | solution.py:88
  39.7 0.1 fusion
  39.8 10.3 %shrink.7 = (f32[144,128]{1,0:T(8,128)S(1)}, f32[144,128]{1,0:T(8,128)S(1)}) custom-call(s32[3]{0:T(128)S(1)} %get-tuple-element.158.plan_ref, s32[4,128]{1,0:T(4,128)S(1)} %get-tuple-element.125.ends_ref, s32[288,1]{1,0:T(8,128)S(1)} %get-tuple-element.126.which_ref, bf16[24,128,2048]{2,1,0:T(8,128)(2,1)} %down_ref.9, ...), custom_call_target="tpu_custom_call" | custom-call | flops 1 | bytes 1 | tf_op jit(solution)/shard_map/shrink/pallas_call | solution.py:249
  50.1 23.8 %collective-permute-done.12.refs_0_ = bf16[240,2048]{1,0:T(8,128)(2,1)} collective-permute-done((bf16[240,2048]{1,0:T(8,128)(2,1)}, bf16[240,2048]{1,0:T(8,128)(2,1)}, u32[]{:S(2)}, u32[]{:S(2)}) %collective-permute-start.12) | collective-permute-done | bytes 983072 | tf_op jit(solution)/shard_map/ppermute | solution.py:405
  73.9 1.8 %sort.5 = (bf16[144,2048]{1,0:T(8,128)(2,1)S(1)}, bf16[96,2048]{1,0:T(8,128)(2,1)S(1)}) custom-call(s32[1,768]{1,0:T(1,128)S(1)} %get-tuple-element.120.slot_ref, bf16[768,2048]{1,0:T(8,128)(2,1)S(1)} %copy-done.1, bf16[240,2048]{1,0:T(8,128)(2,1)} %collective-permute-done.12.refs_0_), custom_call_target="tpu_custom_call" | custom-call | flops 1 | bytes 1 | tf_op jit(solution)/shard_map/sort/pallas_call | solution.py:88
  75.8 0.1 collective-permute-start.19
  75.8 0.0 slice-start.2
  75.8 10.0 %shrink.8 = (f32[120,128]{1,0:T(8,128)S(1)}, f32[120,128]{1,0:T(8,128)S(1)}) custom-call(s32[3]{0:T(128)S(1)} %get-tuple-element.157.plan_ref, s32[4,128]{1,0:T(4,128)S(1)} %get-tuple-element.125.ends_ref, s32[240,1]{1,0:T(8,128)S(1)} %get-tuple-element.130.which_ref, bf16[24,128,2048]{2,1,0:T(8,128)(2,1)} %down_ref.9, ...), custom_call_target="tpu_custom_call" | custom-call | flops 1 | bytes 1 | tf_op jit(solution)/shard_map/shrink/pallas_call | solution.py:249
  85.9 0.0 copy-start.8
  85.9 0.0 copy-start.13
  85.9 0.0 copy-start.9
  85.9 7.3 %shrink.9 = (f32[120,128]{1,0:T(8,128)S(1)}, f32[120,128]{1,0:T(8,128)S(1)}) custom-call(s32[3]{0:T(128)S(1)} %get-tuple-element.156.plan_ref, s32[4,128]{1,0:T(4,128)S(1)} %get-tuple-element.125.ends_ref, s32[240,1]{1,0:T(8,128)S(1)} %get-tuple-element.133.which_ref, bf16[24,128,2048]{2,1,0:T(8,128)(2,1)S(1)} %bitcast.14, ...), custom_call_target="tpu_custom_call" | custom-call | flops 1 | bytes 1 | tf_op jit(solution)/shard_map/shrink/pallas_call | solution.py:249
  93.3 0.1 collective-permute-start.14
  93.4 4.5 %collective-permute-start.23 = (bf16[96,2048]{1,0:T(8,128)(2,1)S(1)}, bf16[96,2048]{1,0:T(8,128)(2,1)S(1)}, u32[]{:S(2)}, u32[]{:S(2)}) collective-permute-start(bf16[96,2048]{1,0:T(8,128)(2,1)S(1)} %get-tuple-element.146), channel_id=1, source_target_pairs={{0,8},{4,12},{8,0},{12,4},{1,9},{5,13},{9,1},{13,5},{2,10},{6,14},... | collective-permute-start | bytes 1179656 | tf_op jit(solution)/shard_map/ppermute | solution.py:405
  97.9 1.5 collective-permute-start.15
  99.4 0.0 collective-permute-done.11
  99.4 0.1 collective-permute-start.16
  99.5 6.2 %collective-permute-done.15.refs_2_ = f32[384,128]{1,0:T(8,128)S(1)} collective-permute-done((f32[384,128]{1,0:T(8,128)S(1)}, f32[384,128]{1,0:T(8,128)S(1)}, u32[]{:S(2)}, u32[]{:S(2)}) %collective-permute-start.15) | collective-permute-done | bytes 196640 | tf_op jit(solution)/shard_map/ppermute | solution.py:405
  105.7 2.7 %collective-permute-done.16.refs_3_ = f32[384,128]{1,0:T(8,128)S(1)} collective-permute-done((f32[384,128]{1,0:T(8,128)S(1)}, f32[384,128]{1,0:T(8,128)S(1)}, u32[]{:S(2)}, u32[]{:S(2)}) %collective-permute-start.16) | collective-permute-done | bytes 196640 | tf_op jit(solution)/shard_map/ppermute | solution.py:405
  108.3 2.3 %expand.5 = (f32[288,256]{1,0:T(8,128)S(1)}, s16[256,256]{1,0:T(8,128)(2,1)S(1)}, s16[256,256]{1,0:T(8,128)(2,1)S(1)}) custom-call(s32[768,1]{1,0:T(8,128)S(1)} %get-tuple-element.123.which_ref, f32[1,24]{1,0:T(1,128)S(1)} %bitcast.20, bf16[1536,256]{1,0:T(8,128)(2,1)S(1)} %bitcast.15, f32[384,128]{1,0:T(8,128)S(1)} %constant_dynamic-update-slice_fusion.refs_0_, ...), custom_call_target="tpu_custom_call" | custom-call | flops 1 | bytes 1 | tf_op jit(solution)/shard_map/expand/pallas_call | solution.py:343
  110.7 0.9 place.1.refs_2_
  111.5 0.0 collective-permute-done.19.refs_0_
  111.6 5.8 %shrink.10 = (f32[72,128]{1,0:T(8,128)S(1)}, f32[72,128]{1,0:T(8,128)S(1)}) custom-call(s32[3]{0:T(128)S(1)} %get-tuple-element.155.plan_ref, s32[4,128]{1,0:T(4,128)S(1)} %get-tuple-element.125.ends_ref, s32[144,1]{1,0:T(8,128)S(1)} %get-tuple-element.142.which_ref, bf16[24,128,2048]{2,1,0:T(8,128)(2,1)S(1)} %bitcast.14, ...), custom_call_target="tpu_custom_call" | custom-call | flops 1 | bytes 1 | tf_op jit(solution)/shard_map/shrink/pallas_call | solution.py:249
  117.4 1.6 %collective-permute-start.20 = (f32[72,128]{1,0:T(8,128)S(1)}, f32[72,128]{1,0:T(8,128)S(1)}, u32[]{:S(2)}, u32[]{:S(2)}) collective-permute-start(f32[72,128]{1,0:T(8,128)S(1)} %get-tuple-element.144), channel_id=1, source_target_pairs={{0,2},{2,0},{1,3},{3,1},{4,6},{6,4},{5,7},{7,5},{8,10},{10,8},{9,1... | collective-permute-start | bytes 110600 | tf_op jit(solution)/shard_map/ppermute | solution.py:405
  119.0 2.7 %collective-permute-done.20 = f32[72,128]{1,0:T(8,128)S(1)} collective-permute-done((f32[72,128]{1,0:T(8,128)S(1)}, f32[72,128]{1,0:T(8,128)S(1)}, u32[]{:S(2)}, u32[]{:S(2)}) %collective-permute-start.20) | collective-permute-done | bytes 36896 | tf_op jit(solution)/shard_map/ppermute | solution.py:405
  121.7 0.0 collective-permute-start.21
  121.7 0.8 collective-permute-start.17
  122.5 1.7 %collective-permute-start.18 = (s16[256,256]{1,0:T(8,128)(2,1)S(1)}, s16[256,256]{1,0:T(8,128)(2,1)S(1)}, u32[]{:S(2)}, u32[]{:S(2)}) collective-permute-start(s16[256,256]{1,0:T(8,128)(2,1)S(1)} %get-tuple-element.141), channel_id=1, source_target_pairs={{0,12},{4,8},{8,4},{12,0},{1,13},{5,9},{9,5},{13,1},{2,14},{6,10},... | collective-permute-start | bytes 393224 | tf_op jit(solution)/shard_map/ppermute | solution.py:405
  124.3 0.0 collective-permute-done.21.refs_1_
  124.3 0.7 expand.6.refs_1_
  125.0 0.0 collective-permute-done.23.refs_0_
  125.0 2.4 %shrink.11 = (f32[48,128]{1,0:T(8,128)S(1)}, f32[48,128]{1,0:T(8,128)S(1)}) custom-call(s32[3]{0:T(128)S(1)} %get-tuple-element.154.plan_ref, s32[4,128]{1,0:T(4,128)S(1)} %get-tuple-element.125.ends_ref, s32[96,1]{1,0:T(8,128)S(1)} %get-tuple-element.145.which_ref, bf16[24,128,2048]{2,1,0:T(8,128)(2,1)S(1)} %bitcast.14, ...), custom_call_target="tpu_custom_call" | custom-call | flops 1 | bytes 1 | tf_op jit(solution)/shard_map/shrink/pallas_call | solution.py:249
  127.4 1.6 %collective-permute-start.24 = (f32[48,128]{1,0:T(8,128)S(1)}, f32[48,128]{1,0:T(8,128)S(1)}, u32[]{:S(2)}, u32[]{:S(2)}) collective-permute-start(f32[48,128]{1,0:T(8,128)S(1)} %get-tuple-element.148), channel_id=1, source_target_pairs={{0,2},{2,0},{1,3},{3,1},{4,6},{6,4},{5,7},{7,5},{8,10},{10,8},{9,1... | collective-permute-start | bytes 73736 | tf_op jit(solution)/shard_map/ppermute | solution.py:405
  129.0 2.3 %collective-permute-done.24 = f32[48,128]{1,0:T(8,128)S(1)} collective-permute-done((f32[48,128]{1,0:T(8,128)S(1)}, f32[48,128]{1,0:T(8,128)S(1)}, u32[]{:S(2)}, u32[]{:S(2)}) %collective-permute-start.24) | collective-permute-done | bytes 24608 | tf_op jit(solution)/shard_map/ppermute | solution.py:405
  131.3 1.9 %collective-permute-start.22 = (s16[160,256]{1,0:T(8,128)(2,1)S(1)}, s16[160,256]{1,0:T(8,128)(2,1)S(1)}, u32[]{:S(2)}, u32[]{:S(2)}) collective-permute-start(s16[160,256]{1,0:T(8,128)(2,1)S(1)} %expand.6.refs_1_), channel_id=1, source_target_pairs={{0,8},{4,12},{8,0},{12,4},{1,9},{5,13},{9,1},{13,5},{2,10},{6,14},... | collective-permute-start | bytes 245768 | tf_op jit(solution)/shard_map/ppermute | solution.py:405
  133.2 0.0 collective-permute-done.25.refs_1_
  133.2 0.7 expand.7
  133.9 1.2 collective-permute-start.26
  135.2 0.0 collective-permute-done.18
  135.2 3.9 %collective-permute-done.22 = s16[160,256]{1,0:T(8,128)(2,1)S(1)} collective-permute-done((s16[160,256]{1,0:T(8,128)(2,1)S(1)}, s16[160,256]{1,0:T(8,128)(2,1)S(1)}, u32[]{:S(2)}, u32[]{:S(2)}) %collective-permute-start.22) | collective-permute-done | bytes 81952 | tf_op jit(solution)/shard_map/ppermute | solution.py:405
  139.1 2.2 %collective-permute-done.26 = s16[112,256]{1,0:T(8,128)(2,1)S(1)} collective-permute-done((s16[112,256]{1,0:T(8,128)(2,1)S(1)}, s16[112,256]{1,0:T(8,128)(2,1)S(1)}, u32[]{:S(2)}, u32[]{:S(2)}) %collective-permute-start.26) | collective-permute-done | bytes 57376 | tf_op jit(solution)/shard_map/ppermute | solution.py:405
  141.3 2.2 %conditional.1 = (bf16[768,256]{1,0:T(8,128)(2,1)S(1)}) conditional(s32[]{:T(128)} %bitcast.3, (s32[768,1]{1,0:T(8,128)S(1)}, f32[768,256]{1,0:T(8,128)}, f32[768,256]{1,0:T(8,128)S(1)}, s16[256,256]{1,0:T(8,128)(2,1)S(1)}, s16[256,256]{1,0:T(8,128)(2,1)S(1)}, /*index=5*/s16[160,256]{1,0:T(8,128)(2,1)S(1)}, s16[112,256]{1,0:T(8,128)(2,1)S(1)}) %tuple.25, ...), branch_computations={%region_1.0_spmd, %region_2.0_spmd} | conditional | flops 9219 | bytes 6306871 | solution.py:518
  141.5 2.0 %merge.2 = bf16[768,256]{1,0:T(8,128)(2,1)S(1)} custom-call(s32[768,1]{1,0:T(8,128)S(1)} %get-tuple-element.55.target_ref, f32[768,256]{1,0:T(8,128)} %get-tuple-element.56.refs_0_, f32[768,256]{1,0:T(8,128)S(1)} %get-tuple-element.57.refs_1_, s16[256,256]{1,0:T(8,128)(2,1)S(1)} %get-tuple-element.58.refs_2_, s16[256,256]{1,0:T(8,128)(2,1)S(1)} %get-tuple-element.59.refs_3_, ...), custom_call_target="tpu_custom_call" | custom-call | flops 1 | bytes 1 | tf_op jit(solution)/shard_map/cond/branch_0_fun/merge/pallas_call | solution.py:395
  143.4 0.0 copy-start.11
  143.5 0.7 copy-done.11
  (41 shorter events, 0.1 us)
Async XLA Ops:
  6.5 134.7 %reduce-scatter.2.cloned.1.call-start = ((), (), s32[]{:S(2)}) async-start(), calls=%async_computation.1 | async-start | bytes 3932160 | tf_op jit(solution)/shard_map/reduce_scatter | solution.py:442
  6.5 8.0 %collective-permute-start.8 = (s32[1,768]{1,0:T(1,128)}, s32[1,768]{1,0:T(1,128)S(1)}, u32[]{:S(2)}, u32[]{:S(2)}) collective-permute-start(s32[1,768]{1,0:T(1,128)} %bitcast.7), channel_id=1, source_target_pairs={{0,4},{4,0},{8,12},{12,8},{1,5},{5,1},{9,13},{13,9},{2,6},{6,2},{1... | collective-permute-start | bytes 9224 | tf_op jit(solution)/shard_map/ppermute | solution.py:405
  9.6 5.0 %collective-permute-start.9 = (s32[1,768]{1,0:T(1,128)}, s32[1,768]{1,0:T(1,128)S(1)}, u32[]{:S(2)}, u32[]{:S(2)}) collective-permute-start(s32[1,768]{1,0:T(1,128)} %bitcast.8), channel_id=1, source_target_pairs={{0,8},{4,12},{8,0},{12,4},{1,9},{5,13},{9,1},{13,5},{2,10},{6,14},... | collective-permute-start | bytes 9224 | tf_op jit(solution)/shard_map/ppermute | solution.py:405
  12.2 5.6 %collective-permute-start.10 = (s32[1,768]{1,0:T(1,128)}, s32[1,768]{1,0:T(1,128)S(1)}, u32[]{:S(2)}, u32[]{:S(2)}) collective-permute-start(s32[1,768]{1,0:T(1,128)} %bitcast.9), channel_id=1, source_target_pairs={{0,12},{4,8},{8,4},{12,0},{1,13},{5,9},{9,5},{13,1},{2,14},{6,10},... | collective-permute-start | bytes 9224 | tf_op jit(solution)/shard_map/ppermute | solution.py:405
  12.2 0.8 copy-start.5
  17.8 1.9 %copy-start = (bf16[768,2048]{1,0:T(8,128)(2,1)S(1)}, bf16[768,2048]{1,0:T(8,128)(2,1)}, u32[]{:S(2)}) copy-start(bf16[768,2048]{1,0:T(8,128)(2,1)} %tok_ref.7) | copy-start | bytes 9437188
  19.6 3.7 %copy-start.1 = (bf16[768,2048]{1,0:T(8,128)(2,1)S(1)}, bf16[768,2048]{1,0:T(8,128)(2,1)}, u32[]{:S(2)}) copy-start(bf16[768,2048]{1,0:T(8,128)(2,1)} %tok_ref.7) | copy-start | bytes 9437188
  22.4 1.0 copy-start.7
  23.3 7.3 %copy-start.4 = (bf16[240,2048]{1,0:T(8,128)(2,1)}, bf16[240,2048]{1,0:T(8,128)(2,1)S(1)}, u32[]{:S(2)}) copy-start(bf16[240,2048]{1,0:T(8,128)(2,1)S(1)} %get-tuple-element.121._) | copy-start | bytes 2949124
  23.3 2.5 %copy-start.2 = (bf16[2048,1024]{1,0:T(8,128)(2,1)S(1)}, bf16[2048,1024]{1,0:T(8,128)(2,1)}, u32[]{:S(2)}) copy-start(bf16[2048,1024]{1,0:T(8,128)(2,1)} %weight_ref.1) | copy-start | bytes 12582916
  30.6 1.6 %copy-start.3 = (f32[768,1024]{1,0:T(8,128)}, f32[768,1024]{1,0:T(8,128)S(1)}, u32[]{:S(2)}) copy-start(f32[768,1024]{1,0:T(8,128)S(1)} %get-tuple-element.122) | copy-start | bytes 9437188
  32.3 0.8 copy-start.6
  32.3 41.6 %collective-permute-start.12 = (bf16[240,2048]{1,0:T(8,128)(2,1)}, bf16[240,2048]{1,0:T(8,128)(2,1)}, u32[]{:S(2)}, u32[]{:S(2)}) collective-permute-start(bf16[240,2048]{1,0:T(8,128)(2,1)} %copy-done.4), channel_id=1, source_target_pairs={{0,4},{4,0},{8,12},{12,8},{1,5},{5,1},{9,13},{13,9},{2,6},{6,2},{1... | collective-permute-start | bytes 2949128 | tf_op jit(solution)/shard_map/ppermute | solution.py:405
  32.4 53.5 %collective-permute-start.13 = (bf16[240,2048]{1,0:T(8,128)(2,1)}, bf16[240,2048]{1,0:T(8,128)(2,1)}, u32[]{:S(2)}, u32[]{:S(2)}) collective-permute-start(bf16[240,2048]{1,0:T(8,128)(2,1)} %copy-done.7), channel_id=1, source_target_pairs={{0,12},{4,8},{8,4},{12,0},{1,13},{5,9},{9,5},{13,1},{2,14},{6,10},... | collective-permute-start | bytes 2949128 | tf_op jit(solution)/shard_map/ppermute | solution.py:405
  34.8 64.5 %collective-permute-start.11 = (s32[1,128]{1,0:T(1,128)S(1)}, s32[1,128]{1,0:T(1,128)S(1)}, u32[]{:S(2)}, u32[]{:S(2)}) collective-permute-start(s32[1,128]{1,0:T(1,128)S(1)} %get-tuple-element.118), channel_id=1, source_target_pairs={{0,16},{16,0},{1,17},{17,1},{2,18},{18,2},{3,19},{19,3},{4,20},{20... | collective-permute-start | bytes 1544 | tf_op jit(solution)/shard_map/ppermute | solution.py:405
  39.7 46.1 %slice-start = ((s8[12582912]{0:T(1024)(128)(4,1)}), s8[4194304]{0:T(1024)(128)(4,1)S(1)}, s32[]{:S(2)}) async-start(s8[12582912]{0:T(1024)(128)(4,1)} %bitcast.13), calls=%async_computation.2 | async-start | bytes 8388608
  39.7 46.1 %slice-start.1 = ((s8[12582912]{0:T(1024)(128)(4,1)}), s8[4194304]{0:T(1024)(128)(4,1)S(1)}, s32[]{:S(2)}) async-start(s8[12582912]{0:T(1024)(128)(4,1)} %bitcast.13), calls=%async_computation.3 | async-start | bytes 8388608
  75.8 35.8 %collective-permute-start.19 = (bf16[144,2048]{1,0:T(8,128)(2,1)S(1)}, bf16[144,2048]{1,0:T(8,128)(2,1)S(1)}, u32[]{:S(2)}, u32[]{:S(2)}) collective-permute-start(bf16[144,2048]{1,0:T(8,128)(2,1)S(1)} %get-tuple-element.131.refs_2_), channel_id=1, source_target_pairs={{0,8},{4,12},{8,0},{12,4},{1,9},{5,13},{9,1},{13,5},{2,10},{6,14},... | collective-permute-start | bytes 1769480 | tf_op jit(solution)/shard_map/ppermute | solution.py:405
  75.8 10.0 %slice-start.2 = ((s8[12582912]{0:T(1024)(128)(4,1)}), s8[4194304]{0:T(1024)(128)(4,1)S(1)}, s32[]{:S(2)}) async-start(s8[12582912]{0:T(1024)(128)(4,1)} %bitcast.13), calls=%async_computation.4 | async-start | bytes 8388608
  85.9 22.5 %copy-start.8 = (bf16[24,64,256]{2,1,0:T(8,128)(2,1)S(1)}, bf16[24,64,256]{2,1,0:T(8,128)(2,1)}, u32[]{:S(2)}) copy-start(bf16[24,64,256]{2,1,0:T(8,128)(2,1)} %param.11) | copy-start | bytes 2359300
  85.9 22.5 %copy-start.13 = (f32[24]{0:T(128)S(1)}, f32[24]{0:T(128)}, u32[]{:S(2)}) copy-start(f32[24]{0:T(128)} %param.12) | copy-start | bytes 292
  85.9 24.8 %copy-start.9 = (s32[768,1]{1,0:T(8,128)S(1)}, s32[768,1]{1,0:T(8,128)}, u32[]{:S(2)}) copy-start(s32[768,1]{1,0:T(8,128)} %get-tuple-element.119.target_ref) | copy-start | bytes 9220
  93.3 6.2 %collective-permute-start.14 = (f32[384,128]{1,0:T(8,128)S(1)}, f32[384,128]{1,0:T(8,128)S(1)}, u32[]{:S(2)}, u32[]{:S(2)}) collective-permute-start(f32[384,128]{1,0:T(8,128)S(1)} %constant_dynamic-update-slice_fusion.refs_0_), channel_id=1, source_target_pairs={{0,1},{1,0},{2,3},{3,2},{4,5},{5,4},{6,7},{7,6},{8,9},{9,8},{10,11... | collective-permute-start | bytes 589832 | tf_op jit(solution)/shard_map/ppermute | solution.py:405
  93.4 31.6 %collective-permute-start.23 = (bf16[96,2048]{1,0:T(8,128)(2,1)S(1)}, bf16[96,2048]{1,0:T(8,128)(2,1)S(1)}, u32[]{:S(2)}, u32[]{:S(2)}) collective-permute-start(bf16[96,2048]{1,0:T(8,128)(2,1)S(1)} %get-tuple-element.146), channel_id=1, source_target_pairs={{0,8},{4,12},{8,0},{12,4},{1,9},{5,13},{9,1},{13,5},{2,10},{6,14},... | collective-permute-start | bytes 1179656 | tf_op jit(solution)/shard_map/ppermute | solution.py:405
  97.9 7.8 %collective-permute-start.15 = (f32[384,128]{1,0:T(8,128)S(1)}, f32[384,128]{1,0:T(8,128)S(1)}, u32[]{:S(2)}, u32[]{:S(2)}) collective-permute-start(f32[384,128]{1,0:T(8,128)S(1)} %constant_dynamic-update-slice_fusion.3), channel_id=1, source_target_pairs={{0,2},{1,3},{2,0},{3,1},{4,6},{5,7},{6,4},{7,5},{8,10},{9,11},{10,... | collective-permute-start | bytes 589832 | tf_op jit(solution)/shard_map/ppermute | solution.py:405
  99.4 9.0 %collective-permute-start.16 = (f32[384,128]{1,0:T(8,128)S(1)}, f32[384,128]{1,0:T(8,128)S(1)}, u32[]{:S(2)}, u32[]{:S(2)}) collective-permute-start(f32[384,128]{1,0:T(8,128)S(1)} %constant_dynamic-update-slice_fusion.3), channel_id=1, source_target_pairs={{0,3},{1,2},{2,1},{3,0},{4,7},{5,6},{6,5},{7,4},{8,11},{9,10},{10,... | collective-permute-start | bytes 589832 | tf_op jit(solution)/shard_map/ppermute | solution.py:405
  117.4 4.3 %collective-permute-start.20 = (f32[72,128]{1,0:T(8,128)S(1)}, f32[72,128]{1,0:T(8,128)S(1)}, u32[]{:S(2)}, u32[]{:S(2)}) collective-permute-start(f32[72,128]{1,0:T(8,128)S(1)} %get-tuple-element.144), channel_id=1, source_target_pairs={{0,2},{2,0},{1,3},{3,1},{4,6},{6,4},{5,7},{7,5},{8,10},{10,8},{9,1... | collective-permute-start | bytes 110600 | tf_op jit(solution)/shard_map/ppermute | solution.py:405
  121.7 2.6 %collective-permute-start.21 = (f32[72,128]{1,0:T(8,128)S(1)}, f32[72,128]{1,0:T(8,128)S(1)}, u32[]{:S(2)}, u32[]{:S(2)}) collective-permute-start(f32[72,128]{1,0:T(8,128)S(1)} %add.15.refs_0_), channel_id=1, source_target_pairs={{0,1},{1,0},{2,3},{3,2},{4,5},{5,4},{6,7},{7,6},{8,9},{9,8},{10,11... | collective-permute-start | bytes 110600 | tf_op jit(solution)/shard_map/ppermute | solution.py:405
  121.7 13.4 %collective-permute-start.17 = (s16[256,256]{1,0:T(8,128)(2,1)S(1)}, s16[256,256]{1,0:T(8,128)(2,1)S(1)}, u32[]{:S(2)}, u32[]{:S(2)}) collective-permute-start(s16[256,256]{1,0:T(8,128)(2,1)S(1)} %get-tuple-element.140), channel_id=1, source_target_pairs={{0,4},{4,0},{8,12},{12,8},{1,5},{5,1},{9,13},{13,9},{2,6},{6,2},{1... | collective-permute-start | bytes 393224 | tf_op jit(solution)/shard_map/ppermute | solution.py:405
  122.5 12.6 %collective-permute-start.18 = (s16[256,256]{1,0:T(8,128)(2,1)S(1)}, s16[256,256]{1,0:T(8,128)(2,1)S(1)}, u32[]{:S(2)}, u32[]{:S(2)}) collective-permute-start(s16[256,256]{1,0:T(8,128)(2,1)S(1)} %get-tuple-element.141), channel_id=1, source_target_pairs={{0,12},{4,8},{8,4},{12,0},{1,13},{5,9},{9,5},{13,1},{2,14},{6,10},... | collective-permute-start | bytes 393224 | tf_op jit(solution)/shard_map/ppermute | solution.py:405
  125.0 16.3 %copy-start.15 = (bf16[48,2048]{1,0:T(8,128)(2,1)S(1)}, bf16[48,2048]{1,0:T(8,128)(2,1)}, u32[]{:S(2)}) copy-start(bf16[48,2048]{1,0:T(8,128)(2,1)} %get-tuple-element.149) | copy-start | bytes 589828
  125.0 16.3 %copy-start.16 = (bf16[48,2048]{1,0:T(8,128)(2,1)S(1)}, bf16[48,2048]{1,0:T(8,128)(2,1)}, u32[]{:S(2)}) copy-start(bf16[48,2048]{1,0:T(8,128)(2,1)} %get-tuple-element.150) | copy-start | bytes 589828
  125.0 16.3 %copy-start.17 = (bf16[48,2048]{1,0:T(8,128)(2,1)S(1)}, bf16[48,2048]{1,0:T(8,128)(2,1)}, u32[]{:S(2)}) copy-start(bf16[48,2048]{1,0:T(8,128)(2,1)} %get-tuple-element.151) | copy-start | bytes 589828
  127.4 3.9 %collective-permute-start.24 = (f32[48,128]{1,0:T(8,128)S(1)}, f32[48,128]{1,0:T(8,128)S(1)}, u32[]{:S(2)}, u32[]{:S(2)}) collective-permute-start(f32[48,128]{1,0:T(8,128)S(1)} %get-tuple-element.148), channel_id=1, source_target_pairs={{0,2},{2,0},{1,3},{3,1},{4,6},{6,4},{5,7},{7,5},{8,10},{10,8},{9,1... | collective-permute-start | bytes 73736 | tf_op jit(solution)/shard_map/ppermute | solution.py:405
  131.3 1.9 %collective-permute-start.25 = (f32[48,128]{1,0:T(8,128)S(1)}, f32[48,128]{1,0:T(8,128)S(1)}, u32[]{:S(2)}, u32[]{:S(2)}) collective-permute-start(f32[48,128]{1,0:T(8,128)S(1)} %add.16.refs_0_), channel_id=1, source_target_pairs={{0,1},{1,0},{2,3},{3,2},{4,5},{5,4},{6,7},{7,6},{8,9},{9,8},{10,11... | collective-permute-start | bytes 73736 | tf_op jit(solution)/shard_map/ppermute | solution.py:405
  131.3 7.8 %collective-permute-start.22 = (s16[160,256]{1,0:T(8,128)(2,1)S(1)}, s16[160,256]{1,0:T(8,128)(2,1)S(1)}, u32[]{:S(2)}, u32[]{:S(2)}) collective-permute-start(s16[160,256]{1,0:T(8,128)(2,1)S(1)} %expand.6.refs_1_), channel_id=1, source_target_pairs={{0,8},{4,12},{8,0},{12,4},{1,9},{5,13},{9,1},{13,5},{2,10},{6,14},... | collective-permute-start | bytes 245768 | tf_op jit(solution)/shard_map/ppermute | solution.py:405
  133.9 7.3 %collective-permute-start.26 = (s16[112,256]{1,0:T(8,128)(2,1)S(1)}, s16[112,256]{1,0:T(8,128)(2,1)S(1)}, u32[]{:S(2)}, u32[]{:S(2)}) collective-permute-start(s16[112,256]{1,0:T(8,128)(2,1)S(1)} %expand.7), channel_id=1, source_target_pairs={{0,8},{4,12},{8,0},{12,4},{1,9},{5,13},{9,1},{13,5},{2,10},{6,14},... | collective-permute-start | bytes 172040 | tf_op jit(solution)/shard_map/ppermute | solution.py:405
  143.4 0.7 copy-start.11
Sparse Core Ops, SparseCore 0:
  32.4 36.1 reduce-scatter.1

commit v10 on v9

--- a/solution.py
+++ b/solution.py
@@ -9,12 +9,13 @@
 
 ADAPTER_RANK = 64
 TOKEN_LIMIT = 12
-VMEM_LIMIT = 16 * 1024 * 1024
+VMEM_LIMIT = 28 * 1024 * 1024
 F32 = jnp.float32
 BF16 = jnp.bfloat16
 I32 = jnp.int32
 ANYWHERE = pl.BlockSpec(memory_space=pl.ANY)
 COST = pl.CostEstimate(flops=1, transcendentals=0, bytes_accessed=1)
+HEAD = pl.CostEstimate(flops=10**9, transcendentals=0, bytes_accessed=1)
 PARAMS = pltpu.CompilerParams(vmem_limit_bytes=VMEM_LIMIT)
 
 
@@ -58,7 +59,7 @@
         ],
         out_shape=[jax.ShapeDtypeStruct((1, rows), I32), jax.ShapeDtypeStruct((rows, 1), I32)],
         compiler_params=PARAMS,
-        cost_estimate=COST,
+        cost_estimate=HEAD,
         name="route",
     )(me, ids_row)
 
@@ -97,7 +98,7 @@
         out_shape=[jax.ShapeDtypeStruct((count, width), BF16) for _, _, count in pieces],
         scratch_shapes=[pltpu.VMEM((sum(c for _, _, c in pieces), rows), BF16)],
         compiler_params=PARAMS,
-        cost_estimate=COST,
+        cost_estimate=HEAD,
         name="sort",
     )(slot, tokens, *later_than)
 
@@ -184,7 +185,7 @@
             jax.ShapeDtypeStruct((8, 128), F32),
         ],
         compiler_params=PARAMS,
-        cost_estimate=COST,
+        cost_estimate=HEAD,
         name="base",
     )(tokens, weight, later_than)
 
@@ -442,8 +443,6 @@
     base = lax.psum_scatter(base_part, feature_axes, scatter_dimension=1, tiled=True)
     packed |= zip([own] + extra, sort_rows(tokens, slot, cap, [own] + extra, (base_done,)))
     gated = [p for pieces in last for p in pieces]
-    packed |= zip(gated, sort_rows(tokens, slot, cap, gated, (received[near],)))
-    received |= {p: swap(packed[p], "dp", owners, p[0]) for p in gated}
 
     early = [own, near] + far
     sets = [[p] for p in early] + [early] + last + ([extra] if extra else [])
@@ -480,13 +479,14 @@
     packed |= zip([own] + extra, sort_rows(tokens, slot, cap, [own] + extra, (base_done,)))
     for d in range(1, lax.axis_size("parts")):
         largest = jnp.maximum(largest, swap(largest, "parts", lax.axis_size("parts"), d))
-    shares, waits = [], ()
-    for k, p in enumerate(early):
-        rows_here = received.get(p, packed[p])
-        shares.append(
-            shrink([p], [rows_here], names[k], ends, plans[k], adapter_down_weight, waits)
-        )
-        waits = (shares[-1][0], packed[gated[0]])
+    down = adapter_down_weight
+    shares = [shrink([own], [packed[own]], names[0], ends, plans[0], down)]
+    packed |= zip(gated, sort_rows(tokens, slot, cap, gated, (shares[0][0],)))
+    received |= {p: swap(packed[p], "dp", owners, p[0]) for p in gated}
+    waits = (packed[gated[0]],)
+    for k, p in enumerate(early[1:], 1):
+        shares.append(shrink([p], [received[p]], names[k], ends, plans[k], down, waits))
+        waits = (shares[-1][0],)
     lines = exchange(*(jnp.concatenate(pair, axis=0) for pair in zip(*shares)), steps=1)
     sizes = tuple(p[2] for p in early)
     here = len(early)

time: 152 us -> 155 us (1.020)
  starting transfers between devices: 23.1 us -> 29.4 us
  local copies, waits for them, and re-layouts: 8.67 us -> 2.6 us
  waiting for transfers between devices: 47.1 us -> 50.1 us
    ppermute x19, starting transfers between devices: 23.1 us -> 29.4 us  [swap(): return lax.ppermute(x, axes, [(i, i ^ distance) for i in range(size)])]
    unnamed x39 -> x35, local copies, waits for them, and re-layouts: 8.59 us -> 2.51 us
    ppermute x19, waiting for transfers between devices: 47.1 us -> 50.1 us  [swap(): return lax.ppermute(x, axes, [(i, i ^ distance) for i in range(size)])]
  transfers between devices with their start and end apart: 20 -> 20, of which waited for: 8 -> 10; matrix products, arithmetic and copies ran while one was open for 0% -> 0% of each run, Pallas kernels for 32% -> 32%
where the time goes in v10:
time: 155 us
  Pallas kernels  59.3 us (38%)
  waiting for transfers between devices  50.1 us (32%)
  starting transfers between devices  29.4 us (19%)
  between operations  13.8 us (9%)
  local copies, waits for them, and re-layouts  2.6 us (2%)
    ppermute x19, waiting for transfers between devices, swap(): return lax.ppermute(x, axes, [(i, i ^ distance) for i in range(size)])  50.1 us
    pallas_call x5, Pallas kernels, shrink(): pl.pallas_call(functools.partial(shrink_kernel, pieces, group, fine), gri...  36.1 us
    ppermute x19, starting transfers between devices, swap(): return lax.ppermute(x, axes, [(i, i ^ distance) for i in range(size)])  29.4 us
    pallas_call x3, Pallas kernels, sort_rows(): pl.pallas_call(functools.partial(sort_kernel, cap, pieces, len(later_than...  7.8 us
    pallas_call x1, Pallas kernels, base_product(): pl.pallas_call(base_kernel, grid=(columns // step,), in_specs=[pl.BlockSp...  5.49 us
    pallas_call x3, Pallas kernels, expand(): pl.pallas_call(functools.partial(expand_kernel, groups, sizes, len(lines)...  3.71 us
  transfers between devices with their start and end apart: 20, of which 10 were waited for; matrix products, arithmetic and copies ran while one was open for 0% of the time, Pallas kernels for 32%

profile of v10, /device:TPU:0, one launch (start us, length us, event | category | flops | bytes accessed | tf_op | source)
XLA Modules:
  0.0 155.4 jit_solution(15481258899869232842)
XLA Ops:
  6.5 3.0 %collective-permute-start.8 = (s32[1,768]{1,0:T(1,128)}, s32[1,768]{1,0:T(1,128)S(1)}, u32[]{:S(2)}, u32[]{:S(2)}) collective-permute-start(s32[1,768]{1,0:T(1,128)} %bitcast.7), channel_id=1, source_target_pairs={{0,4},{4,0},{8,12},{12,8},{1,5},{5,1},{9,13},{13,9},{2,6},{6,2},{1... | collective-permute-start | bytes 9224 | tf_op jit(solution)/shard_map/ppermute | solution.py:406
  9.6 2.6 %collective-permute-start.9 = (s32[1,768]{1,0:T(1,128)}, s32[1,768]{1,0:T(1,128)S(1)}, u32[]{:S(2)}, u32[]{:S(2)}) collective-permute-start(s32[1,768]{1,0:T(1,128)} %bitcast.8), channel_id=1, source_target_pairs={{0,8},{4,12},{8,0},{12,4},{1,9},{5,13},{9,1},{13,5},{2,10},{6,14},... | collective-permute-start | bytes 9224 | tf_op jit(solution)/shard_map/ppermute | solution.py:406
  12.2 0.0 collective-permute-start.10
  12.2 0.7 copy-done.3
  12.9 1.6 %route.1 = (s32[1,768]{1,0:T(1,128)S(1)}, s32[768,1]{1,0:T(8,128)}) custom-call(s32[1]{0:T(128)} %bitcast.me_ref, s32[1,768]{1,0:T(1,128)S(1)} %bitcast.10), custom_call_target="tpu_custom_call" | custom-call | flops 1000000000 | bytes 1 | tf_op jit(solution)/shard_map/route/pallas_call | solution.py:54
  14.5 0.0 collective-permute-done.8.refs_1_.refs_0_
  14.5 0.0 collective-permute-done.9.refs_2_.refs_1_
  14.5 3.2 %collective-permute-done.10.refs_3_.refs_2_ = s32[1,768]{1,0:T(1,128)S(1)} collective-permute-done((s32[1,768]{1,0:T(1,128)}, s32[1,768]{1,0:T(1,128)S(1)}, u32[]{:S(2)}, u32[]{:S(2)}) %collective-permute-start.10) | collective-permute-done | bytes 3104 | tf_op jit(solution)/shard_map/ppermute | solution.py:406
  17.8 2.7 %sort.3 = (bf16[240,2048]{1,0:T(8,128)(2,1)S(1)}, bf16[240,2048]{1,0:T(8,128)(2,1)S(1)}) custom-call(s32[1,768]{1,0:T(1,128)S(1)} %get-tuple-element.120.slot_ref, bf16[768,2048]{1,0:T(8,128)(2,1)S(1)} %copy-done.1, s32[1,768]{1,0:T(1,128)S(1)} %collective-permute-done.8.refs_1_.refs_0_, s32[1,768]{1,0:T(1,128)S(1)} %collective-permute-done.9.refs_2_.refs_1_, ...), custom_call_target="tpu_custom_call" | custom-call | flops 1000000000 | bytes 1 | tf_op jit(solution)/shard_map/sort/pallas_call | solution.py:89
  20.5 0.9 copy-done.5
  21.4 5.5 %base.1 = (f32[768,1024]{1,0:T(8,128)}, f32[8,128]{1,0:T(8,128)S(1)}) custom-call(bf16[768,2048]{1,0:T(8,128)(2,1)S(1)} %copy-done.1, bf16[2048,1024]{1,0:T(8,128)(2,1)S(1)} %copy-done, bf16[240,2048]{1,0:T(8,128)(2,1)S(1)} %get-tuple-element.121._), custom_call_target="tpu_custom_call" | custom-call | flops 1000000000 | bytes 1 | tf_op jit(solution)/shard_map/base/pallas_call | solution.py:171
  26.9 0.0 reduce-scatter.2.cloned.1.call-update
  27.0 0.1 collective-permute-start.12
  27.0 0.7 collective-permute-start.13
  27.7 0.1 pad_add_fusion.here_ref
  27.8 1.7 %name_rows.1 = (s32[288,1]{1,0:T(8,128)S(1)}, s32[240,1]{1,0:T(8,128)S(1)}, s32[240,1]{1,0:T(8,128)S(1)}, s32[768,1]{1,0:T(8,128)S(1)}, s32[144,1]{1,0:T(8,128)S...) custom-call(s32[2]{0:T(128)S(1)} %pad_add_fusion.here_ref, ...), custom_call_target="tpu_custom_call" | custom-call | flops 1 | bytes 1 | tf_op jit(solution)/shard_map/name_rows/pallas_call | solution.py:145
  29.5 1.5 collective-permute-start.11
  31.1 3.2 %sort.4 = (bf16[288,2048]{1,0:T(8,128)(2,1)S(1)}, bf16[48,2048]{1,0:T(8,128)(2,1)}, bf16[48,2048]{1,0:T(8,128)(2,1)}, bf16[48,2048]{1,0:T(8,128)(2,1)}) custom-call(s32[1,768]{1,0:T(1,128)S(1)} %get-tuple-element.120.slot_ref, bf16[768,2048]{1,0:T(8,128)(2,1)S(1)} %copy-done.1, f32[8,128]{1,0:T(8,128)S(1)} %get-tuple-element.127.refs_0_), custom_call_target="tpu_custom_call" | custom-call | flops 1000000000 | bytes 1 | tf_op jit(solution)/shard_map/sort/pallas_call | solution.py:89
  34.3 0.1 fusion
  34.4 10.3 %shrink.7 = (f32[144,128]{1,0:T(8,128)S(1)}, f32[144,128]{1,0:T(8,128)S(1)}) custom-call(s32[3]{0:T(128)S(1)} %get-tuple-element.158.plan_ref, s32[4,128]{1,0:T(4,128)S(1)} %get-tuple-element.125.ends_ref, s32[288,1]{1,0:T(8,128)S(1)} %get-tuple-element.126.which_ref, bf16[24,128,2048]{2,1,0:T(8,128)(2,1)} %down_ref.9, ...), custom_call_target="tpu_custom_call" | custom-call | flops 1 | bytes 1 | tf_op jit(solution)/shard_map/shrink/pallas_call | solution.py:250
  44.7 1.8 %sort.5 = (bf16[144,2048]{1,0:T(8,128)(2,1)S(1)}, bf16[96,2048]{1,0:T(8,128)(2,1)S(1)}) custom-call(s32[1,768]{1,0:T(1,128)S(1)} %get-tuple-element.120.slot_ref, bf16[768,2048]{1,0:T(8,128)(2,1)S(1)} %copy-done.1, f32[144,128]{1,0:T(8,128)S(1)} %get-tuple-element.129.refs_0_), custom_call_target="tpu_custom_call" | custom-call | flops 1000000000 | bytes 1 | tf_op jit(solution)/shard_map/sort/pallas_call | solution.py:89
  46.5 2.9 %collective-permute-start.19 = (bf16[144,2048]{1,0:T(8,128)(2,1)S(1)}, bf16[144,2048]{1,0:T(8,128)(2,1)S(1)}, u32[]{:S(2)}, u32[]{:S(2)}) collective-permute-start(bf16[144,2048]{1,0:T(8,128)(2,1)S(1)} %get-tuple-element.131.refs_1_), channel_id=1, source_target_pairs={{0,8},{4,12},{8,0},{12,4},{1,9},{5,13},{9,1},{13,5},{2,10},{6,14},... | collective-permute-start | bytes 1769480 | tf_op jit(solution)/shard_map/ppermute | solution.py:406
  49.4 0.1 collective-permute-start.23
  49.5 19.9 %collective-permute-done.12.refs_0_ = bf16[240,2048]{1,0:T(8,128)(2,1)} collective-permute-done((bf16[240,2048]{1,0:T(8,128)(2,1)}, bf16[240,2048]{1,0:T(8,128)(2,1)}, u32[]{:S(2)}, u32[]{:S(2)}) %collective-permute-start.12) | collective-permute-done | bytes 983072 | tf_op jit(solution)/shard_map/ppermute | solution.py:406
  69.4 10.0 %shrink.8 = (f32[120,128]{1,0:T(8,128)S(1)}, f32[120,128]{1,0:T(8,128)S(1)}) custom-call(s32[3]{0:T(128)S(1)} %get-tuple-element.157.plan_ref, s32[4,128]{1,0:T(4,128)S(1)} %get-tuple-element.125.ends_ref, s32[240,1]{1,0:T(8,128)S(1)} %get-tuple-element.130.which_ref, bf16[24,128,2048]{2,1,0:T(8,128)(2,1)} %down_ref.9, ...), custom_call_target="tpu_custom_call" | custom-call | flops 1 | bytes 1 | tf_op jit(solution)/shard_map/shrink/pallas_call | solution.py:250
  79.4 0.0 collective-permute-done.13.refs_0_
  79.5 0.0 copy-start.8
  79.5 0.0 copy-start.20
  79.5 0.0 copy-start.10
  79.5 7.3 %shrink.9 = (f32[120,128]{1,0:T(8,128)S(1)}, f32[120,128]{1,0:T(8,128)S(1)}) custom-call(s32[3]{0:T(128)S(1)} %get-tuple-element.156.plan_ref, s32[4,128]{1,0:T(4,128)S(1)} %get-tuple-element.125.ends_ref, s32[240,1]{1,0:T(8,128)S(1)} %get-tuple-element.133.which_ref, bf16[24,128,2048]{2,1,0:T(8,128)(2,1)S(1)} %bitcast.14, ...), custom_call_target="tpu_custom_call" | custom-call | flops 1 | bytes 1 | tf_op jit(solution)/shard_map/shrink/pallas_call | solution.py:250
  86.9 0.1 collective-permute-start.14
  87.0 1.5 collective-permute-start.15
  88.4 0.0 collective-permute-done.11
  88.4 0.4 collective-permute-start.16
  88.9 0.0 collective-permute-done.14.refs_1_
  88.9 5.9 %collective-permute-done.15.refs_2_ = f32[384,128]{1,0:T(8,128)S(1)} collective-permute-done((f32[384,128]{1,0:T(8,128)S(1)}, f32[384,128]{1,0:T(8,128)S(1)}, u32[]{:S(2)}, u32[]{:S(2)}) %collective-permute-start.15) | collective-permute-done | bytes 196640 | tf_op jit(solution)/shard_map/ppermute | solution.py:406
  94.7 3.4 %collective-permute-done.16.refs_3_ = f32[384,128]{1,0:T(8,128)S(1)} collective-permute-done((f32[384,128]{1,0:T(8,128)S(1)}, f32[384,128]{1,0:T(8,128)S(1)}, u32[]{:S(2)}, u32[]{:S(2)}) %collective-permute-start.16) | collective-permute-done | bytes 196640 | tf_op jit(solution)/shard_map/ppermute | solution.py:406
  98.1 2.3 %expand.5 = (f32[288,256]{1,0:T(8,128)S(1)}, s16[256,256]{1,0:T(8,128)(2,1)S(1)}, s16[256,256]{1,0:T(8,128)(2,1)S(1)}) custom-call(s32[768,1]{1,0:T(8,128)S(1)} %get-tuple-element.123.which_ref, f32[1,24]{1,0:T(1,128)S(1)} %bitcast.19, bf16[1536,256]{1,0:T(8,128)(2,1)S(1)} %bitcast.16, f32[384,128]{1,0:T(8,128)S(1)} %constant_dynamic-update-slice_fusion.refs_0_, ...), custom_call_target="tpu_custom_call" | custom-call | flops 1 | bytes 1 | tf_op jit(solution)/shard_map/expand/pallas_call | solution.py:344
  100.5 0.8 place.1.refs_2_
  101.3 5.9 %collective-permute-done.19.refs_0_ = bf16[144,2048]{1,0:T(8,128)(2,1)S(1)} collective-permute-done((bf16[144,2048]{1,0:T(8,128)(2,1)S(1)}, bf16[144,2048]{1,0:T(8,128)(2,1)S(1)}, u32[]{:S(2)}, u32[]{:S(2)}) %collective-permute-start.19) | collective-permute-done | bytes 589856 | tf_op jit(solution)/shard_map/ppermute | solution.py:406
  107.2 5.4 %shrink.10 = (f32[72,128]{1,0:T(8,128)S(1)}, f32[72,128]{1,0:T(8,128)S(1)}) custom-call(s32[3]{0:T(128)S(1)} %get-tuple-element.155.plan_ref, s32[4,128]{1,0:T(4,128)S(1)} %get-tuple-element.125.ends_ref, s32[144,1]{1,0:T(8,128)S(1)} %get-tuple-element.142.which_ref, bf16[24,128,2048]{2,1,0:T(8,128)(2,1)S(1)} %bitcast.14, ...), custom_call_target="tpu_custom_call" | custom-call | flops 1 | bytes 1 | tf_op jit(solution)/shard_map/shrink/pallas_call | solution.py:250
  112.6 1.4 collective-permute-start.20
  114.0 2.6 %collective-permute-done.20 = f32[72,128]{1,0:T(8,128)S(1)} collective-permute-done((f32[72,128]{1,0:T(8,128)S(1)}, f32[72,128]{1,0:T(8,128)S(1)}, u32[]{:S(2)}, u32[]{:S(2)}) %collective-permute-start.20) | collective-permute-done | bytes 36896 | tf_op jit(solution)/shard_map/ppermute | solution.py:406
  116.6 0.0 collective-permute-start.21
  116.6 10.4 %collective-permute-start.17 = (s16[256,256]{1,0:T(8,128)(2,1)S(1)}, s16[256,256]{1,0:T(8,128)(2,1)S(1)}, u32[]{:S(2)}, u32[]{:S(2)}) collective-permute-start(s16[256,256]{1,0:T(8,128)(2,1)S(1)} %get-tuple-element.140), channel_id=1, source_target_pairs={{0,4},{4,0},{8,12},{12,8},{1,5},{5,1},{9,13},{13,9},{2,6},{6,2},{1... | collective-permute-start | bytes 393224 | tf_op jit(solution)/shard_map/ppermute | solution.py:406
  127.0 0.8 collective-permute-start.18
  127.8 0.0 collective-permute-done.21.refs_1_
  127.8 0.7 expand.6.refs_1_
  128.5 0.0 collective-permute-done.23.refs_0_
  128.5 3.2 %shrink.11 = (f32[48,128]{1,0:T(8,128)S(1)}, f32[48,128]{1,0:T(8,128)S(1)}) custom-call(s32[3]{0:T(128)S(1)} %get-tuple-element.154.plan_ref, s32[4,128]{1,0:T(4,128)S(1)} %get-tuple-element.125.ends_ref, s32[96,1]{1,0:T(8,128)S(1)} %get-tuple-element.145.which_ref, bf16[24,128,2048]{2,1,0:T(8,128)(2,1)S(1)} %bitcast.14, ...), custom_call_target="tpu_custom_call" | custom-call | flops 1 | bytes 1 | tf_op jit(solution)/shard_map/shrink/pallas_call | solution.py:250
  131.7 1.6 %collective-permute-start.24 = (f32[48,128]{1,0:T(8,128)S(1)}, f32[48,128]{1,0:T(8,128)S(1)}, u32[]{:S(2)}, u32[]{:S(2)}) collective-permute-start(f32[48,128]{1,0:T(8,128)S(1)} %get-tuple-element.148), channel_id=1, source_target_pairs={{0,2},{2,0},{1,3},{3,1},{4,6},{6,4},{5,7},{7,5},{8,10},{10,8},{9,1... | collective-permute-start | bytes 73736 | tf_op jit(solution)/shard_map/ppermute | solution.py:406
  133.3 2.3 %collective-permute-done.24 = f32[48,128]{1,0:T(8,128)S(1)} collective-permute-done((f32[48,128]{1,0:T(8,128)S(1)}, f32[48,128]{1,0:T(8,128)S(1)}, u32[]{:S(2)}, u32[]{:S(2)}) %collective-permute-start.24) | collective-permute-done | bytes 24608 | tf_op jit(solution)/shard_map/ppermute | solution.py:406
  135.6 0.0 collective-permute-start.25
  135.6 0.4 collective-permute-start.22
  136.1 0.8 collective-permute-done.25.refs_1_
  136.8 0.7 expand.7
  137.5 1.9 %collective-permute-start.26 = (s16[112,256]{1,0:T(8,128)(2,1)S(1)}, s16[112,256]{1,0:T(8,128)(2,1)S(1)}, u32[]{:S(2)}, u32[]{:S(2)}) collective-permute-start(s16[112,256]{1,0:T(8,128)(2,1)S(1)} %expand.7), channel_id=1, source_target_pairs={{0,8},{4,12},{8,0},{12,4},{1,9},{5,13},{9,1},{13,5},{2,10},{6,14},... | collective-permute-start | bytes 172040 | tf_op jit(solution)/shard_map/ppermute | solution.py:406
  139.4 0.0 collective-permute-done.18
  139.5 5.4 %collective-permute-done.22 = s16[160,256]{1,0:T(8,128)(2,1)S(1)} collective-permute-done((s16[160,256]{1,0:T(8,128)(2,1)S(1)}, s16[160,256]{1,0:T(8,128)(2,1)S(1)}, u32[]{:S(2)}, u32[]{:S(2)}) %collective-permute-start.22) | collective-permute-done | bytes 81952 | tf_op jit(solution)/shard_map/ppermute | solution.py:406
  144.8 0.8 collective-permute-done.26
  145.6 2.2 %conditional.1 = (bf16[768,256]{1,0:T(8,128)(2,1)S(1)}) conditional(s32[]{:T(128)} %bitcast.3, (s32[768,1]{1,0:T(8,128)S(1)}, f32[768,256]{1,0:T(8,128)}, f32[768,256]{1,0:T(8,128)S(1)}, s16[256,256]{1,0:T(8,128)(2,1)S(1)}, s16[256,256]{1,0:T(8,128)(2,1)S(1)}, /*index=5*/s16[160,256]{1,0:T(8,128)(2,1)S(1)}, s16[112,256]{1,0:T(8,128)(2,1)S(1)}) %tuple.25, ...), branch_computations={%region_1.0_spmd, %region_2.0_spmd} | conditional | flops 9219 | bytes 17906580 | solution.py:518
  145.8 2.0 %merge.2 = bf16[768,256]{1,0:T(8,128)(2,1)S(1)} custom-call(s32[768,1]{1,0:T(8,128)S(1)} %get-tuple-element.55.target_ref, f32[768,256]{1,0:T(8,128)} %get-tuple-element.56.refs_0_, f32[768,256]{1,0:T(8,128)S(1)} %get-tuple-element.57.refs_1_, s16[256,256]{1,0:T(8,128)(2,1)S(1)} %get-tuple-element.58.refs_2_, s16[256,256]{1,0:T(8,128)(2,1)S(1)} %get-tuple-element.59.refs_3_, ...), custom_call_target="tpu_custom_call" | custom-call | flops 1 | bytes 1 | tf_op jit(solution)/shard_map/cond/branch_0_fun/merge/pallas_call | solution.py:396
  147.8 0.0 copy-start.14
  147.8 0.7 copy-done.14
  (37 shorter events, 0.1 us)
Async XLA Ops:
  6.5 11.2 %copy-start.1 = (bf16[768,2048]{1,0:T(8,128)(2,1)S(1)}, bf16[768,2048]{1,0:T(8,128)(2,1)}, u32[]{:S(2)}) copy-start(bf16[768,2048]{1,0:T(8,128)(2,1)} %tok_ref.7) | copy-start | bytes 9437188
  6.5 139.1 %reduce-scatter.2.cloned.1.call-start = ((), (), s32[]{:S(2)}) async-start(), calls=%async_computation.1 | async-start | bytes 3932160 | tf_op jit(solution)/shard_map/reduce_scatter | solution.py:443
  6.5 8.0 %collective-permute-start.8 = (s32[1,768]{1,0:T(1,128)}, s32[1,768]{1,0:T(1,128)S(1)}, u32[]{:S(2)}, u32[]{:S(2)}) collective-permute-start(s32[1,768]{1,0:T(1,128)} %bitcast.7), channel_id=1, source_target_pairs={{0,4},{4,0},{8,12},{12,8},{1,5},{5,1},{9,13},{13,9},{2,6},{6,2},{1... | collective-permute-start | bytes 9224 | tf_op jit(solution)/shard_map/ppermute | solution.py:406
  9.6 5.0 %collective-permute-start.9 = (s32[1,768]{1,0:T(1,128)}, s32[1,768]{1,0:T(1,128)S(1)}, u32[]{:S(2)}, u32[]{:S(2)}) collective-permute-start(s32[1,768]{1,0:T(1,128)} %bitcast.8), channel_id=1, source_target_pairs={{0,8},{4,12},{8,0},{12,4},{1,9},{5,13},{9,1},{13,5},{2,10},{6,14},... | collective-permute-start | bytes 9224 | tf_op jit(solution)/shard_map/ppermute | solution.py:406
  12.2 5.6 %collective-permute-start.10 = (s32[1,768]{1,0:T(1,128)}, s32[1,768]{1,0:T(1,128)S(1)}, u32[]{:S(2)}, u32[]{:S(2)}) collective-permute-start(s32[1,768]{1,0:T(1,128)} %bitcast.9), channel_id=1, source_target_pairs={{0,12},{4,8},{8,4},{12,0},{1,13},{5,9},{9,5},{13,1},{2,14},{6,10},... | collective-permute-start | bytes 9224 | tf_op jit(solution)/shard_map/ppermute | solution.py:406
  12.2 0.8 copy-start.3
  12.9 8.5 %copy-start = (bf16[2048,1024]{1,0:T(8,128)(2,1)S(1)}, bf16[2048,1024]{1,0:T(8,128)(2,1)}, u32[]{:S(2)}) copy-start(bf16[2048,1024]{1,0:T(8,128)(2,1)} %weight_ref.1) | copy-start | bytes 12582916
  20.5 0.9 copy-start.5
  21.4 5.5 %copy-start.2 = (bf16[240,2048]{1,0:T(8,128)(2,1)}, bf16[240,2048]{1,0:T(8,128)(2,1)S(1)}, u32[]{:S(2)}) copy-start(bf16[240,2048]{1,0:T(8,128)(2,1)S(1)} %get-tuple-element.121._) | copy-start | bytes 2949124
  26.9 0.9 copy-start.4
  27.0 42.5 %collective-permute-start.12 = (bf16[240,2048]{1,0:T(8,128)(2,1)}, bf16[240,2048]{1,0:T(8,128)(2,1)}, u32[]{:S(2)}, u32[]{:S(2)}) collective-permute-start(bf16[240,2048]{1,0:T(8,128)(2,1)} %copy-done.2), channel_id=1, source_target_pairs={{0,4},{4,0},{8,12},{12,8},{1,5},{5,1},{9,13},{13,9},{2,6},{6,2},{1... | collective-permute-start | bytes 2949128 | tf_op jit(solution)/shard_map/ppermute | solution.py:406
  27.0 52.4 %collective-permute-start.13 = (bf16[240,2048]{1,0:T(8,128)(2,1)}, bf16[240,2048]{1,0:T(8,128)(2,1)}, u32[]{:S(2)}, u32[]{:S(2)}) collective-permute-start(bf16[240,2048]{1,0:T(8,128)(2,1)} %copy-done.5), channel_id=1, source_target_pairs={{0,12},{4,8},{8,4},{12,0},{1,13},{5,9},{9,5},{13,1},{2,14},{6,10},... | collective-permute-start | bytes 2949128 | tf_op jit(solution)/shard_map/ppermute | solution.py:406
  29.5 58.9 %collective-permute-start.11 = (s32[1,128]{1,0:T(1,128)S(1)}, s32[1,128]{1,0:T(1,128)S(1)}, u32[]{:S(2)}, u32[]{:S(2)}) collective-permute-start(s32[1,128]{1,0:T(1,128)S(1)} %get-tuple-element.118), channel_id=1, source_target_pairs={{0,16},{16,0},{1,17},{17,1},{2,18},{18,2},{3,19},{19,3},{4,20},{20... | collective-permute-start | bytes 1544 | tf_op jit(solution)/shard_map/ppermute | solution.py:406
  34.4 45.0 %slice-start = ((s8[12582912]{0:T(1024)(128)(4,1)}), s8[4194304]{0:T(1024)(128)(4,1)S(1)}, s32[]{:S(2)}) async-start(s8[12582912]{0:T(1024)(128)(4,1)} %bitcast.13), calls=%async_computation.2 | async-start | bytes 8388608
  34.4 45.1 %slice-start.1 = ((s8[12582912]{0:T(1024)(128)(4,1)}), s8[4194304]{0:T(1024)(128)(4,1)S(1)}, s32[]{:S(2)}) async-start(s8[12582912]{0:T(1024)(128)(4,1)} %bitcast.13), calls=%async_computation.3 | async-start | bytes 8388608
  46.5 60.7 %collective-permute-start.19 = (bf16[144,2048]{1,0:T(8,128)(2,1)S(1)}, bf16[144,2048]{1,0:T(8,128)(2,1)S(1)}, u32[]{:S(2)}, u32[]{:S(2)}) collective-permute-start(bf16[144,2048]{1,0:T(8,128)(2,1)S(1)} %get-tuple-element.131.refs_1_), channel_id=1, source_target_pairs={{0,8},{4,12},{8,0},{12,4},{1,9},{5,13},{9,1},{13,5},{2,10},{6,14},... | collective-permute-start | bytes 1769480 | tf_op jit(solution)/shard_map/ppermute | solution.py:406
  49.4 79.1 %collective-permute-start.23 = (bf16[96,2048]{1,0:T(8,128)(2,1)S(1)}, bf16[96,2048]{1,0:T(8,128)(2,1)S(1)}, u32[]{:S(2)}, u32[]{:S(2)}) collective-permute-start(bf16[96,2048]{1,0:T(8,128)(2,1)S(1)} %get-tuple-element.146), channel_id=1, source_target_pairs={{0,8},{4,12},{8,0},{12,4},{1,9},{5,13},{9,1},{13,5},{2,10},{6,14},... | collective-permute-start | bytes 1179656 | tf_op jit(solution)/shard_map/ppermute | solution.py:406
  69.4 10.0 %slice-start.2 = ((s8[12582912]{0:T(1024)(128)(4,1)}), s8[4194304]{0:T(1024)(128)(4,1)S(1)}, s32[]{:S(2)}) async-start(s8[12582912]{0:T(1024)(128)(4,1)} %bitcast.13), calls=%async_computation.4 | async-start | bytes 8388608
  79.5 18.6 %copy-start.8 = (bf16[24,64,256]{2,1,0:T(8,128)(2,1)S(1)}, bf16[24,64,256]{2,1,0:T(8,128)(2,1)}, u32[]{:S(2)}) copy-start(bf16[24,64,256]{2,1,0:T(8,128)(2,1)} %param.11) | copy-start | bytes 2359300
  79.5 18.6 %copy-start.20 = (f32[24]{0:T(128)S(1)}, f32[24]{0:T(128)}, u32[]{:S(2)}) copy-start(f32[24]{0:T(128)} %param.12) | copy-start | bytes 292
  79.5 21.0 %copy-start.10 = (s32[768,1]{1,0:T(8,128)S(1)}, s32[768,1]{1,0:T(8,128)}, u32[]{:S(2)}) copy-start(s32[768,1]{1,0:T(8,128)} %get-tuple-element.119.target_ref) | copy-start | bytes 9220
  86.9 2.0 %collective-permute-start.14 = (f32[384,128]{1,0:T(8,128)S(1)}, f32[384,128]{1,0:T(8,128)S(1)}, u32[]{:S(2)}, u32[]{:S(2)}) collective-permute-start(f32[384,128]{1,0:T(8,128)S(1)} %constant_dynamic-update-slice_fusion.refs_0_), channel_id=1, source_target_pairs={{0,1},{1,0},{2,3},{3,2},{4,5},{5,4},{6,7},{7,6},{8,9},{9,8},{10,11... | collective-permute-start | bytes 589832 | tf_op jit(solution)/shard_map/ppermute | solution.py:406
  87.0 7.8 %collective-permute-start.15 = (f32[384,128]{1,0:T(8,128)S(1)}, f32[384,128]{1,0:T(8,128)S(1)}, u32[]{:S(2)}, u32[]{:S(2)}) collective-permute-start(f32[384,128]{1,0:T(8,128)S(1)} %constant_dynamic-update-slice_fusion.3), channel_id=1, source_target_pairs={{0,2},{1,3},{2,0},{3,1},{4,6},{5,7},{6,4},{7,5},{8,10},{9,11},{10,... | collective-permute-start | bytes 589832 | tf_op jit(solution)/shard_map/ppermute | solution.py:406
  88.4 9.7 %collective-permute-start.16 = (f32[384,128]{1,0:T(8,128)S(1)}, f32[384,128]{1,0:T(8,128)S(1)}, u32[]{:S(2)}, u32[]{:S(2)}) collective-permute-start(f32[384,128]{1,0:T(8,128)S(1)} %constant_dynamic-update-slice_fusion.3), channel_id=1, source_target_pairs={{0,3},{1,2},{2,1},{3,0},{4,7},{5,6},{6,5},{7,4},{8,11},{9,10},{10,... | collective-permute-start | bytes 589832 | tf_op jit(solution)/shard_map/ppermute | solution.py:406
  112.6 4.0 %collective-permute-start.20 = (f32[72,128]{1,0:T(8,128)S(1)}, f32[72,128]{1,0:T(8,128)S(1)}, u32[]{:S(2)}, u32[]{:S(2)}) collective-permute-start(f32[72,128]{1,0:T(8,128)S(1)} %get-tuple-element.144), channel_id=1, source_target_pairs={{0,2},{2,0},{1,3},{3,1},{4,6},{6,4},{5,7},{7,5},{8,10},{10,8},{9,1... | collective-permute-start | bytes 110600 | tf_op jit(solution)/shard_map/ppermute | solution.py:406
  116.6 11.2 %collective-permute-start.21 = (f32[72,128]{1,0:T(8,128)S(1)}, f32[72,128]{1,0:T(8,128)S(1)}, u32[]{:S(2)}, u32[]{:S(2)}) collective-permute-start(f32[72,128]{1,0:T(8,128)S(1)} %add.15.refs_0_), channel_id=1, source_target_pairs={{0,1},{1,0},{2,3},{3,2},{4,5},{5,4},{6,7},{7,6},{8,9},{9,8},{10,11... | collective-permute-start | bytes 110600 | tf_op jit(solution)/shard_map/ppermute | solution.py:406
  116.6 22.8 %collective-permute-start.17 = (s16[256,256]{1,0:T(8,128)(2,1)S(1)}, s16[256,256]{1,0:T(8,128)(2,1)S(1)}, u32[]{:S(2)}, u32[]{:S(2)}) collective-permute-start(s16[256,256]{1,0:T(8,128)(2,1)S(1)} %get-tuple-element.140), channel_id=1, source_target_pairs={{0,4},{4,0},{8,12},{12,8},{1,5},{5,1},{9,13},{13,9},{2,6},{6,2},{1... | collective-permute-start | bytes 393224 | tf_op jit(solution)/shard_map/ppermute | solution.py:406
  127.0 12.5 %collective-permute-start.18 = (s16[256,256]{1,0:T(8,128)(2,1)S(1)}, s16[256,256]{1,0:T(8,128)(2,1)S(1)}, u32[]{:S(2)}, u32[]{:S(2)}) collective-permute-start(s16[256,256]{1,0:T(8,128)(2,1)S(1)} %get-tuple-element.141), channel_id=1, source_target_pairs={{0,12},{4,8},{8,4},{12,0},{1,13},{5,9},{9,5},{13,1},{2,14},{6,10},... | collective-permute-start | bytes 393224 | tf_op jit(solution)/shard_map/ppermute | solution.py:406
  128.5 17.1 %copy-start.21 = (bf16[48,2048]{1,0:T(8,128)(2,1)S(1)}, bf16[48,2048]{1,0:T(8,128)(2,1)}, u32[]{:S(2)}) copy-start(bf16[48,2048]{1,0:T(8,128)(2,1)} %get-tuple-element.149) | copy-start | bytes 589828
  128.5 17.1 %copy-start.22 = (bf16[48,2048]{1,0:T(8,128)(2,1)S(1)}, bf16[48,2048]{1,0:T(8,128)(2,1)}, u32[]{:S(2)}) copy-start(bf16[48,2048]{1,0:T(8,128)(2,1)} %get-tuple-element.150) | copy-start | bytes 589828
  128.5 17.1 %copy-start.23 = (bf16[48,2048]{1,0:T(8,128)(2,1)S(1)}, bf16[48,2048]{1,0:T(8,128)(2,1)}, u32[]{:S(2)}) copy-start(bf16[48,2048]{1,0:T(8,128)(2,1)} %get-tuple-element.151) | copy-start | bytes 589828
  131.7 3.9 %collective-permute-start.24 = (f32[48,128]{1,0:T(8,128)S(1)}, f32[48,128]{1,0:T(8,128)S(1)}, u32[]{:S(2)}, u32[]{:S(2)}) collective-permute-start(f32[48,128]{1,0:T(8,128)S(1)} %get-tuple-element.148), channel_id=1, source_target_pairs={{0,2},{2,0},{1,3},{3,1},{4,6},{6,4},{5,7},{7,5},{8,10},{10,8},{9,1... | collective-permute-start | bytes 73736 | tf_op jit(solution)/shard_map/ppermute | solution.py:406
  135.6 1.2 collective-permute-start.25
  135.6 9.2 %collective-permute-start.22 = (s16[160,256]{1,0:T(8,128)(2,1)S(1)}, s16[160,256]{1,0:T(8,128)(2,1)S(1)}, u32[]{:S(2)}, u32[]{:S(2)}) collective-permute-start(s16[160,256]{1,0:T(8,128)(2,1)S(1)} %expand.6.refs_1_), channel_id=1, source_target_pairs={{0,8},{4,12},{8,0},{12,4},{1,9},{5,13},{9,1},{13,5},{2,10},{6,14},... | collective-permute-start | bytes 245768 | tf_op jit(solution)/shard_map/ppermute | solution.py:406
  137.5 8.1 %collective-permute-start.26 = (s16[112,256]{1,0:T(8,128)(2,1)S(1)}, s16[112,256]{1,0:T(8,128)(2,1)S(1)}, u32[]{:S(2)}, u32[]{:S(2)}) collective-permute-start(s16[112,256]{1,0:T(8,128)(2,1)S(1)} %expand.7), channel_id=1, source_target_pairs={{0,8},{4,12},{8,0},{12,4},{1,9},{5,13},{9,1},{13,5},{2,10},{6,14},... | collective-permute-start | bytes 172040 | tf_op jit(solution)/shard_map/ppermute | solution.py:406
  147.8 0.7 copy-start.14
Sparse Core Ops, SparseCore 0:
  27.1 36.1 reduce-scatter.1

commit v11 on v10

--- a/solution.py
+++ b/solution.py
@@ -436,12 +436,14 @@
     ids_row = token_adapter_index.reshape(1, rows)
     ids_heard = [ids_row] + [swap(ids_row, "dp", owners, j) for j in range(1, owners)]
     slot, target = route(ids_row, me.reshape(1), owners, owned, cap)
-    sent = far + [near]
-    packed = dict(zip(sent, sort_rows(tokens, slot, cap, sent, tuple(ids_heard[1:]))))
-    received = {p: swap(packed[p], "dp", owners, p[0]) for p in sent}
+    packed = dict(zip([near], sort_rows(tokens, slot, cap, [near], tuple(ids_heard[1:]))))
     base_part, base_done = base_product(tokens, key_value_weight, packed[near])
     base = lax.psum_scatter(base_part, feature_axes, scatter_dimension=1, tiled=True)
-    packed |= zip([own] + extra, sort_rows(tokens, slot, cap, [own] + extra, (base_done,)))
+    received = {near: swap(packed[near], "dp", owners, near[0])}
+    if far:
+        packed |= zip(far, sort_rows(tokens, slot, cap, far, (base_done,)))
+        received |= {p: swap(packed[p], "dp", owners, p[0]) for p in far}
+    packed |= zip([own] + extra, sort_rows(tokens, slot, cap, [own] + extra, (packed[(far or [near])[0]],)))
     gated = [p for pieces in last for p in pieces]
 
     early = [own, near] + far
@@ -463,11 +465,12 @@
             for d in range(1, sharers)
         ]
 
-    def deltas_of(pieces, blocks, names, ends, plan, down, up, scale, later_than):
+    def deltas_of(pieces, blocks, names, ends, plan, down, up, scale, later_than, sooner=()):
         mine, other = shrink(pieces, blocks, names, ends, plan, down, later_than)
         sizes = tuple(b.shape[0] for b in blocks)
         lines = exchange(mine, other)
-        return expand(lines, (mine.shape[0],), names, scale, up, sizes)
+        groups = (mine.shape[0],)
+        return expand(lines, groups, names, scale, up, sizes, later_than=sooner)
 
     def send_back(pieces, deltas):
         return [swap(d, "dp", owners, p[0]) for p, d in zip(pieces, deltas)]
@@ -476,14 +479,14 @@
         return [b * cap + f for b, f, _ in pieces]
 
     weights = (adapter_down_weight, up, scale)
-    packed |= zip([own] + extra, sort_rows(tokens, slot, cap, [own] + extra, (base_done,)))
+    packed |= zip([own] + extra, sort_rows(tokens, slot, cap, [own] + extra, (packed[(far or [near])[0]],)))
     for d in range(1, lax.axis_size("parts")):
         largest = jnp.maximum(largest, swap(largest, "parts", lax.axis_size("parts"), d))
     down = adapter_down_weight
     shares = [shrink([own], [packed[own]], names[0], ends, plans[0], down)]
     packed |= zip(gated, sort_rows(tokens, slot, cap, gated, (shares[0][0],)))
     received |= {p: swap(packed[p], "dp", owners, p[0]) for p in gated}
-    waits = (packed[gated[0]],)
+    waits = (packed[gated[0]], largest)
     for k, p in enumerate(early[1:], 1):
         shares.append(shrink([p], [received[p]], names[k], ends, plans[k], down, waits))
         waits = (shares[-1][0],)
@@ -496,9 +499,10 @@
     done = early[1:]
     for k, pieces in enumerate(last):
         blocks = [received[p] for p in pieces]
-        waits = (deltas[0], parts[1], largest)
+        waits = (deltas[0], parts[1])
+        sooner = tuple(returned[-1:]) if k else ()
         deltas = deltas_of(
-            pieces, blocks, names[here + 1 + k], ends, plans[here + 1 + k], *weights, waits
+            pieces, blocks, names[here + 1 + k], ends, plans[here + 1 + k], *weights, waits, sooner
         )
         returned += send_back(pieces, deltas)
         done += pieces

time: 155 us -> 159 us (1.026)
  waiting for transfers between devices: 50.1 us -> 52.6 us
    ppermute x19, waiting for transfers between devices: 50.1 us -> 52.6 us  [swap(): return lax.ppermute(x, axes, [(i, i ^ distance) for i in range(size)])]
    pallas_call x3 -> x4, Pallas kernels: 7.8 us -> 9.71 us  [sort_rows(): pl.pallas_call(functools.partial(sort_kernel, cap, pieces, len(later_than...]
    unnamed x35 -> x33, local copies, waits for them, and re-layouts: 2.51 us -> 3.19 us
where the time goes in v11:
time: 159 us
  Pallas kernels  60 us (38%)
  waiting for transfers between devices  52.6 us (33%)
  starting transfers between devices  29.2 us (18%)
  between operations  13.8 us (9%)
  local copies, waits for them, and re-layouts  3.27 us (2%)
    ppermute x19, waiting for transfers between devices, swap(): return lax.ppermute(x, axes, [(i, i ^ distance) for i in range(size)])  52.6 us
    pallas_call x5, Pallas kernels, shrink(): pl.pallas_call(functools.partial(shrink_kernel, pieces, group, fine), gri...  35.8 us
    ppermute x19, starting transfers between devices, swap(): return lax.ppermute(x, axes, [(i, i ^ distance) for i in range(size)])  29.2 us
    pallas_call x4, Pallas kernels, sort_rows(): pl.pallas_call(functools.partial(sort_kernel, cap, pieces, len(later_than...  9.71 us
    pallas_call x1, Pallas kernels, base_product(): pl.pallas_call(base_kernel, grid=(columns // step,), in_specs=[pl.BlockSp...  4.74 us
    pallas_call x3, Pallas kernels, expand(): pl.pallas_call(functools.partial(expand_kernel, groups, sizes, len(lines)...  3.69 us
    unnamed x33, local copies, waits for them, and re-layouts  3.19 us
  transfers between devices with their start and end apart: 20, of which 10 were waited for; matrix products, arithmetic and copies ran while one was open for 0% of the time, Pallas kernels for 32%

profile of v11, /device:TPU:0, one launch (start us, length us, event | category | flops | bytes accessed | tf_op | source)
XLA Modules:
  0.0 159.2 jit_solution(18233056589707201731)
XLA Ops:
  6.5 3.0 %collective-permute-start.8 = (s32[1,768]{1,0:T(1,128)}, s32[1,768]{1,0:T(1,128)S(1)}, u32[]{:S(2)}, u32[]{:S(2)}) collective-permute-start(s32[1,768]{1,0:T(1,128)} %bitcast.7), channel_id=1, source_target_pairs={{0,4},{4,0},{8,12},{12,8},{1,5},{5,1},{9,13},{13,9},{2,6},{6,2},{1... | collective-permute-start | bytes 9224 | tf_op jit(solution)/shard_map/ppermute | solution.py:406
  9.6 2.6 %collective-permute-start.9 = (s32[1,768]{1,0:T(1,128)}, s32[1,768]{1,0:T(1,128)S(1)}, u32[]{:S(2)}, u32[]{:S(2)}) collective-permute-start(s32[1,768]{1,0:T(1,128)} %bitcast.8), channel_id=1, source_target_pairs={{0,8},{4,12},{8,0},{12,4},{1,9},{5,13},{9,1},{13,5},{2,10},{6,14},... | collective-permute-start | bytes 9224 | tf_op jit(solution)/shard_map/ppermute | solution.py:406
  12.2 0.0 collective-permute-start.10
  12.2 0.7 copy-done.4
  12.9 1.6 %route.1 = (s32[1,768]{1,0:T(1,128)S(1)}, s32[768,1]{1,0:T(8,128)}) custom-call(s32[1]{0:T(128)} %bitcast.me_ref, s32[1,768]{1,0:T(1,128)S(1)} %bitcast.10), custom_call_target="tpu_custom_call" | custom-call | flops 1000000000 | bytes 1 | tf_op jit(solution)/shard_map/route/pallas_call | solution.py:54
  14.5 0.0 collective-permute-done.8.refs_1_.refs_0_
  14.5 0.0 collective-permute-done.9.refs_2_.refs_1_
  14.5 3.2 %collective-permute-done.10.refs_3_.refs_2_ = s32[1,768]{1,0:T(1,128)S(1)} collective-permute-done((s32[1,768]{1,0:T(1,128)}, s32[1,768]{1,0:T(1,128)S(1)}, u32[]{:S(2)}, u32[]{:S(2)}) %collective-permute-start.10) | collective-permute-done | bytes 3104 | tf_op jit(solution)/shard_map/ppermute | solution.py:406
  17.8 1.8 %sort.4._ = bf16[240,2048]{1,0:T(8,128)(2,1)S(1)} custom-call(s32[1,768]{1,0:T(1,128)S(1)} %get-tuple-element.118.slot_ref, bf16[768,2048]{1,0:T(8,128)(2,1)S(1)} %copy-done, s32[1,768]{1,0:T(1,128)S(1)} %collective-permute-done.8.refs_1_.refs_0_, s32[1,768]{1,0:T(1,128)S(1)} %collective-permute-done.9.refs_2_.refs_1_, ...), custom_call_target="tpu_custom_call" | custom-call | flops 1000000000 | bytes 1 | tf_op jit(solution)/shard_map/sort/pallas_call | solution.py:89
  19.6 4.7 %base.1 = (f32[768,1024]{1,0:T(8,128)S(1)}, f32[8,128]{1,0:T(8,128)S(1)}) custom-call(bf16[768,2048]{1,0:T(8,128)(2,1)S(1)} %copy-done, bf16[2048,1024]{1,0:T(8,128)(2,1)S(1)} %copy-done.1, bf16[240,2048]{1,0:T(8,128)(2,1)S(1)} %sort.4._), custom_call_target="tpu_custom_call" | custom-call | flops 1000000000 | bytes 1 | tf_op jit(solution)/shard_map/base/pallas_call | solution.py:171
  24.4 1.6 %copy-done.3 = f32[768,1024]{1,0:T(8,128)} copy-done((f32[768,1024]{1,0:T(8,128)}, f32[768,1024]{1,0:T(8,128)S(1)}, u32[]{:S(2)}) %copy-start.3) | copy-done | bytes 3145752
  26.0 0.0 reduce-scatter.2.cloned.1.call-update
  26.0 0.1 collective-permute-start.12
  26.1 2.8 %sort.5.refs_0_ = bf16[240,2048]{1,0:T(8,128)(2,1)} custom-call(s32[1,768]{1,0:T(1,128)S(1)} %get-tuple-element.118.slot_ref, bf16[768,2048]{1,0:T(8,128)(2,1)S(1)} %copy-done, f32[8,128]{1,0:T(8,128)S(1)} %get-tuple-element.124.refs_0_), custom_call_target="tpu_custom_call" | custom-call | flops 1000000000 | bytes 1 | tf_op jit(solution)/shard_map/sort/pallas_call | solution.py:89
  29.0 0.6 collective-permute-start.13
  29.5 0.1 pad_add_fusion.here_ref
  29.6 1.7 %name_rows.1 = (s32[288,1]{1,0:T(8,128)S(1)}, s32[240,1]{1,0:T(8,128)S(1)}, s32[240,1]{1,0:T(8,128)S(1)}, s32[768,1]{1,0:T(8,128)S(1)}, s32[144,1]{1,0:T(8,128)S...) custom-call(s32[2]{0:T(128)S(1)} %pad_add_fusion.here_ref, ...), custom_call_target="tpu_custom_call" | custom-call | flops 1 | bytes 1 | tf_op jit(solution)/shard_map/name_rows/pallas_call | solution.py:145
  31.3 1.6 collective-permute-start.11
  32.9 3.2 %sort.6 = (bf16[288,2048]{1,0:T(8,128)(2,1)S(1)}, bf16[48,2048]{1,0:T(8,128)(2,1)S(1)}, bf16[48,2048]{1,0:T(8,128)(2,1)}, bf16[48,2048]{1,0:T(8,128)(2,1)}) custom-call(s32[1,768]{1,0:T(1,128)S(1)} %get-tuple-element.118.slot_ref, bf16[768,2048]{1,0:T(8,128)(2,1)S(1)} %copy-done, bf16[240,2048]{1,0:T(8,128)(2,1)} %sort.5.refs_0_), custom_call_target="tpu_custom_call" | custom-call | flops 1000000000 | bytes 1 | tf_op jit(solution)/shard_map/sort/pallas_call | solution.py:89
  36.1 0.1 fusion
  36.2 9.9 %shrink.7 = (f32[144,128]{1,0:T(8,128)S(1)}, f32[144,128]{1,0:T(8,128)S(1)}) custom-call(s32[3]{0:T(128)S(1)} %get-tuple-element.154.plan_ref, s32[4,128]{1,0:T(4,128)S(1)} %get-tuple-element.122.ends_ref, s32[288,1]{1,0:T(8,128)S(1)} %get-tuple-element.123.which_ref, bf16[24,128,2048]{2,1,0:T(8,128)(2,1)} %down_ref.9, ...), custom_call_target="tpu_custom_call" | custom-call | flops 1 | bytes 1 | tf_op jit(solution)/shard_map/shrink/pallas_call | solution.py:250
  46.1 1.8 %sort.7 = (bf16[144,2048]{1,0:T(8,128)(2,1)S(1)}, bf16[96,2048]{1,0:T(8,128)(2,1)S(1)}) custom-call(s32[1,768]{1,0:T(1,128)S(1)} %get-tuple-element.118.slot_ref, bf16[768,2048]{1,0:T(8,128)(2,1)S(1)} %copy-done, f32[144,128]{1,0:T(8,128)S(1)} %get-tuple-element.126.refs_0_), custom_call_target="tpu_custom_call" | custom-call | flops 1000000000 | bytes 1 | tf_op jit(solution)/shard_map/sort/pallas_call | solution.py:89
  48.0 3.0 %collective-permute-start.19 = (bf16[144,2048]{1,0:T(8,128)(2,1)S(1)}, bf16[144,2048]{1,0:T(8,128)(2,1)S(1)}, u32[]{:S(2)}, u32[]{:S(2)}) collective-permute-start(bf16[144,2048]{1,0:T(8,128)(2,1)S(1)} %get-tuple-element.128.refs_1_), channel_id=1, source_target_pairs={{0,8},{4,12},{8,0},{12,4},{1,9},{5,13},{9,1},{13,5},{2,10},{6,14},... | collective-permute-start | bytes 1769480 | tf_op jit(solution)/shard_map/ppermute | solution.py:406
  50.9 0.1 collective-permute-start.23
  51.0 0.0 collective-permute-done.11
  51.0 16.7 %collective-permute-done.12.refs_0_ = bf16[240,2048]{1,0:T(8,128)(2,1)} collective-permute-done((bf16[240,2048]{1,0:T(8,128)(2,1)}, bf16[240,2048]{1,0:T(8,128)(2,1)}, u32[]{:S(2)}, u32[]{:S(2)}) %collective-permute-start.12) | collective-permute-done | bytes 983072 | tf_op jit(solution)/shard_map/ppermute | solution.py:406
  67.7 10.0 %shrink.8 = (f32[120,128]{1,0:T(8,128)S(1)}, f32[120,128]{1,0:T(8,128)S(1)}) custom-call(s32[3]{0:T(128)S(1)} %get-tuple-element.153.plan_ref, s32[4,128]{1,0:T(4,128)S(1)} %get-tuple-element.122.ends_ref, s32[240,1]{1,0:T(8,128)S(1)} %get-tuple-element.127.which_ref, bf16[24,128,2048]{2,1,0:T(8,128)(2,1)} %down_ref.9, ...), custom_call_target="tpu_custom_call" | custom-call | flops 1 | bytes 1 | tf_op jit(solution)/shard_map/shrink/pallas_call | solution.py:250
  77.7 0.0 collective-permute-done.13.refs_0_
  77.7 0.0 copy-start.6
  77.7 0.0 copy-start.10
  77.7 0.0 copy-start.7
  77.7 7.3 %shrink.9 = (f32[120,128]{1,0:T(8,128)S(1)}, f32[120,128]{1,0:T(8,128)S(1)}) custom-call(s32[3]{0:T(128)S(1)} %get-tuple-element.152.plan_ref, s32[4,128]{1,0:T(4,128)S(1)} %get-tuple-element.122.ends_ref, s32[240,1]{1,0:T(8,128)S(1)} %get-tuple-element.130.which_ref, bf16[24,128,2048]{2,1,0:T(8,128)(2,1)S(1)} %bitcast.14, ...), custom_call_target="tpu_custom_call" | custom-call | flops 1 | bytes 1 | tf_op jit(solution)/shard_map/shrink/pallas_call | solution.py:250
  85.1 0.1 collective-permute-start.14
  85.2 1.6 collective-permute-start.15
  86.7 0.3 collective-permute-start.16
  87.1 0.0 collective-permute-done.14.refs_1_
  87.1 5.9 %collective-permute-done.15.refs_2_ = f32[384,128]{1,0:T(8,128)S(1)} collective-permute-done((f32[384,128]{1,0:T(8,128)S(1)}, f32[384,128]{1,0:T(8,128)S(1)}, u32[]{:S(2)}, u32[]{:S(2)}) %collective-permute-start.15) | collective-permute-done | bytes 196640 | tf_op jit(solution)/shard_map/ppermute | solution.py:406
  93.0 3.4 %collective-permute-done.16.refs_3_ = f32[384,128]{1,0:T(8,128)S(1)} collective-permute-done((f32[384,128]{1,0:T(8,128)S(1)}, f32[384,128]{1,0:T(8,128)S(1)}, u32[]{:S(2)}, u32[]{:S(2)}) %collective-permute-start.16) | collective-permute-done | bytes 196640 | tf_op jit(solution)/shard_map/ppermute | solution.py:406
  96.3 2.3 %expand.5 = (f32[288,256]{1,0:T(8,128)S(1)}, s16[256,256]{1,0:T(8,128)(2,1)S(1)}, s16[256,256]{1,0:T(8,128)(2,1)S(1)}) custom-call(s32[768,1]{1,0:T(8,128)S(1)} %get-tuple-element.120.which_ref, f32[1,24]{1,0:T(1,128)S(1)} %bitcast.19, bf16[1536,256]{1,0:T(8,128)(2,1)S(1)} %bitcast.15, f32[384,128]{1,0:T(8,128)S(1)} %constant_dynamic-update-slice_fusion.refs_0_, ...), custom_call_target="tpu_custom_call" | custom-call | flops 1 | bytes 1 | tf_op jit(solution)/shard_map/expand/pallas_call | solution.py:344
  98.7 0.8 place.1.refs_2_
  99.5 10.5 %collective-permute-done.19.refs_0_ = bf16[144,2048]{1,0:T(8,128)(2,1)S(1)} collective-permute-done((bf16[144,2048]{1,0:T(8,128)(2,1)S(1)}, bf16[144,2048]{1,0:T(8,128)(2,1)S(1)}, u32[]{:S(2)}, u32[]{:S(2)}) %collective-permute-start.19) | collective-permute-done | bytes 589856 | tf_op jit(solution)/shard_map/ppermute | solution.py:406
  110.1 4.9 %shrink.10 = (f32[72,128]{1,0:T(8,128)S(1)}, f32[72,128]{1,0:T(8,128)S(1)}) custom-call(s32[3]{0:T(128)S(1)} %get-tuple-element.151.plan_ref, s32[4,128]{1,0:T(4,128)S(1)} %get-tuple-element.122.ends_ref, s32[144,1]{1,0:T(8,128)S(1)} %get-tuple-element.138.which_ref, bf16[24,128,2048]{2,1,0:T(8,128)(2,1)S(1)} %bitcast.14, ...), custom_call_target="tpu_custom_call" | custom-call | flops 1 | bytes 1 | tf_op jit(solution)/shard_map/shrink/pallas_call | solution.py:250
  115.0 1.6 collective-permute-start.20
  116.6 2.5 %collective-permute-done.20 = f32[72,128]{1,0:T(8,128)S(1)} collective-permute-done((f32[72,128]{1,0:T(8,128)S(1)}, f32[72,128]{1,0:T(8,128)S(1)}, u32[]{:S(2)}, u32[]{:S(2)}) %collective-permute-start.20) | collective-permute-done | bytes 36896 | tf_op jit(solution)/shard_map/ppermute | solution.py:406
  119.1 0.0 collective-permute-start.21
  119.1 1.2 collective-permute-done.21.refs_1_
  120.3 0.7 expand.6.refs_1_
  121.0 10.2 %collective-permute-start.22 = (s16[160,256]{1,0:T(8,128)(2,1)S(1)}, s16[160,256]{1,0:T(8,128)(2,1)S(1)}, u32[]{:S(2)}, u32[]{:S(2)}) collective-permute-start(s16[160,256]{1,0:T(8,128)(2,1)S(1)} %expand.6.refs_1_), channel_id=1, source_target_pairs={{0,8},{4,12},{8,0},{12,4},{1,9},{5,13},{9,1},{13,5},{2,10},{6,14},... | collective-permute-start | bytes 245768 | tf_op jit(solution)/shard_map/ppermute | solution.py:406
  131.2 0.6 collective-permute-start.17
  131.9 2.3 %collective-permute-start.18 = (s16[256,256]{1,0:T(8,128)(2,1)S(1)}, s16[256,256]{1,0:T(8,128)(2,1)S(1)}, u32[]{:S(2)}, u32[]{:S(2)}) collective-permute-start(s16[256,256]{1,0:T(8,128)(2,1)S(1)} %get-tuple-element.137), channel_id=1, source_target_pairs={{0,12},{4,8},{8,4},{12,0},{1,13},{5,9},{9,5},{13,1},{2,14},{6,10},... | collective-permute-start | bytes 393224 | tf_op jit(solution)/shard_map/ppermute | solution.py:406
  134.1 0.0 collective-permute-done.23.refs_0_
  134.1 3.6 %shrink.11 = (f32[48,128]{1,0:T(8,128)S(1)}, f32[48,128]{1,0:T(8,128)S(1)}) custom-call(s32[3]{0:T(128)S(1)} %get-tuple-element.150.plan_ref, s32[4,128]{1,0:T(4,128)S(1)} %get-tuple-element.122.ends_ref, s32[96,1]{1,0:T(8,128)S(1)} %get-tuple-element.141.which_ref, bf16[24,128,2048]{2,1,0:T(8,128)(2,1)S(1)} %bitcast.14, ...), custom_call_target="tpu_custom_call" | custom-call | flops 1 | bytes 1 | tf_op jit(solution)/shard_map/shrink/pallas_call | solution.py:250
  137.8 1.6 collective-permute-start.24
  139.4 2.3 %collective-permute-done.24 = f32[48,128]{1,0:T(8,128)S(1)} collective-permute-done((f32[48,128]{1,0:T(8,128)S(1)}, f32[48,128]{1,0:T(8,128)S(1)}, u32[]{:S(2)}, u32[]{:S(2)}) %collective-permute-start.24) | collective-permute-done | bytes 24608 | tf_op jit(solution)/shard_map/ppermute | solution.py:406
  141.7 0.0 collective-permute-start.25
  141.7 1.2 collective-permute-done.25.refs_1_
  142.9 0.0 collective-permute-done.22.refs_2_
  142.9 0.7 expand.7
  143.6 0.1 collective-permute-start.26
  143.7 5.8 %collective-permute-done.26 = s16[112,256]{1,0:T(8,128)(2,1)S(1)} collective-permute-done((s16[112,256]{1,0:T(8,128)(2,1)S(1)}, s16[112,256]{1,0:T(8,128)(2,1)S(1)}, u32[]{:S(2)}, u32[]{:S(2)}) %collective-permute-start.26) | collective-permute-done | bytes 57376 | tf_op jit(solution)/shard_map/ppermute | solution.py:406
  149.5 2.2 %conditional.1 = (bf16[768,256]{1,0:T(8,128)(2,1)S(1)}) conditional(s32[]{:T(128)} %bitcast.3, (s32[768,1]{1,0:T(8,128)S(1)}, f32[768,256]{1,0:T(8,128)}, f32[768,256]{1,0:T(8,128)S(1)}, s16[256,256]{1,0:T(8,128)(2,1)S(1)}, s16[256,256]{1,0:T(8,128)(2,1)S(1)}, /*index=5*/s16[160,256]{1,0:T(8,128)(2,1)S(1)}, s16[112,256]{1,0:T(8,128)(2,1)S(1)}) %tuple.25, ...), branch_computations={%region_1.0_spmd, %region_2.0_spmd} | conditional | flops 9219 | bytes 6304127 | solution.py:522
  149.7 2.0 %merge.2 = bf16[768,256]{1,0:T(8,128)(2,1)S(1)} custom-call(s32[768,1]{1,0:T(8,128)S(1)} %get-tuple-element.55.target_ref, f32[768,256]{1,0:T(8,128)} %get-tuple-element.56.refs_0_, f32[768,256]{1,0:T(8,128)S(1)} %get-tuple-element.57.refs_1_, s16[256,256]{1,0:T(8,128)(2,1)S(1)} %get-tuple-element.58.refs_2_, s16[256,256]{1,0:T(8,128)(2,1)S(1)} %get-tuple-element.59.refs_3_, ...), custom_call_target="tpu_custom_call" | custom-call | flops 1 | bytes 1 | tf_op jit(solution)/shard_map/cond/branch_0_fun/merge/pallas_call | solution.py:396
  151.6 0.0 copy-start.9
  151.6 0.7 copy-done.9
  (36 shorter events, 0.1 us)
Async XLA Ops:
  6.5 11.2 %copy-start = (bf16[768,2048]{1,0:T(8,128)(2,1)S(1)}, bf16[768,2048]{1,0:T(8,128)(2,1)}, u32[]{:S(2)}) copy-start(bf16[768,2048]{1,0:T(8,128)(2,1)} %tok_ref.9) | copy-start | bytes 9437188
  6.5 142.9 %reduce-scatter.2.cloned.1.call-start = ((), (), s32[]{:S(2)}) async-start(), calls=%async_computation.1 | async-start | bytes 3932160 | tf_op jit(solution)/shard_map/reduce_scatter | solution.py:441
  6.5 8.0 %collective-permute-start.8 = (s32[1,768]{1,0:T(1,128)}, s32[1,768]{1,0:T(1,128)S(1)}, u32[]{:S(2)}, u32[]{:S(2)}) collective-permute-start(s32[1,768]{1,0:T(1,128)} %bitcast.7), channel_id=1, source_target_pairs={{0,4},{4,0},{8,12},{12,8},{1,5},{5,1},{9,13},{13,9},{2,6},{6,2},{1... | collective-permute-start | bytes 9224 | tf_op jit(solution)/shard_map/ppermute | solution.py:406
  9.6 5.0 %collective-permute-start.9 = (s32[1,768]{1,0:T(1,128)}, s32[1,768]{1,0:T(1,128)S(1)}, u32[]{:S(2)}, u32[]{:S(2)}) collective-permute-start(s32[1,768]{1,0:T(1,128)} %bitcast.8), channel_id=1, source_target_pairs={{0,8},{4,12},{8,0},{12,4},{1,9},{5,13},{9,1},{13,5},{2,10},{6,14},... | collective-permute-start | bytes 9224 | tf_op jit(solution)/shard_map/ppermute | solution.py:406
  12.2 5.6 %collective-permute-start.10 = (s32[1,768]{1,0:T(1,128)}, s32[1,768]{1,0:T(1,128)S(1)}, u32[]{:S(2)}, u32[]{:S(2)}) collective-permute-start(s32[1,768]{1,0:T(1,128)} %bitcast.9), channel_id=1, source_target_pairs={{0,12},{4,8},{8,4},{12,0},{1,13},{5,9},{9,5},{13,1},{2,14},{6,10},... | collective-permute-start | bytes 9224 | tf_op jit(solution)/shard_map/ppermute | solution.py:406
  12.2 0.8 copy-start.4
  12.9 6.7 %copy-start.1 = (bf16[2048,1024]{1,0:T(8,128)(2,1)S(1)}, bf16[2048,1024]{1,0:T(8,128)(2,1)}, u32[]{:S(2)}) copy-start(bf16[2048,1024]{1,0:T(8,128)(2,1)} %weight_ref.1) | copy-start | bytes 12582916
  19.6 4.8 %copy-start.2 = (bf16[240,2048]{1,0:T(8,128)(2,1)}, bf16[240,2048]{1,0:T(8,128)(2,1)S(1)}, u32[]{:S(2)}) copy-start(bf16[240,2048]{1,0:T(8,128)(2,1)S(1)} %sort.4._) | copy-start | bytes 2949124
  24.4 1.6 %copy-start.3 = (f32[768,1024]{1,0:T(8,128)}, f32[768,1024]{1,0:T(8,128)S(1)}, u32[]{:S(2)}) copy-start(f32[768,1024]{1,0:T(8,128)S(1)} %get-tuple-element.119) | copy-start | bytes 9437188
  26.0 3.6 %copy-start.5 = (s32[768,1]{0,1:T(1,128)S(1)}, s32[768,1]{0,1:T(1,128)}, u32[]{:S(2)}) copy-start(s32[768,1]{0,1:T(1,128)} %param.13) | copy-start | bytes 9220
  26.0 41.6 %collective-permute-start.12 = (bf16[240,2048]{1,0:T(8,128)(2,1)}, bf16[240,2048]{1,0:T(8,128)(2,1)}, u32[]{:S(2)}, u32[]{:S(2)}) collective-permute-start(bf16[240,2048]{1,0:T(8,128)(2,1)} %copy-done.2), channel_id=1, source_target_pairs={{0,4},{4,0},{8,12},{12,8},{1,5},{5,1},{9,13},{13,9},{2,6},{6,2},{1... | collective-permute-start | bytes 2949128 | tf_op jit(solution)/shard_map/ppermute | solution.py:406
  29.0 48.7 %collective-permute-start.13 = (bf16[240,2048]{1,0:T(8,128)(2,1)}, bf16[240,2048]{1,0:T(8,128)(2,1)}, u32[]{:S(2)}, u32[]{:S(2)}) collective-permute-start(bf16[240,2048]{1,0:T(8,128)(2,1)} %sort.5.refs_0_), channel_id=1, source_target_pairs={{0,12},{4,8},{8,4},{12,0},{1,13},{5,9},{9,5},{13,1},{2,14},{6,10},... | collective-permute-start | bytes 2949128 | tf_op jit(solution)/shard_map/ppermute | solution.py:406
  31.3 19.7 %collective-permute-start.11 = (s32[1,128]{1,0:T(1,128)S(1)}, s32[1,128]{1,0:T(1,128)S(1)}, u32[]{:S(2)}, u32[]{:S(2)}) collective-permute-start(s32[1,128]{1,0:T(1,128)S(1)} %get-tuple-element.116), channel_id=1, source_target_pairs={{0,16},{16,0},{1,17},{17,1},{2,18},{18,2},{3,19},{19,3},{4,20},{20... | collective-permute-start | bytes 1544 | tf_op jit(solution)/shard_map/ppermute | solution.py:406
  36.2 41.5 %slice-start = ((s8[12582912]{0:T(1024)(128)(4,1)}), s8[4194304]{0:T(1024)(128)(4,1)S(1)}, s32[]{:S(2)}) async-start(s8[12582912]{0:T(1024)(128)(4,1)} %bitcast.13), calls=%async_computation.2 | async-start | bytes 8388608
  36.2 41.5 %slice-start.1 = ((s8[12582912]{0:T(1024)(128)(4,1)}), s8[4194304]{0:T(1024)(128)(4,1)S(1)}, s32[]{:S(2)}) async-start(s8[12582912]{0:T(1024)(128)(4,1)} %bitcast.13), calls=%async_computation.3 | async-start | bytes 8388608
  48.0 62.1 %collective-permute-start.19 = (bf16[144,2048]{1,0:T(8,128)(2,1)S(1)}, bf16[144,2048]{1,0:T(8,128)(2,1)S(1)}, u32[]{:S(2)}, u32[]{:S(2)}) collective-permute-start(bf16[144,2048]{1,0:T(8,128)(2,1)S(1)} %get-tuple-element.128.refs_1_), channel_id=1, source_target_pairs={{0,8},{4,12},{8,0},{12,4},{1,9},{5,13},{9,1},{13,5},{2,10},{6,14},... | collective-permute-start | bytes 1769480 | tf_op jit(solution)/shard_map/ppermute | solution.py:406
  50.9 83.2 %collective-permute-start.23 = (bf16[96,2048]{1,0:T(8,128)(2,1)S(1)}, bf16[96,2048]{1,0:T(8,128)(2,1)S(1)}, u32[]{:S(2)}, u32[]{:S(2)}) collective-permute-start(bf16[96,2048]{1,0:T(8,128)(2,1)S(1)} %get-tuple-element.142), channel_id=1, source_target_pairs={{0,8},{4,12},{8,0},{12,4},{1,9},{5,13},{9,1},{13,5},{2,10},{6,14},... | collective-permute-start | bytes 1179656 | tf_op jit(solution)/shard_map/ppermute | solution.py:406
  67.7 10.0 %slice-start.2 = ((s8[12582912]{0:T(1024)(128)(4,1)}), s8[4194304]{0:T(1024)(128)(4,1)S(1)}, s32[]{:S(2)}) async-start(s8[12582912]{0:T(1024)(128)(4,1)} %bitcast.13), calls=%async_computation.4 | async-start | bytes 8388608
  77.7 18.6 %copy-start.6 = (bf16[24,64,256]{2,1,0:T(8,128)(2,1)S(1)}, bf16[24,64,256]{2,1,0:T(8,128)(2,1)}, u32[]{:S(2)}) copy-start(bf16[24,64,256]{2,1,0:T(8,128)(2,1)} %param.11) | copy-start | bytes 2359300
  77.7 18.6 %copy-start.10 = (f32[24]{0:T(128)S(1)}, f32[24]{0:T(128)}, u32[]{:S(2)}) copy-start(f32[24]{0:T(128)} %param.12) | copy-start | bytes 292
  77.7 20.9 %copy-start.7 = (s32[768,1]{1,0:T(8,128)S(1)}, s32[768,1]{1,0:T(8,128)}, u32[]{:S(2)}) copy-start(s32[768,1]{1,0:T(8,128)} %get-tuple-element.117.target_ref) | copy-start | bytes 9220
  85.1 2.0 %collective-permute-start.14 = (f32[384,128]{1,0:T(8,128)S(1)}, f32[384,128]{1,0:T(8,128)S(1)}, u32[]{:S(2)}, u32[]{:S(2)}) collective-permute-start(f32[384,128]{1,0:T(8,128)S(1)} %constant_dynamic-update-slice_fusion.refs_0_), channel_id=1, source_target_pairs={{0,1},{1,0},{2,3},{3,2},{4,5},{5,4},{6,7},{7,6},{8,9},{9,8},{10,11... | collective-permute-start | bytes 589832 | tf_op jit(solution)/shard_map/ppermute | solution.py:406
  85.2 7.8 %collective-permute-start.15 = (f32[384,128]{1,0:T(8,128)S(1)}, f32[384,128]{1,0:T(8,128)S(1)}, u32[]{:S(2)}, u32[]{:S(2)}) collective-permute-start(f32[384,128]{1,0:T(8,128)S(1)} %constant_dynamic-update-slice_fusion.3), channel_id=1, source_target_pairs={{0,2},{1,3},{2,0},{3,1},{4,6},{5,7},{6,4},{7,5},{8,10},{9,11},{10,... | collective-permute-start | bytes 589832 | tf_op jit(solution)/shard_map/ppermute | solution.py:406
  86.7 9.6 %collective-permute-start.16 = (f32[384,128]{1,0:T(8,128)S(1)}, f32[384,128]{1,0:T(8,128)S(1)}, u32[]{:S(2)}, u32[]{:S(2)}) collective-permute-start(f32[384,128]{1,0:T(8,128)S(1)} %constant_dynamic-update-slice_fusion.3), channel_id=1, source_target_pairs={{0,3},{1,2},{2,1},{3,0},{4,7},{5,6},{6,5},{7,4},{8,11},{9,10},{10,... | collective-permute-start | bytes 589832 | tf_op jit(solution)/shard_map/ppermute | solution.py:406
  115.0 4.0 %collective-permute-start.20 = (f32[72,128]{1,0:T(8,128)S(1)}, f32[72,128]{1,0:T(8,128)S(1)}, u32[]{:S(2)}, u32[]{:S(2)}) collective-permute-start(f32[72,128]{1,0:T(8,128)S(1)} %get-tuple-element.140), channel_id=1, source_target_pairs={{0,2},{2,0},{1,3},{3,1},{4,6},{6,4},{5,7},{7,5},{8,10},{10,8},{9,1... | collective-permute-start | bytes 110600 | tf_op jit(solution)/shard_map/ppermute | solution.py:406
  119.1 1.2 collective-permute-start.21
  121.0 21.9 %collective-permute-start.22 = (s16[160,256]{1,0:T(8,128)(2,1)S(1)}, s16[160,256]{1,0:T(8,128)(2,1)S(1)}, u32[]{:S(2)}, u32[]{:S(2)}) collective-permute-start(s16[160,256]{1,0:T(8,128)(2,1)S(1)} %expand.6.refs_1_), channel_id=1, source_target_pairs={{0,8},{4,12},{8,0},{12,4},{1,9},{5,13},{9,1},{13,5},{2,10},{6,14},... | collective-permute-start | bytes 245768 | tf_op jit(solution)/shard_map/ppermute | solution.py:406
  131.2 12.5 %collective-permute-start.17 = (s16[256,256]{1,0:T(8,128)(2,1)S(1)}, s16[256,256]{1,0:T(8,128)(2,1)S(1)}, u32[]{:S(2)}, u32[]{:S(2)}) collective-permute-start(s16[256,256]{1,0:T(8,128)(2,1)S(1)} %get-tuple-element.136), channel_id=1, source_target_pairs={{0,4},{4,0},{8,12},{12,8},{1,5},{5,1},{9,13},{13,9},{2,6},{6,2},{1... | collective-permute-start | bytes 393224 | tf_op jit(solution)/shard_map/ppermute | solution.py:406
  131.9 11.8 %collective-permute-start.18 = (s16[256,256]{1,0:T(8,128)(2,1)S(1)}, s16[256,256]{1,0:T(8,128)(2,1)S(1)}, u32[]{:S(2)}, u32[]{:S(2)}) collective-permute-start(s16[256,256]{1,0:T(8,128)(2,1)S(1)} %get-tuple-element.137), channel_id=1, source_target_pairs={{0,12},{4,8},{8,4},{12,0},{1,13},{5,9},{9,5},{13,1},{2,14},{6,10},... | collective-permute-start | bytes 393224 | tf_op jit(solution)/shard_map/ppermute | solution.py:406
  134.1 15.3 %copy-start.11 = (bf16[48,2048]{1,0:T(8,128)(2,1)S(1)}, bf16[48,2048]{1,0:T(8,128)(2,1)}, u32[]{:S(2)}) copy-start(bf16[48,2048]{1,0:T(8,128)(2,1)} %get-tuple-element.146) | copy-start | bytes 589828
  134.1 15.3 %copy-start.12 = (bf16[48,2048]{1,0:T(8,128)(2,1)S(1)}, bf16[48,2048]{1,0:T(8,128)(2,1)}, u32[]{:S(2)}) copy-start(bf16[48,2048]{1,0:T(8,128)(2,1)} %get-tuple-element.147) | copy-start | bytes 589828
  137.8 3.9 %collective-permute-start.24 = (f32[48,128]{1,0:T(8,128)S(1)}, f32[48,128]{1,0:T(8,128)S(1)}, u32[]{:S(2)}, u32[]{:S(2)}) collective-permute-start(f32[48,128]{1,0:T(8,128)S(1)} %get-tuple-element.144), channel_id=1, source_target_pairs={{0,2},{2,0},{1,3},{3,1},{4,6},{6,4},{5,7},{7,5},{8,10},{10,8},{9,1... | collective-permute-start | bytes 73736 | tf_op jit(solution)/shard_map/ppermute | solution.py:406
  141.7 1.2 collective-permute-start.25
  143.6 5.9 %collective-permute-start.26 = (s16[112,256]{1,0:T(8,128)(2,1)S(1)}, s16[112,256]{1,0:T(8,128)(2,1)S(1)}, u32[]{:S(2)}, u32[]{:S(2)}) collective-permute-start(s16[112,256]{1,0:T(8,128)(2,1)S(1)} %expand.7), channel_id=1, source_target_pairs={{0,8},{4,12},{8,0},{12,4},{1,9},{5,13},{9,1},{13,5},{2,10},{6,14},... | collective-permute-start | bytes 172040 | tf_op jit(solution)/shard_map/ppermute | solution.py:406
  151.6 0.7 copy-start.9
Sparse Core Ops, SparseCore 0:
  26.1 36.1 reduce-scatter.1

commit v12 on v8

--- a/solution.py
+++ b/solution.py
@@ -15,6 +15,7 @@
 I32 = jnp.int32
 ANYWHERE = pl.BlockSpec(memory_space=pl.ANY)
 COST = pl.CostEstimate(flops=1, transcendentals=0, bytes_accessed=1)
+HEAD = pl.CostEstimate(flops=10**9, transcendentals=0, bytes_accessed=1)
 PARAMS = pltpu.CompilerParams(vmem_limit_bytes=VMEM_LIMIT)
 
 
@@ -58,7 +59,7 @@
         ],
         out_shape=[jax.ShapeDtypeStruct((1, rows), I32), jax.ShapeDtypeStruct((rows, 1), I32)],
         compiler_params=PARAMS,
-        cost_estimate=COST,
+        cost_estimate=HEAD,
         name="route",
     )(me, ids_row)
 
@@ -97,7 +98,7 @@
         out_shape=[jax.ShapeDtypeStruct((count, width), BF16) for _, _, count in pieces],
         scratch_shapes=[pltpu.VMEM((sum(c for _, _, c in pieces), rows), BF16)],
         compiler_params=PARAMS,
-        cost_estimate=COST,
+        cost_estimate=HEAD,
         name="sort",
     )(slot, tokens, *later_than)
 
@@ -175,9 +176,9 @@
             ANYWHERE,
         ],
         out_specs=pl.BlockSpec((rows, step), lambda i: (0, i)),
-        out_shape=pltpu.HBM((rows, columns), F32),
-        compiler_params=PARAMS,
-        cost_estimate=COST,
+        out_shape=jax.ShapeDtypeStruct((rows, columns), F32),
+        compiler_params=PARAMS,
+        cost_estimate=HEAD,
         name="base",
     )(tokens, weight, later_than)
 
@@ -471,6 +472,8 @@
 
     weights = (adapter_down_weight, up, scale)
     packed |= zip([own] + extra, sort_rows(tokens, slot, cap, [own] + extra, (base_part,)))
+    for d in range(1, lax.axis_size("parts")):
+        largest = jnp.maximum(largest, swap(largest, "parts", lax.axis_size("parts"), d))
     shares, waits = [], ()
     for k, p in enumerate(early):
         rows_here = received.get(p, packed[p])
@@ -487,7 +490,7 @@
     done = early[1:]
     for k, pieces in enumerate(last):
         blocks = [received[p] for p in pieces]
-        waits = (deltas[0], parts[1])
+        waits = (deltas[0], parts[1], largest)
         deltas = deltas_of(
             pieces, blocks, names[here + 1 + k], ends, plans[here + 1 + k], *weights, waits
         )
@@ -506,8 +509,6 @@
         deltas = send_back(extra, deltas)
         return merge(parts, target, begins(done + extra), returned + deltas, BF16)
 
-    for d in range(1, lax.axis_size("parts")):
-        largest = jnp.maximum(largest, swap(largest, "parts", lax.axis_size("parts"), d))
     return lax.cond(
         largest[0, 0] > usual,
         finish_with_extra,

time: 148 us -> 145 us (0.980)
  local copies, waits for them, and re-layouts: 9.95 us -> 7.14 us
  waiting for transfers between devices: 27.9 us -> 30.3 us
  starting transfers between devices: 39.8 us -> 38.1 us
    unnamed x45 -> x39, local copies, waits for them, and re-layouts: 9.86 us -> 7.05 us
    ppermute x19, waiting for transfers between devices: 27.9 us -> 30.3 us  [swap(): return lax.ppermute(x, axes, [(i, i ^ distance) for i in range(size)])]
    ppermute x19, starting transfers between devices: 39.8 us -> 38.1 us  [swap(): return lax.ppermute(x, axes, [(i, i ^ distance) for i in range(size)])]
  transfers between devices with their start and end apart: 20 -> 20, of which waited for: 10 -> 10; matrix products, arithmetic and copies ran while one was open for 0% -> 0% of each run, Pallas kernels for 31% -> 32%
where the time goes in v12:
time: 145 us
  Pallas kernels  55.6 us (38%)
  starting transfers between devices  38.1 us (26%)
  waiting for transfers between devices  30.3 us (21%)
  between operations  13.7 us (9%)
  local copies, waits for them, and re-layouts  7.14 us (5%)
    ppermute x19, starting transfers between devices, swap(): return lax.ppermute(x, axes, [(i, i ^ distance) for i in range(size)])  38.1 us
    pallas_call x5, Pallas kernels, shrink(): pl.pallas_call(functools.partial(shrink_kernel, pieces, group, fine), gri...  33.2 us
    ppermute x19, waiting for transfers between devices, swap(): return lax.ppermute(x, axes, [(i, i ^ distance) for i in range(size)])  30.3 us
    pallas_call x3, Pallas kernels, sort_rows(): pl.pallas_call(functools.partial(sort_kernel, cap, pieces, len(later_than...  7.82 us
    unnamed x39, local copies, waits for them, and re-layouts  7.05 us
    pallas_call x1, Pallas kernels, base_product(): pl.pallas_call(base_kernel, grid=(columns // step,), in_specs=[pl.BlockSp...  4.71 us
    pallas_call x3, Pallas kernels, expand(): pl.pallas_call(functools.partial(expand_kernel, groups, sizes, len(lines)...  3.69 us
  transfers between devices with their start and end apart: 20, of which 10 were waited for; matrix products, arithmetic and copies ran while one was open for 0% of the time, Pallas kernels for 32%

profile of v12, /device:TPU:0, one launch (start us, length us, event | category | flops | bytes accessed | tf_op | source)
XLA Modules:
  0.0 145.1 jit_solution(1443691047388112251)
XLA Ops:
  6.5 5.0 %collective-permute-start.10 = (s32[1,768]{1,0:T(1,128)}, s32[1,768]{1,0:T(1,128)S(1)}, u32[]{:S(2)}, u32[]{:S(2)}) collective-permute-start(s32[1,768]{1,0:T(1,128)} %bitcast.7), channel_id=1, source_target_pairs={{0,12},{4,8},{8,4},{12,0},{1,13},{5,9},{9,5},{13,1},{2,14},{6,10},... | collective-permute-start | bytes 9224 | tf_op jit(solution)/shard_map/ppermute | solution.py:399
  11.6 0.0 collective-permute-start.8
  11.6 0.6 collective-permute-start.9
  12.2 0.7 copy-done.5
  12.9 1.6 %route.1 = (s32[1,768]{1,0:T(1,128)S(1)}, s32[768,1]{1,0:T(8,128)}) custom-call(s32[1]{0:T(128)} %bitcast.me_ref, s32[1,768]{1,0:T(1,128)S(1)} %bitcast.10), custom_call_target="tpu_custom_call" | custom-call | flops 1000000000 | bytes 1 | tf_op jit(solution)/shard_map/route/pallas_call | solution.py:54
  14.5 0.0 collective-permute-done.10.refs_3_.refs_2_
  14.5 0.9 collective-permute-done.8.refs_1_.refs_0_
  15.4 0.9 collective-permute-done.9.refs_2_.refs_1_
  16.3 2.7 %sort.3 = (bf16[240,2048]{1,0:T(8,128)(2,1)S(1)}, bf16[240,2048]{1,0:T(8,128)(2,1)S(1)}) custom-call(s32[1,768]{1,0:T(1,128)S(1)} %get-tuple-element.118.slot_ref, bf16[768,2048]{1,0:T(8,128)(2,1)S(1)} %copy-done, s32[1,768]{1,0:T(1,128)S(1)} %collective-permute-done.8.refs_1_.refs_0_, s32[1,768]{1,0:T(1,128)S(1)} %collective-permute-done.9.refs_2_.refs_1_, ...), custom_call_target="tpu_custom_call" | custom-call | flops 1000000000 | bytes 1 | tf_op jit(solution)/shard_map/sort/pallas_call | solution.py:89
  19.0 0.9 copy-done.7
  20.0 4.7 %base.1.refs_0_ = f32[768,1024]{1,0:T(8,128)S(1)} custom-call(bf16[768,2048]{1,0:T(8,128)(2,1)S(1)} %copy-done, bf16[2048,1024]{1,0:T(8,128)(2,1)S(1)} %copy-done.3, bf16[240,2048]{1,0:T(8,128)(2,1)S(1)} %get-tuple-element.119._), custom_call_target="tpu_custom_call" | custom-call | flops 1000000000 | bytes 1 | tf_op jit(solution)/shard_map/base/pallas_call | solution.py:170
  24.7 1.6 %copy-done.1 = f32[768,1024]{1,0:T(8,128)} copy-done((f32[768,1024]{1,0:T(8,128)}, f32[768,1024]{1,0:T(8,128)S(1)}, u32[]{:S(2)}) %copy-start.1) | copy-done | bytes 3145752
  26.3 1.0 copy-done.4
  27.3 0.0 reduce-scatter.2.cloned.1.call-update
  27.3 2.1 %collective-permute-start.12 = (bf16[240,2048]{1,0:T(8,128)(2,1)}, bf16[240,2048]{1,0:T(8,128)(2,1)}, u32[]{:S(2)}, u32[]{:S(2)}) collective-permute-start(bf16[240,2048]{1,0:T(8,128)(2,1)} %copy-done.4), channel_id=1, source_target_pairs={{0,4},{4,0},{8,12},{12,8},{1,5},{5,1},{9,13},{13,9},{2,6},{6,2},{1... | collective-permute-start | bytes 2949128 | tf_op jit(solution)/shard_map/ppermute | solution.py:399
  29.4 0.1 collective-permute-start.13
  29.5 0.1 pad_add_fusion.here_ref
  29.6 1.7 %name_rows.1 = (s32[288,1]{1,0:T(8,128)S(1)}, s32[240,1]{1,0:T(8,128)S(1)}, s32[240,1]{1,0:T(8,128)S(1)}, s32[768,1]{1,0:T(8,128)S(1)}, s32[144,1]{1,0:T(8,128)S...) custom-call(s32[2]{0:T(128)S(1)} %pad_add_fusion.here_ref, ...), custom_call_target="tpu_custom_call" | custom-call | flops 1 | bytes 1 | tf_op jit(solution)/shard_map/name_rows/pallas_call | solution.py:145
  31.3 1.7 %collective-permute-start.11 = (s32[1,128]{1,0:T(1,128)S(1)}, s32[1,128]{1,0:T(1,128)S(1)}, u32[]{:S(2)}, u32[]{:S(2)}) collective-permute-start(s32[1,128]{1,0:T(1,128)S(1)} %get-tuple-element.116), channel_id=1, source_target_pairs={{0,16},{16,0},{1,17},{17,1},{2,18},{18,2},{3,19},{19,3},{4,20},{20... | collective-permute-start | bytes 1544 | tf_op jit(solution)/shard_map/ppermute | solution.py:399
  33.0 2.0 %copy-done.2 = f32[768,1024]{1,0:T(8,128)S(1)} copy-done((f32[768,1024]{1,0:T(8,128)S(1)}, f32[768,1024]{1,0:T(8,128)}, u32[]{:S(2)}) %copy-start.2) | copy-done | bytes 3145752
  35.0 3.3 %sort.4 = (bf16[288,2048]{1,0:T(8,128)(2,1)S(1)}, bf16[48,2048]{1,0:T(8,128)(2,1)}, bf16[48,2048]{1,0:T(8,128)(2,1)}, bf16[48,2048]{1,0:T(8,128)(2,1)}) custom-call(s32[1,768]{1,0:T(1,128)S(1)} %get-tuple-element.118.slot_ref, bf16[768,2048]{1,0:T(8,128)(2,1)S(1)} %copy-done, f32[768,1024]{1,0:T(8,128)S(1)} %copy-done.2), custom_call_target="tpu_custom_call" | custom-call | flops 1000000000 | bytes 1 | tf_op jit(solution)/shard_map/sort/pallas_call | solution.py:89
  38.3 0.1 fusion
  38.4 10.0 %shrink.7 = (f32[144,128]{1,0:T(8,128)S(1)}, f32[144,128]{1,0:T(8,128)S(1)}) custom-call(s32[3]{0:T(128)S(1)} %get-tuple-element.154.plan_ref, s32[4,128]{1,0:T(4,128)S(1)} %get-tuple-element.122.ends_ref, s32[288,1]{1,0:T(8,128)S(1)} %get-tuple-element.123.which_ref, bf16[24,128,2048]{2,1,0:T(8,128)(2,1)} %down_ref.9, ...), custom_call_target="tpu_custom_call" | custom-call | flops 1 | bytes 1 | tf_op jit(solution)/shard_map/shrink/pallas_call | solution.py:243
  48.4 3.5 %collective-permute-done.12.refs_0_ = bf16[240,2048]{1,0:T(8,128)(2,1)} collective-permute-done((bf16[240,2048]{1,0:T(8,128)(2,1)}, bf16[240,2048]{1,0:T(8,128)(2,1)}, u32[]{:S(2)}, u32[]{:S(2)}) %collective-permute-start.12) | collective-permute-done | bytes 983072 | tf_op jit(solution)/shard_map/ppermute | solution.py:399
  52.0 1.8 %sort.5 = (bf16[144,2048]{1,0:T(8,128)(2,1)S(1)}, bf16[96,2048]{1,0:T(8,128)(2,1)S(1)}) custom-call(s32[1,768]{1,0:T(1,128)S(1)} %get-tuple-element.118.slot_ref, bf16[768,2048]{1,0:T(8,128)(2,1)S(1)} %copy-done, bf16[240,2048]{1,0:T(8,128)(2,1)} %collective-permute-done.12.refs_0_), custom_call_target="tpu_custom_call" | custom-call | flops 1000000000 | bytes 1 | tf_op jit(solution)/shard_map/sort/pallas_call | solution.py:89
  53.8 1.1 collective-permute-start.19
  54.9 7.3 %shrink.8 = (f32[120,128]{1,0:T(8,128)S(1)}, f32[120,128]{1,0:T(8,128)S(1)}) custom-call(s32[3]{0:T(128)S(1)} %get-tuple-element.153.plan_ref, s32[4,128]{1,0:T(4,128)S(1)} %get-tuple-element.122.ends_ref, s32[240,1]{1,0:T(8,128)S(1)} %get-tuple-element.126.which_ref, bf16[24,128,2048]{2,1,0:T(8,128)(2,1)S(1)} %bitcast.14, ...), custom_call_target="tpu_custom_call" | custom-call | flops 1 | bytes 1 | tf_op jit(solution)/shard_map/shrink/pallas_call | solution.py:243
  62.3 11.3 %collective-permute-done.13.refs_0_ = bf16[240,2048]{1,0:T(8,128)(2,1)} collective-permute-done((bf16[240,2048]{1,0:T(8,128)(2,1)}, bf16[240,2048]{1,0:T(8,128)(2,1)}, u32[]{:S(2)}, u32[]{:S(2)}) %collective-permute-start.13) | collective-permute-done | bytes 983072 | tf_op jit(solution)/shard_map/ppermute | solution.py:399
  73.6 7.3 %shrink.9 = (f32[120,128]{1,0:T(8,128)S(1)}, f32[120,128]{1,0:T(8,128)S(1)}) custom-call(s32[3]{0:T(128)S(1)} %get-tuple-element.152.plan_ref, s32[4,128]{1,0:T(4,128)S(1)} %get-tuple-element.122.ends_ref, s32[240,1]{1,0:T(8,128)S(1)} %get-tuple-element.129.which_ref, bf16[24,128,2048]{2,1,0:T(8,128)(2,1)S(1)} %bitcast.14, ...), custom_call_target="tpu_custom_call" | custom-call | flops 1 | bytes 1 | tf_op jit(solution)/shard_map/shrink/pallas_call | solution.py:243
  80.9 1.8 %collective-permute-start.15 = (f32[384,128]{1,0:T(8,128)S(1)}, f32[384,128]{1,0:T(8,128)S(1)}, u32[]{:S(2)}, u32[]{:S(2)}) collective-permute-start(f32[384,128]{1,0:T(8,128)S(1)} %constant_dynamic-update-slice_fusion.3), channel_id=1, source_target_pairs={{0,2},{1,3},{2,0},{3,1},{4,6},{5,7},{6,4},{7,5},{8,10},{9,11},{10,... | collective-permute-start | bytes 589832 | tf_op jit(solution)/shard_map/ppermute | solution.py:399
  82.7 0.0 collective-permute-start.16
  82.7 12.9 %collective-permute-start.23 = (bf16[96,2048]{1,0:T(8,128)(2,1)S(1)}, bf16[96,2048]{1,0:T(8,128)(2,1)S(1)}, u32[]{:S(2)}, u32[]{:S(2)}) collective-permute-start(bf16[96,2048]{1,0:T(8,128)(2,1)S(1)} %get-tuple-element.142), channel_id=1, source_target_pairs={{0,8},{4,12},{8,0},{12,4},{1,9},{5,13},{9,1},{13,5},{2,10},{6,14},... | collective-permute-start | bytes 1179656 | tf_op jit(solution)/shard_map/ppermute | solution.py:399
  95.7 0.0 collective-permute-done.11
  95.7 0.4 collective-permute-start.14
  96.1 0.0 collective-permute-done.15.refs_2_
  96.1 0.0 collective-permute-done.16.refs_3_
  96.1 1.1 collective-permute-done.14.refs_1_
  97.2 2.3 %expand.5 = (f32[288,256]{1,0:T(8,128)S(1)}, s16[256,256]{1,0:T(8,128)(2,1)S(1)}, s16[256,256]{1,0:T(8,128)(2,1)S(1)}) custom-call(s32[768,1]{1,0:T(8,128)S(1)} %get-tuple-element.120.which_ref, f32[1,24]{1,0:T(1,128)S(1)} %bitcast.20, bf16[1536,256]{1,0:T(8,128)(2,1)S(1)} %bitcast.15, f32[384,128]{1,0:T(8,128)S(1)} %constant_dynamic-update-slice_fusion.refs_0_, ...), custom_call_target="tpu_custom_call" | custom-call | flops 1 | bytes 1 | tf_op jit(solution)/shard_map/expand/pallas_call | solution.py:337
  99.5 0.9 place.1.refs_2_
  100.4 0.0 collective-permute-done.19.refs_0_
  100.4 6.2 %shrink.10 = (f32[72,128]{1,0:T(8,128)S(1)}, f32[72,128]{1,0:T(8,128)S(1)}) custom-call(s32[3]{0:T(128)S(1)} %get-tuple-element.151.plan_ref, s32[4,128]{1,0:T(4,128)S(1)} %get-tuple-element.122.ends_ref, s32[144,1]{1,0:T(8,128)S(1)} %get-tuple-element.138.which_ref, bf16[24,128,2048]{2,1,0:T(8,128)(2,1)S(1)} %bitcast.14, ...), custom_call_target="tpu_custom_call" | custom-call | flops 1 | bytes 1 | tf_op jit(solution)/shard_map/shrink/pallas_call | solution.py:243
  106.6 1.6 %collective-permute-start.20 = (f32[72,128]{1,0:T(8,128)S(1)}, f32[72,128]{1,0:T(8,128)S(1)}, u32[]{:S(2)}, u32[]{:S(2)}) collective-permute-start(f32[72,128]{1,0:T(8,128)S(1)} %get-tuple-element.140), channel_id=1, source_target_pairs={{0,2},{2,0},{1,3},{3,1},{4,6},{6,4},{5,7},{7,5},{8,10},{10,8},{9,1... | collective-permute-start | bytes 110600 | tf_op jit(solution)/shard_map/ppermute | solution.py:399
  108.2 2.5 %collective-permute-done.20 = f32[72,128]{1,0:T(8,128)S(1)} collective-permute-done((f32[72,128]{1,0:T(8,128)S(1)}, f32[72,128]{1,0:T(8,128)S(1)}, u32[]{:S(2)}, u32[]{:S(2)}) %collective-permute-start.20) | collective-permute-done | bytes 36896 | tf_op jit(solution)/shard_map/ppermute | solution.py:399
  110.7 0.0 collective-permute-start.21
  110.7 3.6 %collective-permute-start.17 = (s16[256,256]{1,0:T(8,128)(2,1)S(1)}, s16[256,256]{1,0:T(8,128)(2,1)S(1)}, u32[]{:S(2)}, u32[]{:S(2)}) collective-permute-start(s16[256,256]{1,0:T(8,128)(2,1)S(1)} %get-tuple-element.136), channel_id=1, source_target_pairs={{0,4},{4,0},{8,12},{12,8},{1,5},{5,1},{9,13},{13,9},{2,6},{6,2},{1... | collective-permute-start | bytes 393224 | tf_op jit(solution)/shard_map/ppermute | solution.py:399
  114.3 4.0 %collective-permute-start.18 = (s16[256,256]{1,0:T(8,128)(2,1)S(1)}, s16[256,256]{1,0:T(8,128)(2,1)S(1)}, u32[]{:S(2)}, u32[]{:S(2)}) collective-permute-start(s16[256,256]{1,0:T(8,128)(2,1)S(1)} %get-tuple-element.137), channel_id=1, source_target_pairs={{0,12},{4,8},{8,4},{12,0},{1,13},{5,9},{9,5},{13,1},{2,14},{6,10},... | collective-permute-start | bytes 393224 | tf_op jit(solution)/shard_map/ppermute | solution.py:399
  118.3 0.0 collective-permute-done.21.refs_1_
  118.3 0.7 expand.6.refs_1_
  119.0 0.0 collective-permute-done.23.refs_0_
  119.1 2.4 %shrink.11 = (f32[48,128]{1,0:T(8,128)S(1)}, f32[48,128]{1,0:T(8,128)S(1)}) custom-call(s32[3]{0:T(128)S(1)} %get-tuple-element.150.plan_ref, s32[4,128]{1,0:T(4,128)S(1)} %get-tuple-element.122.ends_ref, s32[96,1]{1,0:T(8,128)S(1)} %get-tuple-element.141.which_ref, bf16[24,128,2048]{2,1,0:T(8,128)(2,1)S(1)} %bitcast.14, ...), custom_call_target="tpu_custom_call" | custom-call | flops 1 | bytes 1 | tf_op jit(solution)/shard_map/shrink/pallas_call | solution.py:243
  121.4 1.1 collective-permute-start.24
  122.6 2.8 %collective-permute-done.24 = f32[48,128]{1,0:T(8,128)S(1)} collective-permute-done((f32[48,128]{1,0:T(8,128)S(1)}, f32[48,128]{1,0:T(8,128)S(1)}, u32[]{:S(2)}, u32[]{:S(2)}) %collective-permute-start.24) | collective-permute-done | bytes 24608 | tf_op jit(solution)/shard_map/ppermute | solution.py:399
  125.3 0.0 collective-permute-start.25
  125.4 0.1 collective-permute-start.22
  125.4 1.1 collective-permute-done.25.refs_1_
  126.5 0.7 expand.7
  127.2 1.9 %collective-permute-start.26 = (s16[112,256]{1,0:T(8,128)(2,1)S(1)}, s16[112,256]{1,0:T(8,128)(2,1)S(1)}, u32[]{:S(2)}, u32[]{:S(2)}) collective-permute-start(s16[112,256]{1,0:T(8,128)(2,1)S(1)} %expand.7), channel_id=1, source_target_pairs={{0,8},{4,12},{8,0},{12,4},{1,9},{5,13},{9,1},{13,5},{2,10},{6,14},... | collective-permute-start | bytes 172040 | tf_op jit(solution)/shard_map/ppermute | solution.py:399
  129.1 0.0 collective-permute-done.17
  129.2 5.2 %collective-permute-done.22 = s16[160,256]{1,0:T(8,128)(2,1)S(1)} collective-permute-done((s16[160,256]{1,0:T(8,128)(2,1)S(1)}, s16[160,256]{1,0:T(8,128)(2,1)S(1)}, u32[]{:S(2)}, u32[]{:S(2)}) %collective-permute-start.22) | collective-permute-done | bytes 81952 | tf_op jit(solution)/shard_map/ppermute | solution.py:399
  134.4 0.9 collective-permute-done.26
  135.3 2.2 %conditional.1 = (bf16[768,256]{1,0:T(8,128)(2,1)S(1)}) conditional(s32[]{:T(128)} %bitcast.3, (s32[768,1]{1,0:T(8,128)S(1)}, f32[768,256]{1,0:T(8,128)}, f32[768,256]{1,0:T(8,128)S(1)}, s16[256,256]{1,0:T(8,128)(2,1)S(1)}, s16[256,256]{1,0:T(8,128)(2,1)S(1)}, /*index=5*/s16[160,256]{1,0:T(8,128)(2,1)S(1)}, s16[112,256]{1,0:T(8,128)(2,1)S(1)}) %tuple.25, ...), branch_computations={%region_1.0_spmd, %region_2.0_spmd} | conditional | flops 9219 | bytes 6306871 | solution.py:512
  135.5 2.0 %merge.2 = bf16[768,256]{1,0:T(8,128)(2,1)S(1)} custom-call(s32[768,1]{1,0:T(8,128)S(1)} %get-tuple-element.55.target_ref, f32[768,256]{1,0:T(8,128)} %get-tuple-element.56.refs_0_, f32[768,256]{1,0:T(8,128)S(1)} %get-tuple-element.57.refs_1_, s16[256,256]{1,0:T(8,128)(2,1)S(1)} %get-tuple-element.58.refs_2_, s16[256,256]{1,0:T(8,128)(2,1)S(1)} %get-tuple-element.59.refs_3_, ...), custom_call_target="tpu_custom_call" | custom-call | flops 1 | bytes 1 | tf_op jit(solution)/shard_map/cond/branch_0_fun/merge/pallas_call | solution.py:389
  137.5 0.0 copy-start.11
  137.5 0.7 copy-done.11
  (41 shorter events, 0.1 us)
Async XLA Ops:
  6.5 9.8 %copy-start = (bf16[768,2048]{1,0:T(8,128)(2,1)S(1)}, bf16[768,2048]{1,0:T(8,128)(2,1)}, u32[]{:S(2)}) copy-start(bf16[768,2048]{1,0:T(8,128)(2,1)} %tok_ref.7) | copy-start | bytes 9437188
  6.5 128.8 %reduce-scatter.2.cloned.1.call-start = ((), (), s32[]{:S(2)}) async-start(), calls=%async_computation.1 | async-start | bytes 3932160 | tf_op jit(solution)/shard_map/reduce_scatter | solution.py:436
  6.5 8.0 %collective-permute-start.10 = (s32[1,768]{1,0:T(1,128)}, s32[1,768]{1,0:T(1,128)S(1)}, u32[]{:S(2)}, u32[]{:S(2)}) collective-permute-start(s32[1,768]{1,0:T(1,128)} %bitcast.7), channel_id=1, source_target_pairs={{0,12},{4,8},{8,4},{12,0},{1,13},{5,9},{9,5},{13,1},{2,14},{6,10},... | collective-permute-start | bytes 9224 | tf_op jit(solution)/shard_map/ppermute | solution.py:399
  11.6 3.8 %collective-permute-start.8 = (s32[1,768]{1,0:T(1,128)}, s32[1,768]{1,0:T(1,128)S(1)}, u32[]{:S(2)}, u32[]{:S(2)}) collective-permute-start(s32[1,768]{1,0:T(1,128)} %bitcast.8), channel_id=1, source_target_pairs={{0,4},{4,0},{8,12},{12,8},{1,5},{5,1},{9,13},{13,9},{2,6},{6,2},{1... | collective-permute-start | bytes 9224 | tf_op jit(solution)/shard_map/ppermute | solution.py:399
  11.6 4.7 %collective-permute-start.9 = (s32[1,768]{1,0:T(1,128)}, s32[1,768]{1,0:T(1,128)S(1)}, u32[]{:S(2)}, u32[]{:S(2)}) collective-permute-start(s32[1,768]{1,0:T(1,128)} %bitcast.9), channel_id=1, source_target_pairs={{0,8},{4,12},{8,0},{12,4},{1,9},{5,13},{9,1},{13,5},{2,10},{6,14},... | collective-permute-start | bytes 9224 | tf_op jit(solution)/shard_map/ppermute | solution.py:399
  12.2 0.7 copy-start.5
  12.9 7.1 %copy-start.3 = (bf16[2048,1024]{1,0:T(8,128)(2,1)S(1)}, bf16[2048,1024]{1,0:T(8,128)(2,1)}, u32[]{:S(2)}) copy-start(bf16[2048,1024]{1,0:T(8,128)(2,1)} %weight_ref.1) | copy-start | bytes 12582916
  19.0 0.9 copy-start.7
  24.7 1.6 %copy-start.1 = (f32[768,1024]{1,0:T(8,128)}, f32[768,1024]{1,0:T(8,128)S(1)}, u32[]{:S(2)}) copy-start(f32[768,1024]{1,0:T(8,128)S(1)} %base.1.refs_0_) | copy-start | bytes 9437188
  26.3 1.0 copy-start.4
  27.3 2.3 %copy-start.6 = (s32[768,1]{0,1:T(1,128)S(1)}, s32[768,1]{0,1:T(1,128)}, u32[]{:S(2)}) copy-start(s32[768,1]{0,1:T(1,128)} %param.13) | copy-start | bytes 9220
  27.3 24.6 %collective-permute-start.12 = (bf16[240,2048]{1,0:T(8,128)(2,1)}, bf16[240,2048]{1,0:T(8,128)(2,1)}, u32[]{:S(2)}, u32[]{:S(2)}) collective-permute-start(bf16[240,2048]{1,0:T(8,128)(2,1)} %copy-done.4), channel_id=1, source_target_pairs={{0,4},{4,0},{8,12},{12,8},{1,5},{5,1},{9,13},{13,9},{2,6},{6,2},{1... | collective-permute-start | bytes 2949128 | tf_op jit(solution)/shard_map/ppermute | solution.py:399
  29.4 44.2 %collective-permute-start.13 = (bf16[240,2048]{1,0:T(8,128)(2,1)}, bf16[240,2048]{1,0:T(8,128)(2,1)}, u32[]{:S(2)}, u32[]{:S(2)}) collective-permute-start(bf16[240,2048]{1,0:T(8,128)(2,1)} %copy-done.7), channel_id=1, source_target_pairs={{0,12},{4,8},{8,4},{12,0},{1,13},{5,9},{9,5},{13,1},{2,14},{6,10},... | collective-permute-start | bytes 2949128 | tf_op jit(solution)/shard_map/ppermute | solution.py:399
  31.3 64.3 %collective-permute-start.11 = (s32[1,128]{1,0:T(1,128)S(1)}, s32[1,128]{1,0:T(1,128)S(1)}, u32[]{:S(2)}, u32[]{:S(2)}) collective-permute-start(s32[1,128]{1,0:T(1,128)S(1)} %get-tuple-element.116), channel_id=1, source_target_pairs={{0,16},{16,0},{1,17},{17,1},{2,18},{18,2},{3,19},{19,3},{4,20},{20... | collective-permute-start | bytes 1544 | tf_op jit(solution)/shard_map/ppermute | solution.py:399
  33.0 2.0 %copy-start.2 = (f32[768,1024]{1,0:T(8,128)S(1)}, f32[768,1024]{1,0:T(8,128)}, u32[]{:S(2)}) copy-start(f32[768,1024]{1,0:T(8,128)} %copy-done.1) | copy-start | bytes 9437188
  35.0 19.9 %slice-start = ((s8[12582912]{0:T(1024)(128)(4,1)}), s8[4194304]{0:T(1024)(128)(4,1)S(1)}, s32[]{:S(2)}) async-start(s8[12582912]{0:T(1024)(128)(4,1)} %bitcast.13), calls=%async_computation.2 | async-start | bytes 8388608
  38.4 16.5 %slice-start.1 = ((s8[12582912]{0:T(1024)(128)(4,1)}), s8[4194304]{0:T(1024)(128)(4,1)S(1)}, s32[]{:S(2)}) async-start(s8[12582912]{0:T(1024)(128)(4,1)} %bitcast.13), calls=%async_computation.3 | async-start | bytes 8388608
  38.4 16.5 %slice-start.2 = ((s8[12582912]{0:T(1024)(128)(4,1)}), s8[4194304]{0:T(1024)(128)(4,1)S(1)}, s32[]{:S(2)}) async-start(s8[12582912]{0:T(1024)(128)(4,1)} %bitcast.13), calls=%async_computation.4 | async-start | bytes 8388608
  53.8 46.6 %collective-permute-start.19 = (bf16[144,2048]{1,0:T(8,128)(2,1)S(1)}, bf16[144,2048]{1,0:T(8,128)(2,1)S(1)}, u32[]{:S(2)}, u32[]{:S(2)}) collective-permute-start(bf16[144,2048]{1,0:T(8,128)(2,1)S(1)} %get-tuple-element.127.refs_2_), channel_id=1, source_target_pairs={{0,8},{4,12},{8,0},{12,4},{1,9},{5,13},{9,1},{13,5},{2,10},{6,14},... | collective-permute-start | bytes 1769480 | tf_op jit(solution)/shard_map/ppermute | solution.py:399
  73.6 23.6 %copy-start.8 = (bf16[24,64,256]{2,1,0:T(8,128)(2,1)S(1)}, bf16[24,64,256]{2,1,0:T(8,128)(2,1)}, u32[]{:S(2)}) copy-start(bf16[24,64,256]{2,1,0:T(8,128)(2,1)} %param.11) | copy-start | bytes 2359300
  73.6 23.6 %copy-start.13 = (f32[24]{0:T(128)S(1)}, f32[24]{0:T(128)}, u32[]{:S(2)}) copy-start(f32[24]{0:T(128)} %param.12) | copy-start | bytes 292
  73.6 25.9 %copy-start.9 = (s32[768,1]{1,0:T(8,128)S(1)}, s32[768,1]{1,0:T(8,128)}, u32[]{:S(2)}) copy-start(s32[768,1]{1,0:T(8,128)} %get-tuple-element.117.target_ref) | copy-start | bytes 9220
  80.9 15.2 %collective-permute-start.15 = (f32[384,128]{1,0:T(8,128)S(1)}, f32[384,128]{1,0:T(8,128)S(1)}, u32[]{:S(2)}, u32[]{:S(2)}) collective-permute-start(f32[384,128]{1,0:T(8,128)S(1)} %constant_dynamic-update-slice_fusion.3), channel_id=1, source_target_pairs={{0,2},{1,3},{2,0},{3,1},{4,6},{5,7},{6,4},{7,5},{8,10},{9,11},{10,... | collective-permute-start | bytes 589832 | tf_op jit(solution)/shard_map/ppermute | solution.py:399
  82.7 13.4 %collective-permute-start.16 = (f32[384,128]{1,0:T(8,128)S(1)}, f32[384,128]{1,0:T(8,128)S(1)}, u32[]{:S(2)}, u32[]{:S(2)}) collective-permute-start(f32[384,128]{1,0:T(8,128)S(1)} %constant_dynamic-update-slice_fusion.3), channel_id=1, source_target_pairs={{0,3},{1,2},{2,1},{3,0},{4,7},{5,6},{6,5},{7,4},{8,11},{9,10},{10,... | collective-permute-start | bytes 589832 | tf_op jit(solution)/shard_map/ppermute | solution.py:399
  82.7 36.3 %collective-permute-start.23 = (bf16[96,2048]{1,0:T(8,128)(2,1)S(1)}, bf16[96,2048]{1,0:T(8,128)(2,1)S(1)}, u32[]{:S(2)}, u32[]{:S(2)}) collective-permute-start(bf16[96,2048]{1,0:T(8,128)(2,1)S(1)} %get-tuple-element.142), channel_id=1, source_target_pairs={{0,8},{4,12},{8,0},{12,4},{1,9},{5,13},{9,1},{13,5},{2,10},{6,14},... | collective-permute-start | bytes 1179656 | tf_op jit(solution)/shard_map/ppermute | solution.py:399
  95.7 1.5 %collective-permute-start.14 = (f32[384,128]{1,0:T(8,128)S(1)}, f32[384,128]{1,0:T(8,128)S(1)}, u32[]{:S(2)}, u32[]{:S(2)}) collective-permute-start(f32[384,128]{1,0:T(8,128)S(1)} %constant_dynamic-update-slice_fusion.refs_0_), channel_id=1, source_target_pairs={{0,1},{1,0},{2,3},{3,2},{4,5},{5,4},{6,7},{7,6},{8,9},{9,8},{10,11... | collective-permute-start | bytes 589832 | tf_op jit(solution)/shard_map/ppermute | solution.py:399
  106.6 4.0 %collective-permute-start.20 = (f32[72,128]{1,0:T(8,128)S(1)}, f32[72,128]{1,0:T(8,128)S(1)}, u32[]{:S(2)}, u32[]{:S(2)}) collective-permute-start(f32[72,128]{1,0:T(8,128)S(1)} %get-tuple-element.140), channel_id=1, source_target_pairs={{0,2},{2,0},{1,3},{3,1},{4,6},{6,4},{5,7},{7,5},{8,10},{10,8},{9,1... | collective-permute-start | bytes 110600 | tf_op jit(solution)/shard_map/ppermute | solution.py:399
  110.7 7.7 %collective-permute-start.21 = (f32[72,128]{1,0:T(8,128)S(1)}, f32[72,128]{1,0:T(8,128)S(1)}, u32[]{:S(2)}, u32[]{:S(2)}) collective-permute-start(f32[72,128]{1,0:T(8,128)S(1)} %add.15.refs_0_), channel_id=1, source_target_pairs={{0,1},{1,0},{2,3},{3,2},{4,5},{5,4},{6,7},{7,6},{8,9},{9,8},{10,11... | collective-permute-start | bytes 110600 | tf_op jit(solution)/shard_map/ppermute | solution.py:399
  110.7 18.5 %collective-permute-start.17 = (s16[256,256]{1,0:T(8,128)(2,1)S(1)}, s16[256,256]{1,0:T(8,128)(2,1)S(1)}, u32[]{:S(2)}, u32[]{:S(2)}) collective-permute-start(s16[256,256]{1,0:T(8,128)(2,1)S(1)} %get-tuple-element.136), channel_id=1, source_target_pairs={{0,4},{4,0},{8,12},{12,8},{1,5},{5,1},{9,13},{13,9},{2,6},{6,2},{1... | collective-permute-start | bytes 393224 | tf_op jit(solution)/shard_map/ppermute | solution.py:399
  114.3 14.8 %collective-permute-start.18 = (s16[256,256]{1,0:T(8,128)(2,1)S(1)}, s16[256,256]{1,0:T(8,128)(2,1)S(1)}, u32[]{:S(2)}, u32[]{:S(2)}) collective-permute-start(s16[256,256]{1,0:T(8,128)(2,1)S(1)} %get-tuple-element.137), channel_id=1, source_target_pairs={{0,12},{4,8},{8,4},{12,0},{1,13},{5,9},{9,5},{13,1},{2,14},{6,10},... | collective-permute-start | bytes 393224 | tf_op jit(solution)/shard_map/ppermute | solution.py:399
  119.0 16.3 %copy-start.15 = (bf16[48,2048]{1,0:T(8,128)(2,1)S(1)}, bf16[48,2048]{1,0:T(8,128)(2,1)}, u32[]{:S(2)}) copy-start(bf16[48,2048]{1,0:T(8,128)(2,1)} %get-tuple-element.145) | copy-start | bytes 589828
  119.1 16.3 %copy-start.16 = (bf16[48,2048]{1,0:T(8,128)(2,1)S(1)}, bf16[48,2048]{1,0:T(8,128)(2,1)}, u32[]{:S(2)}) copy-start(bf16[48,2048]{1,0:T(8,128)(2,1)} %get-tuple-element.146) | copy-start | bytes 589828
  119.1 16.3 %copy-start.17 = (bf16[48,2048]{1,0:T(8,128)(2,1)S(1)}, bf16[48,2048]{1,0:T(8,128)(2,1)}, u32[]{:S(2)}) copy-start(bf16[48,2048]{1,0:T(8,128)(2,1)} %get-tuple-element.147) | copy-start | bytes 589828
  121.4 3.9 %collective-permute-start.24 = (f32[48,128]{1,0:T(8,128)S(1)}, f32[48,128]{1,0:T(8,128)S(1)}, u32[]{:S(2)}, u32[]{:S(2)}) collective-permute-start(f32[48,128]{1,0:T(8,128)S(1)} %get-tuple-element.144), channel_id=1, source_target_pairs={{0,2},{2,0},{1,3},{3,1},{4,6},{6,4},{5,7},{7,5},{8,10},{10,8},{9,1... | collective-permute-start | bytes 73736 | tf_op jit(solution)/shard_map/ppermute | solution.py:399
  125.3 1.2 collective-permute-start.25
  125.4 9.1 %collective-permute-start.22 = (s16[160,256]{1,0:T(8,128)(2,1)S(1)}, s16[160,256]{1,0:T(8,128)(2,1)S(1)}, u32[]{:S(2)}, u32[]{:S(2)}) collective-permute-start(s16[160,256]{1,0:T(8,128)(2,1)S(1)} %expand.6.refs_1_), channel_id=1, source_target_pairs={{0,8},{4,12},{8,0},{12,4},{1,9},{5,13},{9,1},{13,5},{2,10},{6,14},... | collective-permute-start | bytes 245768 | tf_op jit(solution)/shard_map/ppermute | solution.py:399
  127.2 8.1 %collective-permute-start.26 = (s16[112,256]{1,0:T(8,128)(2,1)S(1)}, s16[112,256]{1,0:T(8,128)(2,1)S(1)}, u32[]{:S(2)}, u32[]{:S(2)}) collective-permute-start(s16[112,256]{1,0:T(8,128)(2,1)S(1)} %expand.7), channel_id=1, source_target_pairs={{0,8},{4,12},{8,0},{12,4},{1,9},{5,13},{9,1},{13,5},{2,10},{6,14},... | collective-permute-start | bytes 172040 | tf_op jit(solution)/shard_map/ppermute | solution.py:399
  137.5 0.7 copy-start.11
Sparse Core Ops, SparseCore 0:
  27.4 37.6 reduce-scatter.1

commit v13 on v12

--- a/solution.py
+++ b/solution.py
@@ -458,11 +458,12 @@
             for d in range(1, sharers)
         ]
 
-    def deltas_of(pieces, blocks, names, ends, plan, down, up, scale, later_than):
+    def deltas_of(pieces, blocks, names, ends, plan, down, up, scale, later_than, sooner=()):
         mine, other = shrink(pieces, blocks, names, ends, plan, down, later_than)
         sizes = tuple(b.shape[0] for b in blocks)
         lines = exchange(mine, other)
-        return expand(lines, (mine.shape[0],), names, scale, up, sizes)
+        groups = (mine.shape[0],)
+        return expand(lines, groups, names, scale, up, sizes, later_than=sooner)
 
     def send_back(pieces, deltas):
         return [swap(d, "dp", owners, p[0]) for p, d in zip(pieces, deltas)]
@@ -492,7 +493,7 @@
         blocks = [received[p] for p in pieces]
         waits = (deltas[0], parts[1], largest)
         deltas = deltas_of(
-            pieces, blocks, names[here + 1 + k], ends, plans[here + 1 + k], *weights, waits
+            pieces, blocks, names[here + 1 + k], ends, plans[here + 1 + k], *weights, waits, returned[-1:] if k else ()
         )
         returned += send_back(pieces, deltas)
         done += pieces

time: 145 us -> 145 us (level)
  starting transfers between devices: 38.1 us -> 39.7 us
  waiting for transfers between devices: 30.3 us -> 28.8 us
    ppermute x19, starting transfers between devices: 38.1 us -> 39.7 us  [swap(): return lax.ppermute(x, axes, [(i, i ^ distance) for i in range(size)])]
    ppermute x19, waiting for transfers between devices: 30.3 us -> 28.8 us  [swap(): return lax.ppermute(x, axes, [(i, i ^ distance) for i in range(size)])]
where the time goes in v13:
time: 145 us
  Pallas kernels  55.6 us (38%)
  starting transfers between devices  39.7 us (27%)
  waiting for transfers between devices  28.8 us (20%)
  between operations  13.7 us (9%)
  local copies, waits for them, and re-layouts  7.15 us (5%)
    ppermute x19, starting transfers between devices, swap(): return lax.ppermute(x, axes, [(i, i ^ distance) for i in range(size)])  39.7 us
    pallas_call x5, Pallas kernels, shrink(): pl.pallas_call(functools.partial(shrink_kernel, pieces, group, fine), gri...  33.3 us
    ppermute x19, waiting for transfers between devices, swap(): return lax.ppermute(x, axes, [(i, i ^ distance) for i in range(size)])  28.8 us
    pallas_call x3, Pallas kernels, sort_rows(): pl.pallas_call(functools.partial(sort_kernel, cap, pieces, len(later_than...  7.82 us
    unnamed x39, local copies, waits for them, and re-layouts  7.06 us
    pallas_call x1, Pallas kernels, base_product(): pl.pallas_call(base_kernel, grid=(columns // step,), in_specs=[pl.BlockSp...  4.71 us
    pallas_call x3, Pallas kernels, expand(): pl.pallas_call(functools.partial(expand_kernel, groups, sizes, len(lines)...  3.69 us
  transfers between devices with their start and end apart: 20, of which 10 were waited for; matrix products, arithmetic and copies ran while one was open for 0% of the time, Pallas kernels for 32%

profile of v13, /device:TPU:0, one launch (start us, length us, event | category | flops | bytes accessed | tf_op | source)
XLA Modules:
  0.0 145.2 jit_solution(2359331130111034447)
XLA Ops:
  6.5 5.0 %collective-permute-start.10 = (s32[1,768]{1,0:T(1,128)}, s32[1,768]{1,0:T(1,128)S(1)}, u32[]{:S(2)}, u32[]{:S(2)}) collective-permute-start(s32[1,768]{1,0:T(1,128)} %bitcast.7), channel_id=1, source_target_pairs={{0,12},{4,8},{8,4},{12,0},{1,13},{5,9},{9,5},{13,1},{2,14},{6,10},... | collective-permute-start | bytes 9224 | tf_op jit(solution)/shard_map/ppermute | solution.py:399
  11.6 0.0 collective-permute-start.8
  11.6 0.6 collective-permute-start.9
  12.2 0.7 copy-done.5
  12.9 1.6 %route.1 = (s32[1,768]{1,0:T(1,128)S(1)}, s32[768,1]{1,0:T(8,128)}) custom-call(s32[1]{0:T(128)} %bitcast.me_ref, s32[1,768]{1,0:T(1,128)S(1)} %bitcast.10), custom_call_target="tpu_custom_call" | custom-call | flops 1000000000 | bytes 1 | tf_op jit(solution)/shard_map/route/pallas_call | solution.py:54
  14.5 0.0 collective-permute-done.10.refs_3_.refs_2_
  14.5 0.9 collective-permute-done.8.refs_1_.refs_0_
  15.4 0.9 collective-permute-done.9.refs_2_.refs_1_
  16.3 2.7 %sort.3 = (bf16[240,2048]{1,0:T(8,128)(2,1)S(1)}, bf16[240,2048]{1,0:T(8,128)(2,1)S(1)}) custom-call(s32[1,768]{1,0:T(1,128)S(1)} %get-tuple-element.118.slot_ref, bf16[768,2048]{1,0:T(8,128)(2,1)S(1)} %copy-done, s32[1,768]{1,0:T(1,128)S(1)} %collective-permute-done.8.refs_1_.refs_0_, s32[1,768]{1,0:T(1,128)S(1)} %collective-permute-done.9.refs_2_.refs_1_, ...), custom_call_target="tpu_custom_call" | custom-call | flops 1000000000 | bytes 1 | tf_op jit(solution)/shard_map/sort/pallas_call | solution.py:89
  19.0 0.9 copy-done.7
  20.0 4.7 %base.1.refs_0_ = f32[768,1024]{1,0:T(8,128)S(1)} custom-call(bf16[768,2048]{1,0:T(8,128)(2,1)S(1)} %copy-done, bf16[2048,1024]{1,0:T(8,128)(2,1)S(1)} %copy-done.3, bf16[240,2048]{1,0:T(8,128)(2,1)S(1)} %get-tuple-element.119._), custom_call_target="tpu_custom_call" | custom-call | flops 1000000000 | bytes 1 | tf_op jit(solution)/shard_map/base/pallas_call | solution.py:170
  24.7 1.6 %copy-done.1 = f32[768,1024]{1,0:T(8,128)} copy-done((f32[768,1024]{1,0:T(8,128)}, f32[768,1024]{1,0:T(8,128)S(1)}, u32[]{:S(2)}) %copy-start.1) | copy-done | bytes 3145752
  26.3 1.0 copy-done.4
  27.3 0.0 reduce-scatter.2.cloned.1.call-update
  27.3 2.1 %collective-permute-start.12 = (bf16[240,2048]{1,0:T(8,128)(2,1)}, bf16[240,2048]{1,0:T(8,128)(2,1)}, u32[]{:S(2)}, u32[]{:S(2)}) collective-permute-start(bf16[240,2048]{1,0:T(8,128)(2,1)} %copy-done.4), channel_id=1, source_target_pairs={{0,4},{4,0},{8,12},{12,8},{1,5},{5,1},{9,13},{13,9},{2,6},{6,2},{1... | collective-permute-start | bytes 2949128 | tf_op jit(solution)/shard_map/ppermute | solution.py:399
  29.4 0.1 collective-permute-start.13
  29.5 0.1 pad_add_fusion.here_ref
  29.6 1.7 %name_rows.1 = (s32[288,1]{1,0:T(8,128)S(1)}, s32[240,1]{1,0:T(8,128)S(1)}, s32[240,1]{1,0:T(8,128)S(1)}, s32[768,1]{1,0:T(8,128)S(1)}, s32[144,1]{1,0:T(8,128)S...) custom-call(s32[2]{0:T(128)S(1)} %pad_add_fusion.here_ref, ...), custom_call_target="tpu_custom_call" | custom-call | flops 1 | bytes 1 | tf_op jit(solution)/shard_map/name_rows/pallas_call | solution.py:145
  31.3 1.7 %collective-permute-start.11 = (s32[1,128]{1,0:T(1,128)S(1)}, s32[1,128]{1,0:T(1,128)S(1)}, u32[]{:S(2)}, u32[]{:S(2)}) collective-permute-start(s32[1,128]{1,0:T(1,128)S(1)} %get-tuple-element.116), channel_id=1, source_target_pairs={{0,16},{16,0},{1,17},{17,1},{2,18},{18,2},{3,19},{19,3},{4,20},{20... | collective-permute-start | bytes 1544 | tf_op jit(solution)/shard_map/ppermute | solution.py:399
  33.0 2.0 %copy-done.2 = f32[768,1024]{1,0:T(8,128)S(1)} copy-done((f32[768,1024]{1,0:T(8,128)S(1)}, f32[768,1024]{1,0:T(8,128)}, u32[]{:S(2)}) %copy-start.2) | copy-done | bytes 3145752
  35.0 3.3 %sort.4 = (bf16[288,2048]{1,0:T(8,128)(2,1)S(1)}, bf16[48,2048]{1,0:T(8,128)(2,1)}, bf16[48,2048]{1,0:T(8,128)(2,1)}, bf16[48,2048]{1,0:T(8,128)(2,1)}) custom-call(s32[1,768]{1,0:T(1,128)S(1)} %get-tuple-element.118.slot_ref, bf16[768,2048]{1,0:T(8,128)(2,1)S(1)} %copy-done, f32[768,1024]{1,0:T(8,128)S(1)} %copy-done.2), custom_call_target="tpu_custom_call" | custom-call | flops 1000000000 | bytes 1 | tf_op jit(solution)/shard_map/sort/pallas_call | solution.py:89
  38.3 0.1 fusion
  38.4 10.0 %shrink.7 = (f32[144,128]{1,0:T(8,128)S(1)}, f32[144,128]{1,0:T(8,128)S(1)}) custom-call(s32[3]{0:T(128)S(1)} %get-tuple-element.154.plan_ref, s32[4,128]{1,0:T(4,128)S(1)} %get-tuple-element.122.ends_ref, s32[288,1]{1,0:T(8,128)S(1)} %get-tuple-element.123.which_ref, bf16[24,128,2048]{2,1,0:T(8,128)(2,1)} %down_ref.9, ...), custom_call_target="tpu_custom_call" | custom-call | flops 1 | bytes 1 | tf_op jit(solution)/shard_map/shrink/pallas_call | solution.py:243
  48.4 3.5 %collective-permute-done.12.refs_0_ = bf16[240,2048]{1,0:T(8,128)(2,1)} collective-permute-done((bf16[240,2048]{1,0:T(8,128)(2,1)}, bf16[240,2048]{1,0:T(8,128)(2,1)}, u32[]{:S(2)}, u32[]{:S(2)}) %collective-permute-start.12) | collective-permute-done | bytes 983072 | tf_op jit(solution)/shard_map/ppermute | solution.py:399
  52.0 1.8 %sort.5 = (bf16[144,2048]{1,0:T(8,128)(2,1)S(1)}, bf16[96,2048]{1,0:T(8,128)(2,1)S(1)}) custom-call(s32[1,768]{1,0:T(1,128)S(1)} %get-tuple-element.118.slot_ref, bf16[768,2048]{1,0:T(8,128)(2,1)S(1)} %copy-done, bf16[240,2048]{1,0:T(8,128)(2,1)} %collective-permute-done.12.refs_0_), custom_call_target="tpu_custom_call" | custom-call | flops 1000000000 | bytes 1 | tf_op jit(solution)/shard_map/sort/pallas_call | solution.py:89
  53.8 1.1 collective-permute-start.19
  54.9 7.3 %shrink.8 = (f32[120,128]{1,0:T(8,128)S(1)}, f32[120,128]{1,0:T(8,128)S(1)}) custom-call(s32[3]{0:T(128)S(1)} %get-tuple-element.153.plan_ref, s32[4,128]{1,0:T(4,128)S(1)} %get-tuple-element.122.ends_ref, s32[240,1]{1,0:T(8,128)S(1)} %get-tuple-element.126.which_ref, bf16[24,128,2048]{2,1,0:T(8,128)(2,1)S(1)} %bitcast.14, ...), custom_call_target="tpu_custom_call" | custom-call | flops 1 | bytes 1 | tf_op jit(solution)/shard_map/shrink/pallas_call | solution.py:243
  62.3 11.3 %collective-permute-done.13.refs_0_ = bf16[240,2048]{1,0:T(8,128)(2,1)} collective-permute-done((bf16[240,2048]{1,0:T(8,128)(2,1)}, bf16[240,2048]{1,0:T(8,128)(2,1)}, u32[]{:S(2)}, u32[]{:S(2)}) %collective-permute-start.13) | collective-permute-done | bytes 983072 | tf_op jit(solution)/shard_map/ppermute | solution.py:399
  73.6 7.3 %shrink.9 = (f32[120,128]{1,0:T(8,128)S(1)}, f32[120,128]{1,0:T(8,128)S(1)}) custom-call(s32[3]{0:T(128)S(1)} %get-tuple-element.152.plan_ref, s32[4,128]{1,0:T(4,128)S(1)} %get-tuple-element.122.ends_ref, s32[240,1]{1,0:T(8,128)S(1)} %get-tuple-element.129.which_ref, bf16[24,128,2048]{2,1,0:T(8,128)(2,1)S(1)} %bitcast.14, ...), custom_call_target="tpu_custom_call" | custom-call | flops 1 | bytes 1 | tf_op jit(solution)/shard_map/shrink/pallas_call | solution.py:243
  81.0 1.8 %collective-permute-start.15 = (f32[384,128]{1,0:T(8,128)S(1)}, f32[384,128]{1,0:T(8,128)S(1)}, u32[]{:S(2)}, u32[]{:S(2)}) collective-permute-start(f32[384,128]{1,0:T(8,128)S(1)} %constant_dynamic-update-slice_fusion.3), channel_id=1, source_target_pairs={{0,2},{1,3},{2,0},{3,1},{4,6},{5,7},{6,4},{7,5},{8,10},{9,11},{10,... | collective-permute-start | bytes 589832 | tf_op jit(solution)/shard_map/ppermute | solution.py:399
  82.7 0.0 collective-permute-start.16
  82.7 12.9 %collective-permute-start.23 = (bf16[96,2048]{1,0:T(8,128)(2,1)S(1)}, bf16[96,2048]{1,0:T(8,128)(2,1)S(1)}, u32[]{:S(2)}, u32[]{:S(2)}) collective-permute-start(bf16[96,2048]{1,0:T(8,128)(2,1)S(1)} %get-tuple-element.142), channel_id=1, source_target_pairs={{0,8},{4,12},{8,0},{12,4},{1,9},{5,13},{9,1},{13,5},{2,10},{6,14},... | collective-permute-start | bytes 1179656 | tf_op jit(solution)/shard_map/ppermute | solution.py:399
  95.7 0.0 collective-permute-done.11
  95.7 0.4 collective-permute-start.14
  96.1 0.0 collective-permute-done.15.refs_2_
  96.1 0.0 collective-permute-done.16.refs_3_
  96.1 1.1 collective-permute-done.14.refs_1_
  97.2 2.3 %expand.5 = (f32[288,256]{1,0:T(8,128)S(1)}, s16[256,256]{1,0:T(8,128)(2,1)S(1)}, s16[256,256]{1,0:T(8,128)(2,1)S(1)}) custom-call(s32[768,1]{1,0:T(8,128)S(1)} %get-tuple-element.120.which_ref, f32[1,24]{1,0:T(1,128)S(1)} %bitcast.19, bf16[1536,256]{1,0:T(8,128)(2,1)S(1)} %bitcast.15, f32[384,128]{1,0:T(8,128)S(1)} %constant_dynamic-update-slice_fusion.refs_0_, ...), custom_call_target="tpu_custom_call" | custom-call | flops 1 | bytes 1 | tf_op jit(solution)/shard_map/expand/pallas_call | solution.py:337
  99.5 0.8 place.1.refs_2_
  100.4 0.0 collective-permute-done.19.refs_0_
  100.4 5.8 %shrink.10 = (f32[72,128]{1,0:T(8,128)S(1)}, f32[72,128]{1,0:T(8,128)S(1)}) custom-call(s32[3]{0:T(128)S(1)} %get-tuple-element.151.plan_ref, s32[4,128]{1,0:T(4,128)S(1)} %get-tuple-element.122.ends_ref, s32[144,1]{1,0:T(8,128)S(1)} %get-tuple-element.138.which_ref, bf16[24,128,2048]{2,1,0:T(8,128)(2,1)S(1)} %bitcast.14, ...), custom_call_target="tpu_custom_call" | custom-call | flops 1 | bytes 1 | tf_op jit(solution)/shard_map/shrink/pallas_call | solution.py:243
  106.2 1.6 %collective-permute-start.20 = (f32[72,128]{1,0:T(8,128)S(1)}, f32[72,128]{1,0:T(8,128)S(1)}, u32[]{:S(2)}, u32[]{:S(2)}) collective-permute-start(f32[72,128]{1,0:T(8,128)S(1)} %get-tuple-element.140), channel_id=1, source_target_pairs={{0,2},{2,0},{1,3},{3,1},{4,6},{6,4},{5,7},{7,5},{8,10},{10,8},{9,1... | collective-permute-start | bytes 110600 | tf_op jit(solution)/shard_map/ppermute | solution.py:399
  107.8 2.5 %collective-permute-done.20 = f32[72,128]{1,0:T(8,128)S(1)} collective-permute-done((f32[72,128]{1,0:T(8,128)S(1)}, f32[72,128]{1,0:T(8,128)S(1)}, u32[]{:S(2)}, u32[]{:S(2)}) %collective-permute-start.20) | collective-permute-done | bytes 36896 | tf_op jit(solution)/shard_map/ppermute | solution.py:399
  110.3 0.0 collective-permute-start.21
  110.3 1.2 collective-permute-done.21.refs_1_
  111.5 0.7 expand.6.refs_1_
  112.2 5.7 %collective-permute-start.22 = (s16[160,256]{1,0:T(8,128)(2,1)S(1)}, s16[160,256]{1,0:T(8,128)(2,1)S(1)}, u32[]{:S(2)}, u32[]{:S(2)}) collective-permute-start(s16[160,256]{1,0:T(8,128)(2,1)S(1)} %expand.6.refs_1_), channel_id=1, source_target_pairs={{0,8},{4,12},{8,0},{12,4},{1,9},{5,13},{9,1},{13,5},{2,10},{6,14},... | collective-permute-start | bytes 245768 | tf_op jit(solution)/shard_map/ppermute | solution.py:399
  117.8 2.6 %collective-permute-start.17 = (s16[256,256]{1,0:T(8,128)(2,1)S(1)}, s16[256,256]{1,0:T(8,128)(2,1)S(1)}, u32[]{:S(2)}, u32[]{:S(2)}) collective-permute-start(s16[256,256]{1,0:T(8,128)(2,1)S(1)} %get-tuple-element.136), channel_id=1, source_target_pairs={{0,4},{4,0},{8,12},{12,8},{1,5},{5,1},{9,13},{13,9},{2,6},{6,2},{1... | collective-permute-start | bytes 393224 | tf_op jit(solution)/shard_map/ppermute | solution.py:399
  120.5 0.0 collective-permute-start.18
  120.5 0.0 collective-permute-done.23.refs_0_
  120.5 2.8 %shrink.11 = (f32[48,128]{1,0:T(8,128)S(1)}, f32[48,128]{1,0:T(8,128)S(1)}) custom-call(s32[3]{0:T(128)S(1)} %get-tuple-element.150.plan_ref, s32[4,128]{1,0:T(4,128)S(1)} %get-tuple-element.122.ends_ref, s32[96,1]{1,0:T(8,128)S(1)} %get-tuple-element.141.which_ref, bf16[24,128,2048]{2,1,0:T(8,128)(2,1)S(1)} %bitcast.14, ...), custom_call_target="tpu_custom_call" | custom-call | flops 1 | bytes 1 | tf_op jit(solution)/shard_map/shrink/pallas_call | solution.py:243
  123.3 2.1 %collective-permute-start.24 = (f32[48,128]{1,0:T(8,128)S(1)}, f32[48,128]{1,0:T(8,128)S(1)}, u32[]{:S(2)}, u32[]{:S(2)}) collective-permute-start(f32[48,128]{1,0:T(8,128)S(1)} %get-tuple-element.144), channel_id=1, source_target_pairs={{0,2},{2,0},{1,3},{3,1},{4,6},{6,4},{5,7},{7,5},{8,10},{10,8},{9,1... | collective-permute-start | bytes 73736 | tf_op jit(solution)/shard_map/ppermute | solution.py:399
  125.4 1.8 %collective-permute-done.24 = f32[48,128]{1,0:T(8,128)S(1)} collective-permute-done((f32[48,128]{1,0:T(8,128)S(1)}, f32[48,128]{1,0:T(8,128)S(1)}, u32[]{:S(2)}, u32[]{:S(2)}) %collective-permute-start.24) | collective-permute-done | bytes 24608 | tf_op jit(solution)/shard_map/ppermute | solution.py:399
  127.2 0.0 collective-permute-start.25
  127.2 1.2 collective-permute-done.25.refs_1_
  128.4 0.0 collective-permute-done.22.refs_2_
  128.4 0.7 expand.7
  129.1 1.9 %collective-permute-start.26 = (s16[112,256]{1,0:T(8,128)(2,1)S(1)}, s16[112,256]{1,0:T(8,128)(2,1)S(1)}, u32[]{:S(2)}, u32[]{:S(2)}) collective-permute-start(s16[112,256]{1,0:T(8,128)(2,1)S(1)} %expand.7), channel_id=1, source_target_pairs={{0,8},{4,12},{8,0},{12,4},{1,9},{5,13},{9,1},{13,5},{2,10},{6,14},... | collective-permute-start | bytes 172040 | tf_op jit(solution)/shard_map/ppermute | solution.py:399
  131.0 0.0 collective-permute-done.17
  131.1 4.4 %collective-permute-done.26 = s16[112,256]{1,0:T(8,128)(2,1)S(1)} collective-permute-done((s16[112,256]{1,0:T(8,128)(2,1)S(1)}, s16[112,256]{1,0:T(8,128)(2,1)S(1)}, u32[]{:S(2)}, u32[]{:S(2)}) %collective-permute-start.26) | collective-permute-done | bytes 57376 | tf_op jit(solution)/shard_map/ppermute | solution.py:399
  135.4 2.2 %conditional.1 = (bf16[768,256]{1,0:T(8,128)(2,1)S(1)}) conditional(s32[]{:T(128)} %bitcast.3, (s32[768,1]{1,0:T(8,128)S(1)}, f32[768,256]{1,0:T(8,128)}, f32[768,256]{1,0:T(8,128)S(1)}, s16[256,256]{1,0:T(8,128)(2,1)S(1)}, s16[256,256]{1,0:T(8,128)(2,1)S(1)}, /*index=5*/s16[160,256]{1,0:T(8,128)(2,1)S(1)}, s16[112,256]{1,0:T(8,128)(2,1)S(1)}) %tuple.25, ...), branch_computations={%region_1.0_spmd, %region_2.0_spmd} | conditional | flops 9219 | bytes 6306871 | solution.py:513
  135.6 2.0 %merge.2 = bf16[768,256]{1,0:T(8,128)(2,1)S(1)} custom-call(s32[768,1]{1,0:T(8,128)S(1)} %get-tuple-element.55.target_ref, f32[768,256]{1,0:T(8,128)} %get-tuple-element.56.refs_0_, f32[768,256]{1,0:T(8,128)S(1)} %get-tuple-element.57.refs_1_, s16[256,256]{1,0:T(8,128)(2,1)S(1)} %get-tuple-element.58.refs_2_, s16[256,256]{1,0:T(8,128)(2,1)S(1)} %get-tuple-element.59.refs_3_, ...), custom_call_target="tpu_custom_call" | custom-call | flops 1 | bytes 1 | tf_op jit(solution)/shard_map/cond/branch_0_fun/merge/pallas_call | solution.py:389
  137.6 0.0 copy-start.11
  137.6 0.7 copy-done.11
  (41 shorter events, 0.1 us)
Async XLA Ops:
  6.5 9.8 %copy-start = (bf16[768,2048]{1,0:T(8,128)(2,1)S(1)}, bf16[768,2048]{1,0:T(8,128)(2,1)}, u32[]{:S(2)}) copy-start(bf16[768,2048]{1,0:T(8,128)(2,1)} %tok_ref.7) | copy-start | bytes 9437188
  6.5 128.9 %reduce-scatter.2.cloned.1.call-start = ((), (), s32[]{:S(2)}) async-start(), calls=%async_computation.1 | async-start | bytes 3932160 | tf_op jit(solution)/shard_map/reduce_scatter | solution.py:436
  6.5 8.0 %collective-permute-start.10 = (s32[1,768]{1,0:T(1,128)}, s32[1,768]{1,0:T(1,128)S(1)}, u32[]{:S(2)}, u32[]{:S(2)}) collective-permute-start(s32[1,768]{1,0:T(1,128)} %bitcast.7), channel_id=1, source_target_pairs={{0,12},{4,8},{8,4},{12,0},{1,13},{5,9},{9,5},{13,1},{2,14},{6,10},... | collective-permute-start | bytes 9224 | tf_op jit(solution)/shard_map/ppermute | solution.py:399
  11.6 3.8 %collective-permute-start.8 = (s32[1,768]{1,0:T(1,128)}, s32[1,768]{1,0:T(1,128)S(1)}, u32[]{:S(2)}, u32[]{:S(2)}) collective-permute-start(s32[1,768]{1,0:T(1,128)} %bitcast.8), channel_id=1, source_target_pairs={{0,4},{4,0},{8,12},{12,8},{1,5},{5,1},{9,13},{13,9},{2,6},{6,2},{1... | collective-permute-start | bytes 9224 | tf_op jit(solution)/shard_map/ppermute | solution.py:399
  11.6 4.7 %collective-permute-start.9 = (s32[1,768]{1,0:T(1,128)}, s32[1,768]{1,0:T(1,128)S(1)}, u32[]{:S(2)}, u32[]{:S(2)}) collective-permute-start(s32[1,768]{1,0:T(1,128)} %bitcast.9), channel_id=1, source_target_pairs={{0,8},{4,12},{8,0},{12,4},{1,9},{5,13},{9,1},{13,5},{2,10},{6,14},... | collective-permute-start | bytes 9224 | tf_op jit(solution)/shard_map/ppermute | solution.py:399
  12.2 0.7 copy-start.5
  12.9 7.1 %copy-start.3 = (bf16[2048,1024]{1,0:T(8,128)(2,1)S(1)}, bf16[2048,1024]{1,0:T(8,128)(2,1)}, u32[]{:S(2)}) copy-start(bf16[2048,1024]{1,0:T(8,128)(2,1)} %weight_ref.1) | copy-start | bytes 12582916
  19.0 0.9 copy-start.7
  24.7 1.6 %copy-start.1 = (f32[768,1024]{1,0:T(8,128)}, f32[768,1024]{1,0:T(8,128)S(1)}, u32[]{:S(2)}) copy-start(f32[768,1024]{1,0:T(8,128)S(1)} %base.1.refs_0_) | copy-start | bytes 9437188
  26.3 1.0 copy-start.4
  27.3 2.3 %copy-start.6 = (s32[768,1]{0,1:T(1,128)S(1)}, s32[768,1]{0,1:T(1,128)}, u32[]{:S(2)}) copy-start(s32[768,1]{0,1:T(1,128)} %param.13) | copy-start | bytes 9220
  27.3 24.6 %collective-permute-start.12 = (bf16[240,2048]{1,0:T(8,128)(2,1)}, bf16[240,2048]{1,0:T(8,128)(2,1)}, u32[]{:S(2)}, u32[]{:S(2)}) collective-permute-start(bf16[240,2048]{1,0:T(8,128)(2,1)} %copy-done.4), channel_id=1, source_target_pairs={{0,4},{4,0},{8,12},{12,8},{1,5},{5,1},{9,13},{13,9},{2,6},{6,2},{1... | collective-permute-start | bytes 2949128 | tf_op jit(solution)/shard_map/ppermute | solution.py:399
  29.4 44.2 %collective-permute-start.13 = (bf16[240,2048]{1,0:T(8,128)(2,1)}, bf16[240,2048]{1,0:T(8,128)(2,1)}, u32[]{:S(2)}, u32[]{:S(2)}) collective-permute-start(bf16[240,2048]{1,0:T(8,128)(2,1)} %copy-done.7), channel_id=1, source_target_pairs={{0,12},{4,8},{8,4},{12,0},{1,13},{5,9},{9,5},{13,1},{2,14},{6,10},... | collective-permute-start | bytes 2949128 | tf_op jit(solution)/shard_map/ppermute | solution.py:399
  31.3 64.3 %collective-permute-start.11 = (s32[1,128]{1,0:T(1,128)S(1)}, s32[1,128]{1,0:T(1,128)S(1)}, u32[]{:S(2)}, u32[]{:S(2)}) collective-permute-start(s32[1,128]{1,0:T(1,128)S(1)} %get-tuple-element.116), channel_id=1, source_target_pairs={{0,16},{16,0},{1,17},{17,1},{2,18},{18,2},{3,19},{19,3},{4,20},{20... | collective-permute-start | bytes 1544 | tf_op jit(solution)/shard_map/ppermute | solution.py:399
  33.0 2.0 %copy-start.2 = (f32[768,1024]{1,0:T(8,128)S(1)}, f32[768,1024]{1,0:T(8,128)}, u32[]{:S(2)}) copy-start(f32[768,1024]{1,0:T(8,128)} %copy-done.1) | copy-start | bytes 9437188
  35.0 19.9 %slice-start = ((s8[12582912]{0:T(1024)(128)(4,1)}), s8[4194304]{0:T(1024)(128)(4,1)S(1)}, s32[]{:S(2)}) async-start(s8[12582912]{0:T(1024)(128)(4,1)} %bitcast.13), calls=%async_computation.2 | async-start | bytes 8388608
  38.4 16.5 %slice-start.1 = ((s8[12582912]{0:T(1024)(128)(4,1)}), s8[4194304]{0:T(1024)(128)(4,1)S(1)}, s32[]{:S(2)}) async-start(s8[12582912]{0:T(1024)(128)(4,1)} %bitcast.13), calls=%async_computation.3 | async-start | bytes 8388608
  38.4 16.5 %slice-start.2 = ((s8[12582912]{0:T(1024)(128)(4,1)}), s8[4194304]{0:T(1024)(128)(4,1)S(1)}, s32[]{:S(2)}) async-start(s8[12582912]{0:T(1024)(128)(4,1)} %bitcast.13), calls=%async_computation.4 | async-start | bytes 8388608
  53.8 46.6 %collective-permute-start.19 = (bf16[144,2048]{1,0:T(8,128)(2,1)S(1)}, bf16[144,2048]{1,0:T(8,128)(2,1)S(1)}, u32[]{:S(2)}, u32[]{:S(2)}) collective-permute-start(bf16[144,2048]{1,0:T(8,128)(2,1)S(1)} %get-tuple-element.127.refs_2_), channel_id=1, source_target_pairs={{0,8},{4,12},{8,0},{12,4},{1,9},{5,13},{9,1},{13,5},{2,10},{6,14},... | collective-permute-start | bytes 1769480 | tf_op jit(solution)/shard_map/ppermute | solution.py:399
  73.6 23.6 %copy-start.8 = (bf16[24,64,256]{2,1,0:T(8,128)(2,1)S(1)}, bf16[24,64,256]{2,1,0:T(8,128)(2,1)}, u32[]{:S(2)}) copy-start(bf16[24,64,256]{2,1,0:T(8,128)(2,1)} %param.11) | copy-start | bytes 2359300
  73.6 23.6 %copy-start.13 = (f32[24]{0:T(128)S(1)}, f32[24]{0:T(128)}, u32[]{:S(2)}) copy-start(f32[24]{0:T(128)} %param.12) | copy-start | bytes 292
  73.6 25.9 %copy-start.9 = (s32[768,1]{1,0:T(8,128)S(1)}, s32[768,1]{1,0:T(8,128)}, u32[]{:S(2)}) copy-start(s32[768,1]{1,0:T(8,128)} %get-tuple-element.117.target_ref) | copy-start | bytes 9220
  81.0 15.2 %collective-permute-start.15 = (f32[384,128]{1,0:T(8,128)S(1)}, f32[384,128]{1,0:T(8,128)S(1)}, u32[]{:S(2)}, u32[]{:S(2)}) collective-permute-start(f32[384,128]{1,0:T(8,128)S(1)} %constant_dynamic-update-slice_fusion.3), channel_id=1, source_target_pairs={{0,2},{1,3},{2,0},{3,1},{4,6},{5,7},{6,4},{7,5},{8,10},{9,11},{10,... | collective-permute-start | bytes 589832 | tf_op jit(solution)/shard_map/ppermute | solution.py:399
  82.7 13.4 %collective-permute-start.16 = (f32[384,128]{1,0:T(8,128)S(1)}, f32[384,128]{1,0:T(8,128)S(1)}, u32[]{:S(2)}, u32[]{:S(2)}) collective-permute-start(f32[384,128]{1,0:T(8,128)S(1)} %constant_dynamic-update-slice_fusion.3), channel_id=1, source_target_pairs={{0,3},{1,2},{2,1},{3,0},{4,7},{5,6},{6,5},{7,4},{8,11},{9,10},{10,... | collective-permute-start | bytes 589832 | tf_op jit(solution)/shard_map/ppermute | solution.py:399
  82.7 37.7 %collective-permute-start.23 = (bf16[96,2048]{1,0:T(8,128)(2,1)S(1)}, bf16[96,2048]{1,0:T(8,128)(2,1)S(1)}, u32[]{:S(2)}, u32[]{:S(2)}) collective-permute-start(bf16[96,2048]{1,0:T(8,128)(2,1)S(1)} %get-tuple-element.142), channel_id=1, source_target_pairs={{0,8},{4,12},{8,0},{12,4},{1,9},{5,13},{9,1},{13,5},{2,10},{6,14},... | collective-permute-start | bytes 1179656 | tf_op jit(solution)/shard_map/ppermute | solution.py:399
  95.7 1.5 %collective-permute-start.14 = (f32[384,128]{1,0:T(8,128)S(1)}, f32[384,128]{1,0:T(8,128)S(1)}, u32[]{:S(2)}, u32[]{:S(2)}) collective-permute-start(f32[384,128]{1,0:T(8,128)S(1)} %constant_dynamic-update-slice_fusion.refs_0_), channel_id=1, source_target_pairs={{0,1},{1,0},{2,3},{3,2},{4,5},{5,4},{6,7},{7,6},{8,9},{9,8},{10,11... | collective-permute-start | bytes 589832 | tf_op jit(solution)/shard_map/ppermute | solution.py:399
  106.2 4.0 %collective-permute-start.20 = (f32[72,128]{1,0:T(8,128)S(1)}, f32[72,128]{1,0:T(8,128)S(1)}, u32[]{:S(2)}, u32[]{:S(2)}) collective-permute-start(f32[72,128]{1,0:T(8,128)S(1)} %get-tuple-element.140), channel_id=1, source_target_pairs={{0,2},{2,0},{1,3},{3,1},{4,6},{6,4},{5,7},{7,5},{8,10},{10,8},{9,1... | collective-permute-start | bytes 110600 | tf_op jit(solution)/shard_map/ppermute | solution.py:399
  110.3 1.2 collective-permute-start.21
  112.2 16.2 %collective-permute-start.22 = (s16[160,256]{1,0:T(8,128)(2,1)S(1)}, s16[160,256]{1,0:T(8,128)(2,1)S(1)}, u32[]{:S(2)}, u32[]{:S(2)}) collective-permute-start(s16[160,256]{1,0:T(8,128)(2,1)S(1)} %expand.6.refs_1_), channel_id=1, source_target_pairs={{0,8},{4,12},{8,0},{12,4},{1,9},{5,13},{9,1},{13,5},{2,10},{6,14},... | collective-permute-start | bytes 245768 | tf_op jit(solution)/shard_map/ppermute | solution.py:399
  117.8 13.2 %collective-permute-start.17 = (s16[256,256]{1,0:T(8,128)(2,1)S(1)}, s16[256,256]{1,0:T(8,128)(2,1)S(1)}, u32[]{:S(2)}, u32[]{:S(2)}) collective-permute-start(s16[256,256]{1,0:T(8,128)(2,1)S(1)} %get-tuple-element.136), channel_id=1, source_target_pairs={{0,4},{4,0},{8,12},{12,8},{1,5},{5,1},{9,13},{13,9},{2,6},{6,2},{1... | collective-permute-start | bytes 393224 | tf_op jit(solution)/shard_map/ppermute | solution.py:399
  120.5 10.6 %collective-permute-start.18 = (s16[256,256]{1,0:T(8,128)(2,1)S(1)}, s16[256,256]{1,0:T(8,128)(2,1)S(1)}, u32[]{:S(2)}, u32[]{:S(2)}) collective-permute-start(s16[256,256]{1,0:T(8,128)(2,1)S(1)} %get-tuple-element.137), channel_id=1, source_target_pairs={{0,12},{4,8},{8,4},{12,0},{1,13},{5,9},{9,5},{13,1},{2,14},{6,10},... | collective-permute-start | bytes 393224 | tf_op jit(solution)/shard_map/ppermute | solution.py:399
  120.5 15.0 %copy-start.15 = (bf16[48,2048]{1,0:T(8,128)(2,1)S(1)}, bf16[48,2048]{1,0:T(8,128)(2,1)}, u32[]{:S(2)}) copy-start(bf16[48,2048]{1,0:T(8,128)(2,1)} %get-tuple-element.145) | copy-start | bytes 589828
  120.5 15.0 %copy-start.16 = (bf16[48,2048]{1,0:T(8,128)(2,1)S(1)}, bf16[48,2048]{1,0:T(8,128)(2,1)}, u32[]{:S(2)}) copy-start(bf16[48,2048]{1,0:T(8,128)(2,1)} %get-tuple-element.146) | copy-start | bytes 589828
  120.5 15.0 %copy-start.17 = (bf16[48,2048]{1,0:T(8,128)(2,1)S(1)}, bf16[48,2048]{1,0:T(8,128)(2,1)}, u32[]{:S(2)}) copy-start(bf16[48,2048]{1,0:T(8,128)(2,1)} %get-tuple-element.147) | copy-start | bytes 589828
  123.3 3.9 %collective-permute-start.24 = (f32[48,128]{1,0:T(8,128)S(1)}, f32[48,128]{1,0:T(8,128)S(1)}, u32[]{:S(2)}, u32[]{:S(2)}) collective-permute-start(f32[48,128]{1,0:T(8,128)S(1)} %get-tuple-element.144), channel_id=1, source_target_pairs={{0,2},{2,0},{1,3},{3,1},{4,6},{6,4},{5,7},{7,5},{8,10},{10,8},{9,1... | collective-permute-start | bytes 73736 | tf_op jit(solution)/shard_map/ppermute | solution.py:399
  127.2 1.2 collective-permute-start.25
  129.1 6.4 %collective-permute-start.26 = (s16[112,256]{1,0:T(8,128)(2,1)S(1)}, s16[112,256]{1,0:T(8,128)(2,1)S(1)}, u32[]{:S(2)}, u32[]{:S(2)}) collective-permute-start(s16[112,256]{1,0:T(8,128)(2,1)S(1)} %expand.7), channel_id=1, source_target_pairs={{0,8},{4,12},{8,0},{12,4},{1,9},{5,13},{9,1},{13,5},{2,10},{6,14},... | collective-permute-start | bytes 172040 | tf_op jit(solution)/shard_map/ppermute | solution.py:399
  137.6 0.7 copy-start.11
Sparse Core Ops, SparseCore 0:
  27.4 37.6 reduce-scatter.1

commit v14 on v13

--- a/solution.py
+++ b/solution.py
@@ -83,7 +83,7 @@
         begin += count
 
 
-def sort_rows(tokens, slot, cap, pieces, later_than=()):
+def sort_rows(tokens, slot, cap, pieces, later_than=(), kind=jax.ShapeDtypeStruct):
     rows, width = tokens.shape
     step = min(512, width)
     return pl.pallas_call(
@@ -95,7 +95,7 @@
         ]
         + [ANYWHERE] * len(later_than),
         out_specs=[pl.BlockSpec((count, step), lambda i: (0, i)) for _, _, count in pieces],
-        out_shape=[jax.ShapeDtypeStruct((count, width), BF16) for _, _, count in pieces],
+        out_shape=[kind((count, width), BF16) for _, _, count in pieces],
         scratch_shapes=[pltpu.VMEM((sum(c for _, _, c in pieces), rows), BF16)],
         compiler_params=PARAMS,
         cost_estimate=HEAD,
@@ -430,7 +430,7 @@
     ids_heard = [ids_row] + [swap(ids_row, "dp", owners, j) for j in range(1, owners)]
     slot, target = route(ids_row, me.reshape(1), owners, owned, cap)
     sent = far + [near]
-    packed = dict(zip(sent, sort_rows(tokens, slot, cap, sent, tuple(ids_heard[1:]))))
+    packed = dict(zip(sent, sort_rows(tokens, slot, cap, sent, tuple(ids_heard[1:]), pltpu.HBM)))
     received = {p: swap(packed[p], "dp", owners, p[0]) for p in sent}
     base_part = base_product(tokens, key_value_weight, packed[near])
     base = lax.psum_scatter(base_part, feature_axes, scatter_dimension=1, tiled=True)

time: 145 us -> 146 us (level)
    unnamed x39 -> x35, local copies, waits for them, and re-layouts: 7.06 us -> 6.37 us
  transfers between devices with their start and end apart: 20 -> 20, of which waited for: 10 -> 10; matrix products, arithmetic and copies ran while one was open for 0% -> 0% of each run, Pallas kernels for 32% -> 31%
where the time goes in v14:
time: 146 us
  Pallas kernels  56 us (38%)
  starting transfers between devices  39.6 us (27%)
  waiting for transfers between devices  29.6 us (20%)
  between operations  13.7 us (9%)
  local copies, waits for them, and re-layouts  6.46 us (4%)
    ppermute x19, starting transfers between devices, swap(): return lax.ppermute(x, axes, [(i, i ^ distance) for i in range(size)])  39.6 us
    pallas_call x5, Pallas kernels, shrink(): pl.pallas_call(functools.partial(shrink_kernel, pieces, group, fine), gri...  32.8 us
    ppermute x19, waiting for transfers between devices, swap(): return lax.ppermute(x, axes, [(i, i ^ distance) for i in range(size)])  29.6 us
    pallas_call x3, Pallas kernels, sort_rows(): pl.pallas_call(functools.partial(sort_kernel, cap, pieces, len(later_than...  8.58 us
    unnamed x35, local copies, waits for them, and re-layouts  6.37 us
    pallas_call x1, Pallas kernels, base_product(): pl.pallas_call(base_kernel, grid=(columns // step,), in_specs=[pl.BlockSp...  4.74 us
    pallas_call x3, Pallas kernels, expand(): pl.pallas_call(functools.partial(expand_kernel, groups, sizes, len(lines)...  3.69 us
  transfers between devices with their start and end apart: 20, of which 10 were waited for; matrix products, arithmetic and copies ran while one was open for 0% of the time, Pallas kernels for 31%

profile of v14, /device:TPU:0, one launch (start us, length us, event | category | flops | bytes accessed | tf_op | source)
XLA Modules:
  0.0 145.6 jit_solution(14346960809910869853)
XLA Ops:
  6.5 5.0 %collective-permute-start.10 = (s32[1,768]{1,0:T(1,128)}, s32[1,768]{1,0:T(1,128)S(1)}, u32[]{:S(2)}, u32[]{:S(2)}) collective-permute-start(s32[1,768]{1,0:T(1,128)} %bitcast.7), channel_id=1, source_target_pairs={{0,12},{4,8},{8,4},{12,0},{1,13},{5,9},{9,5},{13,1},{2,14},{6,10},... | collective-permute-start | bytes 9224 | tf_op jit(solution)/shard_map/ppermute | solution.py:399
  11.6 0.0 collective-permute-start.8
  11.6 0.6 collective-permute-start.9
  12.2 0.7 copy-done.5
  12.9 1.6 %route.1 = (s32[1,768]{1,0:T(1,128)S(1)}, s32[768,1]{1,0:T(8,128)}) custom-call(s32[1]{0:T(128)} %bitcast.me_ref, s32[1,768]{1,0:T(1,128)S(1)} %bitcast.10), custom_call_target="tpu_custom_call" | custom-call | flops 1000000000 | bytes 1 | tf_op jit(solution)/shard_map/route/pallas_call | solution.py:54
  14.5 0.0 collective-permute-done.10.refs_3_.refs_2_
  14.5 0.9 collective-permute-done.8.refs_1_.refs_0_
  15.4 0.9 collective-permute-done.9.refs_2_.refs_1_
  16.3 3.5 %sort.3 = (bf16[240,2048]{1,0:T(8,128)(2,1)}, bf16[240,2048]{1,0:T(8,128)(2,1)}) custom-call(s32[1,768]{1,0:T(1,128)S(1)} %get-tuple-element.118.slot_ref, bf16[768,2048]{1,0:T(8,128)(2,1)S(1)} %copy-done, s32[1,768]{1,0:T(1,128)S(1)} %collective-permute-done.8.refs_1_.refs_0_, s32[1,768]{1,0:T(1,128)S(1)} %collective-permute-done.9.refs_2_.refs_1_, ...), custom_call_target="tpu_custom_call" | custom-call | flops 1000000000 | bytes 1 | tf_op jit(solution)/shard_map/sort/pallas_call | solution.py:89
  19.8 1.2 copy-done.4
  21.0 4.7 %base.1.refs_0_ = f32[768,1024]{1,0:T(8,128)S(1)} custom-call(bf16[768,2048]{1,0:T(8,128)(2,1)S(1)} %copy-done, bf16[2048,1024]{1,0:T(8,128)(2,1)S(1)} %copy-done.3, bf16[240,2048]{1,0:T(8,128)(2,1)S(1)} %copy-done.4), custom_call_target="tpu_custom_call" | custom-call | flops 1000000000 | bytes 1 | tf_op jit(solution)/shard_map/base/pallas_call | solution.py:170
  25.8 1.6 %copy-done.1 = f32[768,1024]{1,0:T(8,128)} copy-done((f32[768,1024]{1,0:T(8,128)}, f32[768,1024]{1,0:T(8,128)S(1)}, u32[]{:S(2)}) %copy-start.1) | copy-done | bytes 3145752
  27.4 0.0 reduce-scatter.2.cloned.1.call-update
  27.4 2.1 %collective-permute-start.12 = (bf16[240,2048]{1,0:T(8,128)(2,1)}, bf16[240,2048]{1,0:T(8,128)(2,1)}, u32[]{:S(2)}, u32[]{:S(2)}) collective-permute-start(bf16[240,2048]{1,0:T(8,128)(2,1)} %get-tuple-element.119._), channel_id=1, source_target_pairs={{0,4},{4,0},{8,12},{12,8},{1,5},{5,1},{9,13},{13,9},{2,6},{6,2},{1... | collective-permute-start | bytes 2949128 | tf_op jit(solution)/shard_map/ppermute | solution.py:399
  29.5 0.1 collective-permute-start.13
  29.6 0.1 pad_add_fusion.here_ref
  29.7 1.7 %name_rows.1 = (s32[288,1]{1,0:T(8,128)S(1)}, s32[240,1]{1,0:T(8,128)S(1)}, s32[240,1]{1,0:T(8,128)S(1)}, s32[768,1]{1,0:T(8,128)S(1)}, s32[144,1]{1,0:T(8,128)S...) custom-call(s32[2]{0:T(128)S(1)} %pad_add_fusion.here_ref, ...), custom_call_target="tpu_custom_call" | custom-call | flops 1 | bytes 1 | tf_op jit(solution)/shard_map/name_rows/pallas_call | solution.py:145
  31.4 1.7 %collective-permute-start.11 = (s32[1,128]{1,0:T(1,128)S(1)}, s32[1,128]{1,0:T(1,128)S(1)}, u32[]{:S(2)}, u32[]{:S(2)}) collective-permute-start(s32[1,128]{1,0:T(1,128)S(1)} %get-tuple-element.116), channel_id=1, source_target_pairs={{0,16},{16,0},{1,17},{17,1},{2,18},{18,2},{3,19},{19,3},{4,20},{20... | collective-permute-start | bytes 1544 | tf_op jit(solution)/shard_map/ppermute | solution.py:399
  33.1 2.0 %copy-done.2 = f32[768,1024]{1,0:T(8,128)S(1)} copy-done((f32[768,1024]{1,0:T(8,128)S(1)}, f32[768,1024]{1,0:T(8,128)}, u32[]{:S(2)}) %copy-start.2) | copy-done | bytes 3145752
  35.1 3.2 %sort.4 = (bf16[288,2048]{1,0:T(8,128)(2,1)S(1)}, bf16[48,2048]{1,0:T(8,128)(2,1)S(1)}, bf16[48,2048]{1,0:T(8,128)(2,1)}, bf16[48,2048]{1,0:T(8,128)(2,1)}) custom-call(s32[1,768]{1,0:T(1,128)S(1)} %get-tuple-element.118.slot_ref, bf16[768,2048]{1,0:T(8,128)(2,1)S(1)} %copy-done, f32[768,1024]{1,0:T(8,128)S(1)} %copy-done.2), custom_call_target="tpu_custom_call" | custom-call | flops 1000000000 | bytes 1 | tf_op jit(solution)/shard_map/sort/pallas_call | solution.py:89
  38.4 0.1 fusion
  38.4 10.0 %shrink.7 = (f32[144,128]{1,0:T(8,128)S(1)}, f32[144,128]{1,0:T(8,128)S(1)}) custom-call(s32[3]{0:T(128)S(1)} %get-tuple-element.154.plan_ref, s32[4,128]{1,0:T(4,128)S(1)} %get-tuple-element.122.ends_ref, s32[288,1]{1,0:T(8,128)S(1)} %get-tuple-element.123.which_ref, bf16[24,128,2048]{2,1,0:T(8,128)(2,1)} %down_ref.9, ...), custom_call_target="tpu_custom_call" | custom-call | flops 1 | bytes 1 | tf_op jit(solution)/shard_map/shrink/pallas_call | solution.py:243
  48.5 3.5 %collective-permute-done.12.refs_0_ = bf16[240,2048]{1,0:T(8,128)(2,1)} collective-permute-done((bf16[240,2048]{1,0:T(8,128)(2,1)}, bf16[240,2048]{1,0:T(8,128)(2,1)}, u32[]{:S(2)}, u32[]{:S(2)}) %collective-permute-start.12) | collective-permute-done | bytes 983072 | tf_op jit(solution)/shard_map/ppermute | solution.py:399
  52.0 1.8 %sort.5 = (bf16[144,2048]{1,0:T(8,128)(2,1)S(1)}, bf16[96,2048]{1,0:T(8,128)(2,1)S(1)}) custom-call(s32[1,768]{1,0:T(1,128)S(1)} %get-tuple-element.118.slot_ref, bf16[768,2048]{1,0:T(8,128)(2,1)S(1)} %copy-done, bf16[240,2048]{1,0:T(8,128)(2,1)} %collective-permute-done.12.refs_0_), custom_call_target="tpu_custom_call" | custom-call | flops 1000000000 | bytes 1 | tf_op jit(solution)/shard_map/sort/pallas_call | solution.py:89
  53.9 1.1 collective-permute-start.19
  55.0 7.3 %shrink.8 = (f32[120,128]{1,0:T(8,128)S(1)}, f32[120,128]{1,0:T(8,128)S(1)}) custom-call(s32[3]{0:T(128)S(1)} %get-tuple-element.153.plan_ref, s32[4,128]{1,0:T(4,128)S(1)} %get-tuple-element.122.ends_ref, s32[240,1]{1,0:T(8,128)S(1)} %get-tuple-element.126.which_ref, bf16[24,128,2048]{2,1,0:T(8,128)(2,1)S(1)} %bitcast.14, ...), custom_call_target="tpu_custom_call" | custom-call | flops 1 | bytes 1 | tf_op jit(solution)/shard_map/shrink/pallas_call | solution.py:243
  62.4 11.3 %collective-permute-done.13.refs_0_ = bf16[240,2048]{1,0:T(8,128)(2,1)} collective-permute-done((bf16[240,2048]{1,0:T(8,128)(2,1)}, bf16[240,2048]{1,0:T(8,128)(2,1)}, u32[]{:S(2)}, u32[]{:S(2)}) %collective-permute-start.13) | collective-permute-done | bytes 983072 | tf_op jit(solution)/shard_map/ppermute | solution.py:399
  73.7 7.3 %shrink.9 = (f32[120,128]{1,0:T(8,128)S(1)}, f32[120,128]{1,0:T(8,128)S(1)}) custom-call(s32[3]{0:T(128)S(1)} %get-tuple-element.152.plan_ref, s32[4,128]{1,0:T(4,128)S(1)} %get-tuple-element.122.ends_ref, s32[240,1]{1,0:T(8,128)S(1)} %get-tuple-element.129.which_ref, bf16[24,128,2048]{2,1,0:T(8,128)(2,1)S(1)} %bitcast.14, ...), custom_call_target="tpu_custom_call" | custom-call | flops 1 | bytes 1 | tf_op jit(solution)/shard_map/shrink/pallas_call | solution.py:243
  81.0 1.7 %collective-permute-start.15 = (f32[384,128]{1,0:T(8,128)S(1)}, f32[384,128]{1,0:T(8,128)S(1)}, u32[]{:S(2)}, u32[]{:S(2)}) collective-permute-start(f32[384,128]{1,0:T(8,128)S(1)} %constant_dynamic-update-slice_fusion.3), channel_id=1, source_target_pairs={{0,2},{1,3},{2,0},{3,1},{4,6},{5,7},{6,4},{7,5},{8,10},{9,11},{10,... | collective-permute-start | bytes 589832 | tf_op jit(solution)/shard_map/ppermute | solution.py:399
  82.8 0.0 collective-permute-start.16
  82.8 12.9 %collective-permute-start.23 = (bf16[96,2048]{1,0:T(8,128)(2,1)S(1)}, bf16[96,2048]{1,0:T(8,128)(2,1)S(1)}, u32[]{:S(2)}, u32[]{:S(2)}) collective-permute-start(bf16[96,2048]{1,0:T(8,128)(2,1)S(1)} %get-tuple-element.142), channel_id=1, source_target_pairs={{0,8},{4,12},{8,0},{12,4},{1,9},{5,13},{9,1},{13,5},{2,10},{6,14},... | collective-permute-start | bytes 1179656 | tf_op jit(solution)/shard_map/ppermute | solution.py:399
  95.7 0.0 collective-permute-done.11
  95.7 0.4 collective-permute-start.14
  96.2 0.0 collective-permute-done.15.refs_2_
  96.2 0.0 collective-permute-done.16.refs_3_
  96.2 1.1 collective-permute-done.14.refs_1_
  97.3 2.3 %expand.5 = (f32[288,256]{1,0:T(8,128)S(1)}, s16[256,256]{1,0:T(8,128)(2,1)S(1)}, s16[256,256]{1,0:T(8,128)(2,1)S(1)}) custom-call(s32[768,1]{1,0:T(8,128)S(1)} %get-tuple-element.120.which_ref, f32[1,24]{1,0:T(1,128)S(1)} %bitcast.19, bf16[1536,256]{1,0:T(8,128)(2,1)S(1)} %bitcast.15, f32[384,128]{1,0:T(8,128)S(1)} %constant_dynamic-update-slice_fusion.refs_0_, ...), custom_call_target="tpu_custom_call" | custom-call | flops 1 | bytes 1 | tf_op jit(solution)/shard_map/expand/pallas_call | solution.py:337
  99.6 0.9 place.1.refs_2_
  100.5 0.0 collective-permute-done.19.refs_0_
  100.5 5.0 %shrink.10 = (f32[72,128]{1,0:T(8,128)S(1)}, f32[72,128]{1,0:T(8,128)S(1)}) custom-call(s32[3]{0:T(128)S(1)} %get-tuple-element.151.plan_ref, s32[4,128]{1,0:T(4,128)S(1)} %get-tuple-element.122.ends_ref, s32[144,1]{1,0:T(8,128)S(1)} %get-tuple-element.138.which_ref, bf16[24,128,2048]{2,1,0:T(8,128)(2,1)S(1)} %bitcast.14, ...), custom_call_target="tpu_custom_call" | custom-call | flops 1 | bytes 1 | tf_op jit(solution)/shard_map/shrink/pallas_call | solution.py:243
  105.4 1.6 %collective-permute-start.20 = (f32[72,128]{1,0:T(8,128)S(1)}, f32[72,128]{1,0:T(8,128)S(1)}, u32[]{:S(2)}, u32[]{:S(2)}) collective-permute-start(f32[72,128]{1,0:T(8,128)S(1)} %get-tuple-element.140), channel_id=1, source_target_pairs={{0,2},{2,0},{1,3},{3,1},{4,6},{6,4},{5,7},{7,5},{8,10},{10,8},{9,1... | collective-permute-start | bytes 110600 | tf_op jit(solution)/shard_map/ppermute | solution.py:399
  107.0 2.5 %collective-permute-done.20 = f32[72,128]{1,0:T(8,128)S(1)} collective-permute-done((f32[72,128]{1,0:T(8,128)S(1)}, f32[72,128]{1,0:T(8,128)S(1)}, u32[]{:S(2)}, u32[]{:S(2)}) %collective-permute-start.20) | collective-permute-done | bytes 36896 | tf_op jit(solution)/shard_map/ppermute | solution.py:399
  109.5 0.0 collective-permute-start.21
  109.5 1.2 collective-permute-done.21.refs_1_
  110.7 0.7 expand.6.refs_1_
  111.4 7.0 %collective-permute-start.22 = (s16[160,256]{1,0:T(8,128)(2,1)S(1)}, s16[160,256]{1,0:T(8,128)(2,1)S(1)}, u32[]{:S(2)}, u32[]{:S(2)}) collective-permute-start(s16[160,256]{1,0:T(8,128)(2,1)S(1)} %expand.6.refs_1_), channel_id=1, source_target_pairs={{0,8},{4,12},{8,0},{12,4},{1,9},{5,13},{9,1},{13,5},{2,10},{6,14},... | collective-permute-start | bytes 245768 | tf_op jit(solution)/shard_map/ppermute | solution.py:399
  118.4 2.2 %collective-permute-start.17 = (s16[256,256]{1,0:T(8,128)(2,1)S(1)}, s16[256,256]{1,0:T(8,128)(2,1)S(1)}, u32[]{:S(2)}, u32[]{:S(2)}) collective-permute-start(s16[256,256]{1,0:T(8,128)(2,1)S(1)} %get-tuple-element.136), channel_id=1, source_target_pairs={{0,4},{4,0},{8,12},{12,8},{1,5},{5,1},{9,13},{13,9},{2,6},{6,2},{1... | collective-permute-start | bytes 393224 | tf_op jit(solution)/shard_map/ppermute | solution.py:399
  120.5 0.0 collective-permute-start.18
  120.5 0.0 collective-permute-done.23.refs_0_
  120.6 3.2 %shrink.11 = (f32[48,128]{1,0:T(8,128)S(1)}, f32[48,128]{1,0:T(8,128)S(1)}) custom-call(s32[3]{0:T(128)S(1)} %get-tuple-element.150.plan_ref, s32[4,128]{1,0:T(4,128)S(1)} %get-tuple-element.122.ends_ref, s32[96,1]{1,0:T(8,128)S(1)} %get-tuple-element.141.which_ref, bf16[24,128,2048]{2,1,0:T(8,128)(2,1)S(1)} %bitcast.14, ...), custom_call_target="tpu_custom_call" | custom-call | flops 1 | bytes 1 | tf_op jit(solution)/shard_map/shrink/pallas_call | solution.py:243
  123.8 2.1 %collective-permute-start.24 = (f32[48,128]{1,0:T(8,128)S(1)}, f32[48,128]{1,0:T(8,128)S(1)}, u32[]{:S(2)}, u32[]{:S(2)}) collective-permute-start(f32[48,128]{1,0:T(8,128)S(1)} %get-tuple-element.144), channel_id=1, source_target_pairs={{0,2},{2,0},{1,3},{3,1},{4,6},{6,4},{5,7},{7,5},{8,10},{10,8},{9,1... | collective-permute-start | bytes 73736 | tf_op jit(solution)/shard_map/ppermute | solution.py:399
  125.9 1.8 %collective-permute-done.24 = f32[48,128]{1,0:T(8,128)S(1)} collective-permute-done((f32[48,128]{1,0:T(8,128)S(1)}, f32[48,128]{1,0:T(8,128)S(1)}, u32[]{:S(2)}, u32[]{:S(2)}) %collective-permute-start.24) | collective-permute-done | bytes 24608 | tf_op jit(solution)/shard_map/ppermute | solution.py:399
  127.7 0.0 collective-permute-start.25
  127.7 1.2 collective-permute-done.25.refs_1_
  128.9 0.0 collective-permute-done.22.refs_2_
  128.9 0.7 expand.7
  129.6 1.1 collective-permute-start.26
  130.7 0.0 collective-permute-done.17
  130.7 0.0 collective-permute-done.18
  130.7 5.2 %collective-permute-done.26 = s16[112,256]{1,0:T(8,128)(2,1)S(1)} collective-permute-done((s16[112,256]{1,0:T(8,128)(2,1)S(1)}, s16[112,256]{1,0:T(8,128)(2,1)S(1)}, u32[]{:S(2)}, u32[]{:S(2)}) %collective-permute-start.26) | collective-permute-done | bytes 57376 | tf_op jit(solution)/shard_map/ppermute | solution.py:399
  135.9 2.2 %conditional.1 = (bf16[768,256]{1,0:T(8,128)(2,1)S(1)}) conditional(s32[]{:T(128)} %bitcast.3, (s32[768,1]{1,0:T(8,128)S(1)}, f32[768,256]{1,0:T(8,128)}, f32[768,256]{1,0:T(8,128)S(1)}, s16[256,256]{1,0:T(8,128)(2,1)S(1)}, s16[256,256]{1,0:T(8,128)(2,1)S(1)}, /*index=5*/s16[160,256]{1,0:T(8,128)(2,1)S(1)}, s16[112,256]{1,0:T(8,128)(2,1)S(1)}) %tuple.25, ...), branch_computations={%region_1.0_spmd, %region_2.0_spmd} | conditional | flops 9219 | bytes 6304127 | solution.py:513
  136.1 2.0 %merge.2 = bf16[768,256]{1,0:T(8,128)(2,1)S(1)} custom-call(s32[768,1]{1,0:T(8,128)S(1)} %get-tuple-element.55.target_ref, f32[768,256]{1,0:T(8,128)} %get-tuple-element.56.refs_0_, f32[768,256]{1,0:T(8,128)S(1)} %get-tuple-element.57.refs_1_, s16[256,256]{1,0:T(8,128)(2,1)S(1)} %get-tuple-element.58.refs_2_, s16[256,256]{1,0:T(8,128)(2,1)S(1)} %get-tuple-element.59.refs_3_, ...), custom_call_target="tpu_custom_call" | custom-call | flops 1 | bytes 1 | tf_op jit(solution)/shard_map/cond/branch_0_fun/merge/pallas_call | solution.py:389
  138.0 0.0 copy-start.10
  138.1 0.7 copy-done.10
  (37 shorter events, 0.1 us)
Async XLA Ops:
  6.5 9.8 %copy-start = (bf16[768,2048]{1,0:T(8,128)(2,1)S(1)}, bf16[768,2048]{1,0:T(8,128)(2,1)}, u32[]{:S(2)}) copy-start(bf16[768,2048]{1,0:T(8,128)(2,1)} %tok_ref.7) | copy-start | bytes 9437188
  6.5 129.3 %reduce-scatter.2.cloned.1.call-start = ((), (), s32[]{:S(2)}) async-start(), calls=%async_computation.1 | async-start | bytes 3932160 | tf_op jit(solution)/shard_map/reduce_scatter | solution.py:436
  6.5 8.0 %collective-permute-start.10 = (s32[1,768]{1,0:T(1,128)}, s32[1,768]{1,0:T(1,128)S(1)}, u32[]{:S(2)}, u32[]{:S(2)}) collective-permute-start(s32[1,768]{1,0:T(1,128)} %bitcast.7), channel_id=1, source_target_pairs={{0,12},{4,8},{8,4},{12,0},{1,13},{5,9},{9,5},{13,1},{2,14},{6,10},... | collective-permute-start | bytes 9224 | tf_op jit(solution)/shard_map/ppermute | solution.py:399
  11.6 3.8 %collective-permute-start.8 = (s32[1,768]{1,0:T(1,128)}, s32[1,768]{1,0:T(1,128)S(1)}, u32[]{:S(2)}, u32[]{:S(2)}) collective-permute-start(s32[1,768]{1,0:T(1,128)} %bitcast.8), channel_id=1, source_target_pairs={{0,4},{4,0},{8,12},{12,8},{1,5},{5,1},{9,13},{13,9},{2,6},{6,2},{1... | collective-permute-start | bytes 9224 | tf_op jit(solution)/shard_map/ppermute | solution.py:399
  11.6 4.7 %collective-permute-start.9 = (s32[1,768]{1,0:T(1,128)}, s32[1,768]{1,0:T(1,128)S(1)}, u32[]{:S(2)}, u32[]{:S(2)}) collective-permute-start(s32[1,768]{1,0:T(1,128)} %bitcast.9), channel_id=1, source_target_pairs={{0,8},{4,12},{8,0},{12,4},{1,9},{5,13},{9,1},{13,5},{2,10},{6,14},... | collective-permute-start | bytes 9224 | tf_op jit(solution)/shard_map/ppermute | solution.py:399
  12.2 0.7 copy-start.5
  12.9 7.0 %copy-start.3 = (bf16[2048,1024]{1,0:T(8,128)(2,1)S(1)}, bf16[2048,1024]{1,0:T(8,128)(2,1)}, u32[]{:S(2)}) copy-start(bf16[2048,1024]{1,0:T(8,128)(2,1)} %weight_ref.1) | copy-start | bytes 12582916
  19.8 1.2 copy-start.4
  25.8 1.6 %copy-start.1 = (f32[768,1024]{1,0:T(8,128)}, f32[768,1024]{1,0:T(8,128)S(1)}, u32[]{:S(2)}) copy-start(f32[768,1024]{1,0:T(8,128)S(1)} %base.1.refs_0_) | copy-start | bytes 9437188
  27.4 2.3 %copy-start.6 = (s32[768,1]{0,1:T(1,128)S(1)}, s32[768,1]{0,1:T(1,128)}, u32[]{:S(2)}) copy-start(s32[768,1]{0,1:T(1,128)} %param.13) | copy-start | bytes 9220
  27.4 24.6 %collective-permute-start.12 = (bf16[240,2048]{1,0:T(8,128)(2,1)}, bf16[240,2048]{1,0:T(8,128)(2,1)}, u32[]{:S(2)}, u32[]{:S(2)}) collective-permute-start(bf16[240,2048]{1,0:T(8,128)(2,1)} %get-tuple-element.119._), channel_id=1, source_target_pairs={{0,4},{4,0},{8,12},{12,8},{1,5},{5,1},{9,13},{13,9},{2,6},{6,2},{1... | collective-permute-start | bytes 2949128 | tf_op jit(solution)/shard_map/ppermute | solution.py:399
  29.5 44.2 %collective-permute-start.13 = (bf16[240,2048]{1,0:T(8,128)(2,1)}, bf16[240,2048]{1,0:T(8,128)(2,1)}, u32[]{:S(2)}, u32[]{:S(2)}) collective-permute-start(bf16[240,2048]{1,0:T(8,128)(2,1)} %get-tuple-element.130), channel_id=1, source_target_pairs={{0,12},{4,8},{8,4},{12,0},{1,13},{5,9},{9,5},{13,1},{2,14},{6,10},... | collective-permute-start | bytes 2949128 | tf_op jit(solution)/shard_map/ppermute | solution.py:399
  31.4 64.3 %collective-permute-start.11 = (s32[1,128]{1,0:T(1,128)S(1)}, s32[1,128]{1,0:T(1,128)S(1)}, u32[]{:S(2)}, u32[]{:S(2)}) collective-permute-start(s32[1,128]{1,0:T(1,128)S(1)} %get-tuple-element.116), channel_id=1, source_target_pairs={{0,16},{16,0},{1,17},{17,1},{2,18},{18,2},{3,19},{19,3},{4,20},{20... | collective-permute-start | bytes 1544 | tf_op jit(solution)/shard_map/ppermute | solution.py:399
  33.1 2.0 %copy-start.2 = (f32[768,1024]{1,0:T(8,128)S(1)}, f32[768,1024]{1,0:T(8,128)}, u32[]{:S(2)}) copy-start(f32[768,1024]{1,0:T(8,128)} %copy-done.1) | copy-start | bytes 9437188
  35.1 19.9 %slice-start = ((s8[12582912]{0:T(1024)(128)(4,1)}), s8[4194304]{0:T(1024)(128)(4,1)S(1)}, s32[]{:S(2)}) async-start(s8[12582912]{0:T(1024)(128)(4,1)} %bitcast.13), calls=%async_computation.2 | async-start | bytes 8388608
  38.4 16.6 %slice-start.1 = ((s8[12582912]{0:T(1024)(128)(4,1)}), s8[4194304]{0:T(1024)(128)(4,1)S(1)}, s32[]{:S(2)}) async-start(s8[12582912]{0:T(1024)(128)(4,1)} %bitcast.13), calls=%async_computation.3 | async-start | bytes 8388608
  38.4 16.6 %slice-start.2 = ((s8[12582912]{0:T(1024)(128)(4,1)}), s8[4194304]{0:T(1024)(128)(4,1)S(1)}, s32[]{:S(2)}) async-start(s8[12582912]{0:T(1024)(128)(4,1)} %bitcast.13), calls=%async_computation.4 | async-start | bytes 8388608
  53.9 46.6 %collective-permute-start.19 = (bf16[144,2048]{1,0:T(8,128)(2,1)S(1)}, bf16[144,2048]{1,0:T(8,128)(2,1)S(1)}, u32[]{:S(2)}, u32[]{:S(2)}) collective-permute-start(bf16[144,2048]{1,0:T(8,128)(2,1)S(1)} %get-tuple-element.127.refs_2_), channel_id=1, source_target_pairs={{0,8},{4,12},{8,0},{12,4},{1,9},{5,13},{9,1},{13,5},{2,10},{6,14},... | collective-permute-start | bytes 1769480 | tf_op jit(solution)/shard_map/ppermute | solution.py:399
  73.7 23.6 %copy-start.7 = (bf16[24,64,256]{2,1,0:T(8,128)(2,1)S(1)}, bf16[24,64,256]{2,1,0:T(8,128)(2,1)}, u32[]{:S(2)}) copy-start(bf16[24,64,256]{2,1,0:T(8,128)(2,1)} %param.11) | copy-start | bytes 2359300
  73.7 23.6 %copy-start.11 = (f32[24]{0:T(128)S(1)}, f32[24]{0:T(128)}, u32[]{:S(2)}) copy-start(f32[24]{0:T(128)} %param.12) | copy-start | bytes 292
  73.7 25.9 %copy-start.8 = (s32[768,1]{1,0:T(8,128)S(1)}, s32[768,1]{1,0:T(8,128)}, u32[]{:S(2)}) copy-start(s32[768,1]{1,0:T(8,128)} %get-tuple-element.117.target_ref) | copy-start | bytes 9220
  81.0 15.1 %collective-permute-start.15 = (f32[384,128]{1,0:T(8,128)S(1)}, f32[384,128]{1,0:T(8,128)S(1)}, u32[]{:S(2)}, u32[]{:S(2)}) collective-permute-start(f32[384,128]{1,0:T(8,128)S(1)} %constant_dynamic-update-slice_fusion.3), channel_id=1, source_target_pairs={{0,2},{1,3},{2,0},{3,1},{4,6},{5,7},{6,4},{7,5},{8,10},{9,11},{10,... | collective-permute-start | bytes 589832 | tf_op jit(solution)/shard_map/ppermute | solution.py:399
  82.8 13.4 %collective-permute-start.16 = (f32[384,128]{1,0:T(8,128)S(1)}, f32[384,128]{1,0:T(8,128)S(1)}, u32[]{:S(2)}, u32[]{:S(2)}) collective-permute-start(f32[384,128]{1,0:T(8,128)S(1)} %constant_dynamic-update-slice_fusion.3), channel_id=1, source_target_pairs={{0,3},{1,2},{2,1},{3,0},{4,7},{5,6},{6,5},{7,4},{8,11},{9,10},{10,... | collective-permute-start | bytes 589832 | tf_op jit(solution)/shard_map/ppermute | solution.py:399
  82.8 37.8 %collective-permute-start.23 = (bf16[96,2048]{1,0:T(8,128)(2,1)S(1)}, bf16[96,2048]{1,0:T(8,128)(2,1)S(1)}, u32[]{:S(2)}, u32[]{:S(2)}) collective-permute-start(bf16[96,2048]{1,0:T(8,128)(2,1)S(1)} %get-tuple-element.142), channel_id=1, source_target_pairs={{0,8},{4,12},{8,0},{12,4},{1,9},{5,13},{9,1},{13,5},{2,10},{6,14},... | collective-permute-start | bytes 1179656 | tf_op jit(solution)/shard_map/ppermute | solution.py:399
  95.7 1.5 %collective-permute-start.14 = (f32[384,128]{1,0:T(8,128)S(1)}, f32[384,128]{1,0:T(8,128)S(1)}, u32[]{:S(2)}, u32[]{:S(2)}) collective-permute-start(f32[384,128]{1,0:T(8,128)S(1)} %constant_dynamic-update-slice_fusion.refs_0_), channel_id=1, source_target_pairs={{0,1},{1,0},{2,3},{3,2},{4,5},{5,4},{6,7},{7,6},{8,9},{9,8},{10,11... | collective-permute-start | bytes 589832 | tf_op jit(solution)/shard_map/ppermute | solution.py:399
  105.4 4.0 %collective-permute-start.20 = (f32[72,128]{1,0:T(8,128)S(1)}, f32[72,128]{1,0:T(8,128)S(1)}, u32[]{:S(2)}, u32[]{:S(2)}) collective-permute-start(f32[72,128]{1,0:T(8,128)S(1)} %get-tuple-element.140), channel_id=1, source_target_pairs={{0,2},{2,0},{1,3},{3,1},{4,6},{6,4},{5,7},{7,5},{8,10},{10,8},{9,1... | collective-permute-start | bytes 110600 | tf_op jit(solution)/shard_map/ppermute | solution.py:399
  109.5 1.2 collective-permute-start.21
  111.4 17.5 %collective-permute-start.22 = (s16[160,256]{1,0:T(8,128)(2,1)S(1)}, s16[160,256]{1,0:T(8,128)(2,1)S(1)}, u32[]{:S(2)}, u32[]{:S(2)}) collective-permute-start(s16[160,256]{1,0:T(8,128)(2,1)S(1)} %expand.6.refs_1_), channel_id=1, source_target_pairs={{0,8},{4,12},{8,0},{12,4},{1,9},{5,13},{9,1},{13,5},{2,10},{6,14},... | collective-permute-start | bytes 245768 | tf_op jit(solution)/shard_map/ppermute | solution.py:399
  118.4 12.3 %collective-permute-start.17 = (s16[256,256]{1,0:T(8,128)(2,1)S(1)}, s16[256,256]{1,0:T(8,128)(2,1)S(1)}, u32[]{:S(2)}, u32[]{:S(2)}) collective-permute-start(s16[256,256]{1,0:T(8,128)(2,1)S(1)} %get-tuple-element.136), channel_id=1, source_target_pairs={{0,4},{4,0},{8,12},{12,8},{1,5},{5,1},{9,13},{13,9},{2,6},{6,2},{1... | collective-permute-start | bytes 393224 | tf_op jit(solution)/shard_map/ppermute | solution.py:399
  120.5 10.2 %collective-permute-start.18 = (s16[256,256]{1,0:T(8,128)(2,1)S(1)}, s16[256,256]{1,0:T(8,128)(2,1)S(1)}, u32[]{:S(2)}, u32[]{:S(2)}) collective-permute-start(s16[256,256]{1,0:T(8,128)(2,1)S(1)} %get-tuple-element.137), channel_id=1, source_target_pairs={{0,12},{4,8},{8,4},{12,0},{1,13},{5,9},{9,5},{13,1},{2,14},{6,10},... | collective-permute-start | bytes 393224 | tf_op jit(solution)/shard_map/ppermute | solution.py:399
  120.5 15.3 %copy-start.12 = (bf16[48,2048]{1,0:T(8,128)(2,1)S(1)}, bf16[48,2048]{1,0:T(8,128)(2,1)}, u32[]{:S(2)}) copy-start(bf16[48,2048]{1,0:T(8,128)(2,1)} %get-tuple-element.146) | copy-start | bytes 589828
  120.5 15.3 %copy-start.13 = (bf16[48,2048]{1,0:T(8,128)(2,1)S(1)}, bf16[48,2048]{1,0:T(8,128)(2,1)}, u32[]{:S(2)}) copy-start(bf16[48,2048]{1,0:T(8,128)(2,1)} %get-tuple-element.147) | copy-start | bytes 589828
  123.8 3.9 %collective-permute-start.24 = (f32[48,128]{1,0:T(8,128)S(1)}, f32[48,128]{1,0:T(8,128)S(1)}, u32[]{:S(2)}, u32[]{:S(2)}) collective-permute-start(f32[48,128]{1,0:T(8,128)S(1)} %get-tuple-element.144), channel_id=1, source_target_pairs={{0,2},{2,0},{1,3},{3,1},{4,6},{6,4},{5,7},{7,5},{8,10},{10,8},{9,1... | collective-permute-start | bytes 73736 | tf_op jit(solution)/shard_map/ppermute | solution.py:399
  127.7 1.2 collective-permute-start.25
  129.6 6.3 %collective-permute-start.26 = (s16[112,256]{1,0:T(8,128)(2,1)S(1)}, s16[112,256]{1,0:T(8,128)(2,1)S(1)}, u32[]{:S(2)}, u32[]{:S(2)}) collective-permute-start(s16[112,256]{1,0:T(8,128)(2,1)S(1)} %expand.7), channel_id=1, source_target_pairs={{0,8},{4,12},{8,0},{12,4},{1,9},{5,13},{9,1},{13,5},{2,10},{6,14},... | collective-permute-start | bytes 172040 | tf_op jit(solution)/shard_map/ppermute | solution.py:399
  138.0 0.7 copy-start.10
Sparse Core Ops, SparseCore 0:
  27.5 37.6 reduce-scatter.1
